TPU v7x, 32 devices: a whole 2x2x4 slice. The times are simulated.
32 devices in a mesh: row: 8 (over z, y), col: 4 (over x, core).
Axes of the slice: x: 2, y: 2, z: 4, core: 2. Of those that a mesh axis runs over, the one named last changes fastest.
Arguments:
- object_field: float32 [2, 1024, 512], P(None, 'row', 'col'), may hold values from -4.2 to 4.2
- probe: float32 [2, 128, 128], replicated, may hold values from -8.4 to 8.4
- positions: int32 [8, 4, 2, 4, 2], P('row', 'col'), may hold values from -64 to 64
- counts: int32 [8, 4, 2], P('row', 'col'), may hold values from 1 to 4, as said below
- amplitude: float32 [8, 4, 2, 4, 128, 128], P('row', 'col'), may hold values from 0.5 to 4
Outputs:
- object_out: float32 [2, 1024, 512], P(None, 'row', 'col')
- probe_out: float32 [2, 128, 128], replicated
Inputs may be any that keep to these rules, and one draw needn't show every extreme that they name: `counts`: some tile has all 4 slots live in some mini-batch.
All inputs are finite; a program needn't handle non-finite values.
Results may differ from a plain program's by a relative error of at most 0.00013.
Values sent between devices are 32-bit elements; how exact they have to be, the bound alone decides.
No kernel may reach another device: no remote copies, remote signals or barrier semaphores. Data moves between devices by JAX's collectives and lax.ppermute only.
A program may use at most 64 MiB of HBM per device.

v0:
```python
import functools
import math

import jax
import jax.numpy as jnp
import numpy as np
from jax import lax
from jax.experimental import pallas as pl
from jax.experimental.pallas import tpu as pltpu
from jax.sharding import PartitionSpec as P

RIM = 64
TILE = 8
AXES = ("row", "col")


def dft_tables(size):
    index = np.arange(size)
    angle = (index[:, None] * index[None, :] % size) * (-2.0 * math.pi / size)
    cosine = np.cos(angle) / math.sqrt(size)
    sine = np.sin(angle) / math.sqrt(size)
    full = np.block([[cosine, -sine], [sine, cosine]]).astype(np.float32)
    flip = np.ascontiguousarray(full.T)
    tables = []
    for table in (full, flip):
        high = table.astype(jnp.bfloat16)
        tables += [high, (table - high.astype(np.float32)).astype(jnp.bfloat16)]
    return np.stack(tables)


def split(value):
    high = value.astype(jnp.bfloat16)
    return high, (value - high.astype(jnp.float32)).astype(jnp.bfloat16)


def mul(left, right):
    return jnp.dot(left, right, preferred_element_type=jnp.float32)


def left_product(high, low, value):
    first, second = split(value)
    return mul(high, first) + (mul(high, second) + mul(low, first))


def right_product(value, high, low):
    first, second = split(value)
    return mul(first, high) + (mul(second, high) + mul(first, low))


def slots_kernel(starts, count, field, probe, amps, tables, sums, probe_sums):
    width = probe.shape[1]
    tiles = width // TILE
    lane = lax.broadcasted_iota(jnp.int32, (width + TILE, width), 1)
    sub = lax.broadcasted_iota(jnp.int32, (tiles, TILE, width), 1)
    sums[...] = jnp.zeros_like(sums)
    full_h, full_l, flip_h, flip_l = (tables[k] for k in range(4))
    pro_r, pro_i = probe[0], probe[1]
    weight = pro_r * pro_r + pro_i * pro_i
    total = None
    for slot in range(amps.shape[0]):
        row = starts[2 * slot] + RIM
        col = starts[2 * slot + 1]
        live = jnp.where(slot < count[0], 1.0, 0.0).astype(jnp.float32)
        base = pl.multiple_of(row // TILE * TILE, TILE)
        rows = pl.ds(base, width + TILE)
        skew = row - base
        lift = jnp.where(skew > 0, TILE - skew, 0)
        back = jnp.where(col > 0, width - col, -col)
        ahead = jnp.where(col < 0, width + col, col)
        outside = (lane < col) | (lane >= width + col)

        def window(part):
            mixed = jnp.where(outside, field[part, rows, width:], field[part, rows, :width])
            turned = pltpu.roll(mixed.reshape(tiles + 1, TILE, width), lift, 1)
            lined = jnp.where(sub < TILE - skew, turned[:-1], turned[1:])
            return pltpu.roll(lined.reshape(width, width), back, 1)

        win_r, win_i = window(0), window(1)
        psi_r = pro_r * win_r - pro_i * win_i
        psi_i = pro_r * win_i + pro_i * win_r
        half = left_product(full_h, full_l, jnp.concatenate([psi_r, psi_i], 0))
        far = right_product(jnp.concatenate([half[:width], half[width:]], 1), flip_h, flip_l)
        far_r, far_i = far[:, :width], far[:, width:]
        factor = amps[slot] * lax.rsqrt(jnp.maximum(far_r * far_r + far_i * far_i, 1.0))
        half = left_product(
            flip_h, flip_l, jnp.concatenate([far_r * factor, far_i * factor], 0)
        )
        back_ = right_product(jnp.concatenate([half[:width], half[width:]], 1), full_h, full_l)
        chi_r = (back_[:, :width] - psi_r) * live
        chi_i = (back_[:, width:] - psi_i) * live

        def deposit(part, term):
            moved = pltpu.roll(term, ahead, 1).reshape(tiles, TILE, width)
            turned = pltpu.roll(moved, skew, 1)
            late = jnp.where(sub < skew, turned, 0.0)
            soon = turned - late
            blank = jnp.zeros((1, TILE, width), jnp.float32)
            grown = jnp.concatenate([soon, blank], 0) + jnp.concatenate([blank, late], 0)
            grown = grown.reshape(width + TILE, width)
            sums[part, rows, :width] += jnp.where(outside, 0.0, grown)
            sums[part, rows, width:] += jnp.where(outside, grown, 0.0)

        deposit(0, pro_r * chi_r + pro_i * chi_i)
        deposit(1, pro_r * chi_i - pro_i * chi_r)
        deposit(2, weight * live)
        terms = (
            win_r * chi_r + win_i * chi_i,
            win_r * chi_i - win_i * chi_r,
            (win_r * win_r + win_i * win_i) * live,
        )
        total = terms if total is None else tuple(a + b for a, b in zip(total, terms))
    for part in range(3):
        probe_sums[part] = total[part]


def slot_sums(starts, count, field, probe, amps, tables):
    width = probe.shape[1]
    vmem = pl.BlockSpec(memory_space=pltpu.VMEM)
    smem = pl.BlockSpec(memory_space=pltpu.SMEM)
    slots = amps.shape[0]
    return pl.pallas_call(
        slots_kernel,
        out_shape=(
            jax.ShapeDtypeStruct((3,) + field.shape[1:], jnp.float32),
            jax.ShapeDtypeStruct((3, width, width), jnp.float32),
        ),
        in_specs=[smem, smem, vmem, vmem, vmem, vmem],
        out_specs=(vmem, vmem),
        compiler_params=pltpu.CompilerParams(vmem_limit_bytes=24 * 1024 * 1024),
        cost_estimate=pl.CostEstimate(
            flops=slots * 4 * 2 * 3 * width * width * width * 4,
            bytes_accessed=4 * 1024 * 1024,
            transcendentals=slots * width * width,
        ),
    )(starts, count, field, probe, amps, tables)


def shift(value, axis, step):
    count = lax.axis_size(axis)
    pairs = [(i, i + step) for i in range(count) if 0 <= i + step < count]
    return lax.ppermute(value, axis, pairs)


def swap(value, axis, bit):
    return lax.ppermute(value, axis, [(i, i ^ bit) for i in range(lax.axis_size(axis))])


def together(*values):
    return lax.optimization_barrier(values)


def extend(tile):
    side = tile.shape[2]
    above = shift(tile[:, side - RIM :], "row", 1)
    below = shift(tile[:, :RIM], "row", -1)
    tall = jnp.concatenate([above, tile, below, jnp.zeros_like(tile[:, :TILE])], 1)
    before = shift(jnp.concatenate([tall[0, :, side - RIM :], tall[1, :, side - RIM :]], 1), "col", 1)
    after = shift(jnp.concatenate([tall[0, :, :RIM], tall[1, :, :RIM]], 1), "col", -1)
    sides = jnp.stack(
        [
            jnp.concatenate([after[:, :RIM], before[:, :RIM]], 1),
            jnp.concatenate([after[:, RIM:], before[:, RIM:]], 1),
        ]
    )
    return jnp.concatenate([tall, sides], 2)


def fold(sums, side):
    before = shift(sums[:, :, side : side + RIM], "col", 1)
    after = shift(sums[:, :, side + RIM :], "col", -1)
    tall = sums[:, :, :side] + jnp.concatenate([before, after], 2)
    above = shift(tall[:, RIM + side : 2 * RIM + side], "row", 1)
    below = shift(tall[:, :RIM], "row", -1)
    return tall[:, RIM : RIM + side] + jnp.concatenate([above, below], 1)


def total_over_devices(value):
    rows = value.shape[0] * value.shape[1]
    flat = value.reshape(rows, value.shape[2])
    half = rows // 2
    odd = lax.axis_index("col") % 2
    keep = jnp.where(odd == 0, flat[:half], flat[half:])
    give = jnp.where(odd == 0, flat[half:], flat[:half])
    part = keep + swap(give, "col", 1)
    for axis, first in (("col", 2), ("row", 1)):
        bit = first
        while bit < lax.axis_size(axis):
            part = part + swap(part, axis, bit)
            bit *= 2
    other = swap(part, "col", 1)
    low = jnp.where(odd == 0, part, other)
    high = jnp.where(odd == 0, other, part)
    return jnp.concatenate([low, high], 0).reshape(value.shape)


def body(object_field, probe, positions, counts, amplitude):
    side = object_field.shape[1]
    width = probe.shape[1]
    tables = jnp.asarray(dft_tables(width))
    tile = object_field
    current = probe
    for step in range(positions.shape[2]):
        field = extend(tile)
        starts = positions[0, 0, step].reshape(-1)
        count = counts[0, 0, step].reshape(1)
        sums, probe_sums = slot_sums(starts, count, field, current, amplitude[0, 0, step], tables)
        totals = total_over_devices(probe_sums)
        folded = fold(sums, side)
        tile = tile + folded[0:2] / (folded[2] + 0.1)[None]
        current = current + totals[0:2] / (totals[2] + 0.1)[None]
    return (tile, current)


def solution(mesh):
    return jax.shard_map(
        body,
        mesh=mesh,
        in_specs=(
            P(None, "row", "col"),
            P(),
            P("row", "col", None, None, None),
            P("row", "col", None),
            P("row", "col", None, None, None, None),
        ),
        out_specs=(P(None, "row", "col"), P()),
        check_vma=False,
    )
```

profile of v0, /device:TPU:0, one launch (start us, length us, event | category | flops | bytes accessed | tf_op | source)
XLA Modules:
  0.0 114.7 jit_solution(1077231496626133512)
XLA Ops:
  0.6 0.9 fusion.15
  1.5 4.9 %collective-permute-start = (f32[2,64,128]{2,1,0:T(8,128)S(1)}, f32[2,64,128]{2,1,0:T(8,128)S(1)}, u32[]{:S(2)}, u32[]{:S(2)}) collective-permute-start(f32[2,64,128]{2,1,0:T(8,128)S(1)} %get-tuple-element.42), channel_id=1, source_target_pairs={{0,4},{4,8},{8,12},{12,16},{16,20},{20,24},{24,28},{1,5},{5,9},{9,... | collective-permute-start | bytes 196616 | tf_op jit(solution)/shard_map/ppermute | solution.py:141
  6.4 1.4 %collective-permute-start.1 = (f32[2,64,128]{2,1,0:T(8,128)S(1)}, f32[2,64,128]{2,1,0:T(8,128)S(1)}, u32[]{:S(2)}, u32[]{:S(2)}) collective-permute-start(f32[2,64,128]{2,1,0:T(8,128)S(1)} %get-tuple-element.43), channel_id=1, source_target_pairs={{4,0},{8,4},{12,8},{16,12},{20,16},{24,20},{28,24},{5,1},{9,5},{13... | collective-permute-start | bytes 196616 | tf_op jit(solution)/shard_map/ppermute | solution.py:141
  7.9 1.1 slice_bitcast_fusion
  9.0 3.8 %collective-permute-done.1 = f32[2,64,128]{2,1,0:T(8,128)S(1)} collective-permute-done((f32[2,64,128]{2,1,0:T(8,128)S(1)}, f32[2,64,128]{2,1,0:T(8,128)S(1)}, u32[]{:S(2)}, u32[]{:S(2)}) %collective-permute-start.1) | collective-permute-done | bytes 65568 | tf_op jit(solution)/shard_map/ppermute | solution.py:141
  12.7 0.1 slice_bitcast_fusion.9
  12.9 0.1 pad_maximum_fusion.5
  13.0 1.3 %collective-permute-start.3 = (f32[264,128]{1,0:T(8,128)S(1)}, f32[264,128]{1,0:T(8,128)S(1)}, u32[]{:S(2)}, u32[]{:S(2)}) collective-permute-start(f32[264,128]{1,0:T(8,128)S(1)} %pad_maximum_fusion.5), channel_id=1, source_target_pairs={{0,1},{1,2},{2,3},{4,5},{5,6},{6,7},{8,9},{9,10},{10,11},{12,13},{... | collective-permute-start | bytes 405512 | tf_op jit(solution)/shard_map/ppermute | solution.py:141
  14.3 0.6 fusion.17
  15.1 0.1 pad_maximum_fusion.4
  15.2 1.3 %collective-permute-start.2 = (f32[264,128]{1,0:T(8,128)S(1)}, f32[264,128]{1,0:T(8,128)S(1)}, u32[]{:S(2)}, u32[]{:S(2)}) collective-permute-start(f32[264,128]{1,0:T(8,128)S(1)} %pad_maximum_fusion.4), channel_id=1, source_target_pairs={{1,0},{2,1},{3,2},{5,4},{6,5},{7,6},{9,8},{10,9},{11,10},{13,12},{... | collective-permute-start | bytes 405512 | tf_op jit(solution)/shard_map/ppermute | solution.py:141
  16.5 0.1 fusion.13
  16.6 3.6 %collective-permute-done.2 = f32[264,128]{1,0:T(8,128)S(1)} collective-permute-done((f32[264,128]{1,0:T(8,128)S(1)}, f32[264,128]{1,0:T(8,128)S(1)}, u32[]{:S(2)}, u32[]{:S(2)}) %collective-permute-start.2) | collective-permute-done | bytes 135200 | tf_op jit(solution)/shard_map/ppermute | solution.py:141
  20.3 0.1 maximum_bitcast_fusion
  20.5 0.8 copy-done
  21.3 0.2 copy-done.1
  21.5 4.6 %shard_map.77 = (f32[3,264,256]{2,1,0:T(8,128)S(1)}, f32[3,128,128]{2,1,0:T(8,128)S(1)}) custom-call(s32[8]{0:T(128)S(1)} %reshape_squeeze.12.starts, s32[1]{0:T(128)} %bitcast.count, f32[2,264,256]{2,1,0:T(8,128)S(1)} %fusion.field, f32[2,128,128]{2,1,0:T(8,128)S(1)} %copy-done, f32[4,128,128]{2,1,0:T(8,128)S(1)} %get-tuple-element.15.amps, ...), custom_call_target="tpu_custom_call" | custom-call | flops 805306368 | bytes 4194304 | tf_op jit(solution)/shard_map/pallas_call | solution.py:121
  26.2 3.7 %collective-permute-start.12 = (f32[192,128]{1,0:T(8,128)S(1)}, f32[192,128]{1,0:T(8,128)S(1)}, u32[]{:S(2)}, u32[]{:S(2)}) collective-permute-start(f32[192,128]{1,0:T(8,128)S(1)} %slice_select_fusion.1), channel_id=1, source_target_pairs={{0,1},{1,0},{2,3},{3,2},{4,5},{5,4},{6,7},{7,6},{8,9},{9,8},{10,11... | collective-permute-start | bytes 294920 | tf_op jit(solution)/shard_map/ppermute | solution.py:145
  29.9 0.2 fusion.7
  30.1 1.9 %collective-permute-start.4 = (f32[3,264,64]{2,1,0:T(8,128)S(1)}, f32[3,264,64]{2,1,0:T(8,128)S(1)}, u32[]{:S(2)}, u32[]{:S(2)}) collective-permute-start(f32[3,264,64]{2,1,0:T(8,128)S(1)} %get-tuple-element.12), channel_id=1, source_target_pairs={{0,1},{1,2},{2,3},{4,5},{5,6},{6,7},{8,9},{9,10},{10,11},{12,13},{... | collective-permute-start | bytes 608264 | tf_op jit(solution)/shard_map/ppermute | solution.py:141
  32.0 1.3 %collective-permute-start.5 = (f32[3,264,64]{2,1,0:T(8,128)S(1)}, f32[3,264,64]{2,1,0:T(8,128)S(1)}, u32[]{:S(2)}, u32[]{:S(2)}) collective-permute-start(f32[3,264,64]{2,1,0:T(8,128)S(1)} %get-tuple-element.13), channel_id=1, source_target_pairs={{1,0},{2,1},{3,2},{5,4},{6,5},{7,6},{9,8},{10,9},{11,10},{13,12},{... | collective-permute-start | bytes 608264 | tf_op jit(solution)/shard_map/ppermute | solution.py:141
  33.3 2.3 %collective-permute-start.13 = (f32[192,128]{1,0:T(8,128)S(1)}, f32[192,128]{1,0:T(8,128)S(1)}, u32[]{:S(2)}, u32[]{:S(2)}) collective-permute-start(f32[192,128]{1,0:T(8,128)S(1)} %select_add_fusion.1), channel_id=1, source_target_pairs={{0,2},{1,3},{2,0},{3,1},{4,6},{5,7},{6,4},{7,5},{8,10},{9,11},{10,... | collective-permute-start | bytes 294920 | tf_op jit(solution)/shard_map/ppermute | solution.py:145
  35.7 0.2 maximum_add_fusion
  35.9 4.3 %collective-permute-start.6 = (f32[3,64,128]{2,1,0:T(8,128)S(1)}, f32[3,64,128]{2,1,0:T(8,128)S(1)}, u32[]{:S(2)}, u32[]{:S(2)}) collective-permute-start(f32[3,64,128]{2,1,0:T(8,128)S(1)} %get-tuple-element.18), channel_id=1, source_target_pairs={{0,4},{4,8},{8,12},{12,16},{16,20},{20,24},{24,28},{1,5},{5,9},{9,... | collective-permute-start | bytes 294920 | tf_op jit(solution)/shard_map/ppermute | solution.py:141
  40.2 1.3 %collective-permute-start.7 = (f32[3,64,128]{2,1,0:T(8,128)S(1)}, f32[3,64,128]{2,1,0:T(8,128)S(1)}, u32[]{:S(2)}, u32[]{:S(2)}) collective-permute-start(f32[3,64,128]{2,1,0:T(8,128)S(1)} %get-tuple-element.19), channel_id=1, source_target_pairs={{4,0},{8,4},{12,8},{16,12},{20,16},{24,20},{28,24},{5,1},{9,5},{13... | collective-permute-start | bytes 294920 | tf_op jit(solution)/shard_map/ppermute | solution.py:141
  41.5 2.0 %collective-permute-done.13 = f32[192,128]{1,0:T(8,128)S(1)} collective-permute-done((f32[192,128]{1,0:T(8,128)S(1)}, f32[192,128]{1,0:T(8,128)S(1)}, u32[]{:S(2)}, u32[]{:S(2)}) %collective-permute-start.13) | collective-permute-done | bytes 98336 | tf_op jit(solution)/shard_map/ppermute | solution.py:145
  43.5 2.5 %collective-permute-start.14 = (f32[192,128]{1,0:T(8,128)S(1)}, f32[192,128]{1,0:T(8,128)S(1)}, u32[]{:S(2)}, u32[]{:S(2)}) collective-permute-start(f32[192,128]{1,0:T(8,128)S(1)} %add.83), channel_id=1, source_target_pairs={{0,4},{4,0},{8,12},{12,8},{16,20},{20,16},{24,28},{28,24},{1,5},{5... | collective-permute-start | bytes 294920 | tf_op jit(solution)/shard_map/ppermute | solution.py:145
  46.0 0.7 collective-permute-done.7
  46.8 3.4 %collective-permute-start.8 = (f32[2,64,128]{2,1,0:T(8,128)S(1)}, f32[2,64,128]{2,1,0:T(8,128)S(1)}, u32[]{:S(2)}, u32[]{:S(2)}) collective-permute-start(f32[2,64,128]{2,1,0:T(8,128)S(1)} %get-tuple-element.40), channel_id=1, source_target_pairs={{0,4},{4,8},{8,12},{12,16},{16,20},{20,24},{24,28},{1,5},{5,9},{9,... | collective-permute-start | bytes 196616 | tf_op jit(solution)/shard_map/ppermute | solution.py:141
  50.2 1.3 %collective-permute-start.9 = (f32[2,64,128]{2,1,0:T(8,128)S(1)}, f32[2,64,128]{2,1,0:T(8,128)S(1)}, u32[]{:S(2)}, u32[]{:S(2)}) collective-permute-start(f32[2,64,128]{2,1,0:T(8,128)S(1)} %get-tuple-element.41), channel_id=1, source_target_pairs={{4,0},{8,4},{12,8},{16,12},{20,16},{24,20},{28,24},{5,1},{9,5},{13... | collective-permute-start | bytes 196616 | tf_op jit(solution)/shard_map/ppermute | solution.py:141
  51.6 3.7 %collective-permute-start.15 = (f32[192,128]{1,0:T(8,128)S(1)}, f32[192,128]{1,0:T(8,128)S(1)}, u32[]{:S(2)}, u32[]{:S(2)}) collective-permute-start(f32[192,128]{1,0:T(8,128)S(1)} %add.84), channel_id=1, source_target_pairs={{0,8},{4,12},{8,0},{12,4},{16,24},{20,28},{24,16},{28,20},{1,9},{5... | collective-permute-start | bytes 294920 | tf_op jit(solution)/shard_map/ppermute | solution.py:145
  55.2 1.2 %collective-permute-done.9 = f32[2,64,128]{2,1,0:T(8,128)S(1)} collective-permute-done((f32[2,64,128]{2,1,0:T(8,128)S(1)}, f32[2,64,128]{2,1,0:T(8,128)S(1)}, u32[]{:S(2)}, u32[]{:S(2)}) %collective-permute-start.9) | collective-permute-done | bytes 65568 | tf_op jit(solution)/shard_map/ppermute | solution.py:141
  56.4 0.1 slice_bitcast_fusion.5
  56.6 0.1 pad_maximum_fusion.7
  56.7 6.1 %collective-permute-start.11 = (f32[264,128]{1,0:T(8,128)S(1)}, f32[264,128]{1,0:T(8,128)S(1)}, u32[]{:S(2)}, u32[]{:S(2)}) collective-permute-start(f32[264,128]{1,0:T(8,128)S(1)} %pad_maximum_fusion.7), channel_id=1, source_target_pairs={{0,1},{1,2},{2,3},{4,5},{5,6},{6,7},{8,9},{9,10},{10,11},{12,13},{... | collective-permute-start | bytes 405512 | tf_op jit(solution)/shard_map/ppermute | solution.py:141
  62.7 0.1 copy.11
  62.9 2.6 %collective-permute-start.16 = (f32[192,128]{1,0:T(8,128)S(1)}, f32[192,128]{1,0:T(8,128)S(1)}, u32[]{:S(2)}, u32[]{:S(2)}) collective-permute-start(f32[192,128]{1,0:T(8,128)S(1)} %add.85), channel_id=1, source_target_pairs={{0,16},{4,20},{8,24},{12,28},{16,0},{20,4},{24,8},{28,12},{1,17},{... | collective-permute-start | bytes 294920 | tf_op jit(solution)/shard_map/ppermute | solution.py:145
  65.6 0.1 pad_maximum_fusion.6
  65.7 1.3 %collective-permute-start.10 = (f32[264,128]{1,0:T(8,128)S(1)}, f32[264,128]{1,0:T(8,128)S(1)}, u32[]{:S(2)}, u32[]{:S(2)}) collective-permute-start(f32[264,128]{1,0:T(8,128)S(1)} %pad_maximum_fusion.6), channel_id=1, source_target_pairs={{1,0},{2,1},{3,2},{5,4},{6,5},{7,6},{9,8},{10,9},{11,10},{13,12},{... | collective-permute-start | bytes 405512 | tf_op jit(solution)/shard_map/ppermute | solution.py:141
  67.0 1.5 %collective-permute-done.16 = f32[192,128]{1,0:T(8,128)S(1)} collective-permute-done((f32[192,128]{1,0:T(8,128)S(1)}, f32[192,128]{1,0:T(8,128)S(1)}, u32[]{:S(2)}, u32[]{:S(2)}) %collective-permute-start.16) | collective-permute-done | bytes 98336 | tf_op jit(solution)/shard_map/ppermute | solution.py:145
  68.6 3.0 %collective-permute-start.17 = (f32[192,128]{1,0:T(8,128)S(1)}, f32[192,128]{1,0:T(8,128)S(1)}, u32[]{:S(2)}, u32[]{:S(2)}) collective-permute-start(f32[192,128]{1,0:T(8,128)S(1)} %add.86), channel_id=1, source_target_pairs={{0,1},{1,0},{2,3},{3,2},{4,5},{5,4},{6,7},{7,6},{8,9},{9,8},{10,11... | collective-permute-start | bytes 294920 | tf_op jit(solution)/shard_map/ppermute | solution.py:145
  71.7 0.1 fusion.10
  71.8 0.1 maximum_bitcast_fusion.2
  71.9 0.1 maximum_bitcast_fusion.3
  72.1 0.5 collective-permute-done.17
  72.6 4.7 %shard_map.78 = (f32[3,264,256]{2,1,0:T(8,128)S(1)}, f32[3,128,128]{2,1,0:T(8,128)S(1)}) custom-call(s32[8]{0:T(128)S(1)} %reshape_squeeze.14.starts, s32[1]{0:T(128)} %bitcast.9.count, f32[2,264,256]{2,1,0:T(8,128)S(1)} %fusion.1.field, f32[2,128,128]{2,1,0:T(8,128)S(1)} %divide_add_fusion.1.probe, f32[4,128,128]{2,1,0:T(8,128)S(1)} %get-tuple-element.14.amps, ...), custom_call_target="tpu_custom_call" | custom-call | flops 805306368 | bytes 4194304 | tf_op jit(solution)/shard_map/pallas_call | solution.py:121
  77.3 2.0 %collective-permute-start.22 = (f32[192,128]{1,0:T(8,128)S(1)}, f32[192,128]{1,0:T(8,128)S(1)}, u32[]{:S(2)}, u32[]{:S(2)}) collective-permute-start(f32[192,128]{1,0:T(8,128)S(1)} %slice_select_fusion), channel_id=1, source_target_pairs={{0,1},{1,0},{2,3},{3,2},{4,5},{5,4},{6,7},{7,6},{8,9},{9,8},{10,11... | collective-permute-start | bytes 294920 | tf_op jit(solution)/shard_map/ppermute | solution.py:145
  79.3 0.2 fusion.6
  79.5 1.9 %collective-permute-start.18 = (f32[3,264,64]{2,1,0:T(8,128)S(1)}, f32[3,264,64]{2,1,0:T(8,128)S(1)}, u32[]{:S(2)}, u32[]{:S(2)}) collective-permute-start(f32[3,264,64]{2,1,0:T(8,128)S(1)} %get-tuple-element.10), channel_id=1, source_target_pairs={{0,1},{1,2},{2,3},{4,5},{5,6},{6,7},{8,9},{9,10},{10,11},{12,13},{... | collective-permute-start | bytes 608264 | tf_op jit(solution)/shard_map/ppermute | solution.py:141
  81.5 1.3 %collective-permute-start.19 = (f32[3,264,64]{2,1,0:T(8,128)S(1)}, f32[3,264,64]{2,1,0:T(8,128)S(1)}, u32[]{:S(2)}, u32[]{:S(2)}) collective-permute-start(f32[3,264,64]{2,1,0:T(8,128)S(1)} %get-tuple-element.11), channel_id=1, source_target_pairs={{1,0},{2,1},{3,2},{5,4},{6,5},{7,6},{9,8},{10,9},{11,10},{13,12},{... | collective-permute-start | bytes 608264 | tf_op jit(solution)/shard_map/ppermute | solution.py:141
  82.8 2.3 %collective-permute-start.23 = (f32[192,128]{1,0:T(8,128)S(1)}, f32[192,128]{1,0:T(8,128)S(1)}, u32[]{:S(2)}, u32[]{:S(2)}) collective-permute-start(f32[192,128]{1,0:T(8,128)S(1)} %select_add_fusion), channel_id=1, source_target_pairs={{0,2},{1,3},{2,0},{3,1},{4,6},{5,7},{6,4},{7,5},{8,10},{9,11},{10,... | collective-permute-start | bytes 294920 | tf_op jit(solution)/shard_map/ppermute | solution.py:145
  85.1 7.9 %collective-permute-done.23 = f32[192,128]{1,0:T(8,128)S(1)} collective-permute-done((f32[192,128]{1,0:T(8,128)S(1)}, f32[192,128]{1,0:T(8,128)S(1)}, u32[]{:S(2)}, u32[]{:S(2)}) %collective-permute-start.23) | collective-permute-done | bytes 98336 | tf_op jit(solution)/shard_map/ppermute | solution.py:145
  93.0 1.1 collective-permute-start.24
  94.1 0.2 maximum_add_fusion.1
  94.3 2.9 %collective-permute-start.20 = (f32[3,64,128]{2,1,0:T(8,128)S(1)}, f32[3,64,128]{2,1,0:T(8,128)S(1)}, u32[]{:S(2)}, u32[]{:S(2)}) collective-permute-start(f32[3,64,128]{2,1,0:T(8,128)S(1)} %get-tuple-element.16), channel_id=1, source_target_pairs={{0,4},{4,8},{8,12},{12,16},{16,20},{20,24},{24,28},{1,5},{5,9},{9,... | collective-permute-start | bytes 294920 | tf_op jit(solution)/shard_map/ppermute | solution.py:141
  97.2 1.3 %collective-permute-start.21 = (f32[3,64,128]{2,1,0:T(8,128)S(1)}, f32[3,64,128]{2,1,0:T(8,128)S(1)}, u32[]{:S(2)}, u32[]{:S(2)}) collective-permute-start(f32[3,64,128]{2,1,0:T(8,128)S(1)} %get-tuple-element.17), channel_id=1, source_target_pairs={{4,0},{8,4},{12,8},{16,12},{20,16},{24,20},{28,24},{5,1},{9,5},{13... | collective-permute-start | bytes 294920 | tf_op jit(solution)/shard_map/ppermute | solution.py:141
  98.6 3.4 %collective-permute-start.25 = (f32[192,128]{1,0:T(8,128)S(1)}, f32[192,128]{1,0:T(8,128)S(1)}, u32[]{:S(2)}, u32[]{:S(2)}) collective-permute-start(f32[192,128]{1,0:T(8,128)S(1)} %add.95), channel_id=1, source_target_pairs={{0,8},{4,12},{8,0},{12,4},{16,24},{20,28},{24,16},{28,20},{1,9},{5... | collective-permute-start | bytes 294920 | tf_op jit(solution)/shard_map/ppermute | solution.py:145
  102.0 1.8 %collective-permute-done.21 = f32[3,64,128]{2,1,0:T(8,128)S(1)} collective-permute-done((f32[3,64,128]{2,1,0:T(8,128)S(1)}, f32[3,64,128]{2,1,0:T(8,128)S(1)}, u32[]{:S(2)}, u32[]{:S(2)}) %collective-permute-start.21) | collective-permute-done | bytes 98336 | tf_op jit(solution)/shard_map/ppermute | solution.py:141
  103.8 2.2 %collective-permute-done.25 = f32[192,128]{1,0:T(8,128)S(1)} collective-permute-done((f32[192,128]{1,0:T(8,128)S(1)}, f32[192,128]{1,0:T(8,128)S(1)}, u32[]{:S(2)}, u32[]{:S(2)}) %collective-permute-start.25) | collective-permute-done | bytes 98336 | tf_op jit(solution)/shard_map/ppermute | solution.py:145
  106.0 2.7 %collective-permute-start.26 = (f32[192,128]{1,0:T(8,128)S(1)}, f32[192,128]{1,0:T(8,128)S(1)}, u32[]{:S(2)}, u32[]{:S(2)}) collective-permute-start(f32[192,128]{1,0:T(8,128)S(1)} %add.96), channel_id=1, source_target_pairs={{0,16},{4,20},{8,24},{12,28},{16,0},{20,4},{24,8},{28,12},{1,17},{... | collective-permute-start | bytes 294920 | tf_op jit(solution)/shard_map/ppermute | solution.py:145
  108.7 3.9 %collective-permute-done.26 = f32[192,128]{1,0:T(8,128)S(1)} collective-permute-done((f32[192,128]{1,0:T(8,128)S(1)}, f32[192,128]{1,0:T(8,128)S(1)}, u32[]{:S(2)}, u32[]{:S(2)}) %collective-permute-start.26) | collective-permute-done | bytes 98336 | tf_op jit(solution)/shard_map/ppermute | solution.py:145
  112.7 0.7 fusion.2
  113.4 0.6 collective-permute-done.27
  114.0 0.7 divide_add_fusion
  (63 shorter events, 1.2 us)
Async XLA Ops:
  1.5 7.4 %collective-permute-start = (f32[2,64,128]{2,1,0:T(8,128)S(1)}, f32[2,64,128]{2,1,0:T(8,128)S(1)}, u32[]{:S(2)}, u32[]{:S(2)}) collective-permute-start(f32[2,64,128]{2,1,0:T(8,128)S(1)} %get-tuple-element.42), channel_id=1, source_target_pairs={{0,4},{4,8},{8,12},{12,16},{16,20},{20,24},{24,28},{1,5},{5,9},{9,... | collective-permute-start | bytes 196616 | tf_op jit(solution)/shard_map/ppermute | solution.py:141
  6.4 2.5 %copy-start.3 = (s32[1,1,2,4,2]{3,4,2,1,0:T(2,128)S(1)}, s32[1,1,2,4,2]{3,4,2,1,0:T(2,128)}, u32[]{:S(2)}) copy-start(s32[1,1,2,4,2]{3,4,2,1,0:T(2,128)} %param.8) | copy-start | bytes 196
  6.4 6.3 %copy-start.2 = (f32[2,128,128]{2,1,0:T(8,128)S(1)}, f32[2,128,128]{2,1,0:T(8,128)}, u32[]{:S(2)}) copy-start(f32[2,128,128]{2,1,0:T(8,128)} %param.6) | copy-start | bytes 393220
  6.4 6.3 %collective-permute-start.1 = (f32[2,64,128]{2,1,0:T(8,128)S(1)}, f32[2,64,128]{2,1,0:T(8,128)S(1)}, u32[]{:S(2)}, u32[]{:S(2)}) collective-permute-start(f32[2,64,128]{2,1,0:T(8,128)S(1)} %get-tuple-element.43), channel_id=1, source_target_pairs={{4,0},{8,4},{12,8},{16,12},{20,16},{24,20},{28,24},{5,1},{9,5},{13... | collective-permute-start | bytes 196616 | tf_op jit(solution)/shard_map/ppermute | solution.py:141
  12.9 1.4 %copy-start.4 = (s32[1,1,2]{2,1,0:T(1,128)S(1)}, s32[1,1,2]{2,1,0:T(1,128)}, u32[]{:S(2)}) copy-start(s32[1,1,2]{2,1,0:T(1,128)} %param.9) | copy-start | bytes 28
  13.0 3.5 %collective-permute-start.3 = (f32[264,128]{1,0:T(8,128)S(1)}, f32[264,128]{1,0:T(8,128)S(1)}, u32[]{:S(2)}, u32[]{:S(2)}) collective-permute-start(f32[264,128]{1,0:T(8,128)S(1)} %pad_maximum_fusion.5), channel_id=1, source_target_pairs={{0,1},{1,2},{2,3},{4,5},{5,6},{6,7},{8,9},{9,10},{10,11},{12,13},{... | collective-permute-start | bytes 405512 | tf_op jit(solution)/shard_map/ppermute | solution.py:141
  15.2 5.0 %collective-permute-start.2 = (f32[264,128]{1,0:T(8,128)S(1)}, f32[264,128]{1,0:T(8,128)S(1)}, u32[]{:S(2)}, u32[]{:S(2)}) collective-permute-start(f32[264,128]{1,0:T(8,128)S(1)} %pad_maximum_fusion.4), channel_id=1, source_target_pairs={{1,0},{2,1},{3,2},{5,4},{6,5},{7,6},{9,8},{10,9},{11,10},{13,12},{... | collective-permute-start | bytes 405512 | tf_op jit(solution)/shard_map/ppermute | solution.py:141
  20.4 0.9 copy-start
  20.4 1.1 copy-start.1
  26.2 7.1 %collective-permute-start.12 = (f32[192,128]{1,0:T(8,128)S(1)}, f32[192,128]{1,0:T(8,128)S(1)}, u32[]{:S(2)}, u32[]{:S(2)}) collective-permute-start(f32[192,128]{1,0:T(8,128)S(1)} %slice_select_fusion.1), channel_id=1, source_target_pairs={{0,1},{1,0},{2,3},{3,2},{4,5},{5,4},{6,7},{7,6},{8,9},{9,8},{10,11... | collective-permute-start | bytes 294920 | tf_op jit(solution)/shard_map/ppermute | solution.py:145
  30.1 5.6 %collective-permute-start.4 = (f32[3,264,64]{2,1,0:T(8,128)S(1)}, f32[3,264,64]{2,1,0:T(8,128)S(1)}, u32[]{:S(2)}, u32[]{:S(2)}) collective-permute-start(f32[3,264,64]{2,1,0:T(8,128)S(1)} %get-tuple-element.12), channel_id=1, source_target_pairs={{0,1},{1,2},{2,3},{4,5},{5,6},{6,7},{8,9},{9,10},{10,11},{12,13},{... | collective-permute-start | bytes 608264 | tf_op jit(solution)/shard_map/ppermute | solution.py:141
  32.0 3.6 %collective-permute-start.5 = (f32[3,264,64]{2,1,0:T(8,128)S(1)}, f32[3,264,64]{2,1,0:T(8,128)S(1)}, u32[]{:S(2)}, u32[]{:S(2)}) collective-permute-start(f32[3,264,64]{2,1,0:T(8,128)S(1)} %get-tuple-element.13), channel_id=1, source_target_pairs={{1,0},{2,1},{3,2},{5,4},{6,5},{7,6},{9,8},{10,9},{11,10},{13,12},{... | collective-permute-start | bytes 608264 | tf_op jit(solution)/shard_map/ppermute | solution.py:141
  33.3 10.2 %collective-permute-start.13 = (f32[192,128]{1,0:T(8,128)S(1)}, f32[192,128]{1,0:T(8,128)S(1)}, u32[]{:S(2)}, u32[]{:S(2)}) collective-permute-start(f32[192,128]{1,0:T(8,128)S(1)} %select_add_fusion.1), channel_id=1, source_target_pairs={{0,2},{1,3},{2,0},{3,1},{4,6},{5,7},{6,4},{7,5},{8,10},{9,11},{10,... | collective-permute-start | bytes 294920 | tf_op jit(solution)/shard_map/ppermute | solution.py:145
  35.9 10.2 %collective-permute-start.6 = (f32[3,64,128]{2,1,0:T(8,128)S(1)}, f32[3,64,128]{2,1,0:T(8,128)S(1)}, u32[]{:S(2)}, u32[]{:S(2)}) collective-permute-start(f32[3,64,128]{2,1,0:T(8,128)S(1)} %get-tuple-element.18), channel_id=1, source_target_pairs={{0,4},{4,8},{8,12},{12,16},{16,20},{20,24},{24,28},{1,5},{5,9},{9,... | collective-permute-start | bytes 294920 | tf_op jit(solution)/shard_map/ppermute | solution.py:141
  40.2 6.5 %collective-permute-start.7 = (f32[3,64,128]{2,1,0:T(8,128)S(1)}, f32[3,64,128]{2,1,0:T(8,128)S(1)}, u32[]{:S(2)}, u32[]{:S(2)}) collective-permute-start(f32[3,64,128]{2,1,0:T(8,128)S(1)} %get-tuple-element.19), channel_id=1, source_target_pairs={{4,0},{8,4},{12,8},{16,12},{20,16},{24,20},{28,24},{5,1},{9,5},{13... | collective-permute-start | bytes 294920 | tf_op jit(solution)/shard_map/ppermute | solution.py:141
  43.5 8.0 %collective-permute-start.14 = (f32[192,128]{1,0:T(8,128)S(1)}, f32[192,128]{1,0:T(8,128)S(1)}, u32[]{:S(2)}, u32[]{:S(2)}) collective-permute-start(f32[192,128]{1,0:T(8,128)S(1)} %add.83), channel_id=1, source_target_pairs={{0,4},{4,0},{8,12},{12,8},{16,20},{20,16},{24,28},{28,24},{1,5},{5... | collective-permute-start | bytes 294920 | tf_op jit(solution)/shard_map/ppermute | solution.py:145
  46.8 8.4 %collective-permute-start.8 = (f32[2,64,128]{2,1,0:T(8,128)S(1)}, f32[2,64,128]{2,1,0:T(8,128)S(1)}, u32[]{:S(2)}, u32[]{:S(2)}) collective-permute-start(f32[2,64,128]{2,1,0:T(8,128)S(1)} %get-tuple-element.40), channel_id=1, source_target_pairs={{0,4},{4,8},{8,12},{12,16},{16,20},{20,24},{24,28},{1,5},{5,9},{9,... | collective-permute-start | bytes 196616 | tf_op jit(solution)/shard_map/ppermute | solution.py:141
  50.2 6.2 %collective-permute-start.9 = (f32[2,64,128]{2,1,0:T(8,128)S(1)}, f32[2,64,128]{2,1,0:T(8,128)S(1)}, u32[]{:S(2)}, u32[]{:S(2)}) collective-permute-start(f32[2,64,128]{2,1,0:T(8,128)S(1)} %get-tuple-element.41), channel_id=1, source_target_pairs={{4,0},{8,4},{12,8},{16,12},{20,16},{24,20},{28,24},{5,1},{9,5},{13... | collective-permute-start | bytes 196616 | tf_op jit(solution)/shard_map/ppermute | solution.py:141
  51.6 11.4 %collective-permute-start.15 = (f32[192,128]{1,0:T(8,128)S(1)}, f32[192,128]{1,0:T(8,128)S(1)}, u32[]{:S(2)}, u32[]{:S(2)}) collective-permute-start(f32[192,128]{1,0:T(8,128)S(1)} %add.84), channel_id=1, source_target_pairs={{0,8},{4,12},{8,0},{12,4},{16,24},{20,28},{24,16},{28,20},{1,9},{5... | collective-permute-start | bytes 294920 | tf_op jit(solution)/shard_map/ppermute | solution.py:145
  56.7 14.9 %collective-permute-start.11 = (f32[264,128]{1,0:T(8,128)S(1)}, f32[264,128]{1,0:T(8,128)S(1)}, u32[]{:S(2)}, u32[]{:S(2)}) collective-permute-start(f32[264,128]{1,0:T(8,128)S(1)} %pad_maximum_fusion.7), channel_id=1, source_target_pairs={{0,1},{1,2},{2,3},{4,5},{5,6},{6,7},{8,9},{9,10},{10,11},{12,13},{... | collective-permute-start | bytes 405512 | tf_op jit(solution)/shard_map/ppermute | solution.py:141
  62.9 5.6 %collective-permute-start.16 = (f32[192,128]{1,0:T(8,128)S(1)}, f32[192,128]{1,0:T(8,128)S(1)}, u32[]{:S(2)}, u32[]{:S(2)}) collective-permute-start(f32[192,128]{1,0:T(8,128)S(1)} %add.85), channel_id=1, source_target_pairs={{0,16},{4,20},{8,24},{12,28},{16,0},{20,4},{24,8},{28,12},{1,17},{... | collective-permute-start | bytes 294920 | tf_op jit(solution)/shard_map/ppermute | solution.py:145
  65.7 6.0 %collective-permute-start.10 = (f32[264,128]{1,0:T(8,128)S(1)}, f32[264,128]{1,0:T(8,128)S(1)}, u32[]{:S(2)}, u32[]{:S(2)}) collective-permute-start(f32[264,128]{1,0:T(8,128)S(1)} %pad_maximum_fusion.6), channel_id=1, source_target_pairs={{1,0},{2,1},{3,2},{5,4},{6,5},{7,6},{9,8},{10,9},{11,10},{13,12},{... | collective-permute-start | bytes 405512 | tf_op jit(solution)/shard_map/ppermute | solution.py:141
  68.6 4.0 %collective-permute-start.17 = (f32[192,128]{1,0:T(8,128)S(1)}, f32[192,128]{1,0:T(8,128)S(1)}, u32[]{:S(2)}, u32[]{:S(2)}) collective-permute-start(f32[192,128]{1,0:T(8,128)S(1)} %add.86), channel_id=1, source_target_pairs={{0,1},{1,0},{2,3},{3,2},{4,5},{5,4},{6,7},{7,6},{8,9},{9,8},{10,11... | collective-permute-start | bytes 294920 | tf_op jit(solution)/shard_map/ppermute | solution.py:145
  77.3 5.5 %collective-permute-start.22 = (f32[192,128]{1,0:T(8,128)S(1)}, f32[192,128]{1,0:T(8,128)S(1)}, u32[]{:S(2)}, u32[]{:S(2)}) collective-permute-start(f32[192,128]{1,0:T(8,128)S(1)} %slice_select_fusion), channel_id=1, source_target_pairs={{0,1},{1,0},{2,3},{3,2},{4,5},{5,4},{6,7},{7,6},{8,9},{9,8},{10,11... | collective-permute-start | bytes 294920 | tf_op jit(solution)/shard_map/ppermute | solution.py:145
  79.5 14.5 %collective-permute-start.18 = (f32[3,264,64]{2,1,0:T(8,128)S(1)}, f32[3,264,64]{2,1,0:T(8,128)S(1)}, u32[]{:S(2)}, u32[]{:S(2)}) collective-permute-start(f32[3,264,64]{2,1,0:T(8,128)S(1)} %get-tuple-element.10), channel_id=1, source_target_pairs={{0,1},{1,2},{2,3},{4,5},{5,6},{6,7},{8,9},{9,10},{10,11},{12,13},{... | collective-permute-start | bytes 608264 | tf_op jit(solution)/shard_map/ppermute | solution.py:141
  81.5 12.6 %collective-permute-start.19 = (f32[3,264,64]{2,1,0:T(8,128)S(1)}, f32[3,264,64]{2,1,0:T(8,128)S(1)}, u32[]{:S(2)}, u32[]{:S(2)}) collective-permute-start(f32[3,264,64]{2,1,0:T(8,128)S(1)} %get-tuple-element.11), channel_id=1, source_target_pairs={{1,0},{2,1},{3,2},{5,4},{6,5},{7,6},{9,8},{10,9},{11,10},{13,12},{... | collective-permute-start | bytes 608264 | tf_op jit(solution)/shard_map/ppermute | solution.py:141
  82.8 10.2 %collective-permute-start.23 = (f32[192,128]{1,0:T(8,128)S(1)}, f32[192,128]{1,0:T(8,128)S(1)}, u32[]{:S(2)}, u32[]{:S(2)}) collective-permute-start(f32[192,128]{1,0:T(8,128)S(1)} %select_add_fusion), channel_id=1, source_target_pairs={{0,2},{1,3},{2,0},{3,1},{4,6},{5,7},{6,4},{7,5},{8,10},{9,11},{10,... | collective-permute-start | bytes 294920 | tf_op jit(solution)/shard_map/ppermute | solution.py:145
  93.0 5.5 %collective-permute-start.24 = (f32[192,128]{1,0:T(8,128)S(1)}, f32[192,128]{1,0:T(8,128)S(1)}, u32[]{:S(2)}, u32[]{:S(2)}) collective-permute-start(f32[192,128]{1,0:T(8,128)S(1)} %add.94), channel_id=1, source_target_pairs={{0,4},{4,0},{8,12},{12,8},{16,20},{20,16},{24,28},{28,24},{1,5},{5... | collective-permute-start | bytes 294920 | tf_op jit(solution)/shard_map/ppermute | solution.py:145
  94.3 7.7 %collective-permute-start.20 = (f32[3,64,128]{2,1,0:T(8,128)S(1)}, f32[3,64,128]{2,1,0:T(8,128)S(1)}, u32[]{:S(2)}, u32[]{:S(2)}) collective-permute-start(f32[3,64,128]{2,1,0:T(8,128)S(1)} %get-tuple-element.16), channel_id=1, source_target_pairs={{0,4},{4,8},{8,12},{12,16},{16,20},{20,24},{24,28},{1,5},{5,9},{9,... | collective-permute-start | bytes 294920 | tf_op jit(solution)/shard_map/ppermute | solution.py:141
  97.2 6.5 %collective-permute-start.21 = (f32[3,64,128]{2,1,0:T(8,128)S(1)}, f32[3,64,128]{2,1,0:T(8,128)S(1)}, u32[]{:S(2)}, u32[]{:S(2)}) collective-permute-start(f32[3,64,128]{2,1,0:T(8,128)S(1)} %get-tuple-element.17), channel_id=1, source_target_pairs={{4,0},{8,4},{12,8},{16,12},{20,16},{24,20},{28,24},{5,1},{9,5},{13... | collective-permute-start | bytes 294920 | tf_op jit(solution)/shard_map/ppermute | solution.py:141
  98.6 7.4 %collective-permute-start.25 = (f32[192,128]{1,0:T(8,128)S(1)}, f32[192,128]{1,0:T(8,128)S(1)}, u32[]{:S(2)}, u32[]{:S(2)}) collective-permute-start(f32[192,128]{1,0:T(8,128)S(1)} %add.95), channel_id=1, source_target_pairs={{0,8},{4,12},{8,0},{12,4},{16,24},{20,28},{24,16},{28,20},{1,9},{5... | collective-permute-start | bytes 294920 | tf_op jit(solution)/shard_map/ppermute | solution.py:145
  106.0 6.6 %collective-permute-start.26 = (f32[192,128]{1,0:T(8,128)S(1)}, f32[192,128]{1,0:T(8,128)S(1)}, u32[]{:S(2)}, u32[]{:S(2)}) collective-permute-start(f32[192,128]{1,0:T(8,128)S(1)} %add.96), channel_id=1, source_target_pairs={{0,16},{4,20},{8,24},{12,28},{16,0},{20,4},{24,8},{28,12},{1,17},{... | collective-permute-start | bytes 294920 | tf_op jit(solution)/shard_map/ppermute | solution.py:145
  112.6 1.4 %collective-permute-start.27 = (f32[192,128]{1,0:T(8,128)S(1)}, f32[192,128]{1,0:T(8,128)S(1)}, u32[]{:S(2)}, u32[]{:S(2)}) collective-permute-start(f32[192,128]{1,0:T(8,128)S(1)} %add.97), channel_id=1, source_target_pairs={{0,1},{1,0},{2,3},{3,2},{4,5},{5,4},{6,7},{7,6},{8,9},{9,8},{10,11... | collective-permute-start | bytes 294920 | tf_op jit(solution)/shard_map/ppermute | solution.py:145
where the time goes:
time: 115 us
  starting transfers between devices  66.7 us (58%)
  waiting for transfers between devices  29.5 us (26%)
  Pallas kernels  9.3 us (8%)
  local copies, waits for them, and re-layouts  5.01 us (4%)
  other arithmetic  3.01 us (3%)
  between operations  1.19 us (1%)
    ppermute x16, starting transfers between devices, shift(): return lax.ppermute(value, axis, pairs)  37.3 us
    ppermute x12, starting transfers between devices, swap(): lax.ppermute(value, axis, [(i, i ^ bit) for i in range(lax.axis_size(axis...  29.4 us
    ppermute x12, waiting for transfers between devices, swap(): lax.ppermute(value, axis, [(i, i ^ bit) for i in range(lax.axis_size(axis...  18.6 us
    ppermute x16, waiting for transfers between devices, shift(): return lax.ppermute(value, axis, pairs)  11 us
    pallas_call x2, Pallas kernels, slot_sums(): pl.pallas_call(slots_kernel, out_shape=(jax.ShapeDtypeStruct((3,) + field...  9.3 us
  transfers between devices with their start and end apart: 28, of which 12 were waited for; matrix products, arithmetic and copies ran while one was open for 4% of the time, Pallas kernels for 0%

commit v1 on v0

v1 whole, which is shorter than its diff:
```python
import math

import jax
import jax.numpy as jnp
import numpy as np
from jax import lax
from jax.experimental import pallas as pl
from jax.experimental.pallas import tpu as pltpu
from jax.sharding import PartitionSpec as P

RIM = 64
TILE = 8
EPS = 0.1
MIB = 1024 * 1024


def dft_tables(size):
    index = np.arange(size)
    angle = (index[:, None] * index[None, :] % size) * (-2.0 * math.pi / size)
    cosine = np.cos(angle) / math.sqrt(size)
    sine = np.sin(angle) / math.sqrt(size)
    full = np.block([[cosine, -sine], [sine, cosine]]).astype(np.float32)
    flip = np.ascontiguousarray(full.T)
    tables = []
    for table in (full, flip):
        high = table.astype(jnp.bfloat16)
        tables += [high, (table - high.astype(np.float32)).astype(jnp.bfloat16)]
    return np.stack(tables)


def split(value):
    high = value.astype(jnp.bfloat16)
    return high, (value - high.astype(jnp.float32)).astype(jnp.bfloat16)


def mul(left, right):
    return jnp.dot(left, right, preferred_element_type=jnp.float32)


def left_product(high, low, value):
    first, second = split(value)
    return mul(high, first) + (mul(high, second) + mul(low, first))


def right_product(value, high, low):
    first, second = split(value)
    return mul(first, high) + (mul(second, high) + mul(first, low))


def lanes(shape):
    return lax.broadcasted_iota(jnp.int32, shape, 1)


def pack(real, imag):
    half = real.shape[1] // 2
    first = lanes(real.shape) < half
    low = jnp.where(first, real, pltpu.roll(imag, half, 1))
    high = jnp.where(first, pltpu.roll(real, half, 1), imag)
    return low, high


def unpack(low, high):
    half = low.shape[1] // 2
    first = lanes(low.shape) < half
    real = jnp.where(first, low, pltpu.roll(high, half, 1))
    imag = jnp.where(first, pltpu.roll(low, half, 1), high)
    return real, imag


def grow_rows(term, skew):
    count, width = term.shape
    tiles = count // TILE
    sub = lax.broadcasted_iota(jnp.int32, (tiles, TILE, width), 1)
    turned = pltpu.roll(term.reshape(tiles, TILE, width), skew, 1)
    late = jnp.where(sub < skew, turned, 0.0)
    soon = jnp.where(sub < skew, 0.0, turned)
    blank = jnp.zeros((1, TILE, width), jnp.float32)
    grown = jnp.concatenate([soon, blank], 0) + jnp.concatenate([blank, late], 0)
    return grown.reshape(count + TILE, width)


def lane_turn(col, width):
    return jnp.where(col < 0, col + width, col)


def strips_kernel(place, tile, meta, above, below, tall, near, far):
    side = tile.shape[1]
    odd = place[0] != 0
    for part in range(2):
        tall[part, :RIM] = above[part * RIM : (part + 1) * RIM]
        tall[part, RIM : RIM + side] = tile[part]
        tall[part, RIM + side :] = below[part * RIM : (part + 1) * RIM]
    low, high = pack(tall[0], tall[1])
    rows = low.shape[0]
    near[:rows] = jnp.where(odd, low, high)
    far[:rows] = jnp.where(odd, high, low)
    for out in (near, far):
        out[rows : rows + TILE] = above[2 * RIM :]
        out[rows + TILE : rows + 2 * TILE] = meta[...]
        out[rows + 2 * TILE :] = below[2 * RIM :]


def slots_kernel(
    place, starts, count, tall, near, far, probe, amps, tables,
    core_out, far_out, keep_out, tall_out, field, sums, totals,
):
    width = probe.shape[1]
    rows_all = tall.shape[1]
    tiles = width // TILE
    odd = place[0] != 0
    lane = lanes((width + TILE, width))
    sub = lax.broadcasted_iota(jnp.int32, (tiles, TILE, width), 1)
    from_near, from_far = near[:rows_all], far[:rows_all]
    sides = unpack(jnp.where(odd, from_far, from_near), jnp.where(odd, from_near, from_far))
    for part in range(2):
        field[part, :rows_all, :width] = tall[part]
        field[part, :rows_all, width:] = sides[part]
        field[part, rows_all:] = jnp.zeros_like(field[part, rows_all:])
    sums[...] = jnp.zeros_like(sums)
    full_h, full_l, flip_h, flip_l = (tables[k] for k in range(4))
    pro_r, pro_i = probe[0], probe[1]
    total = None
    for slot in range(amps.shape[0]):
        row = starts[2 * slot] + RIM
        col = starts[2 * slot + 1]
        live = jnp.where(slot < count[0], 1.0, 0.0).astype(jnp.float32)
        base = pl.multiple_of(row // TILE * TILE, TILE)
        rows = pl.ds(base, width + TILE)
        skew = row - base
        lift = jnp.where(skew > 0, TILE - skew, 0)
        ahead = lane_turn(col, width)
        back = lane_turn(-col, width)
        outside = (lane < col) | (lane >= width + col)

        def window(part):
            mixed = jnp.where(outside, field[part, rows, width:], field[part, rows, :width])
            turned = pltpu.roll(mixed.reshape(tiles + 1, TILE, width), lift, 1)
            lined = jnp.where(sub < TILE - skew, turned[:-1], turned[1:])
            return pltpu.roll(lined.reshape(width, width), back, 1)

        win_r, win_i = window(0), window(1)
        psi_r = pro_r * win_r - pro_i * win_i
        psi_i = pro_r * win_i + pro_i * win_r
        half = left_product(full_h, full_l, jnp.concatenate([psi_r, psi_i], 0))
        wave = right_product(jnp.concatenate([half[:width], half[width:]], 1), flip_h, flip_l)
        far_r, far_i = wave[:, :width], wave[:, width:]
        factor = amps[slot] * lax.rsqrt(jnp.maximum(far_r * far_r + far_i * far_i, 1.0))
        half = left_product(
            flip_h, flip_l, jnp.concatenate([far_r * factor, far_i * factor], 0)
        )
        wave = right_product(jnp.concatenate([half[:width], half[width:]], 1), full_h, full_l)
        chi_r = (wave[:, :width] - psi_r) * live
        chi_i = (wave[:, width:] - psi_i) * live

        def deposit(part, term):
            grown = grow_rows(pltpu.roll(term, ahead, 1), skew)
            sums[part, rows, :width] += jnp.where(outside, 0.0, grown)
            sums[part, rows, width:] += jnp.where(outside, grown, 0.0)

        deposit(0, pro_r * chi_r + pro_i * chi_i)
        deposit(1, pro_r * chi_i - pro_i * chi_r)
        terms = (
            win_r * chi_r + win_i * chi_i,
            win_r * chi_i - win_i * chi_r,
            (win_r * win_r + win_i * win_i) * live,
        )
        total = terms if total is None else tuple(a + b for a, b in zip(total, terms))
    half = width // 2
    for part in range(3):
        totals[part] = total[part]
    kept = pl.ds(pl.multiple_of(place[0] * half, half), half)
    given = pl.ds(pl.multiple_of((1 - place[0]) * half, half), half)
    for part in range(3):
        keep_out[part * half : (part + 1) * half] = totals[part, kept]
        core_out[part * half : (part + 1) * half] = totals[part, given]
    for part in range(2):
        tall_out[part] = sums[part, :rows_all, :width]
    low, high = pack(sums[0, :rows_all, width:], sums[1, :rows_all, width:])
    core_out[3 * half :] = jnp.where(odd, high, low)
    far_out[...] = jnp.where(odd, low, high)


def fold_kernel(place, tall, near, far, up, down):
    rows = up.shape[1]
    start = near.shape[0] - tall.shape[1]
    odd = place[0] != 0
    from_near, from_far = near[start:], far[...]
    extra = unpack(jnp.where(odd, from_near, from_far), jnp.where(odd, from_far, from_near))
    for part in range(2):
        whole = tall[part] + extra[part]
        up[part] = whole[:rows]
        down[part] = whole[rows:]


def weight_kernel(metas, probe, out, spread, *, step, slots):
    width = probe.shape[1]
    stride = metas.shape[1]
    lane = lanes((width + TILE, width))
    spread[...] = jnp.zeros_like(spread)
    weight = probe[0] * probe[0] + probe[1] * probe[1]
    for index in range(metas.shape[0]):
        count = metas[index, step * (2 * slots + 1) + 2 * slots]
        for slot in range(slots):
            where = step * (2 * slots + 1) + 2 * slot
            row = metas[index, where] + (RIM + width + (index // 3 - 1) * width)
            col = metas[index, where + 1] + (index % 3 - 1) * width

            @pl.when((slot < count) & (col < width) & (col > -width))
            def _():
                base = pl.multiple_of(row // TILE * TILE, TILE)
                turned = pltpu.roll(weight, lane_turn(col, width), 1)
                grown = grow_rows(turned, row - base)
                inside = (lane >= col) & (lane < width + col)
                spread[pl.ds(base, width + TILE)] += jnp.where(inside, grown, 0.0)

    out[...] = spread[width : width + out.shape[0]]


def update_kernel(place, tall, up, down, above, below, weight, new_tall, near, far):
    rows = up.shape[1]
    odd = place[0] != 0
    first = jnp.where(place[1] != 0, 1.0, 0.0).astype(jnp.float32)
    last = jnp.where(place[2] != 0, 1.0, 0.0).astype(jnp.float32)
    for part in range(2):
        head = tall[part, :rows] + (up[part] + above[part]) / (weight[:rows] + EPS)
        tail = tall[part, rows:] + (down[part] + below[part]) / (weight[rows:] + EPS)
        new_tall[part, :RIM] = head[:RIM] * first
        new_tall[part, RIM:rows] = head[RIM:]
        new_tall[part, rows : 2 * rows - RIM] = tail[: rows - RIM]
        new_tall[part, 2 * rows - RIM :] = tail[rows - RIM :] * last
    low, high = pack(new_tall[0], new_tall[1])
    near[...] = jnp.where(odd, low, high)
    far[...] = jnp.where(odd, high, low)


def call(kernel, shapes, smem_count, operands, flops=1000000, moved=MIB, scratch=(), limit=16):
    vmem = pl.BlockSpec(memory_space=pltpu.VMEM)
    smem = pl.BlockSpec(memory_space=pltpu.SMEM)
    return pl.pallas_call(
        kernel,
        out_shape=tuple(jax.ShapeDtypeStruct(shape, jnp.float32) for shape in shapes),
        in_specs=[smem] * smem_count + [vmem] * (len(operands) - smem_count),
        out_specs=tuple(vmem for _ in shapes),
        scratch_shapes=[pltpu.VMEM(shape, jnp.float32) for shape in scratch],
        compiler_params=pltpu.CompilerParams(vmem_limit_bytes=limit * MIB),
        cost_estimate=pl.CostEstimate(flops=flops, bytes_accessed=moved, transcendentals=0),
    )(*operands)


def shift(value, axis, step):
    count = lax.axis_size(axis)
    pairs = [(i, i + step) for i in range(count) if 0 <= i + step < count]
    return lax.ppermute(value, axis, pairs)


def swap(value, axis, bit):
    return lax.ppermute(value, axis, [(i, i ^ bit) for i in range(lax.axis_size(axis))])


def swap_far(value):
    count = lax.axis_size("col")
    pairs = [(i, i + 1) for i in range(1, count - 1, 2)]
    return lax.ppermute(value, "col", pairs + [(j, i) for i, j in pairs])


def sum_over_chips(part):
    bits = [("row", 1)]
    bit = 2
    while bit < lax.axis_size("col"):
        bits.append(("col", bit))
        bit *= 2
    bit = 2
    while bit < lax.axis_size("row"):
        bits.append(("row", bit))
        bit *= 2
    for axis, bit in bits:
        part = part + swap(part, axis, bit)
    return part


def body(object_field, probe, positions, counts, amplitude):
    side = object_field.shape[1]
    width = probe.shape[1]
    half = width // 2
    steps = positions.shape[2]
    slots = positions.shape[3]
    tall_rows = side + 2 * RIM
    odd = lax.axis_index("col") % 2
    row = lax.axis_index("row")
    place = jnp.stack([odd, row, lax.axis_size("row") - 1 - row]).astype(jnp.int32)
    tables = jnp.asarray(dft_tables(width))

    own = jnp.concatenate([positions[0, 0].reshape(steps, 2 * slots), counts[0, 0][:, None]], 1)
    own = own.reshape(1, -1).astype(jnp.float32)
    meta = jnp.pad(own, ((0, TILE - 1), (0, width - own.shape[1])))
    flat = 2 * RIM
    above = shift(
        jnp.concatenate([object_field[:, side - RIM :].reshape(flat, width), meta], 0), "row", 1
    )
    below = shift(jnp.concatenate([object_field[:, :RIM].reshape(flat, width), meta], 0), "row", -1)
    strip = (tall_rows + 3 * TILE, width)
    tall, near, far = call(
        strips_kernel,
        ((2, tall_rows, side), strip, strip),
        1,
        (place, object_field, meta, above, below),
    )
    near, far = swap(near, "col", 1), swap_far(far)

    def three(value):
        return value[tall_rows:].reshape(3, TILE, width)[:, 0, : own.shape[1]]

    here = jnp.stack([above[flat], meta[0], below[flat]])[:, : own.shape[1]]
    left = jnp.where(odd != 0, three(near), three(far))
    right = jnp.where(odd != 0, three(far), three(near))
    metas = jnp.stack([left, here, right], 1).reshape(9, own.shape[1]).astype(jnp.int32)

    current = probe
    for step in range(steps):
        starts = positions[0, 0, step].reshape(-1)
        count = counts[0, 0, step].reshape(1)
        core, out_far, kept, sums = call(
            slots_kernel,
            (
                (3 * half + tall_rows, width),
                (tall_rows, width),
                (3 * half, width),
                (2, tall_rows, width),
            ),
            3,
            (place, starts, count, tall, near, far, current, amplitude[0, 0, step], tables),
            flops=slots * 96 * width * width * width,
            moved=4 * MIB,
            scratch=(
                (2, tall_rows + TILE, 2 * width),
                (2, tall_rows + TILE, 2 * width),
                (3, width, width),
            ),
            limit=24,
        )
        core = swap(core, "col", 1)
        out_far = swap_far(out_far)
        part = sum_over_chips(kept + core[: 3 * half])
        up, down = call(
            fold_kernel,
            ((2, tall_rows // 2, width), (2, tall_rows // 2, width)),
            1,
            (place, sums, core, out_far),
        )
        (weight,) = call(
            lambda *refs, step=step: weight_kernel(*refs, step=step, slots=slots),
            ((tall_rows, width),),
            1,
            (metas, current),
            scratch=((tall_rows + 2 * width + TILE, width),),
        )
        mine = lax.dynamic_slice_in_dim(current, odd * half, half, 1)
        part = part.reshape(3, half, width)
        mine = mine + part[:2] / (part[2] + EPS)[None]
        if step < steps - 1:
            above = shift(down, "row", 1)
            below = shift(up, "row", -1)
            tall, near, far = call(
                update_kernel,
                ((2, tall_rows, side), (tall_rows, width), (tall_rows, width)),
                1,
                (place, tall, up, down, above, below, weight),
            )
            far = swap_far(far)
            other = swap(jnp.concatenate([near, mine.reshape(2 * half, width)], 0), "col", 1)
            near = other
            other = other[tall_rows:].reshape(2, half, width)
        else:
            above = shift(down[:, side - RIM :], "row", 1)
            below = shift(up[:, :RIM], "row", -1)
            num = jnp.concatenate([up[:, RIM:] + above, down[:, : side - RIM] + below], 1)
            tile = tall[:, RIM : RIM + side] + num / (weight[RIM : RIM + side] + EPS)[None]
            other = swap(mine, "col", 1)
        low = jnp.where(odd == 0, mine, other)
        high = jnp.where(odd == 0, other, mine)
        current = jnp.concatenate([low, high], 1)
    return (tile, current)


def solution(mesh):
    return jax.shard_map(
        body,
        mesh=mesh,
        in_specs=(
            P(None, "row", "col"),
            P(),
            P("row", "col", None, None, None),
            P("row", "col", None),
            P("row", "col", None, None, None, None),
        ),
        out_specs=(P(None, "row", "col"), P()),
        check_vma=False,
    )
```

time: 115 us -> 97.2 us (0.85)
  starting transfers between devices: 66.7 us -> 54.3 us
  waiting for transfers between devices: 29.5 us -> 20.4 us
  Pallas kernels: 9.3 us -> 15.8 us
  local copies, waits for them, and re-layouts: 5.01 us -> 3.03 us
  other arithmetic: 3.01 us -> 1.81 us
    ppermute x16 -> x6, starting transfers between devices: 37.3 us -> 16.9 us  [shift(): return lax.ppermute(value, axis, pairs)]
    ppermute x16 -> x6, waiting for transfers between devices: 11 us -> 1.98 us  [shift(): return lax.ppermute(value, axis, pairs)]
    pallas_call x2 -> x8, Pallas kernels: 9.3 us -> 15.8 us  [call(): pl.pallas_call(kernel, out_shape=tuple((jax.ShapeDtypeStruct(shape, jnp.f...]
    ppermute x12 -> x13, starting transfers between devices: 29.4 us -> 34.8 us  [swap(): lax.ppermute(value, axis, [(i, i ^ bit) for i in range(lax.axis_size(axis...]
    ppermute x0 -> x4, starting transfers between devices: none -> 2.65 us  [swap_far(): return lax.ppermute(value, 'col', pairs + [(j, i) for i, j in pairs])]
    ppermute x12 -> x13, waiting for transfers between devices: 18.6 us -> 18.4 us  [swap(): lax.ppermute(value, axis, [(i, i ^ bit) for i in range(lax.axis_size(axis...]
  transfers between devices with their start and end apart: 28 -> 23, of which waited for: 12 -> 12; matrix products, arithmetic and copies ran while one was open for 4% -> 2% of each run, Pallas kernels for 0% -> 6%
where the time goes in v1:
time: 97.2 us; the launch traced here: 96.6 us
  starting transfers between devices  54.3 us (56%)
  waiting for transfers between devices  20.4 us (21%)
  Pallas kernels  15.8 us (16%)
  local copies, waits for them, and re-layouts  3.03 us (3%)
  other arithmetic  1.81 us (2%)
  between operations  1.16 us (1%)
    ppermute x13, starting transfers between devices, swap(): lax.ppermute(value, axis, [(i, i ^ bit) for i in range(lax.axis_size(axis...  34.8 us
    ppermute x13, waiting for transfers between devices, swap(): lax.ppermute(value, axis, [(i, i ^ bit) for i in range(lax.axis_size(axis...  18.4 us
    ppermute x6, starting transfers between devices, shift(): return lax.ppermute(value, axis, pairs)  16.9 us
    pallas_call x8, Pallas kernels, call(): pl.pallas_call(kernel, out_shape=tuple((jax.ShapeDtypeStruct(shape, jnp.f...  15.8 us
    ppermute x4, starting transfers between devices, swap_far(): return lax.ppermute(value, 'col', pairs + [(j, i) for i, j in pairs])  2.65 us
    ppermute x6, waiting for transfers between devices, shift(): return lax.ppermute(value, axis, pairs)  1.98 us
  transfers between devices with their start and end apart: 23, of which 12 were waited for; matrix products, arithmetic and copies ran while one was open for 2% of the time, Pallas kernels for 6%

profile of v1, /device:TPU:0, one launch (start us, length us, event | category | flops | bytes accessed | tf_op | source)
XLA Modules:
  0.0 96.6 jit_solution(10228959992205639592)
XLA Ops:
  0.7 0.6 copy-done.7
  1.3 0.1 copy.16
  1.4 0.1 copy.15
  1.5 0.1 reshape_squeeze.15
  1.6 0.1 add_convert_fusion
  1.6 0.1 convert_element_type.22
  1.7 0.9 fusion.3
  2.6 1.3 %collective-permute-start.1 = (f32[136,128]{1,0:T(8,128)S(1)}, f32[136,128]{1,0:T(8,128)S(1)}, u32[]{:S(2)}, u32[]{:S(2)}) collective-permute-start(f32[136,128]{1,0:T(8,128)S(1)} %get-tuple-element.48), channel_id=1, source_target_pairs={{4,0},{8,4},{12,8},{16,12},{20,16},{24,20},{28,24},{5,1},{9,5},{13... | collective-permute-start | bytes 208904 | tf_op jit(solution)/shard_map/ppermute | solution.py:253
  4.0 5.5 %collective-permute-start = (f32[136,128]{1,0:T(8,128)S(1)}, f32[136,128]{1,0:T(8,128)S(1)}, u32[]{:S(2)}, u32[]{:S(2)}) collective-permute-start(f32[136,128]{1,0:T(8,128)S(1)} %get-tuple-element.49), channel_id=1, source_target_pairs={{0,4},{4,8},{8,12},{12,16},{16,20},{20,24},{24,28},{1,5},{5,9},{9,... | collective-permute-start | bytes 208904 | tf_op jit(solution)/shard_map/ppermute | solution.py:253
  9.5 0.0 copy-start
  9.5 0.0 copy-start.4
  9.6 0.1 pad_add_fusion.place
  9.7 0.2 collective-permute-done.1.below
  9.8 1.8 %collective-permute-done.above = f32[136,128]{1,0:T(8,128)S(1)} collective-permute-done((f32[136,128]{1,0:T(8,128)S(1)}, f32[136,128]{1,0:T(8,128)S(1)}, u32[]{:S(2)}, u32[]{:S(2)}) %collective-permute-start) | collective-permute-done | bytes 69664 | tf_op jit(solution)/shard_map/ppermute | solution.py:253
  11.6 0.7 shard_map.77
  12.3 0.1 collective-permute-start.2
  12.4 0.7 collective-permute-start.3
  13.1 0.1 copy.17
  13.2 0.1 reshape_squeeze.16.starts
  13.3 0.6 fusion.5
  13.9 0.0 collective-permute-done.3.far
  14.0 4.8 %shard_map.78 = (f32[448,128]{1,0:T(8,128)S(1)}, f32[256,128]{1,0:T(8,128)S(1)}, f32[192,128]{1,0:T(8,128)S(1)}, f32[2,256,128]{2,1,0:T(8,128)S(1)}) custom-call(s32[3]{0:T(128)S(1)} %pad_add_fusion.place, s32[8]{0:T(128)S(1)} %reshape_squeeze.16.starts, s32[1]{0:T(128)} %bitcast.6.count, f32[2,256,128]{2,1,0:T(8,128)S(1)} %get-tuple-element.20.tall, ...), custom_call_target="tpu_custom_call" | custom-call | flops 805306368 | bytes 4194304 | tf_op jit(solution)/shard_map/pallas_call | solution.py:239
  18.8 0.0 slice-start
  18.8 0.0 slice-start.1
  18.8 5.4 %collective-permute-start.4 = (f32[448,128]{1,0:T(8,128)S(1)}, f32[448,128]{1,0:T(8,128)S(1)}, u32[]{:S(2)}, u32[]{:S(2)}) collective-permute-start(f32[448,128]{1,0:T(8,128)S(1)} %get-tuple-element.24), channel_id=1, source_target_pairs={{0,1},{1,0},{2,3},{3,2},{4,5},{5,4},{6,7},{7,6},{8,9},{9,8},{10,11... | collective-permute-start | bytes 688136 | tf_op jit(solution)/shard_map/ppermute | solution.py:257
  24.3 0.7 collective-permute-start.5
  24.9 0.4 collective-permute-done.4.near
  25.4 2.7 %collective-permute-start.8 = (f32[192,128]{1,0:T(8,128)S(1)}, f32[192,128]{1,0:T(8,128)S(1)}, u32[]{:S(2)}, u32[]{:S(2)}) collective-permute-start(f32[192,128]{1,0:T(8,128)S(1)} %slice_add_fusion.1), channel_id=1, source_target_pairs={{0,4},{4,0},{8,12},{12,8},{16,20},{20,16},{24,28},{28,24},{1,5},{5... | collective-permute-start | bytes 294920 | tf_op jit(solution)/shard_map/ppermute | solution.py:257
  28.1 2.6 %collective-permute-done.8 = f32[192,128]{1,0:T(8,128)S(1)} collective-permute-done((f32[192,128]{1,0:T(8,128)S(1)}, f32[192,128]{1,0:T(8,128)S(1)}, u32[]{:S(2)}, u32[]{:S(2)}) %collective-permute-start.8) | collective-permute-done | bytes 98336 | tf_op jit(solution)/shard_map/ppermute | solution.py:257
  30.7 3.1 %collective-permute-start.9 = (f32[192,128]{1,0:T(8,128)S(1)}, f32[192,128]{1,0:T(8,128)S(1)}, u32[]{:S(2)}, u32[]{:S(2)}) collective-permute-start(f32[192,128]{1,0:T(8,128)S(1)} %add.74), channel_id=1, source_target_pairs={{0,2},{1,3},{2,0},{3,1},{4,6},{5,7},{6,4},{7,5},{8,10},{9,11},{10,... | collective-permute-start | bytes 294920 | tf_op jit(solution)/shard_map/ppermute | solution.py:257
  33.8 0.0 collective-permute-done.5.far
  33.8 0.7 shard_map.79
  34.5 1.3 %collective-permute-start.7 = (f32[2,128,128]{2,1,0:T(8,128)S(1)}, f32[2,128,128]{2,1,0:T(8,128)S(1)}, u32[]{:S(2)}, u32[]{:S(2)}) collective-permute-start(f32[2,128,128]{2,1,0:T(8,128)S(1)} %get-tuple-element.26.up), channel_id=1, source_target_pairs={{4,0},{8,4},{12,8},{16,12},{20,16},{24,20},{28,24},{5,1},{9,5},{13... | collective-permute-start | bytes 393224 | tf_op jit(solution)/shard_map/ppermute | solution.py:253
  35.8 4.6 %collective-permute-start.6 = (f32[2,128,128]{2,1,0:T(8,128)S(1)}, f32[2,128,128]{2,1,0:T(8,128)S(1)}, u32[]{:S(2)}, u32[]{:S(2)}) collective-permute-start(f32[2,128,128]{2,1,0:T(8,128)S(1)} %get-tuple-element.27.down), channel_id=1, source_target_pairs={{0,4},{4,8},{8,12},{12,16},{16,20},{20,24},{24,28},{1,5},{5,9},{9,... | collective-permute-start | bytes 393224 | tf_op jit(solution)/shard_map/ppermute | solution.py:253
  40.4 3.9 %collective-permute-start.10 = (f32[192,128]{1,0:T(8,128)S(1)}, f32[192,128]{1,0:T(8,128)S(1)}, u32[]{:S(2)}, u32[]{:S(2)}) collective-permute-start(f32[192,128]{1,0:T(8,128)S(1)} %add.75), channel_id=1, source_target_pairs={{0,8},{4,12},{8,0},{12,4},{16,24},{20,28},{24,16},{28,20},{1,9},{5... | collective-permute-start | bytes 294920 | tf_op jit(solution)/shard_map/ppermute | solution.py:257
  44.3 2.6 %collective-permute-done.10 = f32[192,128]{1,0:T(8,128)S(1)} collective-permute-done((f32[192,128]{1,0:T(8,128)S(1)}, f32[192,128]{1,0:T(8,128)S(1)}, u32[]{:S(2)}, u32[]{:S(2)}) %collective-permute-start.10) | collective-permute-done | bytes 98336 | tf_op jit(solution)/shard_map/ppermute | solution.py:257
  46.9 3.6 %collective-permute-start.11 = (f32[192,128]{1,0:T(8,128)S(1)}, f32[192,128]{1,0:T(8,128)S(1)}, u32[]{:S(2)}, u32[]{:S(2)}) collective-permute-start(f32[192,128]{1,0:T(8,128)S(1)} %add.76), channel_id=1, source_target_pairs={{0,16},{4,20},{8,24},{12,28},{16,0},{20,4},{24,8},{28,12},{1,17},{... | collective-permute-start | bytes 294920 | tf_op jit(solution)/shard_map/ppermute | solution.py:257
  50.5 1.7 %shard_map.80.weight = f32[256,128]{1,0:T(8,128)S(1)} custom-call(s32[9,18]{1,0:T(8,128)S(1)} %convert_element_type.24.refs_0_, f32[2,128,128]{2,1,0:T(8,128)S(1)} %copy-done.1), custom_call_target="tpu_custom_call" | custom-call | flops 1000000 | bytes 1048576 | tf_op jit(solution)/shard_map/pallas_call | solution.py:239
  52.2 0.7 shard_map.81
  52.9 1.2 %collective-permute-done.11 = f32[192,128]{1,0:T(8,128)S(1)} collective-permute-done((f32[192,128]{1,0:T(8,128)S(1)}, f32[192,128]{1,0:T(8,128)S(1)}, u32[]{:S(2)}, u32[]{:S(2)}) %collective-permute-start.11) | collective-permute-done | bytes 98336 | tf_op jit(solution)/shard_map/ppermute | solution.py:257
  54.3 0.1 collective-permute-start.12
  54.3 0.1 copy.21
  54.4 0.1 reshape_squeeze.18.starts
  54.5 0.7 collective-permute-start.13
  55.2 0.6 collective-permute-done.12.near
  55.8 4.9 %shard_map.82 = (f32[448,128]{1,0:T(8,128)S(1)}, f32[256,128]{1,0:T(8,128)S(1)}, f32[192,128]{1,0:T(8,128)S(1)}, f32[2,256,128]{2,1,0:T(8,128)S(1)}) custom-call(s32[3]{0:T(128)S(1)} %pad_add_fusion.place, s32[8]{0:T(128)S(1)} %reshape_squeeze.18.starts, s32[1]{0:T(128)} %bitcast.11.count, f32[2,256,128]{2,1,0:T(8,128)S(1)} %get-tuple-element.28.tall, ...), custom_call_target="tpu_custom_call" | custom-call | flops 805306368 | bytes 4194304 | tf_op jit(solution)/shard_map/pallas_call | solution.py:239
  60.7 5.5 %collective-permute-start.14 = (f32[448,128]{1,0:T(8,128)S(1)}, f32[448,128]{1,0:T(8,128)S(1)}, u32[]{:S(2)}, u32[]{:S(2)}) collective-permute-start(f32[448,128]{1,0:T(8,128)S(1)} %get-tuple-element.33), channel_id=1, source_target_pairs={{0,1},{1,0},{2,3},{3,2},{4,5},{5,4},{6,7},{7,6},{8,9},{9,8},{10,11... | collective-permute-start | bytes 688136 | tf_op jit(solution)/shard_map/ppermute | solution.py:257
  66.2 0.7 collective-permute-start.15
  66.9 0.5 collective-permute-done.14.near
  67.3 1.1 %collective-permute-start.18 = (f32[192,128]{1,0:T(8,128)S(1)}, f32[192,128]{1,0:T(8,128)S(1)}, u32[]{:S(2)}, u32[]{:S(2)}) collective-permute-start(f32[192,128]{1,0:T(8,128)S(1)} %slice_add_fusion), channel_id=1, source_target_pairs={{0,4},{4,0},{8,12},{12,8},{16,20},{20,16},{24,28},{28,24},{1,5},{5... | collective-permute-start | bytes 294920 | tf_op jit(solution)/shard_map/ppermute | solution.py:257
  68.4 0.7 shard_map.83
  69.1 2.9 %collective-permute-start.16 = (f32[2,64,128]{2,1,0:T(8,128)S(1)}, f32[2,64,128]{2,1,0:T(8,128)S(1)}, u32[]{:S(2)}, u32[]{:S(2)}) collective-permute-start(f32[2,64,128]{2,1,0:T(8,128)S(1)} %slice.122), channel_id=1, source_target_pairs={{0,4},{4,8},{8,12},{12,16},{16,20},{20,24},{24,28},{1,5},{5,9},{9,... | collective-permute-start | bytes 196616 | tf_op jit(solution)/shard_map/ppermute | solution.py:253
  72.0 1.7 %shard_map.84 = f32[256,128]{1,0:T(8,128)S(1)} custom-call(s32[9,18]{1,0:T(8,128)S(1)} %convert_element_type.24.refs_0_, f32[2,128,128]{2,1,0:T(8,128)S(1)} %pad_maximum_fusion.1.probe.refs_1_), custom_call_target="tpu_custom_call" | custom-call | flops 1000000 | bytes 1048576 | tf_op jit(solution)/shard_map/pallas_call | solution.py:239
  73.8 5.2 %collective-permute-start.19 = (f32[192,128]{1,0:T(8,128)S(1)}, f32[192,128]{1,0:T(8,128)S(1)}, u32[]{:S(2)}, u32[]{:S(2)}) collective-permute-start(f32[192,128]{1,0:T(8,128)S(1)} %add.86), channel_id=1, source_target_pairs={{0,2},{1,3},{2,0},{3,1},{4,6},{5,7},{6,4},{7,5},{8,10},{9,11},{10,... | collective-permute-start | bytes 294920 | tf_op jit(solution)/shard_map/ppermute | solution.py:257
  79.0 1.3 %collective-permute-start.17 = (f32[2,64,128]{2,1,0:T(8,128)S(1)}, f32[2,64,128]{2,1,0:T(8,128)S(1)}, u32[]{:S(2)}, u32[]{:S(2)}) collective-permute-start(f32[2,64,128]{2,1,0:T(8,128)S(1)} %get-tuple-element.43), channel_id=1, source_target_pairs={{4,0},{8,4},{12,8},{16,12},{20,16},{24,20},{28,24},{5,1},{9,5},{13... | collective-permute-start | bytes 196616 | tf_op jit(solution)/shard_map/ppermute | solution.py:253
  80.3 2.3 %collective-permute-done.19 = f32[192,128]{1,0:T(8,128)S(1)} collective-permute-done((f32[192,128]{1,0:T(8,128)S(1)}, f32[192,128]{1,0:T(8,128)S(1)}, u32[]{:S(2)}, u32[]{:S(2)}) %collective-permute-start.19) | collective-permute-done | bytes 98336 | tf_op jit(solution)/shard_map/ppermute | solution.py:257
  82.6 1.3 %collective-permute-start.20 = (f32[192,128]{1,0:T(8,128)S(1)}, f32[192,128]{1,0:T(8,128)S(1)}, u32[]{:S(2)}, u32[]{:S(2)}) collective-permute-start(f32[192,128]{1,0:T(8,128)S(1)} %add.87), channel_id=1, source_target_pairs={{0,8},{4,12},{8,0},{12,4},{16,24},{20,28},{24,16},{28,20},{1,9},{5... | collective-permute-start | bytes 294920 | tf_op jit(solution)/shard_map/ppermute | solution.py:257
  84.0 3.6 %collective-permute-done.20 = f32[192,128]{1,0:T(8,128)S(1)} collective-permute-done((f32[192,128]{1,0:T(8,128)S(1)}, f32[192,128]{1,0:T(8,128)S(1)}, u32[]{:S(2)}, u32[]{:S(2)}) %collective-permute-start.20) | collective-permute-done | bytes 98336 | tf_op jit(solution)/shard_map/ppermute | solution.py:257
  87.6 2.7 %collective-permute-start.21 = (f32[192,128]{1,0:T(8,128)S(1)}, f32[192,128]{1,0:T(8,128)S(1)}, u32[]{:S(2)}, u32[]{:S(2)}) collective-permute-start(f32[192,128]{1,0:T(8,128)S(1)} %add.88), channel_id=1, source_target_pairs={{0,16},{4,20},{8,24},{12,28},{16,0},{20,4},{24,8},{28,12},{1,17},{... | collective-permute-start | bytes 294920 | tf_op jit(solution)/shard_map/ppermute | solution.py:257
  90.4 4.1 %collective-permute-done.21 = f32[192,128]{1,0:T(8,128)S(1)} collective-permute-done((f32[192,128]{1,0:T(8,128)S(1)}, f32[192,128]{1,0:T(8,128)S(1)}, u32[]{:S(2)}, u32[]{:S(2)}) %collective-permute-start.21) | collective-permute-done | bytes 98336 | tf_op jit(solution)/shard_map/ppermute | solution.py:257
  94.6 0.1 collective-permute-start.22
  94.7 0.7 fusion
  95.3 0.6 collective-permute-done.22
  95.9 0.7 pad_maximum_fusion.2
  (64 shorter events, 0.5 us)
Async XLA Ops:
  0.6 0.7 copy-start.7
  0.6 0.7 copy-start.6
  0.7 8.8 %copy-start.5 = (f32[1,1,2,4,128,128]{5,4,3,2,1,0:T(8,128)S(1)}, f32[1,1,2,4,128,128]{5,4,3,2,1,0:T(8,128)}, u32[]{:S(2)}) copy-start(f32[1,1,2,4,128,128]{5,4,3,2,1,0:T(8,128)} %param.10) | copy-start | bytes 1572868
  2.6 7.2 %collective-permute-start.1 = (f32[136,128]{1,0:T(8,128)S(1)}, f32[136,128]{1,0:T(8,128)S(1)}, u32[]{:S(2)}, u32[]{:S(2)}) collective-permute-start(f32[136,128]{1,0:T(8,128)S(1)} %get-tuple-element.48), channel_id=1, source_target_pairs={{4,0},{8,4},{12,8},{16,12},{20,16},{24,20},{28,24},{5,1},{9,5},{13... | collective-permute-start | bytes 208904 | tf_op jit(solution)/shard_map/ppermute | solution.py:253
  4.0 7.7 %collective-permute-start = (f32[136,128]{1,0:T(8,128)S(1)}, f32[136,128]{1,0:T(8,128)S(1)}, u32[]{:S(2)}, u32[]{:S(2)}) collective-permute-start(f32[136,128]{1,0:T(8,128)S(1)} %get-tuple-element.49), channel_id=1, source_target_pairs={{0,4},{4,8},{8,12},{12,16},{16,20},{20,24},{24,28},{1,5},{5,9},{9,... | collective-permute-start | bytes 208904 | tf_op jit(solution)/shard_map/ppermute | solution.py:253
  9.5 2.1 %copy-start = (f32[2,128,128]{2,1,0:T(8,128)S(1)}, f32[2,128,128]{2,1,0:T(8,128)}, u32[]{:S(2)}) copy-start(f32[2,128,128]{2,1,0:T(8,128)} %tile.1) | copy-start | bytes 393220
  9.5 4.4 %copy-start.4 = (bf16[4,256,256]{2,1,0:T(8,128)(2,1)S(1)}, bf16[4,256,256]{2,1,0:T(8,128)(2,1)}, u32[]{:S(2)}) copy-start(bf16[4,256,256]{2,1,0:T(8,128)(2,1)} %constant.36.clone.tables) | copy-start | bytes 1572868
  9.7 4.3 %copy-start.1 = (f32[2,128,128]{2,1,0:T(8,128)S(1)}, f32[2,128,128]{2,1,0:T(8,128)}, u32[]{:S(2)}) copy-start(f32[2,128,128]{2,1,0:T(8,128)} %refs_1_.1) | copy-start | bytes 393220
  9.8 4.1 %copy-start.2 = (f32[136,128]{1,0:T(8,128)}, f32[136,128]{1,0:T(8,128)S(1)}, u32[]{:S(2)}) copy-start(f32[136,128]{1,0:T(8,128)S(1)} %collective-permute-done.1.below) | copy-start | bytes 208900
  11.6 2.3 %copy-start.3 = (f32[136,128]{1,0:T(8,128)}, f32[136,128]{1,0:T(8,128)S(1)}, u32[]{:S(2)}) copy-start(f32[136,128]{1,0:T(8,128)S(1)} %collective-permute-done.above) | copy-start | bytes 208900
  12.3 1.6 %collective-permute-start.2 = (f32[280,128]{1,0:T(8,128)S(1)}, f32[280,128]{1,0:T(8,128)S(1)}, u32[]{:S(2)}, u32[]{:S(2)}) collective-permute-start(f32[280,128]{1,0:T(8,128)S(1)} %get-tuple-element.21), channel_id=1, source_target_pairs={{0,1},{1,0},{2,3},{3,2},{4,5},{5,4},{6,7},{7,6},{8,9},{9,8},{10,11... | collective-permute-start | bytes 430088 | tf_op jit(solution)/shard_map/ppermute | solution.py:257
  12.4 1.5 %collective-permute-start.3 = (f32[280,128]{1,0:T(8,128)S(1)}, f32[280,128]{1,0:T(8,128)S(1)}, u32[]{:S(2)}, u32[]{:S(2)}) collective-permute-start(f32[280,128]{1,0:T(8,128)S(1)} %get-tuple-element.22), channel_id=1, source_target_pairs={{1,2},{2,1},{5,6},{6,5},{9,10},{10,9},{13,14},{14,13},{17,18},{18,... | collective-permute-start | bytes 430088 | tf_op jit(solution)/shard_map/ppermute | solution.py:263
  18.8 5.4 %slice-start = ((f32[136,128]{1,0:T(8,128)}), f32[1,128]{1,0:T(1,128)S(1)}, s32[]{:S(2)}) async-start(f32[136,128]{1,0:T(8,128)} %copy-done.2), calls=%async_computation | async-start | bytes 1024 | tf_op jit(solution)/shard_map/slice | solution.py:313
  18.8 5.4 %slice-start.1 = ((f32[136,128]{1,0:T(8,128)}), f32[1,128]{1,0:T(1,128)S(1)}, s32[]{:S(2)}) async-start(f32[136,128]{1,0:T(8,128)} %copy-done.3), calls=%async_computation.1 | async-start | bytes 1024 | tf_op jit(solution)/shard_map/slice | solution.py:313
  18.8 6.5 %collective-permute-start.4 = (f32[448,128]{1,0:T(8,128)S(1)}, f32[448,128]{1,0:T(8,128)S(1)}, u32[]{:S(2)}, u32[]{:S(2)}) collective-permute-start(f32[448,128]{1,0:T(8,128)S(1)} %get-tuple-element.24), channel_id=1, source_target_pairs={{0,1},{1,0},{2,3},{3,2},{4,5},{5,4},{6,7},{7,6},{8,9},{9,8},{10,11... | collective-permute-start | bytes 688136 | tf_op jit(solution)/shard_map/ppermute | solution.py:257
  24.3 9.6 %collective-permute-start.5 = (f32[256,128]{1,0:T(8,128)S(1)}, f32[256,128]{1,0:T(8,128)S(1)}, u32[]{:S(2)}, u32[]{:S(2)}) collective-permute-start(f32[256,128]{1,0:T(8,128)S(1)} %get-tuple-element.25), channel_id=1, source_target_pairs={{1,2},{2,1},{5,6},{6,5},{9,10},{10,9},{13,14},{14,13},{17,18},{18,... | collective-permute-start | bytes 393224 | tf_op jit(solution)/shard_map/ppermute | solution.py:263
  25.4 5.3 %collective-permute-start.8 = (f32[192,128]{1,0:T(8,128)S(1)}, f32[192,128]{1,0:T(8,128)S(1)}, u32[]{:S(2)}, u32[]{:S(2)}) collective-permute-start(f32[192,128]{1,0:T(8,128)S(1)} %slice_add_fusion.1), channel_id=1, source_target_pairs={{0,4},{4,0},{8,12},{12,8},{16,20},{20,16},{24,28},{28,24},{1,5},{5... | collective-permute-start | bytes 294920 | tf_op jit(solution)/shard_map/ppermute | solution.py:257
  30.7 9.7 %collective-permute-start.9 = (f32[192,128]{1,0:T(8,128)S(1)}, f32[192,128]{1,0:T(8,128)S(1)}, u32[]{:S(2)}, u32[]{:S(2)}) collective-permute-start(f32[192,128]{1,0:T(8,128)S(1)} %add.74), channel_id=1, source_target_pairs={{0,2},{1,3},{2,0},{3,1},{4,6},{5,7},{6,4},{7,5},{8,10},{9,11},{10,... | collective-permute-start | bytes 294920 | tf_op jit(solution)/shard_map/ppermute | solution.py:257
  34.5 17.7 %collective-permute-start.7 = (f32[2,128,128]{2,1,0:T(8,128)S(1)}, f32[2,128,128]{2,1,0:T(8,128)S(1)}, u32[]{:S(2)}, u32[]{:S(2)}) collective-permute-start(f32[2,128,128]{2,1,0:T(8,128)S(1)} %get-tuple-element.26.up), channel_id=1, source_target_pairs={{4,0},{8,4},{12,8},{16,12},{20,16},{24,20},{28,24},{5,1},{9,5},{13... | collective-permute-start | bytes 393224 | tf_op jit(solution)/shard_map/ppermute | solution.py:253
  35.8 16.4 %collective-permute-start.6 = (f32[2,128,128]{2,1,0:T(8,128)S(1)}, f32[2,128,128]{2,1,0:T(8,128)S(1)}, u32[]{:S(2)}, u32[]{:S(2)}) collective-permute-start(f32[2,128,128]{2,1,0:T(8,128)S(1)} %get-tuple-element.27.down), channel_id=1, source_target_pairs={{0,4},{4,8},{8,12},{12,16},{16,20},{20,24},{24,28},{1,5},{5,9},{9,... | collective-permute-start | bytes 393224 | tf_op jit(solution)/shard_map/ppermute | solution.py:253
  40.4 6.5 %collective-permute-start.10 = (f32[192,128]{1,0:T(8,128)S(1)}, f32[192,128]{1,0:T(8,128)S(1)}, u32[]{:S(2)}, u32[]{:S(2)}) collective-permute-start(f32[192,128]{1,0:T(8,128)S(1)} %add.75), channel_id=1, source_target_pairs={{0,8},{4,12},{8,0},{12,4},{16,24},{20,28},{24,16},{28,20},{1,9},{5... | collective-permute-start | bytes 294920 | tf_op jit(solution)/shard_map/ppermute | solution.py:257
  46.9 7.2 %collective-permute-start.11 = (f32[192,128]{1,0:T(8,128)S(1)}, f32[192,128]{1,0:T(8,128)S(1)}, u32[]{:S(2)}, u32[]{:S(2)}) collective-permute-start(f32[192,128]{1,0:T(8,128)S(1)} %add.76), channel_id=1, source_target_pairs={{0,16},{4,20},{8,24},{12,28},{16,0},{20,4},{24,8},{28,12},{1,17},{... | collective-permute-start | bytes 294920 | tf_op jit(solution)/shard_map/ppermute | solution.py:257
  54.3 1.5 %collective-permute-start.12 = (f32[384,128]{1,0:T(8,128)S(1)}, f32[384,128]{1,0:T(8,128)S(1)}, u32[]{:S(2)}, u32[]{:S(2)}) collective-permute-start(f32[384,128]{1,0:T(8,128)S(1)} %pad_maximum_fusion), channel_id=1, source_target_pairs={{0,1},{1,0},{2,3},{3,2},{4,5},{5,4},{6,7},{7,6},{8,9},{9,8},{10,11... | collective-permute-start | bytes 589832 | tf_op jit(solution)/shard_map/ppermute | solution.py:257
  54.5 1.3 %collective-permute-start.13 = (f32[256,128]{1,0:T(8,128)S(1)}, f32[256,128]{1,0:T(8,128)S(1)}, u32[]{:S(2)}, u32[]{:S(2)}) collective-permute-start(f32[256,128]{1,0:T(8,128)S(1)} %get-tuple-element.31), channel_id=1, source_target_pairs={{1,2},{2,1},{5,6},{6,5},{9,10},{10,9},{13,14},{14,13},{17,18},{18,... | collective-permute-start | bytes 393224 | tf_op jit(solution)/shard_map/ppermute | solution.py:263
  60.7 6.6 %collective-permute-start.14 = (f32[448,128]{1,0:T(8,128)S(1)}, f32[448,128]{1,0:T(8,128)S(1)}, u32[]{:S(2)}, u32[]{:S(2)}) collective-permute-start(f32[448,128]{1,0:T(8,128)S(1)} %get-tuple-element.33), channel_id=1, source_target_pairs={{0,1},{1,0},{2,3},{3,2},{4,5},{5,4},{6,7},{7,6},{8,9},{9,8},{10,11... | collective-permute-start | bytes 688136 | tf_op jit(solution)/shard_map/ppermute | solution.py:257
  66.2 2.2 %collective-permute-start.15 = (f32[256,128]{1,0:T(8,128)S(1)}, f32[256,128]{1,0:T(8,128)S(1)}, u32[]{:S(2)}, u32[]{:S(2)}) collective-permute-start(f32[256,128]{1,0:T(8,128)S(1)} %get-tuple-element.34), channel_id=1, source_target_pairs={{1,2},{2,1},{5,6},{6,5},{9,10},{10,9},{13,14},{14,13},{17,18},{18,... | collective-permute-start | bytes 393224 | tf_op jit(solution)/shard_map/ppermute | solution.py:263
  67.3 6.5 %collective-permute-start.18 = (f32[192,128]{1,0:T(8,128)S(1)}, f32[192,128]{1,0:T(8,128)S(1)}, u32[]{:S(2)}, u32[]{:S(2)}) collective-permute-start(f32[192,128]{1,0:T(8,128)S(1)} %slice_add_fusion), channel_id=1, source_target_pairs={{0,4},{4,0},{8,12},{12,8},{16,20},{20,16},{24,28},{28,24},{1,5},{5... | collective-permute-start | bytes 294920 | tf_op jit(solution)/shard_map/ppermute | solution.py:257
  69.1 9.9 %collective-permute-start.16 = (f32[2,64,128]{2,1,0:T(8,128)S(1)}, f32[2,64,128]{2,1,0:T(8,128)S(1)}, u32[]{:S(2)}, u32[]{:S(2)}) collective-permute-start(f32[2,64,128]{2,1,0:T(8,128)S(1)} %slice.122), channel_id=1, source_target_pairs={{0,4},{4,8},{8,12},{12,16},{16,20},{20,24},{24,28},{1,5},{5,9},{9,... | collective-permute-start | bytes 196616 | tf_op jit(solution)/shard_map/ppermute | solution.py:253
  73.8 8.8 %collective-permute-start.19 = (f32[192,128]{1,0:T(8,128)S(1)}, f32[192,128]{1,0:T(8,128)S(1)}, u32[]{:S(2)}, u32[]{:S(2)}) collective-permute-start(f32[192,128]{1,0:T(8,128)S(1)} %add.86), channel_id=1, source_target_pairs={{0,2},{1,3},{2,0},{3,1},{4,6},{5,7},{6,4},{7,5},{8,10},{9,11},{10,... | collective-permute-start | bytes 294920 | tf_op jit(solution)/shard_map/ppermute | solution.py:257
  79.0 11.3 %collective-permute-start.17 = (f32[2,64,128]{2,1,0:T(8,128)S(1)}, f32[2,64,128]{2,1,0:T(8,128)S(1)}, u32[]{:S(2)}, u32[]{:S(2)}) collective-permute-start(f32[2,64,128]{2,1,0:T(8,128)S(1)} %get-tuple-element.43), channel_id=1, source_target_pairs={{4,0},{8,4},{12,8},{16,12},{20,16},{24,20},{28,24},{5,1},{9,5},{13... | collective-permute-start | bytes 196616 | tf_op jit(solution)/shard_map/ppermute | solution.py:253
  82.6 5.0 %collective-permute-start.20 = (f32[192,128]{1,0:T(8,128)S(1)}, f32[192,128]{1,0:T(8,128)S(1)}, u32[]{:S(2)}, u32[]{:S(2)}) collective-permute-start(f32[192,128]{1,0:T(8,128)S(1)} %add.87), channel_id=1, source_target_pairs={{0,8},{4,12},{8,0},{12,4},{16,24},{20,28},{24,16},{28,20},{1,9},{5... | collective-permute-start | bytes 294920 | tf_op jit(solution)/shard_map/ppermute | solution.py:257
  87.6 6.9 %collective-permute-start.21 = (f32[192,128]{1,0:T(8,128)S(1)}, f32[192,128]{1,0:T(8,128)S(1)}, u32[]{:S(2)}, u32[]{:S(2)}) collective-permute-start(f32[192,128]{1,0:T(8,128)S(1)} %add.88), channel_id=1, source_target_pairs={{0,16},{4,20},{8,24},{12,28},{16,0},{20,4},{24,8},{28,12},{1,17},{... | collective-permute-start | bytes 294920 | tf_op jit(solution)/shard_map/ppermute | solution.py:257
  94.6 1.3 %collective-permute-start.22 = (f32[2,64,128]{2,1,0:T(8,128)S(1)}, f32[2,64,128]{2,1,0:T(8,128)S(1)}, u32[]{:S(2)}, u32[]{:S(2)}) collective-permute-start(f32[2,64,128]{2,1,0:T(8,128)S(1)} %fusion.2), channel_id=1, source_target_pairs={{0,1},{1,0},{2,3},{3,2},{4,5},{5,4},{6,7},{7,6},{8,9},{9,8},{10,11... | collective-permute-start | bytes 196616 | tf_op jit(solution)/shard_map/ppermute | solution.py:257

commit v2 on v1

--- a/solution.py
+++ b/solution.py
@@ -11,6 +11,7 @@
 RIM = 64
 TILE = 8
 EPS = 0.1
+AXES = ("row", "col")
 MIB = 1024 * 1024
 
 
@@ -83,9 +84,11 @@
     return jnp.where(col < 0, col + width, col)
 
 
-def strips_kernel(place, tile, meta, above, below, tall, near, far):
+def strips_kernel(place, tile, meta, first, second, tall, near, far):
     side = tile.shape[1]
-    odd = place[0] != 0
+    odd, odd_row = place[0] != 0, place[1] != 0
+    above = jnp.where(place[2] != 0, jnp.where(odd_row, first[...], second[...]), 0.0)
+    below = jnp.where(place[3] != 0, jnp.where(odd_row, second[...], first[...]), 0.0)
     for part in range(2):
         tall[part, :RIM] = above[part * RIM : (part + 1) * RIM]
         tall[part, RIM : RIM + side] = tile[part]
@@ -110,7 +113,7 @@
     odd = place[0] != 0
     lane = lanes((width + TILE, width))
     sub = lax.broadcasted_iota(jnp.int32, (tiles, TILE, width), 1)
-    from_near, from_far = near[:rows_all], far[:rows_all]
+    from_near, from_far = near[:rows_all], jnp.where(place[4] != 0, far[:rows_all], 0.0)
     sides = unpack(jnp.where(odd, from_far, from_near), jnp.where(odd, from_near, from_far))
     for part in range(2):
         field[part, :rows_all, :width] = tall[part]
@@ -180,16 +183,33 @@
     far_out[...] = jnp.where(odd, low, high)
 
 
-def fold_kernel(place, tall, near, far, up, down):
-    rows = up.shape[1]
+def folded(place, tall, near, far):
     start = near.shape[0] - tall.shape[1]
     odd = place[0] != 0
-    from_near, from_far = near[start:], far[...]
+    from_near, from_far = near[start:], jnp.where(place[4] != 0, far[...], 0.0)
     extra = unpack(jnp.where(odd, from_near, from_far), jnp.where(odd, from_far, from_near))
-    for part in range(2):
-        whole = tall[part] + extra[part]
-        up[part] = whole[:rows]
-        down[part] = whole[rows:]
+    return tall[0] + extra[0], tall[1] + extra[1]
+
+
+def fold_kernel(place, tall, near, far, first, second):
+    rows = first.shape[1]
+    odd_row = place[1] != 0
+    whole = folded(place, tall, near, far)
+    for part in range(2):
+        up, down = whole[part][:rows], whole[part][rows:]
+        first[part] = jnp.where(odd_row, up, down)
+        second[part] = jnp.where(odd_row, down, up)
+
+
+def last_fold_kernel(place, tall, near, far, middle, first, second):
+    rows = middle.shape[1]
+    odd_row = place[1] != 0
+    whole = folded(place, tall, near, far)
+    for part in range(2):
+        up, down = whole[part][:RIM], whole[part][RIM + rows :]
+        middle[part] = whole[part][RIM : RIM + rows]
+        first[part] = jnp.where(odd_row, up, down)
+        second[part] = jnp.where(odd_row, down, up)
 
 
 def weight_kernel(metas, probe, out, spread, *, step, slots):
@@ -216,21 +236,37 @@
     out[...] = spread[width : width + out.shape[0]]
 
 
-def update_kernel(place, tall, up, down, above, below, weight, new_tall, near, far):
-    rows = up.shape[1]
-    odd = place[0] != 0
-    first = jnp.where(place[1] != 0, 1.0, 0.0).astype(jnp.float32)
-    last = jnp.where(place[2] != 0, 1.0, 0.0).astype(jnp.float32)
-    for part in range(2):
-        head = tall[part, :rows] + (up[part] + above[part]) / (weight[:rows] + EPS)
-        tail = tall[part, rows:] + (down[part] + below[part]) / (weight[rows:] + EPS)
-        new_tall[part, :RIM] = head[:RIM] * first
+def update_kernel(place, tall, sent_1, sent_2, got_1, got_2, weight, new_tall, near, far):
+    rows = sent_1.shape[1]
+    odd, odd_row = place[0] != 0, place[1] != 0
+    for part in range(2):
+        up = jnp.where(odd_row, sent_1[part], sent_2[part])
+        down = jnp.where(odd_row, sent_2[part], sent_1[part])
+        above = jnp.where(odd_row, got_1[part], got_2[part])
+        below = jnp.where(odd_row, got_2[part], got_1[part])
+        up = up + jnp.where(place[2] != 0, above, 0.0)
+        down = down + jnp.where(place[3] != 0, below, 0.0)
+        head = tall[part, :rows] + up / (weight[:rows] + EPS)
+        tail = tall[part, rows:] + down / (weight[rows:] + EPS)
+        new_tall[part, :RIM] = jnp.where(place[2] != 0, head[:RIM], 0.0)
         new_tall[part, RIM:rows] = head[RIM:]
         new_tall[part, rows : 2 * rows - RIM] = tail[: rows - RIM]
-        new_tall[part, 2 * rows - RIM :] = tail[rows - RIM :] * last
+        new_tall[part, 2 * rows - RIM :] = jnp.where(place[3] != 0, tail[rows - RIM :], 0.0)
     low, high = pack(new_tall[0], new_tall[1])
     near[...] = jnp.where(odd, low, high)
     far[...] = jnp.where(odd, high, low)
+
+
+def last_kernel(place, tall, middle, got_1, got_2, weight, tile):
+    side = tile.shape[1]
+    odd_row = place[1] != 0
+    for part in range(2):
+        above = jnp.where(odd_row, got_1[part], got_2[part])
+        below = jnp.where(odd_row, got_2[part], got_1[part])
+        above = jnp.where(place[2] != 0, above, 0.0)
+        below = jnp.where(place[3] != 0, below, 0.0)
+        num = middle[part] + jnp.concatenate([above, below], 0)
+        tile[part] = tall[part, RIM : RIM + side] + num / (weight[RIM : RIM + side] + EPS)
 
 
 def call(kernel, shapes, smem_count, operands, flops=1000000, moved=MIB, scratch=(), limit=16):
@@ -247,20 +283,32 @@
     )(*operands)
 
 
-def shift(value, axis, step):
-    count = lax.axis_size(axis)
-    pairs = [(i, i + step) for i in range(count) if 0 <= i + step < count]
-    return lax.ppermute(value, axis, pairs)
-
-
 def swap(value, axis, bit):
     return lax.ppermute(value, axis, [(i, i ^ bit) for i in range(lax.axis_size(axis))])
 
 
 def swap_far(value):
-    count = lax.axis_size("col")
-    pairs = [(i, i + 1) for i in range(1, count - 1, 2)]
-    return lax.ppermute(value, "col", pairs + [(j, i) for i, j in pairs])
+    rows, cols = lax.axis_size("row"), lax.axis_size("col")
+    pairs = []
+    for row in range(rows):
+        for col in range(cols):
+            to_row, to_col = row, col + (1 if col % 2 else -1)
+            if not 0 <= to_col < cols:
+                to_row, to_col = row ^ 1, col
+            pairs.append((row * cols + col, to_row * cols + to_col))
+    return lax.ppermute(value, AXES, pairs)
+
+
+def swap_rows(value):
+    rows, cols = lax.axis_size("row"), lax.axis_size("col")
+    pairs = []
+    for row in range(rows):
+        for col in range(cols):
+            to_row, to_col = row + (1 if row % 2 else -1), col
+            if not 0 <= to_row < rows:
+                to_row, to_col = row, col ^ 1
+            pairs.append((row * cols + col, to_row * cols + to_col))
+    return lax.ppermute(value, AXES, pairs)
 
 
 def sum_over_chips(part):
@@ -285,34 +333,38 @@
     steps = positions.shape[2]
     slots = positions.shape[3]
     tall_rows = side + 2 * RIM
-    odd = lax.axis_index("col") % 2
-    row = lax.axis_index("row")
-    place = jnp.stack([odd, row, lax.axis_size("row") - 1 - row]).astype(jnp.int32)
+    row, col = lax.axis_index("row"), lax.axis_index("col")
+    odd, odd_row = col % 2, row % 2
+    outer = (col == 0) | (col == lax.axis_size("col") - 1)
+    place = jnp.stack([odd, odd_row, row, lax.axis_size("row") - 1 - row, 1 - outer]).astype(jnp.int32)
     tables = jnp.asarray(dft_tables(width))
 
     own = jnp.concatenate([positions[0, 0].reshape(steps, 2 * slots), counts[0, 0][:, None]], 1)
     own = own.reshape(1, -1).astype(jnp.float32)
     meta = jnp.pad(own, ((0, TILE - 1), (0, width - own.shape[1])))
     flat = 2 * RIM
-    above = shift(
-        jnp.concatenate([object_field[:, side - RIM :].reshape(flat, width), meta], 0), "row", 1
-    )
-    below = shift(jnp.concatenate([object_field[:, :RIM].reshape(flat, width), meta], 0), "row", -1)
+    up = jnp.concatenate([object_field[:, :RIM].reshape(flat, width), meta], 0)
+    down = jnp.concatenate([object_field[:, side - RIM :].reshape(flat, width), meta], 0)
+    first = swap(jnp.where(odd_row != 0, up, down), "row", 1)
+    second = swap_rows(jnp.where(odd_row != 0, down, up))
     strip = (tall_rows + 3 * TILE, width)
     tall, near, far = call(
         strips_kernel,
         ((2, tall_rows, side), strip, strip),
         1,
-        (place, object_field, meta, above, below),
+        (place, object_field, meta, first, second),
     )
     near, far = swap(near, "col", 1), swap_far(far)
 
     def three(value):
         return value[tall_rows:].reshape(3, TILE, width)[:, 0, : own.shape[1]]
 
-    here = jnp.stack([above[flat], meta[0], below[flat]])[:, : own.shape[1]]
-    left = jnp.where(odd != 0, three(near), three(far))
-    right = jnp.where(odd != 0, three(far), three(near))
+    above = jnp.where(row > 0, jnp.where(odd_row != 0, first[flat], second[flat]), 0.0)
+    below = jnp.where(row < lax.axis_size("row") - 1, jnp.where(odd_row != 0, second[flat], first[flat]), 0.0)
+    here = jnp.stack([above, meta[0], below])[:, : own.shape[1]]
+    sides = three(near), jnp.where(outer, 0.0, three(far))
+    left = jnp.where(odd != 0, sides[0], sides[1])
+    right = jnp.where(odd != 0, sides[1], sides[0])
     metas = jnp.stack([left, here, right], 1).reshape(9, own.shape[1]).astype(jnp.int32)
 
     current = probe
@@ -341,12 +393,6 @@
         core = swap(core, "col", 1)
         out_far = swap_far(out_far)
         part = sum_over_chips(kept + core[: 3 * half])
-        up, down = call(
-            fold_kernel,
-            ((2, tall_rows // 2, width), (2, tall_rows // 2, width)),
-            1,
-            (place, sums, core, out_far),
-        )
         (weight,) = call(
             lambda *refs, step=step: weight_kernel(*refs, step=step, slots=slots),
             ((tall_rows, width),),
@@ -358,23 +404,37 @@
         part = part.reshape(3, half, width)
         mine = mine + part[:2] / (part[2] + EPS)[None]
         if step < steps - 1:
-            above = shift(down, "row", 1)
-            below = shift(up, "row", -1)
+            sent_1, sent_2 = call(
+                fold_kernel,
+                ((2, tall_rows // 2, width), (2, tall_rows // 2, width)),
+                1,
+                (place, sums, core, out_far),
+            )
+            got_1, got_2 = swap(sent_1, "row", 1), swap_rows(sent_2)
             tall, near, far = call(
                 update_kernel,
                 ((2, tall_rows, side), (tall_rows, width), (tall_rows, width)),
                 1,
-                (place, tall, up, down, above, below, weight),
+                (place, tall, sent_1, sent_2, got_1, got_2, weight),
             )
             far = swap_far(far)
             other = swap(jnp.concatenate([near, mine.reshape(2 * half, width)], 0), "col", 1)
             near = other
             other = other[tall_rows:].reshape(2, half, width)
         else:
-            above = shift(down[:, side - RIM :], "row", 1)
-            below = shift(up[:, :RIM], "row", -1)
-            num = jnp.concatenate([up[:, RIM:] + above, down[:, : side - RIM] + below], 1)
-            tile = tall[:, RIM : RIM + side] + num / (weight[RIM : RIM + side] + EPS)[None]
+            middle, sent_1, sent_2 = call(
+                last_fold_kernel,
+                ((2, side, width), (2, RIM, width), (2, RIM, width)),
+                1,
+                (place, sums, core, out_far),
+            )
+            got_1, got_2 = swap(sent_1, "row", 1), swap_rows(sent_2)
+            (tile,) = call(
+                last_kernel,
+                ((2, side, side),),
+                1,
+                (place, tall, middle, got_1, got_2, weight),
+            )
             other = swap(mine, "col", 1)
         low = jnp.where(odd == 0, mine, other)
         high = jnp.where(odd == 0, other, mine)

time: 97.2 us -> 82.1 us (0.84)
  starting transfers between devices: 54.3 us -> 28.4 us
  waiting for transfers between devices: 20.4 us -> 28.6 us
  local copies, waits for them, and re-layouts: 3.03 us -> 5.12 us
  Pallas kernels: 15.8 us -> 17.1 us
    ppermute x10 -> x7, starting transfers between devices: 19.5 us -> 6.11 us  [the longest x4 6.1 us: swap_far(): return lax.ppermute(value, AXES, pairs)]
    ppermute x13 -> x16, starting transfers between devices: 34.8 us -> 22.2 us  [swap(): lax.ppermute(value, axis, [(i, i ^ bit) for i in range(lax.axis_size(axis...]
    ppermute x10 -> x7, waiting for transfers between devices: 1.99 us -> 6.77 us  [the longest x4 6.76 us: swap_far(): return lax.ppermute(value, AXES, pairs)]
    ppermute x13 -> x16, waiting for transfers between devices: 18.4 us -> 21.8 us  [swap(): lax.ppermute(value, axis, [(i, i ^ bit) for i in range(lax.axis_size(axis...]
    unnamed x17 -> x13, local copies, waits for them, and re-layouts: 0.76 us -> 2.18 us
    pallas_call x8 -> x9, Pallas kernels: 15.8 us -> 17.1 us  [call(): pl.pallas_call(kernel, out_shape=tuple((jax.ShapeDtypeStruct(shape, jnp.f...]
  transfers between devices with their start and end apart: 23 -> 23, of which waited for: 12 -> 14; matrix products, arithmetic and copies ran while one was open for 2% -> 2% of each run, Pallas kernels for 6% -> 8%
where the time goes in v2:
time: 82.1 us; the launch traced here: 81.1 us
  waiting for transfers between devices  28.6 us (35%)
  starting transfers between devices  28.4 us (35%)
  Pallas kernels  17.1 us (21%)
  local copies, waits for them, and re-layouts  5.12 us (6%)
  other arithmetic  1.03 us (1%)
  between operations  0.93 us (1%)
    ppermute x16, starting transfers between devices, swap(): lax.ppermute(value, axis, [(i, i ^ bit) for i in range(lax.axis_size(axis...  22.2 us
    ppermute x16, waiting for transfers between devices, swap(): lax.ppermute(value, axis, [(i, i ^ bit) for i in range(lax.axis_size(axis...  21.8 us
    pallas_call x9, Pallas kernels, call(): pl.pallas_call(kernel, out_shape=tuple((jax.ShapeDtypeStruct(shape, jnp.f...  17.1 us
    ppermute x4, waiting for transfers between devices, swap_far(): return lax.ppermute(value, AXES, pairs)  6.76 us
    ppermute x4, starting transfers between devices, swap_far(): return lax.ppermute(value, AXES, pairs)  6.1 us
    unnamed x13, local copies, waits for them, and re-layouts  2.18 us
  transfers between devices with their start and end apart: 23, of which 14 were waited for; matrix products, arithmetic and copies ran while one was open for 2% of the time, Pallas kernels for 8%

profile of v2, /device:TPU:0, one launch (start us, length us, event | category | flops | bytes accessed | tf_op | source)
XLA Modules:
  0.0 81.1 jit_solution(11211725354758433181)
XLA Ops:
  0.7 0.8 %copy.15 = s32[1,1,2,4,2]{4,3,2,1,0:T(4,128)S(1)} copy(s32[1,1,2,4,2]{3,4,2,1,0:T(2,128)} %param.8) | data formatting | bytes 128 | tf_op args[2]
  1.5 0.1 reshape_squeeze.15
  1.6 0.7 copy.16
  2.3 0.1 add_convert_fusion
  2.4 0.1 convert_element_type.26
  2.5 0.9 %fusion.4 = (f32[2,64,128]{2,1,0:T(8,128)S(1)}, f32[2,64,128]{2,1,0:T(8,128)S(1)}) fusion(f32[2,128,128]{2,1,0:T(8,128)} %tile.1), kind=kLoop, calls=%fused_computation.36 | loop fusion | bytes 262144 | tf_op jit(solution)/shard_map/slice | solution.py:347
  3.4 3.0 %collective-permute-start = (f32[136,128]{1,0:T(8,128)S(1)}, f32[136,128]{1,0:T(8,128)S(1)}, u32[]{:S(2)}, u32[]{:S(2)}) collective-permute-start(f32[136,128]{1,0:T(8,128)S(1)} %get-tuple-element.45), channel_id=1, source_target_pairs={{0,4},{4,0},{8,12},{12,8},{16,20},{20,16},{24,28},{28,24},{1,5},{5... | collective-permute-start | bytes 208904 | tf_op jit(solution)/shard_map/ppermute | solution.py:287
  6.4 0.0 collective-permute-start.1
  6.4 0.7 copy-done.4
  7.1 0.7 copy-done.5
  7.8 0.6 fusion.6
  8.4 0.1 copy.17
  8.5 0.1 reshape_squeeze.16.starts
  8.6 0.1 stack.36.place
  8.7 1.0 %collective-permute-done.first = f32[136,128]{1,0:T(8,128)S(1)} collective-permute-done((f32[136,128]{1,0:T(8,128)S(1)}, f32[136,128]{1,0:T(8,128)S(1)}, u32[]{:S(2)}, u32[]{:S(2)}) %collective-permute-start) | collective-permute-done | bytes 69664 | tf_op jit(solution)/shard_map/ppermute | solution.py:287
  9.7 0.0 collective-permute-done.1.second
  9.7 0.7 shard_map.77
  10.4 0.2 collective-permute-start.2
  10.6 2.6 %collective-permute-start.3 = (f32[280,128]{1,0:T(8,128)S(1)}, f32[280,128]{1,0:T(8,128)S(1)}, u32[]{:S(2)}, u32[]{:S(2)}) collective-permute-start(f32[280,128]{1,0:T(8,128)S(1)} %get-tuple-element.23), channel_id=1, source_target_pairs={{0,4},{1,2},{2,1},{3,7},{4,0},{5,6},{6,5},{7,3},{8,12},{9,10},{10,... | collective-permute-start | bytes 430088 | tf_op jit(solution)/shard_map/ppermute | solution.py:299
  13.2 0.0 collective-permute-done.2.near
  13.2 3.1 %collective-permute-done.3.far = f32[280,128]{1,0:T(8,128)S(1)} collective-permute-done((f32[280,128]{1,0:T(8,128)S(1)}, f32[280,128]{1,0:T(8,128)S(1)}, u32[]{:S(2)}, u32[]{:S(2)}) %collective-permute-start.3) | collective-permute-done | bytes 143392 | tf_op jit(solution)/shard_map/ppermute | solution.py:299
  16.2 4.8 %shard_map.78 = (f32[448,128]{1,0:T(8,128)S(1)}, f32[256,128]{1,0:T(8,128)S(1)}, f32[192,128]{1,0:T(8,128)S(1)}, f32[2,256,128]{2,1,0:T(8,128)S(1)}) custom-call(s32[5]{0:T(128)S(1)} %stack.36.place, s32[8]{0:T(128)S(1)} %reshape_squeeze.16.starts, s32[1]{0:T(128)} %bitcast.8.count, f32[2,256,128]{2,1,0:T(8,128)S(1)} %get-tuple-element.21.tall, ...), custom_call_target="tpu_custom_call" | custom-call | flops 805306368 | bytes 4194304 | tf_op jit(solution)/shard_map/pallas_call | solution.py:275
  21.1 0.1 collective-permute-start.4
  21.2 2.2 %collective-permute-start.5 = (f32[256,128]{1,0:T(8,128)S(1)}, f32[256,128]{1,0:T(8,128)S(1)}, u32[]{:S(2)}, u32[]{:S(2)}) collective-permute-start(f32[256,128]{1,0:T(8,128)S(1)} %get-tuple-element.26), channel_id=1, source_target_pairs={{0,4},{1,2},{2,1},{3,7},{4,0},{5,6},{6,5},{7,3},{8,12},{9,10},{10,... | collective-permute-start | bytes 393224 | tf_op jit(solution)/shard_map/ppermute | solution.py:299
  23.4 1.3 %collective-permute-start.8 = (f32[192,128]{1,0:T(8,128)S(1)}, f32[192,128]{1,0:T(8,128)S(1)}, u32[]{:S(2)}, u32[]{:S(2)}) collective-permute-start(f32[192,128]{1,0:T(8,128)S(1)} %slice_add_fusion.1), channel_id=1, source_target_pairs={{0,4},{4,0},{8,12},{12,8},{16,20},{20,16},{24,28},{28,24},{1,5},{5... | collective-permute-start | bytes 294920 | tf_op jit(solution)/shard_map/ppermute | solution.py:287
  24.7 3.7 %collective-permute-done.8 = f32[192,128]{1,0:T(8,128)S(1)} collective-permute-done((f32[192,128]{1,0:T(8,128)S(1)}, f32[192,128]{1,0:T(8,128)S(1)}, u32[]{:S(2)}, u32[]{:S(2)}) %collective-permute-start.8) | collective-permute-done | bytes 98336 | tf_op jit(solution)/shard_map/ppermute | solution.py:287
  28.4 0.8 %collective-permute-start.9 = (f32[192,128]{1,0:T(8,128)S(1)}, f32[192,128]{1,0:T(8,128)S(1)}, u32[]{:S(2)}, u32[]{:S(2)}) collective-permute-start(f32[192,128]{1,0:T(8,128)S(1)} %add.63), channel_id=1, source_target_pairs={{0,2},{1,3},{2,0},{3,1},{4,6},{5,7},{6,4},{7,5},{8,10},{9,11},{10,... | collective-permute-start | bytes 294920 | tf_op jit(solution)/shard_map/ppermute | solution.py:287
  29.3 0.7 shard_map.79
  30.0 1.7 %collective-permute-start.6 = (f32[2,128,128]{2,1,0:T(8,128)S(1)}, f32[2,128,128]{2,1,0:T(8,128)S(1)}, u32[]{:S(2)}, u32[]{:S(2)}) collective-permute-start(f32[2,128,128]{2,1,0:T(8,128)S(1)} %get-tuple-element.27.sent_1), channel_id=1, source_target_pairs={{0,4},{4,0},{8,12},{12,8},{16,20},{20,16},{24,28},{28,24},{1,5},{5... | collective-permute-start | bytes 393224 | tf_op jit(solution)/shard_map/ppermute | solution.py:287
  31.6 0.0 collective-permute-start.7
  31.6 1.5 %collective-permute-done.9 = f32[192,128]{1,0:T(8,128)S(1)} collective-permute-done((f32[192,128]{1,0:T(8,128)S(1)}, f32[192,128]{1,0:T(8,128)S(1)}, u32[]{:S(2)}, u32[]{:S(2)}) %collective-permute-start.9) | collective-permute-done | bytes 98336 | tf_op jit(solution)/shard_map/ppermute | solution.py:287
  33.1 3.0 %collective-permute-start.10 = (f32[192,128]{1,0:T(8,128)S(1)}, f32[192,128]{1,0:T(8,128)S(1)}, u32[]{:S(2)}, u32[]{:S(2)}) collective-permute-start(f32[192,128]{1,0:T(8,128)S(1)} %add.64), channel_id=1, source_target_pairs={{0,8},{4,12},{8,0},{12,4},{16,24},{20,28},{24,16},{28,20},{1,9},{5... | collective-permute-start | bytes 294920 | tf_op jit(solution)/shard_map/ppermute | solution.py:287
  36.1 2.6 %collective-permute-done.10 = f32[192,128]{1,0:T(8,128)S(1)} collective-permute-done((f32[192,128]{1,0:T(8,128)S(1)}, f32[192,128]{1,0:T(8,128)S(1)}, u32[]{:S(2)}, u32[]{:S(2)}) %collective-permute-start.10) | collective-permute-done | bytes 98336 | tf_op jit(solution)/shard_map/ppermute | solution.py:287
  38.7 3.4 %collective-permute-start.11 = (f32[192,128]{1,0:T(8,128)S(1)}, f32[192,128]{1,0:T(8,128)S(1)}, u32[]{:S(2)}, u32[]{:S(2)}) collective-permute-start(f32[192,128]{1,0:T(8,128)S(1)} %add.65), channel_id=1, source_target_pairs={{0,16},{4,20},{8,24},{12,28},{16,0},{20,4},{24,8},{28,12},{1,17},{... | collective-permute-start | bytes 294920 | tf_op jit(solution)/shard_map/ppermute | solution.py:287
  42.1 1.7 %shard_map.80.weight = f32[256,128]{1,0:T(8,128)S(1)} custom-call(s32[9,18]{1,0:T(8,128)S(1)} %convert_element_type.28.refs_0_, f32[2,128,128]{2,1,0:T(8,128)S(1)} %copy-done.1), custom_call_target="tpu_custom_call" | custom-call | flops 1000000 | bytes 1048576 | tf_op jit(solution)/shard_map/pallas_call | solution.py:275
  43.9 0.0 collective-permute-done.7.got_2
  43.9 0.7 shard_map.81
  44.6 0.1 collective-permute-done.11
  44.8 0.1 collective-permute-start.12
  44.9 0.1 copy.21
  45.0 0.1 reshape_squeeze.18.starts
  45.1 0.7 collective-permute-start.13
  45.8 0.5 collective-permute-done.12.near
  46.4 3.7 %collective-permute-done.13.far = f32[256,128]{1,0:T(8,128)S(1)} collective-permute-done((f32[256,128]{1,0:T(8,128)S(1)}, f32[256,128]{1,0:T(8,128)S(1)}, u32[]{:S(2)}, u32[]{:S(2)}) %collective-permute-start.13) | collective-permute-done | bytes 131104 | tf_op jit(solution)/shard_map/ppermute | solution.py:299
  50.0 4.9 %shard_map.82 = (f32[448,128]{1,0:T(8,128)S(1)}, f32[256,128]{1,0:T(8,128)S(1)}, f32[192,128]{1,0:T(8,128)S(1)}, f32[2,256,128]{2,1,0:T(8,128)S(1)}) custom-call(s32[5]{0:T(128)S(1)} %stack.36.place, s32[8]{0:T(128)S(1)} %reshape_squeeze.18.starts, s32[1]{0:T(128)} %bitcast.13.count, f32[2,256,128]{2,1,0:T(8,128)S(1)} %get-tuple-element.29.tall, ...), custom_call_target="tpu_custom_call" | custom-call | flops 805306368 | bytes 4194304 | tf_op jit(solution)/shard_map/pallas_call | solution.py:275
  54.9 0.3 collective-permute-start.14
  55.2 1.3 %collective-permute-done.14.near = f32[448,128]{1,0:T(8,128)S(1)} collective-permute-done((f32[448,128]{1,0:T(8,128)S(1)}, f32[448,128]{1,0:T(8,128)S(1)}, u32[]{:S(2)}, u32[]{:S(2)}) %collective-permute-start.14) | collective-permute-done | bytes 229408 | tf_op jit(solution)/shard_map/ppermute | solution.py:287
  56.5 0.8 collective-permute-start.18
  57.3 4.2 %collective-permute-done.18 = f32[192,128]{1,0:T(8,128)S(1)} collective-permute-done((f32[192,128]{1,0:T(8,128)S(1)}, f32[192,128]{1,0:T(8,128)S(1)}, u32[]{:S(2)}, u32[]{:S(2)}) %collective-permute-start.18) | collective-permute-done | bytes 98336 | tf_op jit(solution)/shard_map/ppermute | solution.py:287
  61.5 1.8 %collective-permute-start.19 = (f32[192,128]{1,0:T(8,128)S(1)}, f32[192,128]{1,0:T(8,128)S(1)}, u32[]{:S(2)}, u32[]{:S(2)}) collective-permute-start(f32[192,128]{1,0:T(8,128)S(1)} %add.70), channel_id=1, source_target_pairs={{0,2},{1,3},{2,0},{3,1},{4,6},{5,7},{6,4},{7,5},{8,10},{9,11},{10,... | collective-permute-start | bytes 294920 | tf_op jit(solution)/shard_map/ppermute | solution.py:287
  63.3 2.9 %collective-permute-done.19 = f32[192,128]{1,0:T(8,128)S(1)} collective-permute-done((f32[192,128]{1,0:T(8,128)S(1)}, f32[192,128]{1,0:T(8,128)S(1)}, u32[]{:S(2)}, u32[]{:S(2)}) %collective-permute-start.19) | collective-permute-done | bytes 98336 | tf_op jit(solution)/shard_map/ppermute | solution.py:287
  66.2 1.8 %collective-permute-start.20 = (f32[192,128]{1,0:T(8,128)S(1)}, f32[192,128]{1,0:T(8,128)S(1)}, u32[]{:S(2)}, u32[]{:S(2)}) collective-permute-start(f32[192,128]{1,0:T(8,128)S(1)} %add.71), channel_id=1, source_target_pairs={{0,8},{4,12},{8,0},{12,4},{16,24},{20,28},{24,16},{28,20},{1,9},{5... | collective-permute-start | bytes 294920 | tf_op jit(solution)/shard_map/ppermute | solution.py:287
  68.0 0.6 collective-permute-start.15
  68.6 2.3 %collective-permute-done.20 = f32[192,128]{1,0:T(8,128)S(1)} collective-permute-done((f32[192,128]{1,0:T(8,128)S(1)}, f32[192,128]{1,0:T(8,128)S(1)}, u32[]{:S(2)}, u32[]{:S(2)}) %collective-permute-start.20) | collective-permute-done | bytes 98336 | tf_op jit(solution)/shard_map/ppermute | solution.py:287
  70.9 3.2 %collective-permute-start.21 = (f32[192,128]{1,0:T(8,128)S(1)}, f32[192,128]{1,0:T(8,128)S(1)}, u32[]{:S(2)}, u32[]{:S(2)}) collective-permute-start(f32[192,128]{1,0:T(8,128)S(1)} %add.72), channel_id=1, source_target_pairs={{0,16},{4,20},{8,24},{12,28},{16,0},{20,4},{24,8},{28,12},{1,17},{... | collective-permute-start | bytes 294920 | tf_op jit(solution)/shard_map/ppermute | solution.py:287
  74.1 0.7 shard_map.83
  74.8 0.6 collective-permute-start.16
  75.4 0.0 collective-permute-start.17
  75.5 1.4 %collective-permute-done.21 = f32[192,128]{1,0:T(8,128)S(1)} collective-permute-done((f32[192,128]{1,0:T(8,128)S(1)}, f32[192,128]{1,0:T(8,128)S(1)}, u32[]{:S(2)}, u32[]{:S(2)}) %collective-permute-start.21) | collective-permute-done | bytes 98336 | tf_op jit(solution)/shard_map/ppermute | solution.py:287
  76.9 0.1 collective-permute-start.22
  77.0 1.7 %shard_map.84.weight = f32[256,128]{1,0:T(8,128)S(1)} custom-call(s32[9,18]{1,0:T(8,128)S(1)} %convert_element_type.28.refs_0_, f32[2,128,128]{2,1,0:T(8,128)S(1)} %pad_maximum_fusion.1.probe.refs_1_), custom_call_target="tpu_custom_call" | custom-call | flops 1000000 | bytes 1048576 | tf_op jit(solution)/shard_map/pallas_call | solution.py:275
  78.6 0.5 collective-permute-done.16.got_1
  79.1 1.2 %shard_map.85 = f32[2,128,128]{2,1,0:T(8,128)} custom-call(s32[5]{0:T(128)S(1)} %stack.36.place, f32[2,256,128]{2,1,0:T(8,128)S(1)} %get-tuple-element.29.tall, f32[2,128,128]{2,1,0:T(8,128)S(1)} %get-tuple-element.36.middle, f32[2,64,128]{2,1,0:T(8,128)S(1)} %collective-permute-done.16.got_1, f32[2,64,128]{2,1,0:T(8,128)S(1)} %collective-permute-done.17.got_2, ...), custom_call_target="tpu_custom_call" | custom-call | flops 1000000 | bytes 1048576 | tf_op jit(solution)/shard_map/pallas_call | solution.py:275
  80.4 0.7 pad_maximum_fusion.2
  (53 shorter events, 0.4 us)
Async XLA Ops:
  0.6 7.8 %copy-start.3 = (f32[1,1,2,4,128,128]{5,4,3,2,1,0:T(8,128)S(1)}, f32[1,1,2,4,128,128]{5,4,3,2,1,0:T(8,128)}, u32[]{:S(2)}) copy-start(f32[1,1,2,4,128,128]{5,4,3,2,1,0:T(8,128)} %param.10) | copy-start | bytes 1572868
  3.4 6.3 %collective-permute-start = (f32[136,128]{1,0:T(8,128)S(1)}, f32[136,128]{1,0:T(8,128)S(1)}, u32[]{:S(2)}, u32[]{:S(2)}) collective-permute-start(f32[136,128]{1,0:T(8,128)S(1)} %get-tuple-element.45), channel_id=1, source_target_pairs={{0,4},{4,0},{8,12},{12,8},{16,20},{20,16},{24,28},{28,24},{1,5},{5... | collective-permute-start | bytes 208904 | tf_op jit(solution)/shard_map/ppermute | solution.py:287
  6.4 3.2 %collective-permute-start.1 = (f32[136,128]{1,0:T(8,128)S(1)}, f32[136,128]{1,0:T(8,128)S(1)}, u32[]{:S(2)}, u32[]{:S(2)}) collective-permute-start(f32[136,128]{1,0:T(8,128)S(1)} %get-tuple-element.44), channel_id=1, source_target_pairs={{0,1},{1,0},{2,3},{3,2},{4,8},{5,9},{6,10},{7,11},{8,4},{9,5},{10,... | collective-permute-start | bytes 208904 | tf_op jit(solution)/shard_map/ppermute | solution.py:311
  6.4 0.7 copy-start.4
  7.1 0.7 copy-start.5
  8.4 1.3 %copy-start = (f32[2,128,128]{2,1,0:T(8,128)S(1)}, f32[2,128,128]{2,1,0:T(8,128)}, u32[]{:S(2)}) copy-start(f32[2,128,128]{2,1,0:T(8,128)} %tile.1) | copy-start | bytes 393220
  8.4 7.9 %copy-start.2 = (bf16[4,256,256]{2,1,0:T(8,128)(2,1)S(1)}, bf16[4,256,256]{2,1,0:T(8,128)(2,1)}, u32[]{:S(2)}) copy-start(bf16[4,256,256]{2,1,0:T(8,128)(2,1)} %constant.43.clone.tables) | copy-start | bytes 1572868
  8.7 7.5 %copy-start.1 = (f32[2,128,128]{2,1,0:T(8,128)S(1)}, f32[2,128,128]{2,1,0:T(8,128)}, u32[]{:S(2)}) copy-start(f32[2,128,128]{2,1,0:T(8,128)} %refs_1_.1) | copy-start | bytes 393220
  10.4 2.8 %collective-permute-start.2 = (f32[280,128]{1,0:T(8,128)S(1)}, f32[280,128]{1,0:T(8,128)S(1)}, u32[]{:S(2)}, u32[]{:S(2)}) collective-permute-start(f32[280,128]{1,0:T(8,128)S(1)} %get-tuple-element.22), channel_id=1, source_target_pairs={{0,1},{1,0},{2,3},{3,2},{4,5},{5,4},{6,7},{7,6},{8,9},{9,8},{10,11... | collective-permute-start | bytes 430088 | tf_op jit(solution)/shard_map/ppermute | solution.py:287
  10.6 5.7 %collective-permute-start.3 = (f32[280,128]{1,0:T(8,128)S(1)}, f32[280,128]{1,0:T(8,128)S(1)}, u32[]{:S(2)}, u32[]{:S(2)}) collective-permute-start(f32[280,128]{1,0:T(8,128)S(1)} %get-tuple-element.23), channel_id=1, source_target_pairs={{0,4},{1,2},{2,1},{3,7},{4,0},{5,6},{6,5},{7,3},{8,12},{9,10},{10,... | collective-permute-start | bytes 430088 | tf_op jit(solution)/shard_map/ppermute | solution.py:299
  21.1 2.3 %collective-permute-start.4 = (f32[448,128]{1,0:T(8,128)S(1)}, f32[448,128]{1,0:T(8,128)S(1)}, u32[]{:S(2)}, u32[]{:S(2)}) collective-permute-start(f32[448,128]{1,0:T(8,128)S(1)} %get-tuple-element.25), channel_id=1, source_target_pairs={{0,1},{1,0},{2,3},{3,2},{4,5},{5,4},{6,7},{7,6},{8,9},{9,8},{10,11... | collective-permute-start | bytes 688136 | tf_op jit(solution)/shard_map/ppermute | solution.py:287
  21.2 8.1 %collective-permute-start.5 = (f32[256,128]{1,0:T(8,128)S(1)}, f32[256,128]{1,0:T(8,128)S(1)}, u32[]{:S(2)}, u32[]{:S(2)}) collective-permute-start(f32[256,128]{1,0:T(8,128)S(1)} %get-tuple-element.26), channel_id=1, source_target_pairs={{0,4},{1,2},{2,1},{3,7},{4,0},{5,6},{6,5},{7,3},{8,12},{9,10},{10,... | collective-permute-start | bytes 393224 | tf_op jit(solution)/shard_map/ppermute | solution.py:299
  23.4 5.0 %collective-permute-start.8 = (f32[192,128]{1,0:T(8,128)S(1)}, f32[192,128]{1,0:T(8,128)S(1)}, u32[]{:S(2)}, u32[]{:S(2)}) collective-permute-start(f32[192,128]{1,0:T(8,128)S(1)} %slice_add_fusion.1), channel_id=1, source_target_pairs={{0,4},{4,0},{8,12},{12,8},{16,20},{20,16},{24,28},{28,24},{1,5},{5... | collective-permute-start | bytes 294920 | tf_op jit(solution)/shard_map/ppermute | solution.py:287
  28.4 4.7 %collective-permute-start.9 = (f32[192,128]{1,0:T(8,128)S(1)}, f32[192,128]{1,0:T(8,128)S(1)}, u32[]{:S(2)}, u32[]{:S(2)}) collective-permute-start(f32[192,128]{1,0:T(8,128)S(1)} %add.63), channel_id=1, source_target_pairs={{0,2},{1,3},{2,0},{3,1},{4,6},{5,7},{6,4},{7,5},{8,10},{9,11},{10,... | collective-permute-start | bytes 294920 | tf_op jit(solution)/shard_map/ppermute | solution.py:287
  30.0 13.9 %collective-permute-start.6 = (f32[2,128,128]{2,1,0:T(8,128)S(1)}, f32[2,128,128]{2,1,0:T(8,128)S(1)}, u32[]{:S(2)}, u32[]{:S(2)}) collective-permute-start(f32[2,128,128]{2,1,0:T(8,128)S(1)} %get-tuple-element.27.sent_1), channel_id=1, source_target_pairs={{0,4},{4,0},{8,12},{12,8},{16,20},{20,16},{24,28},{28,24},{1,5},{5... | collective-permute-start | bytes 393224 | tf_op jit(solution)/shard_map/ppermute | solution.py:287
  31.6 12.3 %collective-permute-start.7 = (f32[2,128,128]{2,1,0:T(8,128)S(1)}, f32[2,128,128]{2,1,0:T(8,128)S(1)}, u32[]{:S(2)}, u32[]{:S(2)}) collective-permute-start(f32[2,128,128]{2,1,0:T(8,128)S(1)} %get-tuple-element.28.sent_2), channel_id=1, source_target_pairs={{0,1},{1,0},{2,3},{3,2},{4,8},{5,9},{6,10},{7,11},{8,4},{9,5},{10,... | collective-permute-start | bytes 393224 | tf_op jit(solution)/shard_map/ppermute | solution.py:311
  33.1 5.6 %collective-permute-start.10 = (f32[192,128]{1,0:T(8,128)S(1)}, f32[192,128]{1,0:T(8,128)S(1)}, u32[]{:S(2)}, u32[]{:S(2)}) collective-permute-start(f32[192,128]{1,0:T(8,128)S(1)} %add.64), channel_id=1, source_target_pairs={{0,8},{4,12},{8,0},{12,4},{16,24},{20,28},{24,16},{28,20},{1,9},{5... | collective-permute-start | bytes 294920 | tf_op jit(solution)/shard_map/ppermute | solution.py:287
  38.7 6.0 %collective-permute-start.11 = (f32[192,128]{1,0:T(8,128)S(1)}, f32[192,128]{1,0:T(8,128)S(1)}, u32[]{:S(2)}, u32[]{:S(2)}) collective-permute-start(f32[192,128]{1,0:T(8,128)S(1)} %add.65), channel_id=1, source_target_pairs={{0,16},{4,20},{8,24},{12,28},{16,0},{20,4},{24,8},{28,12},{1,17},{... | collective-permute-start | bytes 294920 | tf_op jit(solution)/shard_map/ppermute | solution.py:287
  44.8 1.5 %collective-permute-start.12 = (f32[384,128]{1,0:T(8,128)S(1)}, f32[384,128]{1,0:T(8,128)S(1)}, u32[]{:S(2)}, u32[]{:S(2)}) collective-permute-start(f32[384,128]{1,0:T(8,128)S(1)} %pad_maximum_fusion), channel_id=1, source_target_pairs={{0,1},{1,0},{2,3},{3,2},{4,5},{5,4},{6,7},{7,6},{8,9},{9,8},{10,11... | collective-permute-start | bytes 589832 | tf_op jit(solution)/shard_map/ppermute | solution.py:287
  45.1 5.0 %collective-permute-start.13 = (f32[256,128]{1,0:T(8,128)S(1)}, f32[256,128]{1,0:T(8,128)S(1)}, u32[]{:S(2)}, u32[]{:S(2)}) collective-permute-start(f32[256,128]{1,0:T(8,128)S(1)} %get-tuple-element.32), channel_id=1, source_target_pairs={{0,4},{1,2},{2,1},{3,7},{4,0},{5,6},{6,5},{7,3},{8,12},{9,10},{10,... | collective-permute-start | bytes 393224 | tf_op jit(solution)/shard_map/ppermute | solution.py:299
  54.9 1.6 %collective-permute-start.14 = (f32[448,128]{1,0:T(8,128)S(1)}, f32[448,128]{1,0:T(8,128)S(1)}, u32[]{:S(2)}, u32[]{:S(2)}) collective-permute-start(f32[448,128]{1,0:T(8,128)S(1)} %get-tuple-element.34), channel_id=1, source_target_pairs={{0,1},{1,0},{2,3},{3,2},{4,5},{5,4},{6,7},{7,6},{8,9},{9,8},{10,11... | collective-permute-start | bytes 688136 | tf_op jit(solution)/shard_map/ppermute | solution.py:287
  56.5 5.0 %collective-permute-start.18 = (f32[192,128]{1,0:T(8,128)S(1)}, f32[192,128]{1,0:T(8,128)S(1)}, u32[]{:S(2)}, u32[]{:S(2)}) collective-permute-start(f32[192,128]{1,0:T(8,128)S(1)} %slice_add_fusion), channel_id=1, source_target_pairs={{0,4},{4,0},{8,12},{12,8},{16,20},{20,16},{24,28},{28,24},{1,5},{5... | collective-permute-start | bytes 294920 | tf_op jit(solution)/shard_map/ppermute | solution.py:287
  61.5 4.7 %collective-permute-start.19 = (f32[192,128]{1,0:T(8,128)S(1)}, f32[192,128]{1,0:T(8,128)S(1)}, u32[]{:S(2)}, u32[]{:S(2)}) collective-permute-start(f32[192,128]{1,0:T(8,128)S(1)} %add.70), channel_id=1, source_target_pairs={{0,2},{1,3},{2,0},{3,1},{4,6},{5,7},{6,4},{7,5},{8,10},{9,11},{10,... | collective-permute-start | bytes 294920 | tf_op jit(solution)/shard_map/ppermute | solution.py:287
  66.2 4.7 %collective-permute-start.20 = (f32[192,128]{1,0:T(8,128)S(1)}, f32[192,128]{1,0:T(8,128)S(1)}, u32[]{:S(2)}, u32[]{:S(2)}) collective-permute-start(f32[192,128]{1,0:T(8,128)S(1)} %add.71), channel_id=1, source_target_pairs={{0,8},{4,12},{8,0},{12,4},{16,24},{20,28},{24,16},{28,20},{1,9},{5... | collective-permute-start | bytes 294920 | tf_op jit(solution)/shard_map/ppermute | solution.py:287
  68.0 6.1 %collective-permute-start.15 = (f32[256,128]{1,0:T(8,128)S(1)}, f32[256,128]{1,0:T(8,128)S(1)}, u32[]{:S(2)}, u32[]{:S(2)}) collective-permute-start(f32[256,128]{1,0:T(8,128)S(1)} %get-tuple-element.35), channel_id=1, source_target_pairs={{0,4},{1,2},{2,1},{3,7},{4,0},{5,6},{6,5},{7,3},{8,12},{9,10},{10,... | collective-permute-start | bytes 393224 | tf_op jit(solution)/shard_map/ppermute | solution.py:299
  70.9 5.9 %collective-permute-start.21 = (f32[192,128]{1,0:T(8,128)S(1)}, f32[192,128]{1,0:T(8,128)S(1)}, u32[]{:S(2)}, u32[]{:S(2)}) collective-permute-start(f32[192,128]{1,0:T(8,128)S(1)} %add.72), channel_id=1, source_target_pairs={{0,16},{4,20},{8,24},{12,28},{16,0},{20,4},{24,8},{28,12},{1,17},{... | collective-permute-start | bytes 294920 | tf_op jit(solution)/shard_map/ppermute | solution.py:287
  74.8 4.3 %collective-permute-start.16 = (f32[2,64,128]{2,1,0:T(8,128)S(1)}, f32[2,64,128]{2,1,0:T(8,128)S(1)}, u32[]{:S(2)}, u32[]{:S(2)}) collective-permute-start(f32[2,64,128]{2,1,0:T(8,128)S(1)} %get-tuple-element.37), channel_id=1, source_target_pairs={{0,4},{4,0},{8,12},{12,8},{16,20},{20,16},{24,28},{28,24},{1,5},{5... | collective-permute-start | bytes 196616 | tf_op jit(solution)/shard_map/ppermute | solution.py:287
  75.4 3.7 %collective-permute-start.17 = (f32[2,64,128]{2,1,0:T(8,128)S(1)}, f32[2,64,128]{2,1,0:T(8,128)S(1)}, u32[]{:S(2)}, u32[]{:S(2)}) collective-permute-start(f32[2,64,128]{2,1,0:T(8,128)S(1)} %get-tuple-element.38), channel_id=1, source_target_pairs={{0,1},{1,0},{2,3},{3,2},{4,8},{5,9},{6,10},{7,11},{8,4},{9,5},{10,... | collective-permute-start | bytes 196616 | tf_op jit(solution)/shard_map/ppermute | solution.py:311
  76.9 3.5 %collective-permute-start.22 = (f32[2,64,128]{2,1,0:T(8,128)S(1)}, f32[2,64,128]{2,1,0:T(8,128)S(1)}, u32[]{:S(2)}, u32[]{:S(2)}) collective-permute-start(f32[2,64,128]{2,1,0:T(8,128)S(1)} %fusion.1), channel_id=1, source_target_pairs={{0,1},{1,0},{2,3},{3,2},{4,5},{5,4},{6,7},{7,6},{8,9},{9,8},{10,11... | collective-permute-start | bytes 196616 | tf_op jit(solution)/shard_map/ppermute | solution.py:287

commit v3 on v2

--- a/solution.py
+++ b/solution.py
@@ -1,3 +1,4 @@
+import functools
 import math
 
 import jax
@@ -84,11 +85,46 @@
     return jnp.where(col < 0, col + width, col)
 
 
-def strips_kernel(place, tile, meta, first, second, tall, near, far):
+class Spot:
+    def __init__(self):
+        row, col = lax.axis_index("row"), lax.axis_index("col")
+        self.side = lax.rem(col, 2)
+        self.odd = self.side != 0
+        self.row_side = lax.rem(row, 2)
+        self.odd_row = self.row_side != 0
+        self.has_above = row != 0
+        self.has_below = row != lax.axis_size("row") - 1
+        self.has_far = (col != 0) & (col != lax.axis_size("col") - 1)
+
+
+def first_kernel(tile, scan, first, second, meta, offsets, sems):
+    spot = Spot()
     side = tile.shape[1]
-    odd, odd_row = place[0] != 0, place[1] != 0
-    above = jnp.where(place[2] != 0, jnp.where(odd_row, first[...], second[...]), 0.0)
-    below = jnp.where(place[3] != 0, jnp.where(odd_row, second[...], first[...]), 0.0)
+    near_edge = pl.multiple_of(spot.row_side * RIM, RIM)
+    copies = [pltpu.make_async_copy(scan, offsets, sems.at[0])]
+    for part in range(2):
+        rows = pl.ds(part * RIM, RIM)
+        lower = pl.ds(side - RIM - near_edge, RIM)
+        upper = pl.ds(near_edge, RIM)
+        copies.append(pltpu.make_async_copy(tile.at[part, lower], first.at[rows], sems.at[1 + part]))
+        copies.append(pltpu.make_async_copy(tile.at[part, upper], second.at[rows], sems.at[3 + part]))
+    for copy in copies:
+        copy.start()
+    meta[...] = jnp.zeros_like(meta)
+    copies[0].wait()
+    meta[: scan.shape[0], : scan.shape[1]] = offsets[...].astype(jnp.float32)
+    first[2 * RIM :] = meta[...]
+    second[2 * RIM :] = meta[...]
+    for copy in copies[1:]:
+        copy.wait()
+
+
+def strips_kernel(tile, meta, first, second, tall, near, far):
+    side = tile.shape[1]
+    spot = Spot()
+    odd, odd_row = spot.odd, spot.odd_row
+    above = jnp.where(spot.has_above, jnp.where(odd_row, first[...], second[...]), 0.0)
+    below = jnp.where(spot.has_below, jnp.where(odd_row, second[...], first[...]), 0.0)
     for part in range(2):
         tall[part, :RIM] = above[part * RIM : (part + 1) * RIM]
         tall[part, RIM : RIM + side] = tile[part]
@@ -104,56 +140,84 @@
 
 
 def slots_kernel(
-    place, starts, count, tall, near, far, probe, amps, tables,
-    core_out, far_out, keep_out, tall_out, field, sums, totals,
+    scan, tall, near, far, probe, amps, tables,
+    core_out, far_out, keep_out, tall_out, field, sums, totals, wins, psis, starts, sem, *, step,
 ):
+    fetch = pltpu.make_async_copy(scan, starts, sem)
+    fetch.start()
+    spot = Spot()
     width = probe.shape[1]
     rows_all = tall.shape[1]
     tiles = width // TILE
-    odd = place[0] != 0
+    slots = amps.shape[0]
+    odd = spot.odd
     lane = lanes((width + TILE, width))
     sub = lax.broadcasted_iota(jnp.int32, (tiles, TILE, width), 1)
-    from_near, from_far = near[:rows_all], jnp.where(place[4] != 0, far[:rows_all], 0.0)
+    from_near, from_far = near[:rows_all], jnp.where(spot.has_far, far[:rows_all], 0.0)
     sides = unpack(jnp.where(odd, from_far, from_near), jnp.where(odd, from_near, from_far))
     for part in range(2):
         field[part, :rows_all, :width] = tall[part]
         field[part, :rows_all, width:] = sides[part]
         field[part, rows_all:] = jnp.zeros_like(field[part, rows_all:])
     sums[...] = jnp.zeros_like(sums)
+    fetch.wait()
     full_h, full_l, flip_h, flip_l = (tables[k] for k in range(4))
     pro_r, pro_i = probe[0], probe[1]
+
+    def where(slot):
+        row = starts[3 * step, slot] + RIM
+        col = starts[3 * step + 1, slot]
+        base = pl.multiple_of(row // TILE * TILE, TILE)
+        outside = (lane < col) | (lane >= width + col)
+        return pl.ds(base, width + TILE), row - base, col, outside
+
     total = None
-    for slot in range(amps.shape[0]):
-        row = starts[2 * slot] + RIM
-        col = starts[2 * slot + 1]
-        live = jnp.where(slot < count[0], 1.0, 0.0).astype(jnp.float32)
-        base = pl.multiple_of(row // TILE * TILE, TILE)
-        rows = pl.ds(base, width + TILE)
-        skew = row - base
+    members = range(slots)
+    columns = []
+    for slot in members:
+        rows, skew, col, outside = where(slot)
         lift = jnp.where(skew > 0, TILE - skew, 0)
-        ahead = lane_turn(col, width)
         back = lane_turn(-col, width)
-        outside = (lane < col) | (lane >= width + col)
-
-        def window(part):
+        win = []
+        for part in range(2):
             mixed = jnp.where(outside, field[part, rows, width:], field[part, rows, :width])
             turned = pltpu.roll(mixed.reshape(tiles + 1, TILE, width), lift, 1)
             lined = jnp.where(sub < TILE - skew, turned[:-1], turned[1:])
-            return pltpu.roll(lined.reshape(width, width), back, 1)
-
-        win_r, win_i = window(0), window(1)
-        psi_r = pro_r * win_r - pro_i * win_i
-        psi_i = pro_r * win_i + pro_i * win_r
-        half = left_product(full_h, full_l, jnp.concatenate([psi_r, psi_i], 0))
-        wave = right_product(jnp.concatenate([half[:width], half[width:]], 1), flip_h, flip_l)
-        far_r, far_i = wave[:, :width], wave[:, width:]
+            win.append(pltpu.roll(lined.reshape(width, width), back, 1))
+            wins[slot, part] = win[part]
+        psi_r = pro_r * win[0] - pro_i * win[1]
+        psi_i = pro_r * win[1] + pro_i * win[0]
+        psis[slot, 0] = psi_r
+        psis[slot, 1] = psi_i
+        columns.append(jnp.concatenate([psi_r, psi_i], 0))
+
+    def turn(half):
+        return jnp.concatenate(
+            [
+                jnp.concatenate(
+                    [half[:width, k * width : (k + 1) * width], half[width:, k * width : (k + 1) * width]], 1
+                )
+                for k in range(slots)
+            ],
+            0,
+        )
+
+    half = left_product(full_h, full_l, jnp.concatenate(columns, 1))
+    wave = right_product(turn(half), flip_h, flip_l)
+    columns = []
+    for k, slot in enumerate(members):
+        far_r, far_i = wave[k * width : (k + 1) * width, :width], wave[k * width : (k + 1) * width, width:]
         factor = amps[slot] * lax.rsqrt(jnp.maximum(far_r * far_r + far_i * far_i, 1.0))
-        half = left_product(
-            flip_h, flip_l, jnp.concatenate([far_r * factor, far_i * factor], 0)
-        )
-        wave = right_product(jnp.concatenate([half[:width], half[width:]], 1), full_h, full_l)
-        chi_r = (wave[:, :width] - psi_r) * live
-        chi_i = (wave[:, width:] - psi_i) * live
+        columns.append(jnp.concatenate([far_r * factor, far_i * factor], 0))
+    half = left_product(flip_h, flip_l, jnp.concatenate(columns, 1))
+    wave = right_product(turn(half), full_h, full_l)
+    for k, slot in enumerate(members):
+        rows, skew, col, outside = where(slot)
+        ahead = lane_turn(col, width)
+        live = jnp.where(slot < starts[3 * step + 2, 0], 1.0, 0.0).astype(jnp.float32)
+        win_r, win_i = wins[slot, 0], wins[slot, 1]
+        chi_r = (wave[k * width : (k + 1) * width, :width] - psis[slot, 0]) * live
+        chi_i = (wave[k * width : (k + 1) * width, width:] - psis[slot, 1]) * live
 
         def deposit(part, term):
             grown = grow_rows(pltpu.roll(term, ahead, 1), skew)
@@ -171,8 +235,8 @@
     half = width // 2
     for part in range(3):
         totals[part] = total[part]
-    kept = pl.ds(pl.multiple_of(place[0] * half, half), half)
-    given = pl.ds(pl.multiple_of((1 - place[0]) * half, half), half)
+    kept = pl.ds(pl.multiple_of(spot.side * half, half), half)
+    given = pl.ds(pl.multiple_of((1 - spot.side) * half, half), half)
     for part in range(3):
         keep_out[part * half : (part + 1) * half] = totals[part, kept]
         core_out[part * half : (part + 1) * half] = totals[part, given]
@@ -183,28 +247,30 @@
     far_out[...] = jnp.where(odd, low, high)
 
 
-def folded(place, tall, near, far):
+def folded(spot, tall, near, far):
     start = near.shape[0] - tall.shape[1]
-    odd = place[0] != 0
-    from_near, from_far = near[start:], jnp.where(place[4] != 0, far[...], 0.0)
+    odd = spot.odd
+    from_near, from_far = near[start:], jnp.where(spot.has_far, far[...], 0.0)
     extra = unpack(jnp.where(odd, from_near, from_far), jnp.where(odd, from_far, from_near))
     return tall[0] + extra[0], tall[1] + extra[1]
 
 
-def fold_kernel(place, tall, near, far, first, second):
+def fold_kernel(tall, near, far, first, second):
     rows = first.shape[1]
-    odd_row = place[1] != 0
-    whole = folded(place, tall, near, far)
+    spot = Spot()
+    odd_row = spot.odd_row
+    whole = folded(spot, tall, near, far)
     for part in range(2):
         up, down = whole[part][:rows], whole[part][rows:]
         first[part] = jnp.where(odd_row, up, down)
         second[part] = jnp.where(odd_row, down, up)
 
 
-def last_fold_kernel(place, tall, near, far, middle, first, second):
+def last_fold_kernel(tall, near, far, middle, first, second):
     rows = middle.shape[1]
-    odd_row = place[1] != 0
-    whole = folded(place, tall, near, far)
+    spot = Spot()
+    odd_row = spot.odd_row
+    whole = folded(spot, tall, near, far)
     for part in range(2):
         up, down = whole[part][:RIM], whole[part][RIM + rows :]
         middle[part] = whole[part][RIM : RIM + rows]
@@ -214,16 +280,14 @@
 
 def weight_kernel(metas, probe, out, spread, *, step, slots):
     width = probe.shape[1]
-    stride = metas.shape[1]
     lane = lanes((width + TILE, width))
     spread[...] = jnp.zeros_like(spread)
     weight = probe[0] * probe[0] + probe[1] * probe[1]
     for index in range(metas.shape[0]):
-        count = metas[index, step * (2 * slots + 1) + 2 * slots]
+        count = metas[index, (3 * step + 2) * slots]
         for slot in range(slots):
-            where = step * (2 * slots + 1) + 2 * slot
-            row = metas[index, where] + (RIM + width + (index // 3 - 1) * width)
-            col = metas[index, where + 1] + (index % 3 - 1) * width
+            row = metas[index, 3 * step * slots + slot] + (RIM + width + (index // 3 - 1) * width)
+            col = metas[index, (3 * step + 1) * slots + slot] + (index % 3 - 1) * width
 
             @pl.when((slot < count) & (col < width) & (col > -width))
             def _():
@@ -236,48 +300,51 @@
     out[...] = spread[width : width + out.shape[0]]
 
 
-def update_kernel(place, tall, sent_1, sent_2, got_1, got_2, weight, new_tall, near, far):
+def update_kernel(tall, sent_1, sent_2, got_1, got_2, weight, new_tall, near, far):
     rows = sent_1.shape[1]
-    odd, odd_row = place[0] != 0, place[1] != 0
+    spot = Spot()
+    odd, odd_row = spot.odd, spot.odd_row
     for part in range(2):
         up = jnp.where(odd_row, sent_1[part], sent_2[part])
         down = jnp.where(odd_row, sent_2[part], sent_1[part])
         above = jnp.where(odd_row, got_1[part], got_2[part])
         below = jnp.where(odd_row, got_2[part], got_1[part])
-        up = up + jnp.where(place[2] != 0, above, 0.0)
-        down = down + jnp.where(place[3] != 0, below, 0.0)
+        up = up + jnp.where(spot.has_above, above, 0.0)
+        down = down + jnp.where(spot.has_below, below, 0.0)
         head = tall[part, :rows] + up / (weight[:rows] + EPS)
         tail = tall[part, rows:] + down / (weight[rows:] + EPS)
-        new_tall[part, :RIM] = jnp.where(place[2] != 0, head[:RIM], 0.0)
+        new_tall[part, :RIM] = jnp.where(spot.has_above, head[:RIM], 0.0)
         new_tall[part, RIM:rows] = head[RIM:]
         new_tall[part, rows : 2 * rows - RIM] = tail[: rows - RIM]
-        new_tall[part, 2 * rows - RIM :] = jnp.where(place[3] != 0, tail[rows - RIM :], 0.0)
+        new_tall[part, 2 * rows - RIM :] = jnp.where(spot.has_below, tail[rows - RIM :], 0.0)
     low, high = pack(new_tall[0], new_tall[1])
     near[...] = jnp.where(odd, low, high)
     far[...] = jnp.where(odd, high, low)
 
 
-def last_kernel(place, tall, middle, got_1, got_2, weight, tile):
+def last_kernel(tall, middle, got_1, got_2, weight, tile):
     side = tile.shape[1]
-    odd_row = place[1] != 0
+    spot = Spot()
+    odd_row = spot.odd_row
     for part in range(2):
         above = jnp.where(odd_row, got_1[part], got_2[part])
         below = jnp.where(odd_row, got_2[part], got_1[part])
-        above = jnp.where(place[2] != 0, above, 0.0)
-        below = jnp.where(place[3] != 0, below, 0.0)
+        above = jnp.where(spot.has_above, above, 0.0)
+        below = jnp.where(spot.has_below, below, 0.0)
         num = middle[part] + jnp.concatenate([above, below], 0)
         tile[part] = tall[part, RIM : RIM + side] + num / (weight[RIM : RIM + side] + EPS)
 
 
-def call(kernel, shapes, smem_count, operands, flops=1000000, moved=MIB, scratch=(), limit=16):
+def call(kernel, shapes, places, operands, flops=1000000, moved=MIB, scratch=(), more=(), limit=16):
     vmem = pl.BlockSpec(memory_space=pltpu.VMEM)
     smem = pl.BlockSpec(memory_space=pltpu.SMEM)
+    anywhere = pl.BlockSpec(memory_space=pl.ANY)
     return pl.pallas_call(
         kernel,
         out_shape=tuple(jax.ShapeDtypeStruct(shape, jnp.float32) for shape in shapes),
-        in_specs=[smem] * smem_count + [vmem] * (len(operands) - smem_count),
+        in_specs=[{"s": smem, "a": anywhere}.get(where, vmem) for where in places.ljust(len(operands), "v")],
         out_specs=tuple(vmem for _ in shapes),
-        scratch_shapes=[pltpu.VMEM(shape, jnp.float32) for shape in scratch],
+        scratch_shapes=[pltpu.VMEM(shape, jnp.float32) for shape in scratch] + list(more),
         compiler_params=pltpu.CompilerParams(vmem_limit_bytes=limit * MIB),
         cost_estimate=pl.CostEstimate(flops=flops, bytes_accessed=moved, transcendentals=0),
     )(*operands)
@@ -336,67 +403,71 @@
     row, col = lax.axis_index("row"), lax.axis_index("col")
     odd, odd_row = col % 2, row % 2
     outer = (col == 0) | (col == lax.axis_size("col") - 1)
-    place = jnp.stack([odd, odd_row, row, lax.axis_size("row") - 1 - row, 1 - outer]).astype(jnp.int32)
     tables = jnp.asarray(dft_tables(width))
 
-    own = jnp.concatenate([positions[0, 0].reshape(steps, 2 * slots), counts[0, 0][:, None]], 1)
-    own = own.reshape(1, -1).astype(jnp.float32)
-    meta = jnp.pad(own, ((0, TILE - 1), (0, width - own.shape[1])))
+    offsets = jnp.swapaxes(positions[0, 0], 1, 2)
+    amount = jnp.broadcast_to(counts[0, 0][:, None, None], (steps, 1, slots))
+    scan = jnp.concatenate([offsets, amount], 1).reshape(3 * steps, slots)
     flat = 2 * RIM
-    up = jnp.concatenate([object_field[:, :RIM].reshape(flat, width), meta], 0)
-    down = jnp.concatenate([object_field[:, side - RIM :].reshape(flat, width), meta], 0)
-    first = swap(jnp.where(odd_row != 0, up, down), "row", 1)
-    second = swap_rows(jnp.where(odd_row != 0, down, up))
+    first, second, meta = call(
+        first_kernel,
+        ((flat + TILE, width), (flat + TILE, width), (TILE, width)),
+        "aa",
+        (object_field, scan),
+        more=(pltpu.VMEM(scan.shape, jnp.int32), pltpu.SemaphoreType.DMA((5,))),
+    )
+    first, second = swap(first, "row", 1), swap_rows(second)
     strip = (tall_rows + 3 * TILE, width)
     tall, near, far = call(
         strips_kernel,
         ((2, tall_rows, side), strip, strip),
-        1,
-        (place, object_field, meta, first, second),
+        "",
+        (object_field, meta, first, second),
     )
     near, far = swap(near, "col", 1), swap_far(far)
 
     def three(value):
-        return value[tall_rows:].reshape(3, TILE, width)[:, 0, : own.shape[1]]
-
-    above = jnp.where(row > 0, jnp.where(odd_row != 0, first[flat], second[flat]), 0.0)
-    below = jnp.where(row < lax.axis_size("row") - 1, jnp.where(odd_row != 0, second[flat], first[flat]), 0.0)
-    here = jnp.stack([above, meta[0], below])[:, : own.shape[1]]
+        return value[tall_rows:].reshape(3, TILE, width)[:, : 3 * steps, :slots]
+
+    above = jnp.where(row > 0, jnp.where(odd_row != 0, first[flat:], second[flat:]), 0.0)
+    below = jnp.where(row < lax.axis_size("row") - 1, jnp.where(odd_row != 0, second[flat:], first[flat:]), 0.0)
+    here = jnp.stack([above, meta, below])[:, : 3 * steps, :slots]
     sides = three(near), jnp.where(outer, 0.0, three(far))
     left = jnp.where(odd != 0, sides[0], sides[1])
     right = jnp.where(odd != 0, sides[1], sides[0])
-    metas = jnp.stack([left, here, right], 1).reshape(9, own.shape[1]).astype(jnp.int32)
+    metas = jnp.stack([left, here, right], 1).reshape(9, -1).astype(jnp.int32)
 
     current = probe
     for step in range(steps):
-        starts = positions[0, 0, step].reshape(-1)
-        count = counts[0, 0, step].reshape(1)
         core, out_far, kept, sums = call(
-            slots_kernel,
+            functools.partial(slots_kernel, step=step),
             (
                 (3 * half + tall_rows, width),
                 (tall_rows, width),
                 (3 * half, width),
                 (2, tall_rows, width),
             ),
-            3,
-            (place, starts, count, tall, near, far, current, amplitude[0, 0, step], tables),
+            "a",
+            (scan, tall, near, far, current, amplitude[0, 0, step], tables),
             flops=slots * 96 * width * width * width,
             moved=4 * MIB,
             scratch=(
                 (2, tall_rows + TILE, 2 * width),
                 (2, tall_rows + TILE, 2 * width),
                 (3, width, width),
+                (slots, 2, width, width),
+                (slots, 2, width, width),
             ),
+            more=(pltpu.SMEM(scan.shape, jnp.int32), pltpu.SemaphoreType.DMA(())),
             limit=24,
         )
         core = swap(core, "col", 1)
         out_far = swap_far(out_far)
         part = sum_over_chips(kept + core[: 3 * half])
         (weight,) = call(
-            lambda *refs, step=step: weight_kernel(*refs, step=step, slots=slots),
+            functools.partial(weight_kernel, step=step, slots=slots),
             ((tall_rows, width),),
-            1,
+            "s",
             (metas, current),
             scratch=((tall_rows + 2 * width + TILE, width),),
         )
@@ -407,15 +478,15 @@
             sent_1, sent_2 = call(
                 fold_kernel,
                 ((2, tall_rows // 2, width), (2, tall_rows // 2, width)),
-                1,
-                (place, sums, core, out_far),
+                "",
+                (sums, core, out_far),
             )
             got_1, got_2 = swap(sent_1, "row", 1), swap_rows(sent_2)
             tall, near, far = call(
                 update_kernel,
                 ((2, tall_rows, side), (tall_rows, width), (tall_rows, width)),
-                1,
-                (place, tall, sent_1, sent_2, got_1, got_2, weight),
+                "",
+                (tall, sent_1, sent_2, got_1, got_2, weight),
             )
             far = swap_far(far)
             other = swap(jnp.concatenate([near, mine.reshape(2 * half, width)], 0), "col", 1)
@@ -425,15 +496,15 @@
             middle, sent_1, sent_2 = call(
                 last_fold_kernel,
                 ((2, side, width), (2, RIM, width), (2, RIM, width)),
-                1,
-                (place, sums, core, out_far),
+                "",
+                (sums, core, out_far),
             )
             got_1, got_2 = swap(sent_1, "row", 1), swap_rows(sent_2)
             (tile,) = call(
                 last_kernel,
                 ((2, side, side),),
-                1,
-                (place, tall, middle, got_1, got_2, weight),
+                "",
+                (tall, middle, got_1, got_2, weight),
             )
             other = swap(mine, "col", 1)
         low = jnp.where(odd == 0, mine, other)

time: 82.1 us -> 76.3 us (0.929)
  Pallas kernels: 17.1 us -> 10.5 us
  waiting for transfers between devices: 28.6 us -> 33 us
  starting transfers between devices: 28.4 us -> 26.7 us
  local copies, waits for them, and re-layouts: 5.12 us -> 3.88 us
    pallas_call x9 -> x10, Pallas kernels: 17.1 us -> 10.5 us  [call(): pl.pallas_call(kernel, out_shape=tuple((jax.ShapeDtypeStruct(shape, jnp.f...]
    ppermute x16, waiting for transfers between devices: 21.8 us -> 27.4 us  [swap(): lax.ppermute(value, axis, [(i, i ^ bit) for i in range(lax.axis_size(axis...]
    slice x8 -> x1, local copies, waits for them, and re-layouts: 1.69 us -> 0.11 us  [body(): here = jnp.stack([above, meta, below])[:, :3 * steps, :slots]]
    ppermute x4, waiting for transfers between devices: 6.76 us -> 5.57 us  [swap_far(): return lax.ppermute(value, AXES, pairs)]
    another operation x6 -> x0, local copies, waits for them, and re-layouts: 1.08 us -> none  [the longest x1 0.74 us: body(): counts[0, 0][:, None]]
    squeeze x1, local copies, waits for them, and re-layouts: 0.04 us -> 1.06 us  [body(): amplitude[0, 0, step]]
    ppermute x16, starting transfers between devices: 22.2 us -> 21.2 us  [swap(): lax.ppermute(value, axis, [(i, i ^ bit) for i in range(lax.axis_size(axis...]
    unnamed x13 -> x14, local copies, waits for them, and re-layouts: 2.18 us -> 2.39 us
  transfers between devices with their start and end apart: 23 -> 23, of which waited for: 14 -> 13; matrix products, arithmetic and copies ran while one was open for 2% -> 2% of each run, Pallas kernels for 8% -> 6%
where the time goes in v3:
time: 76.3 us; the launch traced here: 76 us
  waiting for transfers between devices  33 us (43%)
  starting transfers between devices  26.7 us (35%)
  Pallas kernels  10.5 us (14%)
  local copies, waits for them, and re-layouts  3.88 us (5%)
  other arithmetic  0.95 us (1%)
  between operations  0.95 us (1%)
    ppermute x16, waiting for transfers between devices, swap(): lax.ppermute(value, axis, [(i, i ^ bit) for i in range(lax.axis_size(axis...  27.4 us
    ppermute x16, starting transfers between devices, swap(): lax.ppermute(value, axis, [(i, i ^ bit) for i in range(lax.axis_size(axis...  21.2 us
    pallas_call x10, Pallas kernels, call(): pl.pallas_call(kernel, out_shape=tuple((jax.ShapeDtypeStruct(shape, jnp.f...  10.5 us
    ppermute x4, waiting for transfers between devices, swap_far(): return lax.ppermute(value, AXES, pairs)  5.57 us
    ppermute x4, starting transfers between devices, swap_far(): return lax.ppermute(value, AXES, pairs)  5.49 us
    unnamed x14, local copies, waits for them, and re-layouts  2.39 us
  transfers between devices with their start and end apart: 23, of which 13 were waited for; matrix products, arithmetic and copies ran while one was open for 2% of the time, Pallas kernels for 6%

profile of v3, /device:TPU:0, one launch (start us, length us, event | category | flops | bytes accessed | tf_op | source)
XLA Modules:
  0.0 76.0 jit_solution(14632161006992405140)
XLA Ops:
  0.6 0.6 copy-done.5
  1.3 0.1 broadcast_in_dim.19
  1.4 0.6 copy-done.4
  2.0 0.9 %copy-done = f32[2,128,128]{2,1,0:T(8,128)S(1)} copy-done((f32[2,128,128]{2,1,0:T(8,128)S(1)}, f32[2,128,128]{2,1,0:T(8,128)}, u32[]{:S(2)}) %copy-start) | copy-done | bytes 131096
  2.9 0.2 shard_map.77
  3.1 3.0 %collective-permute-start = (f32[136,128]{1,0:T(8,128)S(1)}, f32[136,128]{1,0:T(8,128)S(1)}, u32[]{:S(2)}, u32[]{:S(2)}) collective-permute-start(f32[136,128]{1,0:T(8,128)S(1)} %get-tuple-element.25), channel_id=1, source_target_pairs={{0,4},{4,0},{8,12},{12,8},{16,20},{20,16},{24,28},{28,24},{1,5},{5... | collective-permute-start | bytes 208904 | tf_op jit(solution)/shard_map/ppermute | solution.py:354
  6.2 3.2 %collective-permute-done.first = f32[136,128]{1,0:T(8,128)S(1)} collective-permute-done((f32[136,128]{1,0:T(8,128)S(1)}, f32[136,128]{1,0:T(8,128)S(1)}, u32[]{:S(2)}, u32[]{:S(2)}) %collective-permute-start) | collective-permute-done | bytes 69664 | tf_op jit(solution)/shard_map/ppermute | solution.py:354
  9.4 0.0 collective-permute-done.1.second
  9.4 0.1 shard_map.78
  9.5 0.1 collective-permute-start.2
  9.6 0.0 copy-start.2
  9.6 0.0 copy-start.3
  9.6 2.5 %collective-permute-start.3 = (f32[280,128]{1,0:T(8,128)S(1)}, f32[280,128]{1,0:T(8,128)S(1)}, u32[]{:S(2)}, u32[]{:S(2)}) collective-permute-start(f32[280,128]{1,0:T(8,128)S(1)} %get-tuple-element.29), channel_id=1, source_target_pairs={{0,4},{1,2},{2,1},{3,7},{4,0},{5,6},{6,5},{7,3},{8,12},{9,10},{10,... | collective-permute-start | bytes 430088 | tf_op jit(solution)/shard_map/ppermute | solution.py:366
  12.2 1.1 %slice_bitcast_fusion = (f32[4,128,128]{2,1,0:T(8,128)S(1)}, f32[4,128,128]{2,1,0:T(8,128)S(1)}) fusion(f32[1,1,2,4,128,128]{5,4,3,2,1,0:T(8,128)} %param.10), kind=kLoop, calls=%fused_computation | loop fusion | bytes 1048576 | tf_op jit(solution)/shard_map/squeeze | solution.py:451
  13.2 2.0 %collective-permute-done.3.far = f32[280,128]{1,0:T(8,128)S(1)} collective-permute-done((f32[280,128]{1,0:T(8,128)S(1)}, f32[280,128]{1,0:T(8,128)S(1)}, u32[]{:S(2)}, u32[]{:S(2)}) %collective-permute-start.3) | collective-permute-done | bytes 143392 | tf_op jit(solution)/shard_map/ppermute | solution.py:366
  15.2 2.8 %shard_map.79 = (f32[448,128]{1,0:T(8,128)S(1)}, f32[256,128]{1,0:T(8,128)S(1)}, f32[192,128]{1,0:T(8,128)S(1)}, f32[2,256,128]{2,1,0:T(8,128)S(1)}) custom-call(s32[6,4]{1,0:T(8,128)S(1)} %reshape.43.scan, f32[2,256,128]{2,1,0:T(8,128)S(1)} %get-tuple-element.27.tall, f32[280,128]{1,0:T(8,128)S(1)} %collective-permute-done.2.near, ...), custom_call_target="tpu_custom_call" | custom-call | flops 805306368 | bytes 4194304 | tf_op jit(solution)/shard_map/pallas_call | solution.py:342
  18.0 0.1 collective-permute-start.4
  18.1 0.1 copy.21
  18.2 2.1 %collective-permute-start.5 = (f32[256,128]{1,0:T(8,128)S(1)}, f32[256,128]{1,0:T(8,128)S(1)}, u32[]{:S(2)}, u32[]{:S(2)}) collective-permute-start(f32[256,128]{1,0:T(8,128)S(1)} %get-tuple-element.32), channel_id=1, source_target_pairs={{0,4},{1,2},{2,1},{3,7},{4,0},{5,6},{6,5},{7,3},{8,12},{9,10},{10,... | collective-permute-start | bytes 393224 | tf_op jit(solution)/shard_map/ppermute | solution.py:366
  20.4 0.0 collective-permute-done.4.near
  20.4 1.3 %collective-permute-start.8 = (f32[192,128]{1,0:T(8,128)S(1)}, f32[192,128]{1,0:T(8,128)S(1)}, u32[]{:S(2)}, u32[]{:S(2)}) collective-permute-start(f32[192,128]{1,0:T(8,128)S(1)} %slice_add_fusion.1), channel_id=1, source_target_pairs={{0,4},{4,0},{8,12},{12,8},{16,20},{20,16},{24,28},{28,24},{1,5},{5... | collective-permute-start | bytes 294920 | tf_op jit(solution)/shard_map/ppermute | solution.py:354
  21.7 3.7 %collective-permute-done.8 = f32[192,128]{1,0:T(8,128)S(1)} collective-permute-done((f32[192,128]{1,0:T(8,128)S(1)}, f32[192,128]{1,0:T(8,128)S(1)}, u32[]{:S(2)}, u32[]{:S(2)}) %collective-permute-start.8) | collective-permute-done | bytes 98336 | tf_op jit(solution)/shard_map/ppermute | solution.py:354
  25.4 0.9 %collective-permute-start.9 = (f32[192,128]{1,0:T(8,128)S(1)}, f32[192,128]{1,0:T(8,128)S(1)}, u32[]{:S(2)}, u32[]{:S(2)}) collective-permute-start(f32[192,128]{1,0:T(8,128)S(1)} %add.61), channel_id=1, source_target_pairs={{0,2},{1,3},{2,0},{3,1},{4,6},{5,7},{6,4},{7,5},{8,10},{9,11},{10,... | collective-permute-start | bytes 294920 | tf_op jit(solution)/shard_map/ppermute | solution.py:354
  26.4 0.1 copy.25
  26.5 0.1 copy.26
  26.6 0.1 shard_map.80
  26.7 1.7 %collective-permute-start.6 = (f32[2,128,128]{2,1,0:T(8,128)S(1)}, f32[2,128,128]{2,1,0:T(8,128)S(1)}, u32[]{:S(2)}, u32[]{:S(2)}) collective-permute-start(f32[2,128,128]{2,1,0:T(8,128)S(1)} %get-tuple-element.33.sent_1), channel_id=1, source_target_pairs={{0,4},{4,0},{8,12},{12,8},{16,20},{20,16},{24,28},{28,24},{1,5},{5... | collective-permute-start | bytes 393224 | tf_op jit(solution)/shard_map/ppermute | solution.py:354
  28.4 0.0 collective-permute-start.7
  28.4 1.7 %collective-permute-done.9 = f32[192,128]{1,0:T(8,128)S(1)} collective-permute-done((f32[192,128]{1,0:T(8,128)S(1)}, f32[192,128]{1,0:T(8,128)S(1)}, u32[]{:S(2)}, u32[]{:S(2)}) %collective-permute-start.9) | collective-permute-done | bytes 98336 | tf_op jit(solution)/shard_map/ppermute | solution.py:354
  30.1 3.2 %collective-permute-start.10 = (f32[192,128]{1,0:T(8,128)S(1)}, f32[192,128]{1,0:T(8,128)S(1)}, u32[]{:S(2)}, u32[]{:S(2)}) collective-permute-start(f32[192,128]{1,0:T(8,128)S(1)} %add.62), channel_id=1, source_target_pairs={{0,8},{4,12},{8,0},{12,4},{16,24},{20,28},{24,16},{28,20},{1,9},{5... | collective-permute-start | bytes 294920 | tf_op jit(solution)/shard_map/ppermute | solution.py:354
  33.3 2.6 %collective-permute-done.10 = f32[192,128]{1,0:T(8,128)S(1)} collective-permute-done((f32[192,128]{1,0:T(8,128)S(1)}, f32[192,128]{1,0:T(8,128)S(1)}, u32[]{:S(2)}, u32[]{:S(2)}) %collective-permute-start.10) | collective-permute-done | bytes 98336 | tf_op jit(solution)/shard_map/ppermute | solution.py:354
  35.9 3.4 %collective-permute-start.11 = (f32[192,128]{1,0:T(8,128)S(1)}, f32[192,128]{1,0:T(8,128)S(1)}, u32[]{:S(2)}, u32[]{:S(2)}) collective-permute-start(f32[192,128]{1,0:T(8,128)S(1)} %add.63), channel_id=1, source_target_pairs={{0,16},{4,20},{8,24},{12,28},{16,0},{20,4},{24,8},{28,12},{1,17},{... | collective-permute-start | bytes 294920 | tf_op jit(solution)/shard_map/ppermute | solution.py:354
  39.4 0.1 copy.22
  39.5 0.1 convert_element_type.6.metas
  39.6 1.8 %shard_map.81.weight = f32[256,128]{1,0:T(8,128)S(1)} custom-call(s32[9,24]{1,0:T(8,128)S(1)} %convert_element_type.6.metas, f32[2,128,128]{2,1,0:T(8,128)S(1)} %copy-done.2), custom_call_target="tpu_custom_call" | custom-call | flops 1000000 | bytes 1048576 | tf_op jit(solution)/shard_map/pallas_call | solution.py:342
  41.4 0.0 collective-permute-done.6.got_1
  41.5 0.2 shard_map.82
  41.6 0.3 collective-permute-done.11
  42.1 0.1 collective-permute-start.12
  42.1 0.5 collective-permute-start.13
  42.7 0.9 %collective-permute-done.12.near = f32[384,128]{1,0:T(8,128)S(1)} collective-permute-done((f32[384,128]{1,0:T(8,128)S(1)}, f32[384,128]{1,0:T(8,128)S(1)}, u32[]{:S(2)}, u32[]{:S(2)}) %collective-permute-start.12) | collective-permute-done | bytes 196640 | tf_op jit(solution)/shard_map/ppermute | solution.py:354
  43.6 3.6 %collective-permute-done.13.far = f32[256,128]{1,0:T(8,128)S(1)} collective-permute-done((f32[256,128]{1,0:T(8,128)S(1)}, f32[256,128]{1,0:T(8,128)S(1)}, u32[]{:S(2)}, u32[]{:S(2)}) %collective-permute-start.13) | collective-permute-done | bytes 131104 | tf_op jit(solution)/shard_map/ppermute | solution.py:366
  47.2 2.8 %shard_map.83 = (f32[448,128]{1,0:T(8,128)S(1)}, f32[256,128]{1,0:T(8,128)S(1)}, f32[192,128]{1,0:T(8,128)S(1)}, f32[2,256,128]{2,1,0:T(8,128)S(1)}) custom-call(s32[6,4]{1,0:T(8,128)S(1)} %reshape.43.scan, f32[2,256,128]{2,1,0:T(8,128)S(1)} %get-tuple-element.35.tall, f32[384,128]{1,0:T(8,128)S(1)} %collective-permute-done.12.near, ...), custom_call_target="tpu_custom_call" | custom-call | flops 805306368 | bytes 4194304 | tf_op jit(solution)/shard_map/pallas_call | solution.py:342
  50.0 0.2 collective-permute-start.14
  50.2 1.4 %collective-permute-done.14.near = f32[448,128]{1,0:T(8,128)S(1)} collective-permute-done((f32[448,128]{1,0:T(8,128)S(1)}, f32[448,128]{1,0:T(8,128)S(1)}, u32[]{:S(2)}, u32[]{:S(2)}) %collective-permute-start.14) | collective-permute-done | bytes 229408 | tf_op jit(solution)/shard_map/ppermute | solution.py:354
  51.5 0.5 collective-permute-start.18
  52.1 4.4 %collective-permute-done.18 = f32[192,128]{1,0:T(8,128)S(1)} collective-permute-done((f32[192,128]{1,0:T(8,128)S(1)}, f32[192,128]{1,0:T(8,128)S(1)}, u32[]{:S(2)}, u32[]{:S(2)}) %collective-permute-start.18) | collective-permute-done | bytes 98336 | tf_op jit(solution)/shard_map/ppermute | solution.py:354
  56.5 1.2 %collective-permute-start.19 = (f32[192,128]{1,0:T(8,128)S(1)}, f32[192,128]{1,0:T(8,128)S(1)}, u32[]{:S(2)}, u32[]{:S(2)}) collective-permute-start(f32[192,128]{1,0:T(8,128)S(1)} %add.68), channel_id=1, source_target_pairs={{0,2},{1,3},{2,0},{3,1},{4,6},{5,7},{6,4},{7,5},{8,10},{9,11},{10,... | collective-permute-start | bytes 294920 | tf_op jit(solution)/shard_map/ppermute | solution.py:354
  57.6 3.5 %collective-permute-done.19 = f32[192,128]{1,0:T(8,128)S(1)} collective-permute-done((f32[192,128]{1,0:T(8,128)S(1)}, f32[192,128]{1,0:T(8,128)S(1)}, u32[]{:S(2)}, u32[]{:S(2)}) %collective-permute-start.19) | collective-permute-done | bytes 98336 | tf_op jit(solution)/shard_map/ppermute | solution.py:354
  61.2 1.9 %collective-permute-start.20 = (f32[192,128]{1,0:T(8,128)S(1)}, f32[192,128]{1,0:T(8,128)S(1)}, u32[]{:S(2)}, u32[]{:S(2)}) collective-permute-start(f32[192,128]{1,0:T(8,128)S(1)} %add.69), channel_id=1, source_target_pairs={{0,8},{4,12},{8,0},{12,4},{16,24},{20,28},{24,16},{28,20},{1,9},{5... | collective-permute-start | bytes 294920 | tf_op jit(solution)/shard_map/ppermute | solution.py:354
  63.0 0.3 collective-permute-start.15
  63.4 2.5 %collective-permute-done.20 = f32[192,128]{1,0:T(8,128)S(1)} collective-permute-done((f32[192,128]{1,0:T(8,128)S(1)}, f32[192,128]{1,0:T(8,128)S(1)}, u32[]{:S(2)}, u32[]{:S(2)}) %collective-permute-start.20) | collective-permute-done | bytes 98336 | tf_op jit(solution)/shard_map/ppermute | solution.py:354
  65.9 3.3 %collective-permute-start.21 = (f32[192,128]{1,0:T(8,128)S(1)}, f32[192,128]{1,0:T(8,128)S(1)}, u32[]{:S(2)}, u32[]{:S(2)}) collective-permute-start(f32[192,128]{1,0:T(8,128)S(1)} %add.70), channel_id=1, source_target_pairs={{0,16},{4,20},{8,24},{12,28},{16,0},{20,4},{24,8},{28,12},{1,17},{... | collective-permute-start | bytes 294920 | tf_op jit(solution)/shard_map/ppermute | solution.py:354
  69.1 0.0 collective-permute-done.15.far
  69.1 0.1 shard_map.84
  69.3 0.4 collective-permute-start.16
  69.7 0.0 collective-permute-start.17
  69.7 3.1 %collective-permute-done.21 = f32[192,128]{1,0:T(8,128)S(1)} collective-permute-done((f32[192,128]{1,0:T(8,128)S(1)}, f32[192,128]{1,0:T(8,128)S(1)}, u32[]{:S(2)}, u32[]{:S(2)}) %collective-permute-start.21) | collective-permute-done | bytes 98336 | tf_op jit(solution)/shard_map/ppermute | solution.py:354
  72.9 0.1 collective-permute-start.22
  73.0 1.6 %shard_map.85.weight = f32[256,128]{1,0:T(8,128)S(1)} custom-call(s32[9,24]{1,0:T(8,128)S(1)} %convert_element_type.6.metas, f32[2,128,128]{2,1,0:T(8,128)S(1)} %pad_maximum_fusion.1.probe), custom_call_target="tpu_custom_call" | custom-call | flops 1000000 | bytes 1048576 | tf_op jit(solution)/shard_map/pallas_call | solution.py:342
  74.6 0.0 collective-permute-done.16.got_1
  74.6 0.0 collective-permute-done.17.got_2
  74.6 0.7 shard_map.86
  75.3 0.7 pad_maximum_fusion.2
  (41 shorter events, 0.3 us)
Async XLA Ops:
  0.6 0.7 copy-start.5
  1.3 0.7 copy-start.4
  2.0 0.9 %copy-start = (f32[2,128,128]{2,1,0:T(8,128)S(1)}, f32[2,128,128]{2,1,0:T(8,128)}, u32[]{:S(2)}) copy-start(f32[2,128,128]{2,1,0:T(8,128)} %tile.3) | copy-start | bytes 393220
  2.9 6.5 %copy-start.1 = (f32[2,128,128]{2,1,0:T(8,128)S(1)}, f32[2,128,128]{2,1,0:T(8,128)}, u32[]{:S(2)}) copy-start(f32[2,128,128]{2,1,0:T(8,128)} %tile.3) | copy-start | bytes 393220
  3.1 6.3 %collective-permute-start = (f32[136,128]{1,0:T(8,128)S(1)}, f32[136,128]{1,0:T(8,128)S(1)}, u32[]{:S(2)}, u32[]{:S(2)}) collective-permute-start(f32[136,128]{1,0:T(8,128)S(1)} %get-tuple-element.25), channel_id=1, source_target_pairs={{0,4},{4,0},{8,12},{12,8},{16,20},{20,16},{24,28},{28,24},{1,5},{5... | collective-permute-start | bytes 208904 | tf_op jit(solution)/shard_map/ppermute | solution.py:354
  6.2 3.2 %collective-permute-start.1 = (f32[136,128]{1,0:T(8,128)S(1)}, f32[136,128]{1,0:T(8,128)S(1)}, u32[]{:S(2)}, u32[]{:S(2)}) collective-permute-start(f32[136,128]{1,0:T(8,128)S(1)} %get-tuple-element.26), channel_id=1, source_target_pairs={{0,1},{1,0},{2,3},{3,2},{4,8},{5,9},{6,10},{7,11},{8,4},{9,5},{10,... | collective-permute-start | bytes 208904 | tf_op jit(solution)/shard_map/ppermute | solution.py:378
  9.5 3.7 %collective-permute-start.2 = (f32[280,128]{1,0:T(8,128)S(1)}, f32[280,128]{1,0:T(8,128)S(1)}, u32[]{:S(2)}, u32[]{:S(2)}) collective-permute-start(f32[280,128]{1,0:T(8,128)S(1)} %get-tuple-element.28), channel_id=1, source_target_pairs={{0,1},{1,0},{2,3},{3,2},{4,5},{5,4},{6,7},{7,6},{8,9},{9,8},{10,11... | collective-permute-start | bytes 430088 | tf_op jit(solution)/shard_map/ppermute | solution.py:354
  9.6 5.6 %copy-start.2 = (f32[2,128,128]{2,1,0:T(8,128)S(1)}, f32[2,128,128]{2,1,0:T(8,128)}, u32[]{:S(2)}) copy-start(f32[2,128,128]{2,1,0:T(8,128)} %probe.3) | copy-start | bytes 393220
  9.6 5.6 %copy-start.3 = (bf16[4,256,256]{2,1,0:T(8,128)(2,1)S(1)}, bf16[4,256,256]{2,1,0:T(8,128)(2,1)}, u32[]{:S(2)}) copy-start(bf16[4,256,256]{2,1,0:T(8,128)(2,1)} %constant.41.clone.tables) | copy-start | bytes 1572868
  9.6 5.6 %collective-permute-start.3 = (f32[280,128]{1,0:T(8,128)S(1)}, f32[280,128]{1,0:T(8,128)S(1)}, u32[]{:S(2)}, u32[]{:S(2)}) collective-permute-start(f32[280,128]{1,0:T(8,128)S(1)} %get-tuple-element.29), channel_id=1, source_target_pairs={{0,4},{1,2},{2,1},{3,7},{4,0},{5,6},{6,5},{7,3},{8,12},{9,10},{10,... | collective-permute-start | bytes 430088 | tf_op jit(solution)/shard_map/ppermute | solution.py:366
  18.0 2.3 %collective-permute-start.4 = (f32[448,128]{1,0:T(8,128)S(1)}, f32[448,128]{1,0:T(8,128)S(1)}, u32[]{:S(2)}, u32[]{:S(2)}) collective-permute-start(f32[448,128]{1,0:T(8,128)S(1)} %get-tuple-element.31), channel_id=1, source_target_pairs={{0,1},{1,0},{2,3},{3,2},{4,5},{5,4},{6,7},{7,6},{8,9},{9,8},{10,11... | collective-permute-start | bytes 688136 | tf_op jit(solution)/shard_map/ppermute | solution.py:354
  18.2 8.3 %collective-permute-start.5 = (f32[256,128]{1,0:T(8,128)S(1)}, f32[256,128]{1,0:T(8,128)S(1)}, u32[]{:S(2)}, u32[]{:S(2)}) collective-permute-start(f32[256,128]{1,0:T(8,128)S(1)} %get-tuple-element.32), channel_id=1, source_target_pairs={{0,4},{1,2},{2,1},{3,7},{4,0},{5,6},{6,5},{7,3},{8,12},{9,10},{10,... | collective-permute-start | bytes 393224 | tf_op jit(solution)/shard_map/ppermute | solution.py:366
  20.4 5.0 %collective-permute-start.8 = (f32[192,128]{1,0:T(8,128)S(1)}, f32[192,128]{1,0:T(8,128)S(1)}, u32[]{:S(2)}, u32[]{:S(2)}) collective-permute-start(f32[192,128]{1,0:T(8,128)S(1)} %slice_add_fusion.1), channel_id=1, source_target_pairs={{0,4},{4,0},{8,12},{12,8},{16,20},{20,16},{24,28},{28,24},{1,5},{5... | collective-permute-start | bytes 294920 | tf_op jit(solution)/shard_map/ppermute | solution.py:354
  25.4 4.7 %collective-permute-start.9 = (f32[192,128]{1,0:T(8,128)S(1)}, f32[192,128]{1,0:T(8,128)S(1)}, u32[]{:S(2)}, u32[]{:S(2)}) collective-permute-start(f32[192,128]{1,0:T(8,128)S(1)} %add.61), channel_id=1, source_target_pairs={{0,2},{1,3},{2,0},{3,1},{4,6},{5,7},{6,4},{7,5},{8,10},{9,11},{10,... | collective-permute-start | bytes 294920 | tf_op jit(solution)/shard_map/ppermute | solution.py:354
  26.7 14.7 %collective-permute-start.6 = (f32[2,128,128]{2,1,0:T(8,128)S(1)}, f32[2,128,128]{2,1,0:T(8,128)S(1)}, u32[]{:S(2)}, u32[]{:S(2)}) collective-permute-start(f32[2,128,128]{2,1,0:T(8,128)S(1)} %get-tuple-element.33.sent_1), channel_id=1, source_target_pairs={{0,4},{4,0},{8,12},{12,8},{16,20},{20,16},{24,28},{28,24},{1,5},{5... | collective-permute-start | bytes 393224 | tf_op jit(solution)/shard_map/ppermute | solution.py:354
  28.4 13.0 %collective-permute-start.7 = (f32[2,128,128]{2,1,0:T(8,128)S(1)}, f32[2,128,128]{2,1,0:T(8,128)S(1)}, u32[]{:S(2)}, u32[]{:S(2)}) collective-permute-start(f32[2,128,128]{2,1,0:T(8,128)S(1)} %get-tuple-element.34.sent_2), channel_id=1, source_target_pairs={{0,1},{1,0},{2,3},{3,2},{4,8},{5,9},{6,10},{7,11},{8,4},{9,5},{10,... | collective-permute-start | bytes 393224 | tf_op jit(solution)/shard_map/ppermute | solution.py:378
  30.1 5.8 %collective-permute-start.10 = (f32[192,128]{1,0:T(8,128)S(1)}, f32[192,128]{1,0:T(8,128)S(1)}, u32[]{:S(2)}, u32[]{:S(2)}) collective-permute-start(f32[192,128]{1,0:T(8,128)S(1)} %add.62), channel_id=1, source_target_pairs={{0,8},{4,12},{8,0},{12,4},{16,24},{20,28},{24,16},{28,20},{1,9},{5... | collective-permute-start | bytes 294920 | tf_op jit(solution)/shard_map/ppermute | solution.py:354
  35.9 6.1 %collective-permute-start.11 = (f32[192,128]{1,0:T(8,128)S(1)}, f32[192,128]{1,0:T(8,128)S(1)}, u32[]{:S(2)}, u32[]{:S(2)}) collective-permute-start(f32[192,128]{1,0:T(8,128)S(1)} %add.63), channel_id=1, source_target_pairs={{0,16},{4,20},{8,24},{12,28},{16,0},{20,4},{24,8},{28,12},{1,17},{... | collective-permute-start | bytes 294920 | tf_op jit(solution)/shard_map/ppermute | solution.py:354
  42.1 1.5 %collective-permute-start.12 = (f32[384,128]{1,0:T(8,128)S(1)}, f32[384,128]{1,0:T(8,128)S(1)}, u32[]{:S(2)}, u32[]{:S(2)}) collective-permute-start(f32[384,128]{1,0:T(8,128)S(1)} %pad_maximum_fusion), channel_id=1, source_target_pairs={{0,1},{1,0},{2,3},{3,2},{4,5},{5,4},{6,7},{7,6},{8,9},{9,8},{10,11... | collective-permute-start | bytes 589832 | tf_op jit(solution)/shard_map/ppermute | solution.py:354
  42.1 5.0 %collective-permute-start.13 = (f32[256,128]{1,0:T(8,128)S(1)}, f32[256,128]{1,0:T(8,128)S(1)}, u32[]{:S(2)}, u32[]{:S(2)}) collective-permute-start(f32[256,128]{1,0:T(8,128)S(1)} %get-tuple-element.38), channel_id=1, source_target_pairs={{0,4},{1,2},{2,1},{3,7},{4,0},{5,6},{6,5},{7,3},{8,12},{9,10},{10,... | collective-permute-start | bytes 393224 | tf_op jit(solution)/shard_map/ppermute | solution.py:366
  50.0 1.6 %collective-permute-start.14 = (f32[448,128]{1,0:T(8,128)S(1)}, f32[448,128]{1,0:T(8,128)S(1)}, u32[]{:S(2)}, u32[]{:S(2)}) collective-permute-start(f32[448,128]{1,0:T(8,128)S(1)} %get-tuple-element.40), channel_id=1, source_target_pairs={{0,1},{1,0},{2,3},{3,2},{4,5},{5,4},{6,7},{7,6},{8,9},{9,8},{10,11... | collective-permute-start | bytes 688136 | tf_op jit(solution)/shard_map/ppermute | solution.py:354
  51.5 4.9 %collective-permute-start.18 = (f32[192,128]{1,0:T(8,128)S(1)}, f32[192,128]{1,0:T(8,128)S(1)}, u32[]{:S(2)}, u32[]{:S(2)}) collective-permute-start(f32[192,128]{1,0:T(8,128)S(1)} %slice_add_fusion), channel_id=1, source_target_pairs={{0,4},{4,0},{8,12},{12,8},{16,20},{20,16},{24,28},{28,24},{1,5},{5... | collective-permute-start | bytes 294920 | tf_op jit(solution)/shard_map/ppermute | solution.py:354
  56.5 4.7 %collective-permute-start.19 = (f32[192,128]{1,0:T(8,128)S(1)}, f32[192,128]{1,0:T(8,128)S(1)}, u32[]{:S(2)}, u32[]{:S(2)}) collective-permute-start(f32[192,128]{1,0:T(8,128)S(1)} %add.68), channel_id=1, source_target_pairs={{0,2},{1,3},{2,0},{3,1},{4,6},{5,7},{6,4},{7,5},{8,10},{9,11},{10,... | collective-permute-start | bytes 294920 | tf_op jit(solution)/shard_map/ppermute | solution.py:354
  61.2 4.7 %collective-permute-start.20 = (f32[192,128]{1,0:T(8,128)S(1)}, f32[192,128]{1,0:T(8,128)S(1)}, u32[]{:S(2)}, u32[]{:S(2)}) collective-permute-start(f32[192,128]{1,0:T(8,128)S(1)} %add.69), channel_id=1, source_target_pairs={{0,8},{4,12},{8,0},{12,4},{16,24},{20,28},{24,16},{28,20},{1,9},{5... | collective-permute-start | bytes 294920 | tf_op jit(solution)/shard_map/ppermute | solution.py:354
  63.0 6.1 %collective-permute-start.15 = (f32[256,128]{1,0:T(8,128)S(1)}, f32[256,128]{1,0:T(8,128)S(1)}, u32[]{:S(2)}, u32[]{:S(2)}) collective-permute-start(f32[256,128]{1,0:T(8,128)S(1)} %get-tuple-element.41), channel_id=1, source_target_pairs={{0,4},{1,2},{2,1},{3,7},{4,0},{5,6},{6,5},{7,3},{8,12},{9,10},{10,... | collective-permute-start | bytes 393224 | tf_op jit(solution)/shard_map/ppermute | solution.py:366
  65.9 6.9 %collective-permute-start.21 = (f32[192,128]{1,0:T(8,128)S(1)}, f32[192,128]{1,0:T(8,128)S(1)}, u32[]{:S(2)}, u32[]{:S(2)}) collective-permute-start(f32[192,128]{1,0:T(8,128)S(1)} %add.70), channel_id=1, source_target_pairs={{0,16},{4,20},{8,24},{12,28},{16,0},{20,4},{24,8},{28,12},{1,17},{... | collective-permute-start | bytes 294920 | tf_op jit(solution)/shard_map/ppermute | solution.py:354
  69.3 5.3 %collective-permute-start.16 = (f32[2,64,128]{2,1,0:T(8,128)S(1)}, f32[2,64,128]{2,1,0:T(8,128)S(1)}, u32[]{:S(2)}, u32[]{:S(2)}) collective-permute-start(f32[2,64,128]{2,1,0:T(8,128)S(1)} %get-tuple-element.43), channel_id=1, source_target_pairs={{0,4},{4,0},{8,12},{12,8},{16,20},{20,16},{24,28},{28,24},{1,5},{5... | collective-permute-start | bytes 196616 | tf_op jit(solution)/shard_map/ppermute | solution.py:354
  69.7 4.9 %collective-permute-start.17 = (f32[2,64,128]{2,1,0:T(8,128)S(1)}, f32[2,64,128]{2,1,0:T(8,128)S(1)}, u32[]{:S(2)}, u32[]{:S(2)}) collective-permute-start(f32[2,64,128]{2,1,0:T(8,128)S(1)} %get-tuple-element.44), channel_id=1, source_target_pairs={{0,1},{1,0},{2,3},{3,2},{4,8},{5,9},{6,10},{7,11},{8,4},{9,5},{10,... | collective-permute-start | bytes 196616 | tf_op jit(solution)/shard_map/ppermute | solution.py:378
  72.9 2.4 %collective-permute-start.22 = (f32[2,64,128]{2,1,0:T(8,128)S(1)}, f32[2,64,128]{2,1,0:T(8,128)S(1)}, u32[]{:S(2)}, u32[]{:S(2)}) collective-permute-start(f32[2,64,128]{2,1,0:T(8,128)S(1)} %fusion.1), channel_id=1, source_target_pairs={{0,1},{1,0},{2,3},{3,2},{4,5},{5,4},{6,7},{7,6},{8,9},{9,8},{10,11... | collective-permute-start | bytes 196616 | tf_op jit(solution)/shard_map/ppermute | solution.py:354

commit v4 on v3

--- a/solution.py
+++ b/solution.py
@@ -97,25 +97,33 @@
         self.has_far = (col != 0) & (col != lax.axis_size("col") - 1)
 
 
-def first_kernel(tile, scan, first, second, meta, offsets, sems):
+def first_kernel(tile, offsets, counts, first, second, meta, offsets_here, counts_here, sems):
     spot = Spot()
     side = tile.shape[1]
+    steps, _, slots = offsets.shape
     near_edge = pl.multiple_of(spot.row_side * RIM, RIM)
-    copies = [pltpu.make_async_copy(scan, offsets, sems.at[0])]
+    copies = [
+        pltpu.make_async_copy(offsets, offsets_here, sems.at[0]),
+        pltpu.make_async_copy(counts, counts_here, sems.at[1]),
+    ]
     for part in range(2):
         rows = pl.ds(part * RIM, RIM)
         lower = pl.ds(side - RIM - near_edge, RIM)
         upper = pl.ds(near_edge, RIM)
-        copies.append(pltpu.make_async_copy(tile.at[part, lower], first.at[rows], sems.at[1 + part]))
-        copies.append(pltpu.make_async_copy(tile.at[part, upper], second.at[rows], sems.at[3 + part]))
+        copies.append(pltpu.make_async_copy(tile.at[part, lower], first.at[rows], sems.at[2 + part]))
+        copies.append(pltpu.make_async_copy(tile.at[part, upper], second.at[rows], sems.at[4 + part]))
     for copy in copies:
         copy.start()
     meta[...] = jnp.zeros_like(meta)
-    copies[0].wait()
-    meta[: scan.shape[0], : scan.shape[1]] = offsets[...].astype(jnp.float32)
+    for copy in copies[:2]:
+        copy.wait()
+    for step in range(steps):
+        meta[3 * step : 3 * step + 2, :slots] = offsets_here[step].astype(jnp.float32)
+        count = counts_here[:, step : step + 1].astype(jnp.float32)
+        meta[3 * step + 2 : 3 * step + 3] = jnp.broadcast_to(count, (1, meta.shape[1]))
     first[2 * RIM :] = meta[...]
     second[2 * RIM :] = meta[...]
-    for copy in copies[1:]:
+    for copy in copies[2:]:
         copy.wait()
 
 
@@ -378,19 +386,22 @@
     return lax.ppermute(value, AXES, pairs)
 
 
-def sum_over_chips(part):
-    bits = [("row", 1)]
-    bit = 2
-    while bit < lax.axis_size("col"):
-        bits.append(("col", bit))
-        bit *= 2
-    bit = 2
-    while bit < lax.axis_size("row"):
-        bits.append(("row", bit))
-        bit *= 2
-    for axis, bit in bits:
-        part = part + swap(part, axis, bit)
-    return part
+def after(*values):
+    return lax.optimization_barrier(values)
+
+
+def chip_steps():
+    steps = [("row", 1)]
+    for axis in ("col", "row"):
+        bit = 2
+        while bit < lax.axis_size(axis):
+            steps.append((axis, bit))
+            bit *= 2
+    return steps
+
+
+def add_step(part, step):
+    return part + swap(part, *step)
 
 
 def body(object_field, probe, positions, counts, amplitude):
@@ -406,16 +417,20 @@
     tables = jnp.asarray(dft_tables(width))
 
     offsets = jnp.swapaxes(positions[0, 0], 1, 2)
-    amount = jnp.broadcast_to(counts[0, 0][:, None, None], (steps, 1, slots))
-    scan = jnp.concatenate([offsets, amount], 1).reshape(3 * steps, slots)
     flat = 2 * RIM
     first, second, meta = call(
         first_kernel,
         ((flat + TILE, width), (flat + TILE, width), (TILE, width)),
-        "aa",
-        (object_field, scan),
-        more=(pltpu.VMEM(scan.shape, jnp.int32), pltpu.SemaphoreType.DMA((5,))),
+        "aaa",
+        (object_field, offsets, counts[0]),
+        more=(
+            pltpu.VMEM(offsets.shape, jnp.int32),
+            pltpu.VMEM((1, steps), jnp.int32),
+            pltpu.SemaphoreType.DMA((6,)),
+        ),
+        limit=60,
     )
+    scan = meta[: 3 * steps, :slots].astype(jnp.int32)
     first, second = swap(first, "row", 1), swap_rows(second)
     strip = (tall_rows + 3 * TILE, width)
     tall, near, far = call(
@@ -463,7 +478,9 @@
         )
         core = swap(core, "col", 1)
         out_far = swap_far(out_far)
-        part = sum_over_chips(kept + core[: 3 * half])
+        last = step == steps - 1
+        first_step, second_step, *others, last_step = chip_steps()
+        part = add_step(kept + core[: 3 * half], first_step)
         (weight,) = call(
             functools.partial(weight_kernel, step=step, slots=slots),
             ((tall_rows, width),),
@@ -471,42 +488,52 @@
             (metas, current),
             scratch=((tall_rows + 2 * width + TILE, width),),
         )
-        mine = lax.dynamic_slice_in_dim(current, odd * half, half, 1)
-        part = part.reshape(3, half, width)
-        mine = mine + part[:2] / (part[2] + EPS)[None]
-        if step < steps - 1:
+        part, weight = after(part, weight)
+        part = add_step(part, second_step)
+        if last:
+            middle, sent_1, sent_2 = call(
+                last_fold_kernel,
+                ((2, side, width), (2, RIM, width), (2, RIM, width)),
+                "",
+                (sums, core, out_far),
+            )
+        else:
             sent_1, sent_2 = call(
                 fold_kernel,
                 ((2, tall_rows // 2, width), (2, tall_rows // 2, width)),
                 "",
                 (sums, core, out_far),
             )
-            got_1, got_2 = swap(sent_1, "row", 1), swap_rows(sent_2)
+        got_1, got_2 = swap(sent_1, "row", 1), swap_rows(sent_2)
+        for other_step in others:
+            part = add_step(part, other_step)
+        if last:
+            (tile,) = call(
+                last_kernel,
+                ((2, side, side),),
+                "",
+                (tall, middle, got_1, got_2, weight),
+            )
+            part = add_step(part, last_step)
+        else:
             tall, near, far = call(
                 update_kernel,
                 ((2, tall_rows, side), (tall_rows, width), (tall_rows, width)),
                 "",
                 (tall, sent_1, sent_2, got_1, got_2, weight),
             )
-            far = swap_far(far)
-            other = swap(jnp.concatenate([near, mine.reshape(2 * half, width)], 0), "col", 1)
-            near = other
-            other = other[tall_rows:].reshape(2, half, width)
+            far_1, far_2 = swap_far(far[: tall_rows // 2]), swap_far(far[tall_rows // 2 :])
+            part = add_step(part, last_step)
+            part, far_1, far_2 = after(part, far_1, far_2)
+            far = jnp.concatenate([far_1, far_2], 0)
+        mine = lax.dynamic_slice_in_dim(current, odd * half, half, 1)
+        part = part.reshape(3, half, width)
+        mine = mine + part[:2] / (part[2] + EPS)[None]
+        if last:
+            other = swap(mine, "col", 1)
         else:
-            middle, sent_1, sent_2 = call(
-                last_fold_kernel,
-                ((2, side, width), (2, RIM, width), (2, RIM, width)),
-                "",
-                (sums, core, out_far),
-            )
-            got_1, got_2 = swap(sent_1, "row", 1), swap_rows(sent_2)
-            (tile,) = call(
-                last_kernel,
-                ((2, side, side),),
-                "",
-                (tall, middle, got_1, got_2, weight),
-            )
-            other = swap(mine, "col", 1)
+            near = swap(jnp.concatenate([near, mine.reshape(2 * half, width)], 0), "col", 1)
+            other = near[tall_rows:].reshape(2, half, width)
         low = jnp.where(odd == 0, mine, other)
         high = jnp.where(odd == 0, other, mine)
         current = jnp.concatenate([low, high], 1)

time: 76.3 us -> 72.7 us (0.953)
  waiting for transfers between devices: 33 us -> 29.9 us
  local copies, waits for them, and re-layouts: 3.88 us -> 1.72 us
  Pallas kernels: 10.5 us -> 11.9 us
    ppermute x16, waiting for transfers between devices: 27.4 us -> 23.8 us  [swap(): lax.ppermute(value, axis, [(i, i ^ bit) for i in range(lax.axis_size(axis...]
    ppermute x4 -> x5, starting transfers between devices: 5.49 us -> 7.95 us  [swap_far(): return lax.ppermute(value, AXES, pairs)]
    ppermute x16, starting transfers between devices: 21.2 us -> 19.1 us  [swap(): lax.ppermute(value, axis, [(i, i ^ bit) for i in range(lax.axis_size(axis...]
    unnamed x14 -> x10, local copies, waits for them, and re-layouts: 2.39 us -> 0.23 us
    pallas_call x10, Pallas kernels: 10.5 us -> 11.9 us  [call(): pl.pallas_call(kernel, out_shape=tuple((jax.ShapeDtypeStruct(shape, jnp.f...]
    ppermute x4 -> x5, waiting for transfers between devices: 5.57 us -> 6.11 us  [swap_far(): return lax.ppermute(value, AXES, pairs)]
  transfers between devices with their start and end apart: 23 -> 24, of which waited for: 13 -> 17; matrix products, arithmetic and copies ran while one was open for 2% -> 3% of each run, Pallas kernels for 6% -> 6%
where the time goes in v4:
time: 72.7 us; the launch traced here: 72.5 us
  waiting for transfers between devices  29.9 us (41%)
  starting transfers between devices  27 us (37%)
  Pallas kernels  11.9 us (16%)
  local copies, waits for them, and re-layouts  1.72 us (2%)
  other arithmetic  0.96 us (1%)
  between operations  0.95 us (1%)
    ppermute x16, waiting for transfers between devices, swap(): lax.ppermute(value, axis, [(i, i ^ bit) for i in range(lax.axis_size(axis...  23.8 us
    ppermute x16, starting transfers between devices, swap(): lax.ppermute(value, axis, [(i, i ^ bit) for i in range(lax.axis_size(axis...  19.1 us
    pallas_call x10, Pallas kernels, call(): pl.pallas_call(kernel, out_shape=tuple((jax.ShapeDtypeStruct(shape, jnp.f...  11.9 us
    ppermute x5, starting transfers between devices, swap_far(): return lax.ppermute(value, AXES, pairs)  7.95 us
    ppermute x5, waiting for transfers between devices, swap_far(): return lax.ppermute(value, AXES, pairs)  6.11 us
  transfers between devices with their start and end apart: 24, of which 17 were waited for; matrix products, arithmetic and copies ran while one was open for 3% of the time, Pallas kernels for 6%

profile of v4, /device:TPU:0, one launch (start us, length us, event | category | flops | bytes accessed | tf_op | source)
XLA Modules:
  0.0 72.5 jit_solution(14768764031425711302)
XLA Ops:
  0.6 1.5 %shard_map.77 = (f32[136,128]{1,0:T(8,128)}, f32[136,128]{1,0:T(8,128)}, f32[8,128]{1,0:T(8,128)}) custom-call(f32[2,128,128]{2,1,0:T(8,128)} %tile.3, s32[2,2,4]{2,1,0:T(2,128)} %bitcast.36, s32[1,2]{1,0:T(1,128)} %bitcast.37), custom_call_target="tpu_custom_call" | custom-call | flops 1000000 | bytes 1048576 | tf_op jit(solution)/shard_map/pallas_call | solution.py:350
  2.2 3.0 %collective-permute-start = (f32[136,128]{1,0:T(8,128)}, f32[136,128]{1,0:T(8,128)S(1)}, u32[]{:S(2)}, u32[]{:S(2)}) collective-permute-start(f32[136,128]{1,0:T(8,128)} %get-tuple-element.32), channel_id=1, source_target_pairs={{0,4},{4,0},{8,12},{12,8},{16,20},{20,16},{24,28},{28,24},{1,5},{5... | collective-permute-start | bytes 208904 | tf_op jit(solution)/shard_map/ppermute | solution.py:362
  5.2 0.0 collective-permute-start.1
  5.2 1.1 %slice_bitcast_fusion = (f32[4,128,128]{2,1,0:T(8,128)S(1)}, f32[4,128,128]{2,1,0:T(8,128)S(1)}) fusion(f32[1,1,2,4,128,128]{5,4,3,2,1,0:T(8,128)} %param.10), kind=kLoop, calls=%fused_computation | loop fusion | bytes 1048576 | tf_op jit(solution)/shard_map/squeeze | solution.py:466
  6.4 0.0 copy-start.1
  6.4 2.3 %collective-permute-done.first = f32[136,128]{1,0:T(8,128)S(1)} collective-permute-done((f32[136,128]{1,0:T(8,128)}, f32[136,128]{1,0:T(8,128)S(1)}, u32[]{:S(2)}, u32[]{:S(2)}) %collective-permute-start) | collective-permute-done | bytes 69664 | tf_op jit(solution)/shard_map/ppermute | solution.py:362
  8.8 0.0 collective-permute-done.1.second
  8.8 0.1 shard_map.78
  8.9 0.1 collective-permute-start.2
  9.0 2.4 %collective-permute-start.3 = (f32[280,128]{1,0:T(8,128)S(1)}, f32[280,128]{1,0:T(8,128)S(1)}, u32[]{:S(2)}, u32[]{:S(2)}) collective-permute-start(f32[280,128]{1,0:T(8,128)S(1)} %get-tuple-element.36), channel_id=1, source_target_pairs={{0,4},{1,2},{2,1},{3,7},{4,0},{5,6},{6,5},{7,3},{8,12},{9,10},{10,... | collective-permute-start | bytes 430088 | tf_op jit(solution)/shard_map/ppermute | solution.py:374
  11.4 0.1 copy.14
  11.5 0.0 collective-permute-done.2.near
  11.5 3.0 %collective-permute-done.3.far = f32[280,128]{1,0:T(8,128)S(1)} collective-permute-done((f32[280,128]{1,0:T(8,128)S(1)}, f32[280,128]{1,0:T(8,128)S(1)}, u32[]{:S(2)}, u32[]{:S(2)}) %collective-permute-start.3) | collective-permute-done | bytes 143392 | tf_op jit(solution)/shard_map/ppermute | solution.py:374
  14.5 2.8 %shard_map.79 = (f32[448,128]{1,0:T(8,128)S(1)}, f32[256,128]{1,0:T(8,128)S(1)}, f32[192,128]{1,0:T(8,128)S(1)}, f32[2,256,128]{2,1,0:T(8,128)S(1)}) custom-call(s32[6,4]{1,0:T(8,128)S(1)} %slice_convert_fusion.scan, f32[2,256,128]{2,1,0:T(8,128)S(1)} %get-tuple-element.34.tall, f32[280,128]{1,0:T(8,128)S(1)} %collective-permute-done.2.near, ...), custom_call_target="tpu_custom_call" | custom-call | flops 805306368 | bytes 4194304 | tf_op jit(solution)/shard_map/pallas_call | solution.py:350
  17.3 0.1 collective-permute-start.4
  17.4 2.1 %collective-permute-start.5 = (f32[256,128]{1,0:T(8,128)S(1)}, f32[256,128]{1,0:T(8,128)S(1)}, u32[]{:S(2)}, u32[]{:S(2)}) collective-permute-start(f32[256,128]{1,0:T(8,128)S(1)} %get-tuple-element.39), channel_id=1, source_target_pairs={{0,4},{1,2},{2,1},{3,7},{4,0},{5,6},{6,5},{7,3},{8,12},{9,10},{10,... | collective-permute-start | bytes 393224 | tf_op jit(solution)/shard_map/ppermute | solution.py:374
  19.5 0.1 copy.16
  19.6 0.1 copy.17
  19.7 0.0 collective-permute-done.4.near
  19.7 1.2 %collective-permute-start.8 = (f32[192,128]{1,0:T(8,128)S(1)}, f32[192,128]{1,0:T(8,128)S(1)}, u32[]{:S(2)}, u32[]{:S(2)}) collective-permute-start(f32[192,128]{1,0:T(8,128)S(1)} %slice_add_fusion.1), channel_id=1, source_target_pairs={{0,4},{4,0},{8,12},{12,8},{16,20},{20,16},{24,28},{28,24},{1,5},{5... | collective-permute-start | bytes 294920 | tf_op jit(solution)/shard_map/ppermute | solution.py:362
  21.0 0.1 copy.15
  21.1 0.1 convert_element_type.10.metas
  21.2 1.7 %shard_map.81.weight = f32[256,128]{1,0:T(8,128)S(1)} custom-call(s32[9,24]{1,0:T(8,128)S(1)} %convert_element_type.10.metas, f32[2,128,128]{2,1,0:T(8,128)S(1)} %copy-done.1), custom_call_target="tpu_custom_call" | custom-call | flops 1000000 | bytes 1048576 | tf_op jit(solution)/shard_map/pallas_call | solution.py:350
  22.8 1.7 %collective-permute-done.8 = f32[192,128]{1,0:T(8,128)S(1)} collective-permute-done((f32[192,128]{1,0:T(8,128)S(1)}, f32[192,128]{1,0:T(8,128)S(1)}, u32[]{:S(2)}, u32[]{:S(2)}) %collective-permute-start.8) | collective-permute-done | bytes 98336 | tf_op jit(solution)/shard_map/ppermute | solution.py:362
  24.6 1.1 %collective-permute-start.9 = (f32[192,128]{1,0:T(8,128)S(1)}, f32[192,128]{1,0:T(8,128)S(1)}, u32[]{:S(2)}, u32[]{:S(2)}) collective-permute-start(f32[192,128]{1,0:T(8,128)S(1)} %add.58), channel_id=1, source_target_pairs={{0,2},{1,3},{2,0},{3,1},{4,6},{5,7},{6,4},{7,5},{8,10},{9,11},{10,... | collective-permute-start | bytes 294920 | tf_op jit(solution)/shard_map/ppermute | solution.py:362
  25.7 0.0 collective-permute-done.5.far
  25.7 0.1 shard_map.80
  25.8 1.5 %collective-permute-start.6 = (f32[2,128,128]{2,1,0:T(8,128)S(1)}, f32[2,128,128]{2,1,0:T(8,128)S(1)}, u32[]{:S(2)}, u32[]{:S(2)}) collective-permute-start(f32[2,128,128]{2,1,0:T(8,128)S(1)} %get-tuple-element.40.sent_1), channel_id=1, source_target_pairs={{0,4},{4,0},{8,12},{12,8},{16,20},{20,16},{24,28},{28,24},{1,5},{5... | collective-permute-start | bytes 393224 | tf_op jit(solution)/shard_map/ppermute | solution.py:362
  27.3 0.0 collective-permute-start.7
  27.3 1.9 %collective-permute-done.9 = f32[192,128]{1,0:T(8,128)S(1)} collective-permute-done((f32[192,128]{1,0:T(8,128)S(1)}, f32[192,128]{1,0:T(8,128)S(1)}, u32[]{:S(2)}, u32[]{:S(2)}) %collective-permute-start.9) | collective-permute-done | bytes 98336 | tf_op jit(solution)/shard_map/ppermute | solution.py:362
  29.3 3.2 %collective-permute-start.10 = (f32[192,128]{1,0:T(8,128)S(1)}, f32[192,128]{1,0:T(8,128)S(1)}, u32[]{:S(2)}, u32[]{:S(2)}) collective-permute-start(f32[192,128]{1,0:T(8,128)S(1)} %add.62), channel_id=1, source_target_pairs={{0,8},{4,12},{8,0},{12,4},{16,24},{20,28},{24,16},{28,20},{1,9},{5... | collective-permute-start | bytes 294920 | tf_op jit(solution)/shard_map/ppermute | solution.py:362
  32.4 0.2 collective-permute-done.6.got_1
  32.6 0.2 shard_map.82
  32.8 2.2 %collective-permute-done.10 = f32[192,128]{1,0:T(8,128)S(1)} collective-permute-done((f32[192,128]{1,0:T(8,128)S(1)}, f32[192,128]{1,0:T(8,128)S(1)}, u32[]{:S(2)}, u32[]{:S(2)}) %collective-permute-start.10) | collective-permute-done | bytes 98336 | tf_op jit(solution)/shard_map/ppermute | solution.py:362
  35.0 3.3 %collective-permute-start.11 = (f32[192,128]{1,0:T(8,128)S(1)}, f32[192,128]{1,0:T(8,128)S(1)}, u32[]{:S(2)}, u32[]{:S(2)}) collective-permute-start(f32[192,128]{1,0:T(8,128)S(1)} %add.63), channel_id=1, source_target_pairs={{0,16},{4,20},{8,24},{12,28},{16,0},{20,4},{24,8},{28,12},{1,17},{... | collective-permute-start | bytes 294920 | tf_op jit(solution)/shard_map/ppermute | solution.py:362
  38.3 0.5 collective-permute-start.12
  38.8 1.6 %collective-permute-start.13 = (f32[128,128]{1,0:T(8,128)S(1)}, f32[128,128]{1,0:T(8,128)S(1)}, u32[]{:S(2)}, u32[]{:S(2)}) collective-permute-start(f32[128,128]{1,0:T(8,128)S(1)} %get-tuple-element.68), channel_id=1, source_target_pairs={{0,4},{1,2},{2,1},{3,7},{4,0},{5,6},{6,5},{7,3},{8,12},{9,10},{10,... | collective-permute-start | bytes 196616 | tf_op jit(solution)/shard_map/ppermute | solution.py:374
  40.4 0.5 collective-permute-done.11
  40.9 1.7 %collective-permute-done.12 = f32[128,128]{1,0:T(8,128)S(1)} collective-permute-done((f32[128,128]{1,0:T(8,128)S(1)}, f32[128,128]{1,0:T(8,128)S(1)}, u32[]{:S(2)}, u32[]{:S(2)}) %collective-permute-start.12) | collective-permute-done | bytes 65568 | tf_op jit(solution)/shard_map/ppermute | solution.py:374
  42.7 0.7 collective-permute-done.13
  43.4 0.1 collective-permute-start.14
  43.5 1.4 %collective-permute-done.14.near = f32[384,128]{1,0:T(8,128)S(1)} collective-permute-done((f32[384,128]{1,0:T(8,128)S(1)}, f32[384,128]{1,0:T(8,128)S(1)}, u32[]{:S(2)}, u32[]{:S(2)}) %collective-permute-start.14) | collective-permute-done | bytes 196640 | tf_op jit(solution)/shard_map/ppermute | solution.py:362
  45.0 2.8 %shard_map.83 = (f32[448,128]{1,0:T(8,128)S(1)}, f32[256,128]{1,0:T(8,128)S(1)}, f32[192,128]{1,0:T(8,128)S(1)}, f32[2,256,128]{2,1,0:T(8,128)S(1)}) custom-call(s32[6,4]{1,0:T(8,128)S(1)} %slice_convert_fusion.scan, f32[2,256,128]{2,1,0:T(8,128)S(1)} %get-tuple-element.44.tall, f32[384,128]{1,0:T(8,128)S(1)} %collective-permute-done.14.near, ...), custom_call_target="tpu_custom_call" | custom-call | flops 805306368 | bytes 4194304 | tf_op jit(solution)/shard_map/pallas_call | solution.py:350
  47.8 0.2 collective-permute-start.15
  48.0 1.4 %collective-permute-done.15.near = f32[448,128]{1,0:T(8,128)S(1)} collective-permute-done((f32[448,128]{1,0:T(8,128)S(1)}, f32[448,128]{1,0:T(8,128)S(1)}, u32[]{:S(2)}, u32[]{:S(2)}) %collective-permute-start.15) | collective-permute-done | bytes 229408 | tf_op jit(solution)/shard_map/ppermute | solution.py:362
  49.4 1.4 %collective-permute-start.19 = (f32[192,128]{1,0:T(8,128)S(1)}, f32[192,128]{1,0:T(8,128)S(1)}, u32[]{:S(2)}, u32[]{:S(2)}) collective-permute-start(f32[192,128]{1,0:T(8,128)S(1)} %slice_add_fusion), channel_id=1, source_target_pairs={{0,4},{4,0},{8,12},{12,8},{16,20},{20,16},{24,28},{28,24},{1,5},{5... | collective-permute-start | bytes 294920 | tf_op jit(solution)/shard_map/ppermute | solution.py:362
  50.8 1.8 %shard_map.85.weight = f32[256,128]{1,0:T(8,128)S(1)} custom-call(s32[9,24]{1,0:T(8,128)S(1)} %convert_element_type.10.metas, f32[2,128,128]{2,1,0:T(8,128)S(1)} %pad_maximum_fusion.1.probe), custom_call_target="tpu_custom_call" | custom-call | flops 1000000 | bytes 1048576 | tf_op jit(solution)/shard_map/pallas_call | solution.py:350
  52.6 1.7 %collective-permute-done.19 = f32[192,128]{1,0:T(8,128)S(1)} collective-permute-done((f32[192,128]{1,0:T(8,128)S(1)}, f32[192,128]{1,0:T(8,128)S(1)}, u32[]{:S(2)}, u32[]{:S(2)}) %collective-permute-start.19) | collective-permute-done | bytes 98336 | tf_op jit(solution)/shard_map/ppermute | solution.py:362
  54.3 0.1 collective-permute-start.20
  54.4 4.6 %collective-permute-done.20 = f32[192,128]{1,0:T(8,128)S(1)} collective-permute-done((f32[192,128]{1,0:T(8,128)S(1)}, f32[192,128]{1,0:T(8,128)S(1)}, u32[]{:S(2)}, u32[]{:S(2)}) %collective-permute-start.20) | collective-permute-done | bytes 98336 | tf_op jit(solution)/shard_map/ppermute | solution.py:362
  59.0 1.5 %collective-permute-start.21 = (f32[192,128]{1,0:T(8,128)S(1)}, f32[192,128]{1,0:T(8,128)S(1)}, u32[]{:S(2)}, u32[]{:S(2)}) collective-permute-start(f32[192,128]{1,0:T(8,128)S(1)} %add.69), channel_id=1, source_target_pairs={{0,8},{4,12},{8,0},{12,4},{16,24},{20,28},{24,16},{28,20},{1,9},{5... | collective-permute-start | bytes 294920 | tf_op jit(solution)/shard_map/ppermute | solution.py:362
  60.4 1.3 %collective-permute-start.16 = (f32[256,128]{1,0:T(8,128)S(1)}, f32[256,128]{1,0:T(8,128)S(1)}, u32[]{:S(2)}, u32[]{:S(2)}) collective-permute-start(f32[256,128]{1,0:T(8,128)S(1)} %get-tuple-element.53), channel_id=1, source_target_pairs={{0,4},{1,2},{2,1},{3,7},{4,0},{5,6},{6,5},{7,3},{8,12},{9,10},{10,... | collective-permute-start | bytes 393224 | tf_op jit(solution)/shard_map/ppermute | solution.py:374
  61.8 1.9 %collective-permute-done.21 = f32[192,128]{1,0:T(8,128)S(1)} collective-permute-done((f32[192,128]{1,0:T(8,128)S(1)}, f32[192,128]{1,0:T(8,128)S(1)}, u32[]{:S(2)}, u32[]{:S(2)}) %collective-permute-start.21) | collective-permute-done | bytes 98336 | tf_op jit(solution)/shard_map/ppermute | solution.py:362
  63.7 1.0 %collective-permute-start.22 = (f32[192,128]{1,0:T(8,128)S(1)}, f32[192,128]{1,0:T(8,128)S(1)}, u32[]{:S(2)}, u32[]{:S(2)}) collective-permute-start(f32[192,128]{1,0:T(8,128)S(1)} %add.70), channel_id=1, source_target_pairs={{0,16},{4,20},{8,24},{12,28},{16,0},{20,4},{24,8},{28,12},{1,17},{... | collective-permute-start | bytes 294920 | tf_op jit(solution)/shard_map/ppermute | solution.py:362
  64.7 0.7 collective-permute-done.16.far
  65.4 0.1 shard_map.84
  65.6 1.4 %collective-permute-start.17 = (f32[2,64,128]{2,1,0:T(8,128)S(1)}, f32[2,64,128]{2,1,0:T(8,128)S(1)}, u32[]{:S(2)}, u32[]{:S(2)}) collective-permute-start(f32[2,64,128]{2,1,0:T(8,128)S(1)} %get-tuple-element.55), channel_id=1, source_target_pairs={{0,4},{4,0},{8,12},{12,8},{16,20},{20,16},{24,28},{28,24},{1,5},{5... | collective-permute-start | bytes 196616 | tf_op jit(solution)/shard_map/ppermute | solution.py:362
  66.9 0.0 collective-permute-start.18
  66.9 3.4 %collective-permute-done.22 = f32[192,128]{1,0:T(8,128)S(1)} collective-permute-done((f32[192,128]{1,0:T(8,128)S(1)}, f32[192,128]{1,0:T(8,128)S(1)}, u32[]{:S(2)}, u32[]{:S(2)}) %collective-permute-start.22) | collective-permute-done | bytes 98336 | tf_op jit(solution)/shard_map/ppermute | solution.py:362
  70.5 0.1 collective-permute-start.23
  70.6 0.0 collective-permute-done.18.got_2
  70.6 0.7 shard_map.86
  71.3 0.5 collective-permute-done.23
  71.8 0.7 pad_maximum_fusion.3
  (39 shorter events, 0.3 us)
Async XLA Ops:
  2.2 6.6 %collective-permute-start = (f32[136,128]{1,0:T(8,128)}, f32[136,128]{1,0:T(8,128)S(1)}, u32[]{:S(2)}, u32[]{:S(2)}) collective-permute-start(f32[136,128]{1,0:T(8,128)} %get-tuple-element.32), channel_id=1, source_target_pairs={{0,4},{4,0},{8,12},{12,8},{16,20},{20,16},{24,28},{28,24},{1,5},{5... | collective-permute-start | bytes 208904 | tf_op jit(solution)/shard_map/ppermute | solution.py:362
  5.2 9.3 %copy-start.3 = (bf16[4,256,256]{2,1,0:T(8,128)(2,1)S(1)}, bf16[4,256,256]{2,1,0:T(8,128)(2,1)}, u32[]{:S(2)}) copy-start(bf16[4,256,256]{2,1,0:T(8,128)(2,1)} %constant.41.clone.tables) | copy-start | bytes 1572868
  5.2 3.6 %collective-permute-start.1 = (f32[136,128]{1,0:T(8,128)}, f32[136,128]{1,0:T(8,128)S(1)}, u32[]{:S(2)}, u32[]{:S(2)}) collective-permute-start(f32[136,128]{1,0:T(8,128)} %get-tuple-element.33), channel_id=1, source_target_pairs={{0,1},{1,0},{2,3},{3,2},{4,8},{5,9},{6,10},{7,11},{8,4},{9,5},{10,... | collective-permute-start | bytes 208904 | tf_op jit(solution)/shard_map/ppermute | solution.py:386
  5.2 1.1 %copy-start.2 = (f32[8,128]{1,0:T(8,128)S(1)}, f32[8,128]{1,0:T(8,128)}, u32[]{:S(2)}) copy-start(f32[8,128]{1,0:T(8,128)} %get-tuple-element.31.meta) | copy-start | bytes 12292
  5.2 3.5 %copy-start = (f32[2,128,128]{2,1,0:T(8,128)S(1)}, f32[2,128,128]{2,1,0:T(8,128)}, u32[]{:S(2)}) copy-start(f32[2,128,128]{2,1,0:T(8,128)} %tile.3) | copy-start | bytes 393220
  6.4 8.1 %copy-start.1 = (f32[2,128,128]{2,1,0:T(8,128)S(1)}, f32[2,128,128]{2,1,0:T(8,128)}, u32[]{:S(2)}) copy-start(f32[2,128,128]{2,1,0:T(8,128)} %probe.3) | copy-start | bytes 393220
  8.9 2.6 %collective-permute-start.2 = (f32[280,128]{1,0:T(8,128)S(1)}, f32[280,128]{1,0:T(8,128)S(1)}, u32[]{:S(2)}, u32[]{:S(2)}) collective-permute-start(f32[280,128]{1,0:T(8,128)S(1)} %get-tuple-element.35), channel_id=1, source_target_pairs={{0,1},{1,0},{2,3},{3,2},{4,5},{5,4},{6,7},{7,6},{8,9},{9,8},{10,11... | collective-permute-start | bytes 430088 | tf_op jit(solution)/shard_map/ppermute | solution.py:362
  9.0 5.5 %collective-permute-start.3 = (f32[280,128]{1,0:T(8,128)S(1)}, f32[280,128]{1,0:T(8,128)S(1)}, u32[]{:S(2)}, u32[]{:S(2)}) collective-permute-start(f32[280,128]{1,0:T(8,128)S(1)} %get-tuple-element.36), channel_id=1, source_target_pairs={{0,4},{1,2},{2,1},{3,7},{4,0},{5,6},{6,5},{7,3},{8,12},{9,10},{10,... | collective-permute-start | bytes 430088 | tf_op jit(solution)/shard_map/ppermute | solution.py:374
  17.3 2.4 %collective-permute-start.4 = (f32[448,128]{1,0:T(8,128)S(1)}, f32[448,128]{1,0:T(8,128)S(1)}, u32[]{:S(2)}, u32[]{:S(2)}) collective-permute-start(f32[448,128]{1,0:T(8,128)S(1)} %get-tuple-element.38), channel_id=1, source_target_pairs={{0,1},{1,0},{2,3},{3,2},{4,5},{5,4},{6,7},{7,6},{8,9},{9,8},{10,11... | collective-permute-start | bytes 688136 | tf_op jit(solution)/shard_map/ppermute | solution.py:362
  17.4 8.3 %collective-permute-start.5 = (f32[256,128]{1,0:T(8,128)S(1)}, f32[256,128]{1,0:T(8,128)S(1)}, u32[]{:S(2)}, u32[]{:S(2)}) collective-permute-start(f32[256,128]{1,0:T(8,128)S(1)} %get-tuple-element.39), channel_id=1, source_target_pairs={{0,4},{1,2},{2,1},{3,7},{4,0},{5,6},{6,5},{7,3},{8,12},{9,10},{10,... | collective-permute-start | bytes 393224 | tf_op jit(solution)/shard_map/ppermute | solution.py:374
  19.7 4.8 %collective-permute-start.8 = (f32[192,128]{1,0:T(8,128)S(1)}, f32[192,128]{1,0:T(8,128)S(1)}, u32[]{:S(2)}, u32[]{:S(2)}) collective-permute-start(f32[192,128]{1,0:T(8,128)S(1)} %slice_add_fusion.1), channel_id=1, source_target_pairs={{0,4},{4,0},{8,12},{12,8},{16,20},{20,16},{24,28},{28,24},{1,5},{5... | collective-permute-start | bytes 294920 | tf_op jit(solution)/shard_map/ppermute | solution.py:362
  24.6 4.7 %collective-permute-start.9 = (f32[192,128]{1,0:T(8,128)S(1)}, f32[192,128]{1,0:T(8,128)S(1)}, u32[]{:S(2)}, u32[]{:S(2)}) collective-permute-start(f32[192,128]{1,0:T(8,128)S(1)} %add.58), channel_id=1, source_target_pairs={{0,2},{1,3},{2,0},{3,1},{4,6},{5,7},{6,4},{7,5},{8,10},{9,11},{10,... | collective-permute-start | bytes 294920 | tf_op jit(solution)/shard_map/ppermute | solution.py:362
  25.8 6.8 %collective-permute-start.6 = (f32[2,128,128]{2,1,0:T(8,128)S(1)}, f32[2,128,128]{2,1,0:T(8,128)S(1)}, u32[]{:S(2)}, u32[]{:S(2)}) collective-permute-start(f32[2,128,128]{2,1,0:T(8,128)S(1)} %get-tuple-element.40.sent_1), channel_id=1, source_target_pairs={{0,4},{4,0},{8,12},{12,8},{16,20},{20,16},{24,28},{28,24},{1,5},{5... | collective-permute-start | bytes 393224 | tf_op jit(solution)/shard_map/ppermute | solution.py:362
  27.3 5.3 %collective-permute-start.7 = (f32[2,128,128]{2,1,0:T(8,128)S(1)}, f32[2,128,128]{2,1,0:T(8,128)S(1)}, u32[]{:S(2)}, u32[]{:S(2)}) collective-permute-start(f32[2,128,128]{2,1,0:T(8,128)S(1)} %get-tuple-element.41.sent_2), channel_id=1, source_target_pairs={{0,1},{1,0},{2,3},{3,2},{4,8},{5,9},{6,10},{7,11},{8,4},{9,5},{10,... | collective-permute-start | bytes 393224 | tf_op jit(solution)/shard_map/ppermute | solution.py:386
  29.3 5.8 %collective-permute-start.10 = (f32[192,128]{1,0:T(8,128)S(1)}, f32[192,128]{1,0:T(8,128)S(1)}, u32[]{:S(2)}, u32[]{:S(2)}) collective-permute-start(f32[192,128]{1,0:T(8,128)S(1)} %add.62), channel_id=1, source_target_pairs={{0,8},{4,12},{8,0},{12,4},{16,24},{20,28},{24,16},{28,20},{1,9},{5... | collective-permute-start | bytes 294920 | tf_op jit(solution)/shard_map/ppermute | solution.py:362
  35.0 5.9 %collective-permute-start.11 = (f32[192,128]{1,0:T(8,128)S(1)}, f32[192,128]{1,0:T(8,128)S(1)}, u32[]{:S(2)}, u32[]{:S(2)}) collective-permute-start(f32[192,128]{1,0:T(8,128)S(1)} %add.63), channel_id=1, source_target_pairs={{0,16},{4,20},{8,24},{12,28},{16,0},{20,4},{24,8},{28,12},{1,17},{... | collective-permute-start | bytes 294920 | tf_op jit(solution)/shard_map/ppermute | solution.py:362
  38.3 4.3 %collective-permute-start.12 = (f32[128,128]{1,0:T(8,128)S(1)}, f32[128,128]{1,0:T(8,128)S(1)}, u32[]{:S(2)}, u32[]{:S(2)}) collective-permute-start(f32[128,128]{1,0:T(8,128)S(1)} %get-tuple-element.69), channel_id=1, source_target_pairs={{0,4},{1,2},{2,1},{3,7},{4,0},{5,6},{6,5},{7,3},{8,12},{9,10},{10,... | collective-permute-start | bytes 196616 | tf_op jit(solution)/shard_map/ppermute | solution.py:374
  38.8 4.6 %collective-permute-start.13 = (f32[128,128]{1,0:T(8,128)S(1)}, f32[128,128]{1,0:T(8,128)S(1)}, u32[]{:S(2)}, u32[]{:S(2)}) collective-permute-start(f32[128,128]{1,0:T(8,128)S(1)} %get-tuple-element.68), channel_id=1, source_target_pairs={{0,4},{1,2},{2,1},{3,7},{4,0},{5,6},{6,5},{7,3},{8,12},{9,10},{10,... | collective-permute-start | bytes 196616 | tf_op jit(solution)/shard_map/ppermute | solution.py:374
  43.4 1.5 %collective-permute-start.14 = (f32[384,128]{1,0:T(8,128)S(1)}, f32[384,128]{1,0:T(8,128)S(1)}, u32[]{:S(2)}, u32[]{:S(2)}) collective-permute-start(f32[384,128]{1,0:T(8,128)S(1)} %pad_maximum_fusion), channel_id=1, source_target_pairs={{0,1},{1,0},{2,3},{3,2},{4,5},{5,4},{6,7},{7,6},{8,9},{9,8},{10,11... | collective-permute-start | bytes 589832 | tf_op jit(solution)/shard_map/ppermute | solution.py:362
  47.8 1.6 %collective-permute-start.15 = (f32[448,128]{1,0:T(8,128)S(1)}, f32[448,128]{1,0:T(8,128)S(1)}, u32[]{:S(2)}, u32[]{:S(2)}) collective-permute-start(f32[448,128]{1,0:T(8,128)S(1)} %get-tuple-element.52), channel_id=1, source_target_pairs={{0,1},{1,0},{2,3},{3,2},{4,5},{5,4},{6,7},{7,6},{8,9},{9,8},{10,11... | collective-permute-start | bytes 688136 | tf_op jit(solution)/shard_map/ppermute | solution.py:362
  49.4 4.9 %collective-permute-start.19 = (f32[192,128]{1,0:T(8,128)S(1)}, f32[192,128]{1,0:T(8,128)S(1)}, u32[]{:S(2)}, u32[]{:S(2)}) collective-permute-start(f32[192,128]{1,0:T(8,128)S(1)} %slice_add_fusion), channel_id=1, source_target_pairs={{0,4},{4,0},{8,12},{12,8},{16,20},{20,16},{24,28},{28,24},{1,5},{5... | collective-permute-start | bytes 294920 | tf_op jit(solution)/shard_map/ppermute | solution.py:362
  54.3 4.7 %collective-permute-start.20 = (f32[192,128]{1,0:T(8,128)S(1)}, f32[192,128]{1,0:T(8,128)S(1)}, u32[]{:S(2)}, u32[]{:S(2)}) collective-permute-start(f32[192,128]{1,0:T(8,128)S(1)} %add.68), channel_id=1, source_target_pairs={{0,2},{1,3},{2,0},{3,1},{4,6},{5,7},{6,4},{7,5},{8,10},{9,11},{10,... | collective-permute-start | bytes 294920 | tf_op jit(solution)/shard_map/ppermute | solution.py:362
  59.0 4.7 %collective-permute-start.21 = (f32[192,128]{1,0:T(8,128)S(1)}, f32[192,128]{1,0:T(8,128)S(1)}, u32[]{:S(2)}, u32[]{:S(2)}) collective-permute-start(f32[192,128]{1,0:T(8,128)S(1)} %add.69), channel_id=1, source_target_pairs={{0,8},{4,12},{8,0},{12,4},{16,24},{20,28},{24,16},{28,20},{1,9},{5... | collective-permute-start | bytes 294920 | tf_op jit(solution)/shard_map/ppermute | solution.py:362
  60.4 5.0 %collective-permute-start.16 = (f32[256,128]{1,0:T(8,128)S(1)}, f32[256,128]{1,0:T(8,128)S(1)}, u32[]{:S(2)}, u32[]{:S(2)}) collective-permute-start(f32[256,128]{1,0:T(8,128)S(1)} %get-tuple-element.53), channel_id=1, source_target_pairs={{0,4},{1,2},{2,1},{3,7},{4,0},{5,6},{6,5},{7,3},{8,12},{9,10},{10,... | collective-permute-start | bytes 393224 | tf_op jit(solution)/shard_map/ppermute | solution.py:374
  63.7 6.7 %collective-permute-start.22 = (f32[192,128]{1,0:T(8,128)S(1)}, f32[192,128]{1,0:T(8,128)S(1)}, u32[]{:S(2)}, u32[]{:S(2)}) collective-permute-start(f32[192,128]{1,0:T(8,128)S(1)} %add.70), channel_id=1, source_target_pairs={{0,16},{4,20},{8,24},{12,28},{16,0},{20,4},{24,8},{28,12},{1,17},{... | collective-permute-start | bytes 294920 | tf_op jit(solution)/shard_map/ppermute | solution.py:362
  65.6 5.0 %collective-permute-start.17 = (f32[2,64,128]{2,1,0:T(8,128)S(1)}, f32[2,64,128]{2,1,0:T(8,128)S(1)}, u32[]{:S(2)}, u32[]{:S(2)}) collective-permute-start(f32[2,64,128]{2,1,0:T(8,128)S(1)} %get-tuple-element.55), channel_id=1, source_target_pairs={{0,4},{4,0},{8,12},{12,8},{16,20},{20,16},{24,28},{28,24},{1,5},{5... | collective-permute-start | bytes 196616 | tf_op jit(solution)/shard_map/ppermute | solution.py:362
  66.9 3.6 %collective-permute-start.18 = (f32[2,64,128]{2,1,0:T(8,128)S(1)}, f32[2,64,128]{2,1,0:T(8,128)S(1)}, u32[]{:S(2)}, u32[]{:S(2)}) collective-permute-start(f32[2,64,128]{2,1,0:T(8,128)S(1)} %get-tuple-element.56), channel_id=1, source_target_pairs={{0,1},{1,0},{2,3},{3,2},{4,8},{5,9},{6,10},{7,11},{8,4},{9,5},{10,... | collective-permute-start | bytes 196616 | tf_op jit(solution)/shard_map/ppermute | solution.py:386
  70.5 1.3 %collective-permute-start.23 = (f32[2,64,128]{2,1,0:T(8,128)S(1)}, f32[2,64,128]{2,1,0:T(8,128)S(1)}, u32[]{:S(2)}, u32[]{:S(2)}) collective-permute-start(f32[2,64,128]{2,1,0:T(8,128)S(1)} %fusion.1), channel_id=1, source_target_pairs={{0,1},{1,0},{2,3},{3,2},{4,5},{5,4},{6,7},{7,6},{8,9},{9,8},{10,11... | collective-permute-start | bytes 196616 | tf_op jit(solution)/shard_map/ppermute | solution.py:362

commit v5 on v4

--- a/solution.py
+++ b/solution.py
@@ -83,6 +83,15 @@
 
 def lane_turn(col, width):
     return jnp.where(col < 0, col + width, col)
+
+
+class Plain:
+    def __init__(self, value):
+        self.value = value
+
+    def __getitem__(self, where):
+        row, col = where
+        return self.value[row, col]
 
 
 class Spot:
@@ -147,85 +156,101 @@
         out[rows + 2 * TILE :] = below[2 * RIM :]
 
 
-def slots_kernel(
-    scan, tall, near, far, probe, amps, tables,
-    core_out, far_out, keep_out, tall_out, field, sums, totals, wins, psis, starts, sem, *, step,
-):
-    fetch = pltpu.make_async_copy(scan, starts, sem)
-    fetch.start()
-    spot = Spot()
-    width = probe.shape[1]
-    rows_all = tall.shape[1]
+def window_place(starts, step, slot, width):
+    row = starts[3 * step, slot] + RIM
+    col = starts[3 * step + 1, slot]
+    base = pl.multiple_of(row // TILE * TILE, TILE)
+    lane = lanes((width + TILE, width))
+    outside = (lane < col) | (lane >= width + col)
+    return pl.ds(base, width + TILE), row - base, col, outside
+
+
+def take_windows(starts, field, wins, weight, step):
+    slots, _, width, _ = wins.shape
     tiles = width // TILE
-    slots = amps.shape[0]
-    odd = spot.odd
-    lane = lanes((width + TILE, width))
     sub = lax.broadcasted_iota(jnp.int32, (tiles, TILE, width), 1)
-    from_near, from_far = near[:rows_all], jnp.where(spot.has_far, far[:rows_all], 0.0)
-    sides = unpack(jnp.where(odd, from_far, from_near), jnp.where(odd, from_near, from_far))
-    for part in range(2):
-        field[part, :rows_all, :width] = tall[part]
-        field[part, :rows_all, width:] = sides[part]
-        field[part, rows_all:] = jnp.zeros_like(field[part, rows_all:])
-    sums[...] = jnp.zeros_like(sums)
-    fetch.wait()
-    full_h, full_l, flip_h, flip_l = (tables[k] for k in range(4))
-    pro_r, pro_i = probe[0], probe[1]
-
-    def where(slot):
-        row = starts[3 * step, slot] + RIM
-        col = starts[3 * step + 1, slot]
-        base = pl.multiple_of(row // TILE * TILE, TILE)
-        outside = (lane < col) | (lane >= width + col)
-        return pl.ds(base, width + TILE), row - base, col, outside
-
     total = None
-    members = range(slots)
-    columns = []
-    for slot in members:
-        rows, skew, col, outside = where(slot)
+    for slot in range(slots):
+        rows, skew, col, outside = window_place(starts, step, slot, width)
+        live = jnp.where(slot < starts[3 * step + 2, 0], 1.0, 0.0).astype(jnp.float32)
         lift = jnp.where(skew > 0, TILE - skew, 0)
         back = lane_turn(-col, width)
-        win = []
+        power = None
         for part in range(2):
             mixed = jnp.where(outside, field[part, rows, width:], field[part, rows, :width])
             turned = pltpu.roll(mixed.reshape(tiles + 1, TILE, width), lift, 1)
             lined = jnp.where(sub < TILE - skew, turned[:-1], turned[1:])
-            win.append(pltpu.roll(lined.reshape(width, width), back, 1))
-            wins[slot, part] = win[part]
-        psi_r = pro_r * win[0] - pro_i * win[1]
-        psi_i = pro_r * win[1] + pro_i * win[0]
+            win = pltpu.roll(lined.reshape(width, width), back, 1)
+            wins[slot, part] = win
+            power = win * win if power is None else power + win * win
+        total = power * live if total is None else total + power * live
+    weight[...] = total
+
+
+def field_kernel(scan, tall, near, far, wins, weight, field, *, step):
+    spot = Spot()
+    width = tall.shape[2]
+    rows = tall.shape[1]
+    from_near, from_far = near[:rows], jnp.where(spot.has_far, far[:rows], 0.0)
+    sides = unpack(
+        jnp.where(spot.odd, from_far, from_near), jnp.where(spot.odd, from_near, from_far)
+    )
+    for part in range(2):
+        field[part, :rows, :width] = tall[part]
+        field[part, :rows, width:] = sides[part]
+        field[part, rows:] = jnp.zeros_like(field[part, rows:])
+    starts = Plain(scan[...])
+    take_windows(starts, field, wins, weight, step)
+
+
+def slots_kernel(
+    scan, wins, win_weight, probe, amps, tables,
+    core_out, far_out, keep_out, sums_out, sums, totals, psis, *, step,
+):
+    starts = Plain(scan[...])
+    spot = Spot()
+    width = probe.shape[1]
+    rows_all = sums_out.shape[1]
+    slots = amps.shape[0]
+    odd = spot.odd
+    sums[...] = jnp.zeros_like(sums)
+    full_h, full_l, flip_h, flip_l = (tables[k] for k in range(4))
+    pro_r, pro_i = probe[0], probe[1]
+    columns = []
+    for slot in range(slots):
+        psi_r = pro_r * wins[slot, 0] - pro_i * wins[slot, 1]
+        psi_i = pro_r * wins[slot, 1] + pro_i * wins[slot, 0]
         psis[slot, 0] = psi_r
         psis[slot, 1] = psi_i
         columns.append(jnp.concatenate([psi_r, psi_i], 0))
 
+    def block(value, k):
+        return value[k * width : (k + 1) * width]
+
     def turn(half):
-        return jnp.concatenate(
-            [
-                jnp.concatenate(
-                    [half[:width, k * width : (k + 1) * width], half[width:, k * width : (k + 1) * width]], 1
-                )
-                for k in range(slots)
-            ],
-            0,
-        )
+        parts = []
+        for k in range(slots):
+            both = half[:, k * width : (k + 1) * width]
+            parts.append(jnp.concatenate([both[:width], both[width:]], 1))
+        return jnp.concatenate(parts, 0)
 
     half = left_product(full_h, full_l, jnp.concatenate(columns, 1))
     wave = right_product(turn(half), flip_h, flip_l)
     columns = []
-    for k, slot in enumerate(members):
-        far_r, far_i = wave[k * width : (k + 1) * width, :width], wave[k * width : (k + 1) * width, width:]
+    for slot in range(slots):
+        far_r, far_i = block(wave, slot)[:, :width], block(wave, slot)[:, width:]
         factor = amps[slot] * lax.rsqrt(jnp.maximum(far_r * far_r + far_i * far_i, 1.0))
         columns.append(jnp.concatenate([far_r * factor, far_i * factor], 0))
     half = left_product(flip_h, flip_l, jnp.concatenate(columns, 1))
     wave = right_product(turn(half), full_h, full_l)
-    for k, slot in enumerate(members):
-        rows, skew, col, outside = where(slot)
+    total = None
+    for slot in range(slots):
+        rows, skew, col, outside = window_place(starts, step, slot, width)
         ahead = lane_turn(col, width)
         live = jnp.where(slot < starts[3 * step + 2, 0], 1.0, 0.0).astype(jnp.float32)
         win_r, win_i = wins[slot, 0], wins[slot, 1]
-        chi_r = (wave[k * width : (k + 1) * width, :width] - psis[slot, 0]) * live
-        chi_i = (wave[k * width : (k + 1) * width, width:] - psis[slot, 1]) * live
+        chi_r = (block(wave, slot)[:, :width] - psis[slot, 0]) * live
+        chi_i = (block(wave, slot)[:, width:] - psis[slot, 1]) * live
 
         def deposit(part, term):
             grown = grow_rows(pltpu.roll(term, ahead, 1), skew)
@@ -234,22 +259,17 @@
 
         deposit(0, pro_r * chi_r + pro_i * chi_i)
         deposit(1, pro_r * chi_i - pro_i * chi_r)
-        terms = (
-            win_r * chi_r + win_i * chi_i,
-            win_r * chi_i - win_i * chi_r,
-            (win_r * win_r + win_i * win_i) * live,
-        )
+        terms = (win_r * chi_r + win_i * chi_i, win_r * chi_i - win_i * chi_r)
         total = terms if total is None else tuple(a + b for a, b in zip(total, terms))
     half = width // 2
-    for part in range(3):
-        totals[part] = total[part]
+    totals[0], totals[1], totals[2] = total[0], total[1], win_weight[...]
     kept = pl.ds(pl.multiple_of(spot.side * half, half), half)
     given = pl.ds(pl.multiple_of((1 - spot.side) * half, half), half)
     for part in range(3):
         keep_out[part * half : (part + 1) * half] = totals[part, kept]
         core_out[part * half : (part + 1) * half] = totals[part, given]
     for part in range(2):
-        tall_out[part] = sums[part, :rows_all, :width]
+        sums_out[part] = sums[part, :rows_all, :width]
     low, high = pack(sums[0, :rows_all, width:], sums[1, :rows_all, width:])
     core_out[3 * half :] = jnp.where(odd, high, low)
     far_out[...] = jnp.where(odd, low, high)
@@ -297,18 +317,16 @@
             row = metas[index, 3 * step * slots + slot] + (RIM + width + (index // 3 - 1) * width)
             col = metas[index, (3 * step + 1) * slots + slot] + (index % 3 - 1) * width
 
-            @pl.when((slot < count) & (col < width) & (col > -width))
-            def _():
-                base = pl.multiple_of(row // TILE * TILE, TILE)
-                turned = pltpu.roll(weight, lane_turn(col, width), 1)
-                grown = grow_rows(turned, row - base)
-                inside = (lane >= col) & (lane < width + col)
-                spread[pl.ds(base, width + TILE)] += jnp.where(inside, grown, 0.0)
+            base = pl.multiple_of(row // TILE * TILE, TILE)
+            grown = grow_rows(pltpu.roll(weight, lax.rem(col + 2 * width, width), 1), row - base)
+            edge = jnp.where(slot < count, col, 2 * width)
+            inside = (lane >= edge) & (lane < width + edge)
+            spread[pl.ds(base, width + TILE)] += jnp.where(inside, grown, 0.0)
 
     out[...] = spread[width : width + out.shape[0]]
 
 
-def update_kernel(tall, sent_1, sent_2, got_1, got_2, weight, new_tall, near, far):
+def update_kernel(tall, sent_1, sent_2, got_1, got_2, weight, _, new_tall, near, far):
     rows = sent_1.shape[1]
     spot = Spot()
     odd, odd_row = spot.odd, spot.odd_row
@@ -398,6 +416,23 @@
             steps.append((axis, bit))
             bit *= 2
     return steps
+
+
+def swap_both(value):
+    rows, cols = lax.axis_size("row"), lax.axis_size("col")
+    pairs = [(r * cols + c, (r ^ 1) * cols + (c ^ 2)) for r in range(rows) for c in range(cols)]
+    return lax.ppermute(value, AXES, pairs)
+
+
+def chain_steps():
+    return lax.axis_size("row").bit_length() - 2
+
+
+def add_plane(part, weight):
+    part_y, part_x, part_xy = swap(part, "row", 1), swap(part, "col", 2), swap_both(part)
+    if weight is not None:
+        part_xy, weight = after(part_xy, weight)
+    return (part + part_y) + (part_x + part_xy)
 
 
 def add_step(part, step):
@@ -452,8 +487,19 @@
     right = jnp.where(odd != 0, sides[1], sides[0])
     metas = jnp.stack([left, here, right], 1).reshape(9, -1).astype(jnp.int32)
 
+    def windows(step, tall, near, far):
+        return call(
+            functools.partial(field_kernel, step=step),
+            ((slots, 2, width, width), (width, width)),
+            "",
+            (scan, tall, near, far),
+            scratch=((2, tall_rows + TILE, 2 * width),),
+        )
+
+    wins, win_weight = windows(0, tall, near, far)
     current = probe
     for step in range(steps):
+        last = step == steps - 1
         core, out_far, kept, sums = call(
             functools.partial(slots_kernel, step=step),
             (
@@ -462,25 +508,19 @@
                 (3 * half, width),
                 (2, tall_rows, width),
             ),
-            "a",
-            (scan, tall, near, far, current, amplitude[0, 0, step], tables),
+            "",
+            (scan, wins, win_weight, current, amplitude[0, 0, step], tables),
             flops=slots * 96 * width * width * width,
             moved=4 * MIB,
             scratch=(
                 (2, tall_rows + TILE, 2 * width),
-                (2, tall_rows + TILE, 2 * width),
                 (3, width, width),
                 (slots, 2, width, width),
-                (slots, 2, width, width),
             ),
-            more=(pltpu.SMEM(scan.shape, jnp.int32), pltpu.SemaphoreType.DMA(())),
             limit=24,
         )
         core = swap(core, "col", 1)
         out_far = swap_far(out_far)
-        last = step == steps - 1
-        first_step, second_step, *others, last_step = chip_steps()
-        part = add_step(kept + core[: 3 * half], first_step)
         (weight,) = call(
             functools.partial(weight_kernel, step=step, slots=slots),
             ((tall_rows, width),),
@@ -488,8 +528,7 @@
             (metas, current),
             scratch=((tall_rows + 2 * width + TILE, width),),
         )
-        part, weight = after(part, weight)
-        part = add_step(part, second_step)
+        part = kept + core[: 3 * half]
         if last:
             middle, sent_1, sent_2 = call(
                 last_fold_kernel,
@@ -497,6 +536,17 @@
                 "",
                 (sums, core, out_far),
             )
+            got_1, got_2 = swap(sent_1, "row", 1), swap_rows(sent_2)
+            (tile,) = call(
+                last_kernel,
+                ((2, side, side),),
+                "",
+                (tall, middle, got_1, got_2, weight),
+            )
+            part = add_plane(part, weight)
+            for other_step in chip_steps()[-chain_steps() : -1]:
+                part = add_step(part, other_step)
+            part = add_step(part, chip_steps()[-1])
         else:
             sent_1, sent_2 = call(
                 fold_kernel,
@@ -504,36 +554,25 @@
                 "",
                 (sums, core, out_far),
             )
-        got_1, got_2 = swap(sent_1, "row", 1), swap_rows(sent_2)
-        for other_step in others:
-            part = add_step(part, other_step)
-        if last:
-            (tile,) = call(
-                last_kernel,
-                ((2, side, side),),
-                "",
-                (tall, middle, got_1, got_2, weight),
-            )
-            part = add_step(part, last_step)
-        else:
+            got_1, got_2 = swap(sent_1, "row", 1), swap_rows(sent_2)
+            part = add_plane(part, weight)
+            for other_step in chip_steps()[-chain_steps() : -1]:
+                part = add_step(part, other_step)
             tall, near, far = call(
                 update_kernel,
                 ((2, tall_rows, side), (tall_rows, width), (tall_rows, width)),
                 "",
-                (tall, sent_1, sent_2, got_1, got_2, weight),
+                (tall, sent_1, sent_2, got_1, got_2, weight, part[:TILE]),
             )
+            near = swap(near, "col", 1)
             far_1, far_2 = swap_far(far[: tall_rows // 2]), swap_far(far[tall_rows // 2 :])
-            part = add_step(part, last_step)
-            part, far_1, far_2 = after(part, far_1, far_2)
+            part = add_step(part, chip_steps()[-1])
             far = jnp.concatenate([far_1, far_2], 0)
+            wins, win_weight = windows(step + 1, tall, near, far)
         mine = lax.dynamic_slice_in_dim(current, odd * half, half, 1)
         part = part.reshape(3, half, width)
         mine = mine + part[:2] / (part[2] + EPS)[None]
-        if last:
-            other = swap(mine, "col", 1)
-        else:
-            near = swap(jnp.concatenate([near, mine.reshape(2 * half, width)], 0), "col", 1)
-            other = near[tall_rows:].reshape(2, half, width)
+        other = swap(mine, "col", 1)
         low = jnp.where(odd == 0, mine, other)
         high = jnp.where(odd == 0, other, mine)
         current = jnp.concatenate([low, high], 1)

time: 72.7 us -> 68.4 us (0.941)
  waiting for transfers between devices: 29.9 us -> 25.4 us
  Pallas kernels: 11.9 us -> 10.6 us
  starting transfers between devices: 27 us -> 28.1 us
    ppermute x16 -> x17, waiting for transfers between devices: 23.8 us -> 17.8 us  [swap(): lax.ppermute(value, axis, [(i, i ^ bit) for i in range(lax.axis_size(axis...]
    ppermute x0 -> x2, waiting for transfers between devices: none -> 2.62 us  [swap_both(): return lax.ppermute(value, AXES, pairs)]
    ppermute x0 -> x2, starting transfers between devices: none -> 2.38 us  [swap_both(): return lax.ppermute(value, AXES, pairs)]
    pallas_call x10 -> x12, Pallas kernels: 11.9 us -> 10.6 us  [call(): pl.pallas_call(kernel, out_shape=tuple((jax.ShapeDtypeStruct(shape, jnp.f...]
    ppermute x5, waiting for transfers between devices: 6.11 us -> 5.02 us  [swap_far(): return lax.ppermute(value, AXES, pairs)]
    ppermute x16 -> x17, starting transfers between devices: 19.1 us -> 18.4 us  [swap(): lax.ppermute(value, axis, [(i, i ^ bit) for i in range(lax.axis_size(axis...]
  transfers between devices with their start and end apart: 24 -> 27, of which waited for: 17 -> 17; matrix products, arithmetic and copies ran while one was open for 3% -> 3% of each run, Pallas kernels for 6% -> 6%
where the time goes in v5:
time: 68.4 us; the launch traced here: 68.2 us
  starting transfers between devices  28.1 us (41%)
  waiting for transfers between devices  25.4 us (37%)
  Pallas kernels  10.6 us (15%)
  local copies, waits for them, and re-layouts  2.11 us (3%)
  between operations  1.01 us (1%)
  other arithmetic  0.93 us (1%)
    ppermute x17, starting transfers between devices, swap(): lax.ppermute(value, axis, [(i, i ^ bit) for i in range(lax.axis_size(axis...  18.4 us
    ppermute x17, waiting for transfers between devices, swap(): lax.ppermute(value, axis, [(i, i ^ bit) for i in range(lax.axis_size(axis...  17.8 us
    pallas_call x12, Pallas kernels, call(): pl.pallas_call(kernel, out_shape=tuple((jax.ShapeDtypeStruct(shape, jnp.f...  10.6 us
    ppermute x5, starting transfers between devices, swap_far(): return lax.ppermute(value, AXES, pairs)  7.32 us
    ppermute x5, waiting for transfers between devices, swap_far(): return lax.ppermute(value, AXES, pairs)  5.02 us
    ppermute x2, waiting for transfers between devices, swap_both(): return lax.ppermute(value, AXES, pairs)  2.62 us
    ppermute x2, starting transfers between devices, swap_both(): return lax.ppermute(value, AXES, pairs)  2.38 us
  transfers between devices with their start and end apart: 27, of which 17 were waited for; matrix products, arithmetic and copies ran while one was open for 3% of the time, Pallas kernels for 6%

profile of v5, /device:TPU:0, one launch (start us, length us, event | category | flops | bytes accessed | tf_op | source)
XLA Modules:
  0.0 68.2 jit_solution(4270588097055104722)
XLA Ops:
  0.6 1.5 %shard_map.77 = (f32[136,128]{1,0:T(8,128)}, f32[136,128]{1,0:T(8,128)}, f32[8,128]{1,0:T(8,128)}) custom-call(f32[2,128,128]{2,1,0:T(8,128)} %tile.3, s32[2,2,4]{2,1,0:T(2,128)} %bitcast.32, s32[1,2]{1,0:T(1,128)} %bitcast.33), custom_call_target="tpu_custom_call" | custom-call | flops 1000000 | bytes 1048576 | tf_op jit(solution)/shard_map/pallas_call | solution.py:368
  2.2 3.0 %collective-permute-start = (f32[136,128]{1,0:T(8,128)}, f32[136,128]{1,0:T(8,128)S(1)}, u32[]{:S(2)}, u32[]{:S(2)}) collective-permute-start(f32[136,128]{1,0:T(8,128)} %get-tuple-element.31), channel_id=1, source_target_pairs={{0,4},{4,0},{8,12},{12,8},{16,20},{20,16},{24,28},{28,24},{1,5},{5... | collective-permute-start | bytes 208904 | tf_op jit(solution)/shard_map/ppermute | solution.py:380
  5.2 0.0 collective-permute-start.1
  5.2 1.1 %slice_bitcast_fusion = (f32[4,128,128]{2,1,0:T(8,128)S(1)}, f32[4,128,128]{2,1,0:T(8,128)S(1)}) fusion(f32[1,1,2,4,128,128]{5,4,3,2,1,0:T(8,128)} %param.10), kind=kLoop, calls=%fused_computation | loop fusion | bytes 1048576 | tf_op jit(solution)/shard_map/squeeze | solution.py:512
  6.3 0.0 copy-start.3
  6.4 2.4 %collective-permute-done.first = f32[136,128]{1,0:T(8,128)S(1)} collective-permute-done((f32[136,128]{1,0:T(8,128)}, f32[136,128]{1,0:T(8,128)S(1)}, u32[]{:S(2)}, u32[]{:S(2)}) %collective-permute-start) | collective-permute-done | bytes 69664 | tf_op jit(solution)/shard_map/ppermute | solution.py:380
  8.8 0.0 collective-permute-done.1.second
  8.8 0.1 shard_map.78
  8.9 0.1 collective-permute-start.2
  9.0 2.4 %collective-permute-start.3 = (f32[280,128]{1,0:T(8,128)S(1)}, f32[280,128]{1,0:T(8,128)S(1)}, u32[]{:S(2)}, u32[]{:S(2)}) collective-permute-start(f32[280,128]{1,0:T(8,128)S(1)} %get-tuple-element.35), channel_id=1, source_target_pairs={{0,4},{1,2},{2,1},{3,7},{4,0},{5,6},{6,5},{7,3},{8,12},{9,10},{10,... | collective-permute-start | bytes 430088 | tf_op jit(solution)/shard_map/ppermute | solution.py:392
  11.4 0.1 copy.14
  11.5 0.0 collective-permute-done.2.near
  11.5 3.0 %collective-permute-done.3.far = f32[280,128]{1,0:T(8,128)S(1)} collective-permute-done((f32[280,128]{1,0:T(8,128)S(1)}, f32[280,128]{1,0:T(8,128)S(1)}, u32[]{:S(2)}, u32[]{:S(2)}) %collective-permute-start.3) | collective-permute-done | bytes 143392 | tf_op jit(solution)/shard_map/ppermute | solution.py:392
  14.5 0.5 shard_map.79
  15.0 0.4 copy-done.1
  15.4 2.1 %shard_map.80 = (f32[448,128]{1,0:T(8,128)S(1)}, f32[256,128]{1,0:T(8,128)S(1)}, f32[192,128]{1,0:T(8,128)S(1)}, f32[2,256,128]{2,1,0:T(8,128)S(1)}) custom-call(s32[6,4]{1,0:T(8,128)S(1)} %slice_convert_fusion.scan, f32[4,2,128,128]{3,2,1,0:T(8,128)S(1)} %get-tuple-element.36.wins, f32[128,128]{1,0:T(8,128)S(1)} %get-tuple-element.37.win_weight, ...), custom_call_target="tpu_custom_call" | custom-call | flops 805306368 | bytes 4194304 | tf_op jit(solution)/shard_map/pallas_call | solution.py:368
  17.5 0.1 collective-permute-start.4
  17.6 0.1 copy.16
  17.7 0.1 copy.17
  17.8 2.1 %collective-permute-start.5 = (f32[256,128]{1,0:T(8,128)S(1)}, f32[256,128]{1,0:T(8,128)S(1)}, u32[]{:S(2)}, u32[]{:S(2)}) collective-permute-start(f32[256,128]{1,0:T(8,128)S(1)} %get-tuple-element.40), channel_id=1, source_target_pairs={{0,4},{1,2},{2,1},{3,7},{4,0},{5,6},{6,5},{7,3},{8,12},{9,10},{10,... | collective-permute-start | bytes 393224 | tf_op jit(solution)/shard_map/ppermute | solution.py:392
  19.9 1.7 %collective-permute-start.10 = (f32[192,128]{1,0:T(8,128)S(1)}, f32[192,128]{1,0:T(8,128)S(1)}, u32[]{:S(2)}, u32[]{:S(2)}) collective-permute-start(f32[192,128]{1,0:T(8,128)S(1)} %slice_add_fusion.1), channel_id=1, source_target_pairs={{0,6},{1,7},{2,4},{3,5},{4,2},{5,3},{6,0},{7,1},{8,14},{9,15},{10,... | collective-permute-start | bytes 294920 | tf_op jit(solution)/shard_map/ppermute | solution.py:424
  21.6 1.0 %collective-permute-start.9 = (f32[192,128]{1,0:T(8,128)S(1)}, f32[192,128]{1,0:T(8,128)S(1)}, u32[]{:S(2)}, u32[]{:S(2)}) collective-permute-start(f32[192,128]{1,0:T(8,128)S(1)} %slice_add_fusion.1), channel_id=1, source_target_pairs={{0,2},{1,3},{2,0},{3,1},{4,6},{5,7},{6,4},{7,5},{8,10},{9,11},{10,... | collective-permute-start | bytes 294920 | tf_op jit(solution)/shard_map/ppermute | solution.py:380
  22.6 0.9 %collective-permute-start.8 = (f32[192,128]{1,0:T(8,128)S(1)}, f32[192,128]{1,0:T(8,128)S(1)}, u32[]{:S(2)}, u32[]{:S(2)}) collective-permute-start(f32[192,128]{1,0:T(8,128)S(1)} %slice_add_fusion.1), channel_id=1, source_target_pairs={{0,4},{4,0},{8,12},{12,8},{16,20},{20,16},{24,28},{28,24},{1,5},{5... | collective-permute-start | bytes 294920 | tf_op jit(solution)/shard_map/ppermute | solution.py:380
  23.5 0.1 copy.15
  23.6 0.1 convert_element_type.10.metas
  23.7 1.4 %shard_map.82.weight = f32[256,128]{1,0:T(8,128)S(1)} custom-call(s32[9,24]{1,0:T(8,128)S(1)} %convert_element_type.10.metas, f32[2,128,128]{2,1,0:T(8,128)S(1)} %copy-done.1), custom_call_target="tpu_custom_call" | custom-call | flops 1000000 | bytes 1048576 | tf_op jit(solution)/shard_map/pallas_call | solution.py:368
  25.1 0.1 shard_map.81
  25.2 1.2 %collective-permute-start.6 = (f32[2,128,128]{2,1,0:T(8,128)S(1)}, f32[2,128,128]{2,1,0:T(8,128)S(1)}, u32[]{:S(2)}, u32[]{:S(2)}) collective-permute-start(f32[2,128,128]{2,1,0:T(8,128)S(1)} %get-tuple-element.41.sent_1), channel_id=1, source_target_pairs={{0,4},{4,0},{8,12},{12,8},{16,20},{20,16},{24,28},{28,24},{1,5},{5... | collective-permute-start | bytes 393224 | tf_op jit(solution)/shard_map/ppermute | solution.py:380
  26.4 0.9 %collective-permute-done.10 = f32[192,128]{1,0:T(8,128)S(1)} collective-permute-done((f32[192,128]{1,0:T(8,128)S(1)}, f32[192,128]{1,0:T(8,128)S(1)}, u32[]{:S(2)}, u32[]{:S(2)}) %collective-permute-start.10) | collective-permute-done | bytes 98336 | tf_op jit(solution)/shard_map/ppermute | solution.py:424
  27.4 0.2 collective-permute-done.9
  27.5 1.0 %collective-permute-done.8 = f32[192,128]{1,0:T(8,128)S(1)} collective-permute-done((f32[192,128]{1,0:T(8,128)S(1)}, f32[192,128]{1,0:T(8,128)S(1)}, u32[]{:S(2)}, u32[]{:S(2)}) %collective-permute-start.8) | collective-permute-done | bytes 98336 | tf_op jit(solution)/shard_map/ppermute | solution.py:380
  28.6 1.8 %collective-permute-start.11 = (f32[192,128]{1,0:T(8,128)S(1)}, f32[192,128]{1,0:T(8,128)S(1)}, u32[]{:S(2)}, u32[]{:S(2)}) collective-permute-start(f32[192,128]{1,0:T(8,128)S(1)} %add_add_fusion.1), channel_id=1, source_target_pairs={{0,8},{4,12},{8,0},{12,4},{16,24},{20,28},{24,16},{28,20},{1,9},{5... | collective-permute-start | bytes 294920 | tf_op jit(solution)/shard_map/ppermute | solution.py:380
  30.5 3.4 %collective-permute-done.11 = f32[192,128]{1,0:T(8,128)S(1)} collective-permute-done((f32[192,128]{1,0:T(8,128)S(1)}, f32[192,128]{1,0:T(8,128)S(1)}, u32[]{:S(2)}, u32[]{:S(2)}) %collective-permute-start.11) | collective-permute-done | bytes 98336 | tf_op jit(solution)/shard_map/ppermute | solution.py:380
  33.9 3.3 %collective-permute-start.15 = (f32[192,128]{1,0:T(8,128)S(1)}, f32[192,128]{1,0:T(8,128)S(1)}, u32[]{:S(2)}, u32[]{:S(2)}) collective-permute-start(f32[192,128]{1,0:T(8,128)S(1)} %add.69), channel_id=1, source_target_pairs={{0,16},{4,20},{8,24},{12,28},{16,0},{20,4},{24,8},{28,12},{1,17},{... | collective-permute-start | bytes 294920 | tf_op jit(solution)/shard_map/ppermute | solution.py:380
  37.2 0.2 shard_map.83
  37.4 0.8 %collective-permute-start.13 = (f32[128,128]{1,0:T(8,128)S(1)}, f32[128,128]{1,0:T(8,128)S(1)}, u32[]{:S(2)}, u32[]{:S(2)}) collective-permute-start(f32[128,128]{1,0:T(8,128)S(1)} %get-tuple-element.66), channel_id=1, source_target_pairs={{0,4},{1,2},{2,1},{3,7},{4,0},{5,6},{6,5},{7,3},{8,12},{9,10},{10,... | collective-permute-start | bytes 196616 | tf_op jit(solution)/shard_map/ppermute | solution.py:392
  38.1 1.3 %collective-permute-start.14 = (f32[128,128]{1,0:T(8,128)S(1)}, f32[128,128]{1,0:T(8,128)S(1)}, u32[]{:S(2)}, u32[]{:S(2)}) collective-permute-start(f32[128,128]{1,0:T(8,128)S(1)} %get-tuple-element.67), channel_id=1, source_target_pairs={{0,4},{1,2},{2,1},{3,7},{4,0},{5,6},{6,5},{7,3},{8,12},{9,10},{10,... | collective-permute-start | bytes 196616 | tf_op jit(solution)/shard_map/ppermute | solution.py:392
  39.4 1.4 %collective-permute-done.15 = f32[192,128]{1,0:T(8,128)S(1)} collective-permute-done((f32[192,128]{1,0:T(8,128)S(1)}, f32[192,128]{1,0:T(8,128)S(1)}, u32[]{:S(2)}, u32[]{:S(2)}) %collective-permute-start.15) | collective-permute-done | bytes 98336 | tf_op jit(solution)/shard_map/ppermute | solution.py:380
  40.9 0.1 collective-permute-start.16
  41.0 0.7 collective-permute-done.13
  41.7 0.7 %collective-permute-done.14 = f32[128,128]{1,0:T(8,128)S(1)} collective-permute-done((f32[128,128]{1,0:T(8,128)S(1)}, f32[128,128]{1,0:T(8,128)S(1)}, u32[]{:S(2)}, u32[]{:S(2)}) %collective-permute-start.14) | collective-permute-done | bytes 65568 | tf_op jit(solution)/shard_map/ppermute | solution.py:392
  42.4 0.5 shard_map.84
  43.0 2.1 %shard_map.85 = (f32[448,128]{1,0:T(8,128)S(1)}, f32[256,128]{1,0:T(8,128)S(1)}, f32[192,128]{1,0:T(8,128)S(1)}, f32[2,256,128]{2,1,0:T(8,128)S(1)}) custom-call(s32[6,4]{1,0:T(8,128)S(1)} %slice_convert_fusion.scan, f32[4,2,128,128]{3,2,1,0:T(8,128)S(1)} %get-tuple-element.48.wins, f32[128,128]{1,0:T(8,128)S(1)} %get-tuple-element.49.win_weight, ...), custom_call_target="tpu_custom_call" | custom-call | flops 805306368 | bytes 4194304 | tf_op jit(solution)/shard_map/pallas_call | solution.py:368
  45.0 0.1 collective-permute-start.17
  45.2 1.4 %collective-permute-done.17.near = f32[448,128]{1,0:T(8,128)S(1)} collective-permute-done((f32[448,128]{1,0:T(8,128)S(1)}, f32[448,128]{1,0:T(8,128)S(1)}, u32[]{:S(2)}, u32[]{:S(2)}) %collective-permute-start.17) | collective-permute-done | bytes 229408 | tf_op jit(solution)/shard_map/ppermute | solution.py:380
  46.6 0.7 %collective-permute-start.23 = (f32[192,128]{1,0:T(8,128)S(1)}, f32[192,128]{1,0:T(8,128)S(1)}, u32[]{:S(2)}, u32[]{:S(2)}) collective-permute-start(f32[192,128]{1,0:T(8,128)S(1)} %slice_add_fusion), channel_id=1, source_target_pairs={{0,6},{1,7},{2,4},{3,5},{4,2},{5,3},{6,0},{7,1},{8,14},{9,15},{10,... | collective-permute-start | bytes 294920 | tf_op jit(solution)/shard_map/ppermute | solution.py:424
  47.3 2.1 %collective-permute-start.22 = (f32[192,128]{1,0:T(8,128)S(1)}, f32[192,128]{1,0:T(8,128)S(1)}, u32[]{:S(2)}, u32[]{:S(2)}) collective-permute-start(f32[192,128]{1,0:T(8,128)S(1)} %slice_add_fusion), channel_id=1, source_target_pairs={{0,2},{1,3},{2,0},{3,1},{4,6},{5,7},{6,4},{7,5},{8,10},{9,11},{10,... | collective-permute-start | bytes 294920 | tf_op jit(solution)/shard_map/ppermute | solution.py:380
  49.4 0.7 %collective-permute-start.21 = (f32[192,128]{1,0:T(8,128)S(1)}, f32[192,128]{1,0:T(8,128)S(1)}, u32[]{:S(2)}, u32[]{:S(2)}) collective-permute-start(f32[192,128]{1,0:T(8,128)S(1)} %slice_add_fusion), channel_id=1, source_target_pairs={{0,4},{4,0},{8,12},{12,8},{16,20},{20,16},{24,28},{28,24},{1,5},{5... | collective-permute-start | bytes 294920 | tf_op jit(solution)/shard_map/ppermute | solution.py:380
  50.2 1.4 %shard_map.87.weight = f32[256,128]{1,0:T(8,128)S(1)} custom-call(s32[9,24]{1,0:T(8,128)S(1)} %convert_element_type.10.metas, f32[2,128,128]{2,1,0:T(8,128)S(1)} %pad_maximum_fusion.probe), custom_call_target="tpu_custom_call" | custom-call | flops 1000000 | bytes 1048576 | tf_op jit(solution)/shard_map/pallas_call | solution.py:368
  51.5 1.7 %collective-permute-done.23 = f32[192,128]{1,0:T(8,128)S(1)} collective-permute-done((f32[192,128]{1,0:T(8,128)S(1)}, f32[192,128]{1,0:T(8,128)S(1)}, u32[]{:S(2)}, u32[]{:S(2)}) %collective-permute-start.23) | collective-permute-done | bytes 98336 | tf_op jit(solution)/shard_map/ppermute | solution.py:424
  53.2 1.1 %collective-permute-done.22 = f32[192,128]{1,0:T(8,128)S(1)} collective-permute-done((f32[192,128]{1,0:T(8,128)S(1)}, f32[192,128]{1,0:T(8,128)S(1)}, u32[]{:S(2)}, u32[]{:S(2)}) %collective-permute-start.22) | collective-permute-done | bytes 98336 | tf_op jit(solution)/shard_map/ppermute | solution.py:380
  54.4 0.2 collective-permute-done.21
  54.5 1.6 %collective-permute-start.24 = (f32[192,128]{1,0:T(8,128)S(1)}, f32[192,128]{1,0:T(8,128)S(1)}, u32[]{:S(2)}, u32[]{:S(2)}) collective-permute-start(f32[192,128]{1,0:T(8,128)S(1)} %add_add_fusion), channel_id=1, source_target_pairs={{0,8},{4,12},{8,0},{12,4},{16,24},{20,28},{24,16},{28,20},{1,9},{5... | collective-permute-start | bytes 294920 | tf_op jit(solution)/shard_map/ppermute | solution.py:380
  56.2 0.7 %collective-permute-start.18 = (f32[256,128]{1,0:T(8,128)S(1)}, f32[256,128]{1,0:T(8,128)S(1)}, u32[]{:S(2)}, u32[]{:S(2)}) collective-permute-start(f32[256,128]{1,0:T(8,128)S(1)} %get-tuple-element.52), channel_id=1, source_target_pairs={{0,4},{1,2},{2,1},{3,7},{4,0},{5,6},{6,5},{7,3},{8,12},{9,10},{10,... | collective-permute-start | bytes 393224 | tf_op jit(solution)/shard_map/ppermute | solution.py:392
  56.9 2.4 %collective-permute-done.24 = f32[192,128]{1,0:T(8,128)S(1)} collective-permute-done((f32[192,128]{1,0:T(8,128)S(1)}, f32[192,128]{1,0:T(8,128)S(1)}, u32[]{:S(2)}, u32[]{:S(2)}) %collective-permute-start.24) | collective-permute-done | bytes 98336 | tf_op jit(solution)/shard_map/ppermute | solution.py:380
  59.2 1.2 %collective-permute-start.25 = (f32[192,128]{1,0:T(8,128)S(1)}, f32[192,128]{1,0:T(8,128)S(1)}, u32[]{:S(2)}, u32[]{:S(2)}) collective-permute-start(f32[192,128]{1,0:T(8,128)S(1)} %add.78), channel_id=1, source_target_pairs={{0,16},{4,20},{8,24},{12,28},{16,0},{20,4},{24,8},{28,12},{1,17},{... | collective-permute-start | bytes 294920 | tf_op jit(solution)/shard_map/ppermute | solution.py:380
  60.5 0.7 collective-permute-done.18.far
  61.1 0.1 shard_map.86
  61.3 1.0 %collective-permute-start.19 = (f32[2,64,128]{2,1,0:T(8,128)S(1)}, f32[2,64,128]{2,1,0:T(8,128)S(1)}, u32[]{:S(2)}, u32[]{:S(2)}) collective-permute-start(f32[2,64,128]{2,1,0:T(8,128)S(1)} %get-tuple-element.54), channel_id=1, source_target_pairs={{0,4},{4,0},{8,12},{12,8},{16,20},{20,16},{24,28},{28,24},{1,5},{5... | collective-permute-start | bytes 196616 | tf_op jit(solution)/shard_map/ppermute | solution.py:380
  62.3 3.8 %collective-permute-done.25 = f32[192,128]{1,0:T(8,128)S(1)} collective-permute-done((f32[192,128]{1,0:T(8,128)S(1)}, f32[192,128]{1,0:T(8,128)S(1)}, u32[]{:S(2)}, u32[]{:S(2)}) %collective-permute-start.25) | collective-permute-done | bytes 98336 | tf_op jit(solution)/shard_map/ppermute | solution.py:380
  66.2 0.1 collective-permute-start.26
  66.3 0.7 %shard_map.88 = f32[2,128,128]{2,1,0:T(8,128)} custom-call(f32[2,256,128]{2,1,0:T(8,128)S(1)} %get-tuple-element.45.tall, f32[2,128,128]{2,1,0:T(8,128)S(1)} %get-tuple-element.53.middle, f32[2,64,128]{2,1,0:T(8,128)S(1)} %collective-permute-done.19.got_1, f32[2,64,128]{2,1,0:T(8,128)S(1)} %collective-permute-done.20.got_2, f32[256,128]{1,0:T(8,128)S(1)} %shard_map.87.weight), custom_call_target="tpu_custom_call" | custom-call | flops 1000000 | bytes 1048576 | tf_op jit(solution)/shard_map/pallas_call | solution.py:368
  67.0 0.5 collective-permute-done.26
  67.5 0.7 pad_maximum_fusion.2
  (44 shorter events, 0.3 us)
Async XLA Ops:
  2.2 6.6 %collective-permute-start = (f32[136,128]{1,0:T(8,128)}, f32[136,128]{1,0:T(8,128)S(1)}, u32[]{:S(2)}, u32[]{:S(2)}) collective-permute-start(f32[136,128]{1,0:T(8,128)} %get-tuple-element.31), channel_id=1, source_target_pairs={{0,4},{4,0},{8,12},{12,8},{16,20},{20,16},{24,28},{28,24},{1,5},{5... | collective-permute-start | bytes 208904 | tf_op jit(solution)/shard_map/ppermute | solution.py:380
  5.2 3.6 %collective-permute-start.1 = (f32[136,128]{1,0:T(8,128)}, f32[136,128]{1,0:T(8,128)S(1)}, u32[]{:S(2)}, u32[]{:S(2)}) collective-permute-start(f32[136,128]{1,0:T(8,128)} %get-tuple-element.32), channel_id=1, source_target_pairs={{0,1},{1,0},{2,3},{3,2},{4,8},{5,9},{6,10},{7,11},{8,4},{9,5},{10,... | collective-permute-start | bytes 208904 | tf_op jit(solution)/shard_map/ppermute | solution.py:404
  5.2 1.1 %copy-start.2 = (f32[8,128]{1,0:T(8,128)S(1)}, f32[8,128]{1,0:T(8,128)}, u32[]{:S(2)}) copy-start(f32[8,128]{1,0:T(8,128)} %get-tuple-element.30.meta) | copy-start | bytes 12292
  5.2 3.5 %copy-start = (f32[2,128,128]{2,1,0:T(8,128)S(1)}, f32[2,128,128]{2,1,0:T(8,128)}, u32[]{:S(2)}) copy-start(f32[2,128,128]{2,1,0:T(8,128)} %tile.3) | copy-start | bytes 393220
  6.3 8.6 %copy-start.3 = (bf16[4,256,256]{2,1,0:T(8,128)(2,1)S(1)}, bf16[4,256,256]{2,1,0:T(8,128)(2,1)}, u32[]{:S(2)}) copy-start(bf16[4,256,256]{2,1,0:T(8,128)(2,1)} %constant.41.clone.tables) | copy-start | bytes 1572868
  8.9 2.6 %collective-permute-start.2 = (f32[280,128]{1,0:T(8,128)S(1)}, f32[280,128]{1,0:T(8,128)S(1)}, u32[]{:S(2)}, u32[]{:S(2)}) collective-permute-start(f32[280,128]{1,0:T(8,128)S(1)} %get-tuple-element.34), channel_id=1, source_target_pairs={{0,1},{1,0},{2,3},{3,2},{4,5},{5,4},{6,7},{7,6},{8,9},{9,8},{10,11... | collective-permute-start | bytes 430088 | tf_op jit(solution)/shard_map/ppermute | solution.py:380
  9.0 5.5 %collective-permute-start.3 = (f32[280,128]{1,0:T(8,128)S(1)}, f32[280,128]{1,0:T(8,128)S(1)}, u32[]{:S(2)}, u32[]{:S(2)}) collective-permute-start(f32[280,128]{1,0:T(8,128)S(1)} %get-tuple-element.35), channel_id=1, source_target_pairs={{0,4},{1,2},{2,1},{3,7},{4,0},{5,6},{6,5},{7,3},{8,12},{9,10},{10,... | collective-permute-start | bytes 430088 | tf_op jit(solution)/shard_map/ppermute | solution.py:392
  14.5 0.9 %copy-start.1 = (f32[2,128,128]{2,1,0:T(8,128)S(1)}, f32[2,128,128]{2,1,0:T(8,128)}, u32[]{:S(2)}) copy-start(f32[2,128,128]{2,1,0:T(8,128)} %probe.3) | copy-start | bytes 393220
  17.5 2.4 %collective-permute-start.4 = (f32[448,128]{1,0:T(8,128)S(1)}, f32[448,128]{1,0:T(8,128)S(1)}, u32[]{:S(2)}, u32[]{:S(2)}) collective-permute-start(f32[448,128]{1,0:T(8,128)S(1)} %get-tuple-element.39), channel_id=1, source_target_pairs={{0,1},{1,0},{2,3},{3,2},{4,5},{5,4},{6,7},{7,6},{8,9},{9,8},{10,11... | collective-permute-start | bytes 688136 | tf_op jit(solution)/shard_map/ppermute | solution.py:380
  17.8 7.3 %collective-permute-start.5 = (f32[256,128]{1,0:T(8,128)S(1)}, f32[256,128]{1,0:T(8,128)S(1)}, u32[]{:S(2)}, u32[]{:S(2)}) collective-permute-start(f32[256,128]{1,0:T(8,128)S(1)} %get-tuple-element.40), channel_id=1, source_target_pairs={{0,4},{1,2},{2,1},{3,7},{4,0},{5,6},{6,5},{7,3},{8,12},{9,10},{10,... | collective-permute-start | bytes 393224 | tf_op jit(solution)/shard_map/ppermute | solution.py:392
  19.9 7.5 %collective-permute-start.10 = (f32[192,128]{1,0:T(8,128)S(1)}, f32[192,128]{1,0:T(8,128)S(1)}, u32[]{:S(2)}, u32[]{:S(2)}) collective-permute-start(f32[192,128]{1,0:T(8,128)S(1)} %slice_add_fusion.1), channel_id=1, source_target_pairs={{0,6},{1,7},{2,4},{3,5},{4,2},{5,3},{6,0},{7,1},{8,14},{9,15},{10,... | collective-permute-start | bytes 294920 | tf_op jit(solution)/shard_map/ppermute | solution.py:424
  21.6 6.0 %collective-permute-start.9 = (f32[192,128]{1,0:T(8,128)S(1)}, f32[192,128]{1,0:T(8,128)S(1)}, u32[]{:S(2)}, u32[]{:S(2)}) collective-permute-start(f32[192,128]{1,0:T(8,128)S(1)} %slice_add_fusion.1), channel_id=1, source_target_pairs={{0,2},{1,3},{2,0},{3,1},{4,6},{5,7},{6,4},{7,5},{8,10},{9,11},{10,... | collective-permute-start | bytes 294920 | tf_op jit(solution)/shard_map/ppermute | solution.py:380
  22.6 6.0 %collective-permute-start.8 = (f32[192,128]{1,0:T(8,128)S(1)}, f32[192,128]{1,0:T(8,128)S(1)}, u32[]{:S(2)}, u32[]{:S(2)}) collective-permute-start(f32[192,128]{1,0:T(8,128)S(1)} %slice_add_fusion.1), channel_id=1, source_target_pairs={{0,4},{4,0},{8,12},{12,8},{16,20},{20,16},{24,28},{28,24},{1,5},{5... | collective-permute-start | bytes 294920 | tf_op jit(solution)/shard_map/ppermute | solution.py:380
  25.2 11.9 %collective-permute-start.6 = (f32[2,128,128]{2,1,0:T(8,128)S(1)}, f32[2,128,128]{2,1,0:T(8,128)S(1)}, u32[]{:S(2)}, u32[]{:S(2)}) collective-permute-start(f32[2,128,128]{2,1,0:T(8,128)S(1)} %get-tuple-element.41.sent_1), channel_id=1, source_target_pairs={{0,4},{4,0},{8,12},{12,8},{16,20},{20,16},{24,28},{28,24},{1,5},{5... | collective-permute-start | bytes 393224 | tf_op jit(solution)/shard_map/ppermute | solution.py:380
  26.4 10.7 %collective-permute-start.7 = (f32[2,128,128]{2,1,0:T(8,128)S(1)}, f32[2,128,128]{2,1,0:T(8,128)S(1)}, u32[]{:S(2)}, u32[]{:S(2)}) collective-permute-start(f32[2,128,128]{2,1,0:T(8,128)S(1)} %get-tuple-element.42.sent_2), channel_id=1, source_target_pairs={{0,1},{1,0},{2,3},{3,2},{4,8},{5,9},{6,10},{7,11},{8,4},{9,5},{10,... | collective-permute-start | bytes 393224 | tf_op jit(solution)/shard_map/ppermute | solution.py:404
  28.6 5.2 %collective-permute-start.11 = (f32[192,128]{1,0:T(8,128)S(1)}, f32[192,128]{1,0:T(8,128)S(1)}, u32[]{:S(2)}, u32[]{:S(2)}) collective-permute-start(f32[192,128]{1,0:T(8,128)S(1)} %add_add_fusion.1), channel_id=1, source_target_pairs={{0,8},{4,12},{8,0},{12,4},{16,24},{20,28},{24,16},{28,20},{1,9},{5... | collective-permute-start | bytes 294920 | tf_op jit(solution)/shard_map/ppermute | solution.py:380
  33.9 7.0 %collective-permute-start.15 = (f32[192,128]{1,0:T(8,128)S(1)}, f32[192,128]{1,0:T(8,128)S(1)}, u32[]{:S(2)}, u32[]{:S(2)}) collective-permute-start(f32[192,128]{1,0:T(8,128)S(1)} %add.69), channel_id=1, source_target_pairs={{0,16},{4,20},{8,24},{12,28},{16,0},{20,4},{24,8},{28,12},{1,17},{... | collective-permute-start | bytes 294920 | tf_op jit(solution)/shard_map/ppermute | solution.py:380
  37.4 4.3 %collective-permute-start.13 = (f32[128,128]{1,0:T(8,128)S(1)}, f32[128,128]{1,0:T(8,128)S(1)}, u32[]{:S(2)}, u32[]{:S(2)}) collective-permute-start(f32[128,128]{1,0:T(8,128)S(1)} %get-tuple-element.66), channel_id=1, source_target_pairs={{0,4},{1,2},{2,1},{3,7},{4,0},{5,6},{6,5},{7,3},{8,12},{9,10},{10,... | collective-permute-start | bytes 196616 | tf_op jit(solution)/shard_map/ppermute | solution.py:392
  38.1 4.3 %collective-permute-start.14 = (f32[128,128]{1,0:T(8,128)S(1)}, f32[128,128]{1,0:T(8,128)S(1)}, u32[]{:S(2)}, u32[]{:S(2)}) collective-permute-start(f32[128,128]{1,0:T(8,128)S(1)} %get-tuple-element.67), channel_id=1, source_target_pairs={{0,4},{1,2},{2,1},{3,7},{4,0},{5,6},{6,5},{7,3},{8,12},{9,10},{10,... | collective-permute-start | bytes 196616 | tf_op jit(solution)/shard_map/ppermute | solution.py:392
  39.4 3.0 %collective-permute-start.12 = (f32[256,128]{1,0:T(8,128)S(1)}, f32[256,128]{1,0:T(8,128)S(1)}, u32[]{:S(2)}, u32[]{:S(2)}) collective-permute-start(f32[256,128]{1,0:T(8,128)S(1)} %get-tuple-element.46), channel_id=1, source_target_pairs={{0,1},{1,0},{2,3},{3,2},{4,5},{5,4},{6,7},{7,6},{8,9},{9,8},{10,11... | collective-permute-start | bytes 393224 | tf_op jit(solution)/shard_map/ppermute | solution.py:380
  40.9 2.0 %collective-permute-start.16 = (f32[2,64,128]{2,1,0:T(8,128)S(1)}, f32[2,64,128]{2,1,0:T(8,128)S(1)}, u32[]{:S(2)}, u32[]{:S(2)}) collective-permute-start(f32[2,64,128]{2,1,0:T(8,128)S(1)} %divide_add_fusion), channel_id=1, source_target_pairs={{0,1},{1,0},{2,3},{3,2},{4,5},{5,4},{6,7},{7,6},{8,9},{9,8},{10,11... | collective-permute-start | bytes 196616 | tf_op jit(solution)/shard_map/ppermute | solution.py:380
  45.0 1.6 %collective-permute-start.17 = (f32[448,128]{1,0:T(8,128)S(1)}, f32[448,128]{1,0:T(8,128)S(1)}, u32[]{:S(2)}, u32[]{:S(2)}) collective-permute-start(f32[448,128]{1,0:T(8,128)S(1)} %get-tuple-element.51), channel_id=1, source_target_pairs={{0,1},{1,0},{2,3},{3,2},{4,5},{5,4},{6,7},{7,6},{8,9},{9,8},{10,11... | collective-permute-start | bytes 688136 | tf_op jit(solution)/shard_map/ppermute | solution.py:380
  46.6 6.6 %collective-permute-start.23 = (f32[192,128]{1,0:T(8,128)S(1)}, f32[192,128]{1,0:T(8,128)S(1)}, u32[]{:S(2)}, u32[]{:S(2)}) collective-permute-start(f32[192,128]{1,0:T(8,128)S(1)} %slice_add_fusion), channel_id=1, source_target_pairs={{0,6},{1,7},{2,4},{3,5},{4,2},{5,3},{6,0},{7,1},{8,14},{9,15},{10,... | collective-permute-start | bytes 294920 | tf_op jit(solution)/shard_map/ppermute | solution.py:424
  47.3 7.0 %collective-permute-start.22 = (f32[192,128]{1,0:T(8,128)S(1)}, f32[192,128]{1,0:T(8,128)S(1)}, u32[]{:S(2)}, u32[]{:S(2)}) collective-permute-start(f32[192,128]{1,0:T(8,128)S(1)} %slice_add_fusion), channel_id=1, source_target_pairs={{0,2},{1,3},{2,0},{3,1},{4,6},{5,7},{6,4},{7,5},{8,10},{9,11},{10,... | collective-permute-start | bytes 294920 | tf_op jit(solution)/shard_map/ppermute | solution.py:380
  49.4 5.1 %collective-permute-start.21 = (f32[192,128]{1,0:T(8,128)S(1)}, f32[192,128]{1,0:T(8,128)S(1)}, u32[]{:S(2)}, u32[]{:S(2)}) collective-permute-start(f32[192,128]{1,0:T(8,128)S(1)} %slice_add_fusion), channel_id=1, source_target_pairs={{0,4},{4,0},{8,12},{12,8},{16,20},{20,16},{24,28},{28,24},{1,5},{5... | collective-permute-start | bytes 294920 | tf_op jit(solution)/shard_map/ppermute | solution.py:380
  54.5 4.7 %collective-permute-start.24 = (f32[192,128]{1,0:T(8,128)S(1)}, f32[192,128]{1,0:T(8,128)S(1)}, u32[]{:S(2)}, u32[]{:S(2)}) collective-permute-start(f32[192,128]{1,0:T(8,128)S(1)} %add_add_fusion), channel_id=1, source_target_pairs={{0,8},{4,12},{8,0},{12,4},{16,24},{20,28},{24,16},{28,20},{1,9},{5... | collective-permute-start | bytes 294920 | tf_op jit(solution)/shard_map/ppermute | solution.py:380
  56.2 5.0 %collective-permute-start.18 = (f32[256,128]{1,0:T(8,128)S(1)}, f32[256,128]{1,0:T(8,128)S(1)}, u32[]{:S(2)}, u32[]{:S(2)}) collective-permute-start(f32[256,128]{1,0:T(8,128)S(1)} %get-tuple-element.52), channel_id=1, source_target_pairs={{0,4},{1,2},{2,1},{3,7},{4,0},{5,6},{6,5},{7,3},{8,12},{9,10},{10,... | collective-permute-start | bytes 393224 | tf_op jit(solution)/shard_map/ppermute | solution.py:392
  59.2 6.8 %collective-permute-start.25 = (f32[192,128]{1,0:T(8,128)S(1)}, f32[192,128]{1,0:T(8,128)S(1)}, u32[]{:S(2)}, u32[]{:S(2)}) collective-permute-start(f32[192,128]{1,0:T(8,128)S(1)} %add.78), channel_id=1, source_target_pairs={{0,16},{4,20},{8,24},{12,28},{16,0},{20,4},{24,8},{28,12},{1,17},{... | collective-permute-start | bytes 294920 | tf_op jit(solution)/shard_map/ppermute | solution.py:380
  61.3 5.0 %collective-permute-start.19 = (f32[2,64,128]{2,1,0:T(8,128)S(1)}, f32[2,64,128]{2,1,0:T(8,128)S(1)}, u32[]{:S(2)}, u32[]{:S(2)}) collective-permute-start(f32[2,64,128]{2,1,0:T(8,128)S(1)} %get-tuple-element.54), channel_id=1, source_target_pairs={{0,4},{4,0},{8,12},{12,8},{16,20},{20,16},{24,28},{28,24},{1,5},{5... | collective-permute-start | bytes 196616 | tf_op jit(solution)/shard_map/ppermute | solution.py:380
  62.3 4.0 %collective-permute-start.20 = (f32[2,64,128]{2,1,0:T(8,128)S(1)}, f32[2,64,128]{2,1,0:T(8,128)S(1)}, u32[]{:S(2)}, u32[]{:S(2)}) collective-permute-start(f32[2,64,128]{2,1,0:T(8,128)S(1)} %get-tuple-element.55), channel_id=1, source_target_pairs={{0,1},{1,0},{2,3},{3,2},{4,8},{5,9},{6,10},{7,11},{8,4},{9,5},{10,... | collective-permute-start | bytes 196616 | tf_op jit(solution)/shard_map/ppermute | solution.py:404
  66.2 1.3 %collective-permute-start.26 = (f32[2,64,128]{2,1,0:T(8,128)S(1)}, f32[2,64,128]{2,1,0:T(8,128)S(1)}, u32[]{:S(2)}, u32[]{:S(2)}) collective-permute-start(f32[2,64,128]{2,1,0:T(8,128)S(1)} %fusion.1), channel_id=1, source_target_pairs={{0,1},{1,0},{2,3},{3,2},{4,5},{5,4},{6,7},{7,6},{8,9},{9,8},{10,11... | collective-permute-start | bytes 196616 | tf_op jit(solution)/shard_map/ppermute | solution.py:380

commit v6 on v5

--- a/solution.py
+++ b/solution.py
@@ -21,13 +21,12 @@
     angle = (index[:, None] * index[None, :] % size) * (-2.0 * math.pi / size)
     cosine = np.cos(angle) / math.sqrt(size)
     sine = np.sin(angle) / math.sqrt(size)
-    full = np.block([[cosine, -sine], [sine, cosine]]).astype(np.float32)
-    flip = np.ascontiguousarray(full.T)
     tables = []
-    for table in (full, flip):
+    for table in (cosine.astype(np.float32), sine.astype(np.float32)):
         high = table.astype(jnp.bfloat16)
-        tables += [high, (table - high.astype(np.float32)).astype(jnp.bfloat16)]
-    return np.stack(tables)
+        low = (table - high.astype(np.float32)).astype(jnp.bfloat16)
+        tables += [high, low]
+    return np.stack(tables + [-tables[2], -tables[3]])
 
 
 def split(value):
@@ -136,6 +135,16 @@
         copy.wait()
 
 
+def early_kernel(tile, meta, first, far):
+    odd = Spot().odd
+    side = tile.shape[1]
+    for at, real, imag in ((0, first[:RIM], first[RIM : 2 * RIM]), (RIM, tile[0], tile[1])):
+        low, high = pack(real, imag)
+        far[at : at + low.shape[0]] = jnp.where(odd, high, low)
+    far[RIM + side : RIM + side + TILE] = first[2 * RIM :]
+    far[RIM + side + TILE :] = meta[...]
+
+
 def strips_kernel(tile, meta, first, second, tall, near, far):
     side = tile.shape[1]
     spot = Spot()
@@ -149,11 +158,12 @@
     low, high = pack(tall[0], tall[1])
     rows = low.shape[0]
     near[:rows] = jnp.where(odd, low, high)
-    far[:rows] = jnp.where(odd, high, low)
-    for out in (near, far):
-        out[rows : rows + TILE] = above[2 * RIM :]
-        out[rows + TILE : rows + 2 * TILE] = meta[...]
-        out[rows + 2 * TILE :] = below[2 * RIM :]
+    near[rows : rows + TILE] = above[2 * RIM :]
+    near[rows + TILE : rows + 2 * TILE] = meta[...]
+    near[rows + 2 * TILE :] = below[2 * RIM :]
+    out = jnp.where(odd, high, low)
+    far[:RIM] = jnp.where(odd_row, out[RIM + side :], out[:RIM])
+    far[RIM:] = jnp.where(odd_row, below[2 * RIM :], above[2 * RIM :])
 
 
 def window_place(starts, step, slot, width):
@@ -214,7 +224,14 @@
     slots = amps.shape[0]
     odd = spot.odd
     sums[...] = jnp.zeros_like(sums)
-    full_h, full_l, flip_h, flip_l = (tables[k] for k in range(4))
+    cos_h, cos_l, sin_h, sin_l, neg_h, neg_l = (tables[k] for k in range(6))
+
+    def square(left_up, right_up, left_down, right_down):
+        upper = jnp.concatenate([left_up, right_up], 1)
+        return jnp.concatenate([upper, jnp.concatenate([left_down, right_down], 1)], 0)
+
+    full_h, full_l = square(cos_h, neg_h, sin_h, cos_h), square(cos_l, neg_l, sin_l, cos_l)
+    flip_h, flip_l = square(cos_h, sin_h, neg_h, cos_h), square(cos_l, sin_l, neg_l, cos_l)
     pro_r, pro_i = probe[0], probe[1]
     columns = []
     for slot in range(slots):
@@ -348,10 +365,11 @@
     far[...] = jnp.where(odd, high, low)
 
 
-def last_kernel(tall, middle, got_1, got_2, weight, tile):
+def last_kernel(tall, middle, got_1, got_2, weight, mine, other, tile, probe):
     side = tile.shape[1]
-    spot = Spot()
-    odd_row = spot.odd_row
+    half = mine.shape[1]
+    spot = Spot()
+    odd, odd_row = spot.odd, spot.odd_row
     for part in range(2):
         above = jnp.where(odd_row, got_1[part], got_2[part])
         below = jnp.where(odd_row, got_2[part], got_1[part])
@@ -359,6 +377,8 @@
         below = jnp.where(spot.has_below, below, 0.0)
         num = middle[part] + jnp.concatenate([above, below], 0)
         tile[part] = tall[part, RIM : RIM + side] + num / (weight[RIM : RIM + side] + EPS)
+        probe[part, :half] = jnp.where(odd, other[part], mine[part])
+        probe[part, half:] = jnp.where(odd, mine[part], other[part])
 
 
 def call(kernel, shapes, places, operands, flops=1000000, moved=MIB, scratch=(), more=(), limit=16):
@@ -467,14 +487,34 @@
     )
     scan = meta[: 3 * steps, :slots].astype(jnp.int32)
     first, second = swap(first, "row", 1), swap_rows(second)
-    strip = (tall_rows + 3 * TILE, width)
-    tall, near, far = call(
+    (early,) = call(
+        early_kernel,
+        ((RIM + side + 2 * TILE, width),),
+        "",
+        (object_field, meta, first),
+    )
+    early = swap_far(early)
+    tall, near, late = call(
         strips_kernel,
-        ((2, tall_rows, side), strip, strip),
+        ((2, tall_rows, side), (tall_rows + 3 * TILE, width), (RIM + TILE, width)),
         "",
         (object_field, meta, first, second),
     )
-    near, far = swap(near, "col", 1), swap_far(far)
+    near, late = swap(near, "col", 1), swap_far(late)
+    turned = odd_row != 0
+    sides = early[:RIM], late[:RIM]
+    ends = early[RIM + side : RIM + side + TILE], late[RIM:]
+    far = jnp.concatenate(
+        [
+            jnp.where(turned, sides[0], sides[1]),
+            early[RIM : RIM + side],
+            jnp.where(turned, sides[1], sides[0]),
+            jnp.where(turned, ends[0], ends[1]),
+            early[RIM + side + TILE :],
+            jnp.where(turned, ends[1], ends[0]),
+        ],
+        0,
+    )
 
     def three(value):
         return value[tall_rows:].reshape(3, TILE, width)[:, : 3 * steps, :slots]
@@ -535,14 +575,9 @@
                 ((2, side, width), (2, RIM, width), (2, RIM, width)),
                 "",
                 (sums, core, out_far),
+                moved=16 * MIB,
             )
             got_1, got_2 = swap(sent_1, "row", 1), swap_rows(sent_2)
-            (tile,) = call(
-                last_kernel,
-                ((2, side, side),),
-                "",
-                (tall, middle, got_1, got_2, weight),
-            )
             part = add_plane(part, weight)
             for other_step in chip_steps()[-chain_steps() : -1]:
                 part = add_step(part, other_step)
@@ -573,10 +608,17 @@
         part = part.reshape(3, half, width)
         mine = mine + part[:2] / (part[2] + EPS)[None]
         other = swap(mine, "col", 1)
+        if last:
+            return call(
+                last_kernel,
+                ((2, side, side), (2, width, width)),
+                "",
+                (tall, middle, got_1, got_2, weight, mine, other),
+                moved=4 * MIB,
+            )
         low = jnp.where(odd == 0, mine, other)
         high = jnp.where(odd == 0, other, mine)
         current = jnp.concatenate([low, high], 1)
-    return (tile, current)
 
 
 def solution(mesh):

time: 68.4 us -> 68.1 us (level)
  waiting for transfers between devices: 25.4 us -> 29.3 us
  starting transfers between devices: 28.1 us -> 24.3 us
    ppermute x17, waiting for transfers between devices: 17.8 us -> 22.4 us  [swap(): lax.ppermute(value, axis, [(i, i ^ bit) for i in range(lax.axis_size(axis...]
    ppermute x17, starting transfers between devices: 18.4 us -> 16.8 us  [swap(): lax.ppermute(value, axis, [(i, i ^ bit) for i in range(lax.axis_size(axis...]
    ppermute x2, starting transfers between devices: 2.38 us -> 1.29 us  [swap_both(): return lax.ppermute(value, AXES, pairs)]
    ppermute x5 -> x6, starting transfers between devices: 7.32 us -> 6.23 us  [swap_far(): return lax.ppermute(value, AXES, pairs)]
    pallas_call x12 -> x13, Pallas kernels: 10.6 us -> 10.8 us  [call(): pl.pallas_call(kernel, out_shape=tuple((jax.ShapeDtypeStruct(shape, jnp.f...]
    ppermute x5 -> x6, waiting for transfers between devices: 5.02 us -> 4.96 us  [swap_far(): return lax.ppermute(value, AXES, pairs)]
  transfers between devices with their start and end apart: 27 -> 28, of which waited for: 17 -> 18; matrix products, arithmetic and copies ran while one was open for 3% -> 3% of each run, Pallas kernels for 6% -> 6%
where the time goes in v6:
time: 68.1 us; the launch traced here: 67.9 us
  waiting for transfers between devices  29.3 us (43%)
  starting transfers between devices  24.3 us (36%)
  Pallas kernels  10.8 us (16%)
  local copies, waits for them, and re-layouts  2.19 us (3%)
  between operations  1.04 us (2%)
    ppermute x17, waiting for transfers between devices, swap(): lax.ppermute(value, axis, [(i, i ^ bit) for i in range(lax.axis_size(axis...  22.4 us
    ppermute x17, starting transfers between devices, swap(): lax.ppermute(value, axis, [(i, i ^ bit) for i in range(lax.axis_size(axis...  16.8 us
    pallas_call x13, Pallas kernels, call(): pl.pallas_call(kernel, out_shape=tuple((jax.ShapeDtypeStruct(shape, jnp.f...  10.8 us
    ppermute x6, starting transfers between devices, swap_far(): return lax.ppermute(value, AXES, pairs)  6.23 us
    ppermute x6, waiting for transfers between devices, swap_far(): return lax.ppermute(value, AXES, pairs)  4.96 us
    ppermute x2, waiting for transfers between devices, swap_both(): return lax.ppermute(value, AXES, pairs)  1.96 us
  transfers between devices with their start and end apart: 28, of which 18 were waited for; matrix products, arithmetic and copies ran while one was open for 3% of the time, Pallas kernels for 6%

profile of v6, /device:TPU:0, one launch (start us, length us, event | category | flops | bytes accessed | tf_op | source)
XLA Modules:
  0.0 67.9 jit_solution(1483591632999775802)
XLA Ops:
  0.6 1.5 %shard_map.77 = (f32[136,128]{1,0:T(8,128)}, f32[136,128]{1,0:T(8,128)}, f32[8,128]{1,0:T(8,128)}) custom-call(f32[2,128,128]{2,1,0:T(8,128)} %tile.5, s32[2,2,4]{2,1,0:T(2,128)} %bitcast.32, s32[1,2]{1,0:T(1,128)} %bitcast.33), custom_call_target="tpu_custom_call" | custom-call | flops 1000000 | bytes 1048576 | tf_op jit(solution)/shard_map/pallas_call | solution.py:388
  2.2 3.0 %collective-permute-start = (f32[136,128]{1,0:T(8,128)}, f32[136,128]{1,0:T(8,128)S(1)}, u32[]{:S(2)}, u32[]{:S(2)}) collective-permute-start(f32[136,128]{1,0:T(8,128)} %get-tuple-element.31), channel_id=1, source_target_pairs={{0,4},{4,0},{8,12},{12,8},{16,20},{20,16},{24,28},{28,24},{1,5},{5... | collective-permute-start | bytes 208904 | tf_op jit(solution)/shard_map/ppermute | solution.py:400
  5.2 1.1 %slice_bitcast_fusion = (f32[4,128,128]{2,1,0:T(8,128)S(1)}, f32[4,128,128]{2,1,0:T(8,128)S(1)}) fusion(f32[1,1,2,4,128,128]{5,4,3,2,1,0:T(8,128)} %param.10), kind=kLoop, calls=%fused_computation | loop fusion | bytes 1048576 | tf_op jit(solution)/shard_map/squeeze | solution.py:552
  6.4 2.4 %collective-permute-done.first = f32[136,128]{1,0:T(8,128)S(1)} collective-permute-done((f32[136,128]{1,0:T(8,128)}, f32[136,128]{1,0:T(8,128)S(1)}, u32[]{:S(2)}, u32[]{:S(2)}) %collective-permute-start) | collective-permute-done | bytes 69664 | tf_op jit(solution)/shard_map/ppermute | solution.py:400
  8.8 0.1 shard_map.79
  8.9 2.4 %collective-permute-start.3 = (f32[208,128]{1,0:T(8,128)S(1)}, f32[208,128]{1,0:T(8,128)S(1)}, u32[]{:S(2)}, u32[]{:S(2)}) collective-permute-start(f32[208,128]{1,0:T(8,128)S(1)} %shard_map.79), channel_id=1, source_target_pairs={{0,4},{1,2},{2,1},{3,7},{4,0},{5,6},{6,5},{7,3},{8,12},{9,10},{10,... | collective-permute-start | bytes 319496 | tf_op jit(solution)/shard_map/ppermute | solution.py:412
  11.3 0.0 collective-permute-done.1.second
  11.3 0.1 shard_map.78
  11.4 0.1 collective-permute-start.4
  11.6 0.1 copy.14
  11.7 0.0 collective-permute-start.2
  11.7 3.8 %collective-permute-done.4 = f32[72,128]{1,0:T(8,128)S(1)} collective-permute-done((f32[72,128]{1,0:T(8,128)S(1)}, f32[72,128]{1,0:T(8,128)S(1)}, u32[]{:S(2)}, u32[]{:S(2)}) %collective-permute-start.4) | collective-permute-done | bytes 36896 | tf_op jit(solution)/shard_map/ppermute | solution.py:412
  15.6 0.1 copy.17
  15.7 0.5 shard_map.80
  16.2 0.4 copy-done.1
  16.6 0.1 copy-done.3
  16.7 2.0 %shard_map.81 = (f32[448,128]{1,0:T(8,128)S(1)}, f32[256,128]{1,0:T(8,128)S(1)}, f32[192,128]{1,0:T(8,128)S(1)}, f32[2,256,128]{2,1,0:T(8,128)S(1)}) custom-call(s32[6,4]{1,0:T(8,128)S(1)} %slice_convert_fusion.scan, f32[4,2,128,128]{3,2,1,0:T(8,128)S(1)} %get-tuple-element.36.wins, f32[128,128]{1,0:T(8,128)S(1)} %get-tuple-element.37.win_weight, ...), custom_call_target="tpu_custom_call" | custom-call | flops 805306368 | bytes 4194304 | tf_op jit(solution)/shard_map/pallas_call | solution.py:388
  18.7 0.1 collective-permute-start.5
  18.8 0.1 copy.16
  18.9 0.9 %collective-permute-start.6 = (f32[256,128]{1,0:T(8,128)S(1)}, f32[256,128]{1,0:T(8,128)S(1)}, u32[]{:S(2)}, u32[]{:S(2)}) collective-permute-start(f32[256,128]{1,0:T(8,128)S(1)} %get-tuple-element.40), channel_id=1, source_target_pairs={{0,4},{1,2},{2,1},{3,7},{4,0},{5,6},{6,5},{7,3},{8,12},{9,10},{10,... | collective-permute-start | bytes 393224 | tf_op jit(solution)/shard_map/ppermute | solution.py:412
  19.8 0.4 collective-permute-done.5.near
  20.3 1.2 %collective-permute-start.11 = (f32[192,128]{1,0:T(8,128)S(1)}, f32[192,128]{1,0:T(8,128)S(1)}, u32[]{:S(2)}, u32[]{:S(2)}) collective-permute-start(f32[192,128]{1,0:T(8,128)S(1)} %slice_add_fusion.1), channel_id=1, source_target_pairs={{0,6},{1,7},{2,4},{3,5},{4,2},{5,3},{6,0},{7,1},{8,14},{9,15},{10,... | collective-permute-start | bytes 294920 | tf_op jit(solution)/shard_map/ppermute | solution.py:444
  21.5 1.2 %collective-permute-start.10 = (f32[192,128]{1,0:T(8,128)S(1)}, f32[192,128]{1,0:T(8,128)S(1)}, u32[]{:S(2)}, u32[]{:S(2)}) collective-permute-start(f32[192,128]{1,0:T(8,128)S(1)} %slice_add_fusion.1), channel_id=1, source_target_pairs={{0,2},{1,3},{2,0},{3,1},{4,6},{5,7},{6,4},{7,5},{8,10},{9,11},{10,... | collective-permute-start | bytes 294920 | tf_op jit(solution)/shard_map/ppermute | solution.py:400
  22.7 1.1 %collective-permute-start.9 = (f32[192,128]{1,0:T(8,128)S(1)}, f32[192,128]{1,0:T(8,128)S(1)}, u32[]{:S(2)}, u32[]{:S(2)}) collective-permute-start(f32[192,128]{1,0:T(8,128)S(1)} %slice_add_fusion.1), channel_id=1, source_target_pairs={{0,4},{4,0},{8,12},{12,8},{16,20},{20,16},{24,28},{28,24},{1,5},{5... | collective-permute-start | bytes 294920 | tf_op jit(solution)/shard_map/ppermute | solution.py:400
  23.9 0.1 copy.15
  24.0 0.1 convert_element_type.10.metas
  24.1 1.4 %shard_map.83.weight = f32[256,128]{1,0:T(8,128)S(1)} custom-call(s32[9,24]{1,0:T(8,128)S(1)} %convert_element_type.10.metas, f32[2,128,128]{2,1,0:T(8,128)S(1)} %copy-done.1), custom_call_target="tpu_custom_call" | custom-call | flops 1000000 | bytes 1048576 | tf_op jit(solution)/shard_map/pallas_call | solution.py:388
  25.5 0.1 shard_map.82
  25.6 1.0 %collective-permute-start.7 = (f32[2,128,128]{2,1,0:T(8,128)S(1)}, f32[2,128,128]{2,1,0:T(8,128)S(1)}, u32[]{:S(2)}, u32[]{:S(2)}) collective-permute-start(f32[2,128,128]{2,1,0:T(8,128)S(1)} %get-tuple-element.41.sent_1), channel_id=1, source_target_pairs={{0,4},{4,0},{8,12},{12,8},{16,20},{20,16},{24,28},{28,24},{1,5},{5... | collective-permute-start | bytes 393224 | tf_op jit(solution)/shard_map/ppermute | solution.py:400
  26.6 0.3 collective-permute-done.11
  26.9 1.3 %collective-permute-done.10 = f32[192,128]{1,0:T(8,128)S(1)} collective-permute-done((f32[192,128]{1,0:T(8,128)S(1)}, f32[192,128]{1,0:T(8,128)S(1)}, u32[]{:S(2)}, u32[]{:S(2)}) %collective-permute-start.10) | collective-permute-done | bytes 98336 | tf_op jit(solution)/shard_map/ppermute | solution.py:400
  28.2 0.5 collective-permute-done.9
  28.7 1.0 %collective-permute-start.12 = (f32[192,128]{1,0:T(8,128)S(1)}, f32[192,128]{1,0:T(8,128)S(1)}, u32[]{:S(2)}, u32[]{:S(2)}) collective-permute-start(f32[192,128]{1,0:T(8,128)S(1)} %add_add_fusion.1), channel_id=1, source_target_pairs={{0,8},{4,12},{8,0},{12,4},{16,24},{20,28},{24,16},{28,20},{1,9},{5... | collective-permute-start | bytes 294920 | tf_op jit(solution)/shard_map/ppermute | solution.py:400
  29.7 4.5 %collective-permute-done.12 = f32[192,128]{1,0:T(8,128)S(1)} collective-permute-done((f32[192,128]{1,0:T(8,128)S(1)}, f32[192,128]{1,0:T(8,128)S(1)}, u32[]{:S(2)}, u32[]{:S(2)}) %collective-permute-start.12) | collective-permute-done | bytes 98336 | tf_op jit(solution)/shard_map/ppermute | solution.py:400
  34.2 2.0 %collective-permute-start.16 = (f32[192,128]{1,0:T(8,128)S(1)}, f32[192,128]{1,0:T(8,128)S(1)}, u32[]{:S(2)}, u32[]{:S(2)}) collective-permute-start(f32[192,128]{1,0:T(8,128)S(1)} %add.69), channel_id=1, source_target_pairs={{0,16},{4,20},{8,24},{12,28},{16,0},{20,4},{24,8},{28,12},{1,17},{... | collective-permute-start | bytes 294920 | tf_op jit(solution)/shard_map/ppermute | solution.py:400
  36.3 0.2 shard_map.84
  36.5 0.4 collective-permute-start.14
  36.9 1.7 %collective-permute-start.15 = (f32[128,128]{1,0:T(8,128)S(1)}, f32[128,128]{1,0:T(8,128)S(1)}, u32[]{:S(2)}, u32[]{:S(2)}) collective-permute-start(f32[128,128]{1,0:T(8,128)S(1)} %get-tuple-element.69), channel_id=1, source_target_pairs={{0,4},{1,2},{2,1},{3,7},{4,0},{5,6},{6,5},{7,3},{8,12},{9,10},{10,... | collective-permute-start | bytes 196616 | tf_op jit(solution)/shard_map/ppermute | solution.py:412
  38.6 2.0 %collective-permute-done.16 = f32[192,128]{1,0:T(8,128)S(1)} collective-permute-done((f32[192,128]{1,0:T(8,128)S(1)}, f32[192,128]{1,0:T(8,128)S(1)}, u32[]{:S(2)}, u32[]{:S(2)}) %collective-permute-start.16) | collective-permute-done | bytes 98336 | tf_op jit(solution)/shard_map/ppermute | solution.py:400
  40.6 0.1 collective-permute-start.17
  40.7 0.1 collective-permute-done.14
  40.8 0.7 %collective-permute-done.15 = f32[128,128]{1,0:T(8,128)S(1)} collective-permute-done((f32[128,128]{1,0:T(8,128)S(1)}, f32[128,128]{1,0:T(8,128)S(1)}, u32[]{:S(2)}, u32[]{:S(2)}) %collective-permute-start.15) | collective-permute-done | bytes 65568 | tf_op jit(solution)/shard_map/ppermute | solution.py:412
  41.5 0.5 shard_map.85
  42.0 2.1 %shard_map.86 = (f32[448,128]{1,0:T(8,128)S(1)}, f32[256,128]{1,0:T(8,128)S(1)}, f32[192,128]{1,0:T(8,128)S(1)}, f32[2,256,128]{2,1,0:T(8,128)S(1)}) custom-call(s32[6,4]{1,0:T(8,128)S(1)} %slice_convert_fusion.scan, f32[4,2,128,128]{3,2,1,0:T(8,128)S(1)} %get-tuple-element.48.wins, f32[128,128]{1,0:T(8,128)S(1)} %get-tuple-element.49.win_weight, ...), custom_call_target="tpu_custom_call" | custom-call | flops 805306368 | bytes 4194304 | tf_op jit(solution)/shard_map/pallas_call | solution.py:388
  44.1 0.2 collective-permute-start.18
  44.3 1.4 %collective-permute-done.18.near = f32[448,128]{1,0:T(8,128)S(1)} collective-permute-done((f32[448,128]{1,0:T(8,128)S(1)}, f32[448,128]{1,0:T(8,128)S(1)}, u32[]{:S(2)}, u32[]{:S(2)}) %collective-permute-start.18) | collective-permute-done | bytes 229408 | tf_op jit(solution)/shard_map/ppermute | solution.py:400
  45.7 0.1 collective-permute-start.24
  45.8 2.8 %collective-permute-start.23 = (f32[192,128]{1,0:T(8,128)S(1)}, f32[192,128]{1,0:T(8,128)S(1)}, u32[]{:S(2)}, u32[]{:S(2)}) collective-permute-start(f32[192,128]{1,0:T(8,128)S(1)} %slice_add_fusion), channel_id=1, source_target_pairs={{0,2},{1,3},{2,0},{3,1},{4,6},{5,7},{6,4},{7,5},{8,10},{9,11},{10,... | collective-permute-start | bytes 294920 | tf_op jit(solution)/shard_map/ppermute | solution.py:400
  48.5 0.7 %collective-permute-start.22 = (f32[192,128]{1,0:T(8,128)S(1)}, f32[192,128]{1,0:T(8,128)S(1)}, u32[]{:S(2)}, u32[]{:S(2)}) collective-permute-start(f32[192,128]{1,0:T(8,128)S(1)} %slice_add_fusion), channel_id=1, source_target_pairs={{0,4},{4,0},{8,12},{12,8},{16,20},{20,16},{24,28},{28,24},{1,5},{5... | collective-permute-start | bytes 294920 | tf_op jit(solution)/shard_map/ppermute | solution.py:400
  49.2 1.4 %shard_map.88.weight = f32[256,128]{1,0:T(8,128)S(1)} custom-call(s32[9,24]{1,0:T(8,128)S(1)} %convert_element_type.10.metas, f32[2,128,128]{2,1,0:T(8,128)S(1)} %pad_maximum_fusion.probe), custom_call_target="tpu_custom_call" | custom-call | flops 1000000 | bytes 1048576 | tf_op jit(solution)/shard_map/pallas_call | solution.py:388
  50.6 1.7 %collective-permute-done.24 = f32[192,128]{1,0:T(8,128)S(1)} collective-permute-done((f32[192,128]{1,0:T(8,128)S(1)}, f32[192,128]{1,0:T(8,128)S(1)}, u32[]{:S(2)}, u32[]{:S(2)}) %collective-permute-start.24) | collective-permute-done | bytes 98336 | tf_op jit(solution)/shard_map/ppermute | solution.py:444
  52.3 1.2 %collective-permute-done.23 = f32[192,128]{1,0:T(8,128)S(1)} collective-permute-done((f32[192,128]{1,0:T(8,128)S(1)}, f32[192,128]{1,0:T(8,128)S(1)}, u32[]{:S(2)}, u32[]{:S(2)}) %collective-permute-start.23) | collective-permute-done | bytes 98336 | tf_op jit(solution)/shard_map/ppermute | solution.py:400
  53.4 0.2 collective-permute-done.22
  53.6 1.4 %collective-permute-start.25 = (f32[192,128]{1,0:T(8,128)S(1)}, f32[192,128]{1,0:T(8,128)S(1)}, u32[]{:S(2)}, u32[]{:S(2)}) collective-permute-start(f32[192,128]{1,0:T(8,128)S(1)} %add_add_fusion), channel_id=1, source_target_pairs={{0,8},{4,12},{8,0},{12,4},{16,24},{20,28},{24,16},{28,20},{1,9},{5... | collective-permute-start | bytes 294920 | tf_op jit(solution)/shard_map/ppermute | solution.py:400
  55.0 0.7 %collective-permute-start.19 = (f32[256,128]{1,0:T(8,128)S(1)}, f32[256,128]{1,0:T(8,128)S(1)}, u32[]{:S(2)}, u32[]{:S(2)}) collective-permute-start(f32[256,128]{1,0:T(8,128)S(1)} %get-tuple-element.52), channel_id=1, source_target_pairs={{0,4},{1,2},{2,1},{3,7},{4,0},{5,6},{6,5},{7,3},{8,12},{9,10},{10,... | collective-permute-start | bytes 393224 | tf_op jit(solution)/shard_map/ppermute | solution.py:412
  55.7 2.6 %collective-permute-done.25 = f32[192,128]{1,0:T(8,128)S(1)} collective-permute-done((f32[192,128]{1,0:T(8,128)S(1)}, f32[192,128]{1,0:T(8,128)S(1)}, u32[]{:S(2)}, u32[]{:S(2)}) %collective-permute-start.25) | collective-permute-done | bytes 98336 | tf_op jit(solution)/shard_map/ppermute | solution.py:400
  58.3 1.3 %collective-permute-start.26 = (f32[192,128]{1,0:T(8,128)S(1)}, f32[192,128]{1,0:T(8,128)S(1)}, u32[]{:S(2)}, u32[]{:S(2)}) collective-permute-start(f32[192,128]{1,0:T(8,128)S(1)} %add.78), channel_id=1, source_target_pairs={{0,16},{4,20},{8,24},{12,28},{16,0},{20,4},{24,8},{28,12},{1,17},{... | collective-permute-start | bytes 294920 | tf_op jit(solution)/shard_map/ppermute | solution.py:400
  59.7 0.3 collective-permute-done.19.far
  60.0 0.1 shard_map.87
  60.1 0.8 %collective-permute-start.20 = (f32[2,64,128]{2,1,0:T(8,128)S(1)}, f32[2,64,128]{2,1,0:T(8,128)S(1)}, u32[]{:S(2)}, u32[]{:S(2)}) collective-permute-start(f32[2,64,128]{2,1,0:T(8,128)S(1)} %get-tuple-element.54), channel_id=1, source_target_pairs={{0,4},{4,0},{8,12},{12,8},{16,20},{20,16},{24,28},{28,24},{1,5},{5... | collective-permute-start | bytes 196616 | tf_op jit(solution)/shard_map/ppermute | solution.py:400
  60.9 4.8 %collective-permute-done.26 = f32[192,128]{1,0:T(8,128)S(1)} collective-permute-done((f32[192,128]{1,0:T(8,128)S(1)}, f32[192,128]{1,0:T(8,128)S(1)}, u32[]{:S(2)}, u32[]{:S(2)}) %collective-permute-start.26) | collective-permute-done | bytes 98336 | tf_op jit(solution)/shard_map/ppermute | solution.py:400
  65.8 0.1 collective-permute-start.27
  65.9 1.2 %collective-permute-done.27.other = f32[2,64,128]{2,1,0:T(8,128)S(1)} collective-permute-done((f32[2,64,128]{2,1,0:T(8,128)S(1)}, f32[2,64,128]{2,1,0:T(8,128)S(1)}, u32[]{:S(2)}, u32[]{:S(2)}) %collective-permute-start.27) | collective-permute-done | bytes 65568 | tf_op jit(solution)/shard_map/ppermute | solution.py:400
  67.2 0.7 %shard_map.89 = (f32[2,128,128]{2,1,0:T(8,128)}, f32[2,128,128]{2,1,0:T(8,128)}) custom-call(f32[2,256,128]{2,1,0:T(8,128)S(1)} %get-tuple-element.45.tall, f32[2,128,128]{2,1,0:T(8,128)S(1)} %get-tuple-element.53.middle, f32[2,64,128]{2,1,0:T(8,128)S(1)} %collective-permute-done.20.got_1, f32[2,64,128]{2,1,0:T(8,128)S(1)} %collective-permute-done.21.got_2, ...), custom_call_target="tpu_custom_call" | custom-call | flops 1000000 | bytes 4194304 | tf_op jit(solution)/shard_map/pallas_call | solution.py:388
  (51 shorter events, 0.4 us)
Async XLA Ops:
  2.2 6.6 %collective-permute-start = (f32[136,128]{1,0:T(8,128)}, f32[136,128]{1,0:T(8,128)S(1)}, u32[]{:S(2)}, u32[]{:S(2)}) collective-permute-start(f32[136,128]{1,0:T(8,128)} %get-tuple-element.31), channel_id=1, source_target_pairs={{0,4},{4,0},{8,12},{12,8},{16,20},{20,16},{24,28},{28,24},{1,5},{5... | collective-permute-start | bytes 208904 | tf_op jit(solution)/shard_map/ppermute | solution.py:400
  5.2 6.1 %collective-permute-start.1 = (f32[136,128]{1,0:T(8,128)}, f32[136,128]{1,0:T(8,128)S(1)}, u32[]{:S(2)}, u32[]{:S(2)}) collective-permute-start(f32[136,128]{1,0:T(8,128)} %get-tuple-element.32), channel_id=1, source_target_pairs={{0,1},{1,0},{2,3},{3,2},{4,8},{5,9},{6,10},{7,11},{8,4},{9,5},{10,... | collective-permute-start | bytes 208904 | tf_op jit(solution)/shard_map/ppermute | solution.py:424
  5.2 1.1 %copy-start.2 = (f32[8,128]{1,0:T(8,128)S(1)}, f32[8,128]{1,0:T(8,128)}, u32[]{:S(2)}) copy-start(f32[8,128]{1,0:T(8,128)} %get-tuple-element.30.meta) | copy-start | bytes 12292
  5.2 3.5 %copy-start = (f32[2,128,128]{2,1,0:T(8,128)S(1)}, f32[2,128,128]{2,1,0:T(8,128)}, u32[]{:S(2)}) copy-start(f32[2,128,128]{2,1,0:T(8,128)} %tile.5) | copy-start | bytes 393220
  8.9 6.6 %collective-permute-start.3 = (f32[208,128]{1,0:T(8,128)S(1)}, f32[208,128]{1,0:T(8,128)S(1)}, u32[]{:S(2)}, u32[]{:S(2)}) collective-permute-start(f32[208,128]{1,0:T(8,128)S(1)} %shard_map.79), channel_id=1, source_target_pairs={{0,4},{1,2},{2,1},{3,7},{4,0},{5,6},{6,5},{7,3},{8,12},{9,10},{10,... | collective-permute-start | bytes 319496 | tf_op jit(solution)/shard_map/ppermute | solution.py:412
  11.4 4.0 %collective-permute-start.4 = (f32[72,128]{1,0:T(8,128)S(1)}, f32[72,128]{1,0:T(8,128)S(1)}, u32[]{:S(2)}, u32[]{:S(2)}) collective-permute-start(f32[72,128]{1,0:T(8,128)S(1)} %get-tuple-element.35), channel_id=1, source_target_pairs={{0,4},{1,2},{2,1},{3,7},{4,0},{5,6},{6,5},{7,3},{8,12},{9,10},{10,... | collective-permute-start | bytes 110600 | tf_op jit(solution)/shard_map/ppermute | solution.py:412
  11.7 4.0 %collective-permute-start.2 = (f32[280,128]{1,0:T(8,128)S(1)}, f32[280,128]{1,0:T(8,128)S(1)}, u32[]{:S(2)}, u32[]{:S(2)}) collective-permute-start(f32[280,128]{1,0:T(8,128)S(1)} %get-tuple-element.34), channel_id=1, source_target_pairs={{0,1},{1,0},{2,3},{3,2},{4,5},{5,4},{6,7},{7,6},{8,9},{9,8},{10,11... | collective-permute-start | bytes 430088 | tf_op jit(solution)/shard_map/ppermute | solution.py:400
  15.7 0.9 %copy-start.1 = (f32[2,128,128]{2,1,0:T(8,128)S(1)}, f32[2,128,128]{2,1,0:T(8,128)}, u32[]{:S(2)}) copy-start(f32[2,128,128]{2,1,0:T(8,128)} %probe.3) | copy-start | bytes 393220
  15.7 1.0 %copy-start.3 = (bf16[6,128,128]{2,1,0:T(8,128)(2,1)S(1)}, bf16[6,128,128]{2,1,0:T(8,128)(2,1)}, u32[]{:S(2)}) copy-start(bf16[6,128,128]{2,1,0:T(8,128)(2,1)} %constant.41.clone.tables) | copy-start | bytes 589828
  18.7 1.6 %collective-permute-start.5 = (f32[448,128]{1,0:T(8,128)S(1)}, f32[448,128]{1,0:T(8,128)S(1)}, u32[]{:S(2)}, u32[]{:S(2)}) collective-permute-start(f32[448,128]{1,0:T(8,128)S(1)} %get-tuple-element.39), channel_id=1, source_target_pairs={{0,1},{1,0},{2,3},{3,2},{4,5},{5,4},{6,7},{7,6},{8,9},{9,8},{10,11... | collective-permute-start | bytes 688136 | tf_op jit(solution)/shard_map/ppermute | solution.py:400
  18.9 6.5 %collective-permute-start.6 = (f32[256,128]{1,0:T(8,128)S(1)}, f32[256,128]{1,0:T(8,128)S(1)}, u32[]{:S(2)}, u32[]{:S(2)}) collective-permute-start(f32[256,128]{1,0:T(8,128)S(1)} %get-tuple-element.40), channel_id=1, source_target_pairs={{0,4},{1,2},{2,1},{3,7},{4,0},{5,6},{6,5},{7,3},{8,12},{9,10},{10,... | collective-permute-start | bytes 393224 | tf_op jit(solution)/shard_map/ppermute | solution.py:412
  20.3 6.6 %collective-permute-start.11 = (f32[192,128]{1,0:T(8,128)S(1)}, f32[192,128]{1,0:T(8,128)S(1)}, u32[]{:S(2)}, u32[]{:S(2)}) collective-permute-start(f32[192,128]{1,0:T(8,128)S(1)} %slice_add_fusion.1), channel_id=1, source_target_pairs={{0,6},{1,7},{2,4},{3,5},{4,2},{5,3},{6,0},{7,1},{8,14},{9,15},{10,... | collective-permute-start | bytes 294920 | tf_op jit(solution)/shard_map/ppermute | solution.py:444
  21.5 6.7 %collective-permute-start.10 = (f32[192,128]{1,0:T(8,128)S(1)}, f32[192,128]{1,0:T(8,128)S(1)}, u32[]{:S(2)}, u32[]{:S(2)}) collective-permute-start(f32[192,128]{1,0:T(8,128)S(1)} %slice_add_fusion.1), channel_id=1, source_target_pairs={{0,2},{1,3},{2,0},{3,1},{4,6},{5,7},{6,4},{7,5},{8,10},{9,11},{10,... | collective-permute-start | bytes 294920 | tf_op jit(solution)/shard_map/ppermute | solution.py:400
  22.7 6.0 %collective-permute-start.9 = (f32[192,128]{1,0:T(8,128)S(1)}, f32[192,128]{1,0:T(8,128)S(1)}, u32[]{:S(2)}, u32[]{:S(2)}) collective-permute-start(f32[192,128]{1,0:T(8,128)S(1)} %slice_add_fusion.1), channel_id=1, source_target_pairs={{0,4},{4,0},{8,12},{12,8},{16,20},{20,16},{24,28},{28,24},{1,5},{5... | collective-permute-start | bytes 294920 | tf_op jit(solution)/shard_map/ppermute | solution.py:400
  25.6 10.7 %collective-permute-start.7 = (f32[2,128,128]{2,1,0:T(8,128)S(1)}, f32[2,128,128]{2,1,0:T(8,128)S(1)}, u32[]{:S(2)}, u32[]{:S(2)}) collective-permute-start(f32[2,128,128]{2,1,0:T(8,128)S(1)} %get-tuple-element.41.sent_1), channel_id=1, source_target_pairs={{0,4},{4,0},{8,12},{12,8},{16,20},{20,16},{24,28},{28,24},{1,5},{5... | collective-permute-start | bytes 393224 | tf_op jit(solution)/shard_map/ppermute | solution.py:400
  26.6 9.7 %collective-permute-start.8 = (f32[2,128,128]{2,1,0:T(8,128)S(1)}, f32[2,128,128]{2,1,0:T(8,128)S(1)}, u32[]{:S(2)}, u32[]{:S(2)}) collective-permute-start(f32[2,128,128]{2,1,0:T(8,128)S(1)} %get-tuple-element.42.sent_2), channel_id=1, source_target_pairs={{0,1},{1,0},{2,3},{3,2},{4,8},{5,9},{6,10},{7,11},{8,4},{9,5},{10,... | collective-permute-start | bytes 393224 | tf_op jit(solution)/shard_map/ppermute | solution.py:424
  28.7 5.5 %collective-permute-start.12 = (f32[192,128]{1,0:T(8,128)S(1)}, f32[192,128]{1,0:T(8,128)S(1)}, u32[]{:S(2)}, u32[]{:S(2)}) collective-permute-start(f32[192,128]{1,0:T(8,128)S(1)} %add_add_fusion.1), channel_id=1, source_target_pairs={{0,8},{4,12},{8,0},{12,4},{16,24},{20,28},{24,16},{28,20},{1,9},{5... | collective-permute-start | bytes 294920 | tf_op jit(solution)/shard_map/ppermute | solution.py:400
  34.2 6.3 %collective-permute-start.16 = (f32[192,128]{1,0:T(8,128)S(1)}, f32[192,128]{1,0:T(8,128)S(1)}, u32[]{:S(2)}, u32[]{:S(2)}) collective-permute-start(f32[192,128]{1,0:T(8,128)S(1)} %add.69), channel_id=1, source_target_pairs={{0,16},{4,20},{8,24},{12,28},{16,0},{20,4},{24,8},{28,12},{1,17},{... | collective-permute-start | bytes 294920 | tf_op jit(solution)/shard_map/ppermute | solution.py:400
  36.5 4.3 %collective-permute-start.14 = (f32[128,128]{1,0:T(8,128)S(1)}, f32[128,128]{1,0:T(8,128)S(1)}, u32[]{:S(2)}, u32[]{:S(2)}) collective-permute-start(f32[128,128]{1,0:T(8,128)S(1)} %get-tuple-element.68), channel_id=1, source_target_pairs={{0,4},{1,2},{2,1},{3,7},{4,0},{5,6},{6,5},{7,3},{8,12},{9,10},{10,... | collective-permute-start | bytes 196616 | tf_op jit(solution)/shard_map/ppermute | solution.py:412
  36.9 4.6 %collective-permute-start.15 = (f32[128,128]{1,0:T(8,128)S(1)}, f32[128,128]{1,0:T(8,128)S(1)}, u32[]{:S(2)}, u32[]{:S(2)}) collective-permute-start(f32[128,128]{1,0:T(8,128)S(1)} %get-tuple-element.69), channel_id=1, source_target_pairs={{0,4},{1,2},{2,1},{3,7},{4,0},{5,6},{6,5},{7,3},{8,12},{9,10},{10,... | collective-permute-start | bytes 196616 | tf_op jit(solution)/shard_map/ppermute | solution.py:412
  38.6 3.0 %collective-permute-start.13 = (f32[256,128]{1,0:T(8,128)S(1)}, f32[256,128]{1,0:T(8,128)S(1)}, u32[]{:S(2)}, u32[]{:S(2)}) collective-permute-start(f32[256,128]{1,0:T(8,128)S(1)} %get-tuple-element.46), channel_id=1, source_target_pairs={{0,1},{1,0},{2,3},{3,2},{4,5},{5,4},{6,7},{7,6},{8,9},{9,8},{10,11... | collective-permute-start | bytes 393224 | tf_op jit(solution)/shard_map/ppermute | solution.py:400
  40.6 1.4 %collective-permute-start.17 = (f32[2,64,128]{2,1,0:T(8,128)S(1)}, f32[2,64,128]{2,1,0:T(8,128)S(1)}, u32[]{:S(2)}, u32[]{:S(2)}) collective-permute-start(f32[2,64,128]{2,1,0:T(8,128)S(1)} %divide_add_fusion), channel_id=1, source_target_pairs={{0,1},{1,0},{2,3},{3,2},{4,5},{5,4},{6,7},{7,6},{8,9},{9,8},{10,11... | collective-permute-start | bytes 196616 | tf_op jit(solution)/shard_map/ppermute | solution.py:400
  44.1 1.6 %collective-permute-start.18 = (f32[448,128]{1,0:T(8,128)S(1)}, f32[448,128]{1,0:T(8,128)S(1)}, u32[]{:S(2)}, u32[]{:S(2)}) collective-permute-start(f32[448,128]{1,0:T(8,128)S(1)} %get-tuple-element.51), channel_id=1, source_target_pairs={{0,1},{1,0},{2,3},{3,2},{4,5},{5,4},{6,7},{7,6},{8,9},{9,8},{10,11... | collective-permute-start | bytes 688136 | tf_op jit(solution)/shard_map/ppermute | solution.py:400
  45.7 6.6 %collective-permute-start.24 = (f32[192,128]{1,0:T(8,128)S(1)}, f32[192,128]{1,0:T(8,128)S(1)}, u32[]{:S(2)}, u32[]{:S(2)}) collective-permute-start(f32[192,128]{1,0:T(8,128)S(1)} %slice_add_fusion), channel_id=1, source_target_pairs={{0,6},{1,7},{2,4},{3,5},{4,2},{5,3},{6,0},{7,1},{8,14},{9,15},{10,... | collective-permute-start | bytes 294920 | tf_op jit(solution)/shard_map/ppermute | solution.py:444
  45.8 7.7 %collective-permute-start.23 = (f32[192,128]{1,0:T(8,128)S(1)}, f32[192,128]{1,0:T(8,128)S(1)}, u32[]{:S(2)}, u32[]{:S(2)}) collective-permute-start(f32[192,128]{1,0:T(8,128)S(1)} %slice_add_fusion), channel_id=1, source_target_pairs={{0,2},{1,3},{2,0},{3,1},{4,6},{5,7},{6,4},{7,5},{8,10},{9,11},{10,... | collective-permute-start | bytes 294920 | tf_op jit(solution)/shard_map/ppermute | solution.py:400
  48.5 5.1 %collective-permute-start.22 = (f32[192,128]{1,0:T(8,128)S(1)}, f32[192,128]{1,0:T(8,128)S(1)}, u32[]{:S(2)}, u32[]{:S(2)}) collective-permute-start(f32[192,128]{1,0:T(8,128)S(1)} %slice_add_fusion), channel_id=1, source_target_pairs={{0,4},{4,0},{8,12},{12,8},{16,20},{20,16},{24,28},{28,24},{1,5},{5... | collective-permute-start | bytes 294920 | tf_op jit(solution)/shard_map/ppermute | solution.py:400
  53.6 4.7 %collective-permute-start.25 = (f32[192,128]{1,0:T(8,128)S(1)}, f32[192,128]{1,0:T(8,128)S(1)}, u32[]{:S(2)}, u32[]{:S(2)}) collective-permute-start(f32[192,128]{1,0:T(8,128)S(1)} %add_add_fusion), channel_id=1, source_target_pairs={{0,8},{4,12},{8,0},{12,4},{16,24},{20,28},{24,16},{28,20},{1,9},{5... | collective-permute-start | bytes 294920 | tf_op jit(solution)/shard_map/ppermute | solution.py:400
  55.0 5.0 %collective-permute-start.19 = (f32[256,128]{1,0:T(8,128)S(1)}, f32[256,128]{1,0:T(8,128)S(1)}, u32[]{:S(2)}, u32[]{:S(2)}) collective-permute-start(f32[256,128]{1,0:T(8,128)S(1)} %get-tuple-element.52), channel_id=1, source_target_pairs={{0,4},{1,2},{2,1},{3,7},{4,0},{5,6},{6,5},{7,3},{8,12},{9,10},{10,... | collective-permute-start | bytes 393224 | tf_op jit(solution)/shard_map/ppermute | solution.py:412
  58.3 7.4 %collective-permute-start.26 = (f32[192,128]{1,0:T(8,128)S(1)}, f32[192,128]{1,0:T(8,128)S(1)}, u32[]{:S(2)}, u32[]{:S(2)}) collective-permute-start(f32[192,128]{1,0:T(8,128)S(1)} %add.78), channel_id=1, source_target_pairs={{0,16},{4,20},{8,24},{12,28},{16,0},{20,4},{24,8},{28,12},{1,17},{... | collective-permute-start | bytes 294920 | tf_op jit(solution)/shard_map/ppermute | solution.py:400
  60.1 5.8 %collective-permute-start.20 = (f32[2,64,128]{2,1,0:T(8,128)S(1)}, f32[2,64,128]{2,1,0:T(8,128)S(1)}, u32[]{:S(2)}, u32[]{:S(2)}) collective-permute-start(f32[2,64,128]{2,1,0:T(8,128)S(1)} %get-tuple-element.54), channel_id=1, source_target_pairs={{0,4},{4,0},{8,12},{12,8},{16,20},{20,16},{24,28},{28,24},{1,5},{5... | collective-permute-start | bytes 196616 | tf_op jit(solution)/shard_map/ppermute | solution.py:400
  60.9 5.0 %collective-permute-start.21 = (f32[2,64,128]{2,1,0:T(8,128)S(1)}, f32[2,64,128]{2,1,0:T(8,128)S(1)}, u32[]{:S(2)}, u32[]{:S(2)}) collective-permute-start(f32[2,64,128]{2,1,0:T(8,128)S(1)} %get-tuple-element.55), channel_id=1, source_target_pairs={{0,1},{1,0},{2,3},{3,2},{4,8},{5,9},{6,10},{7,11},{8,4},{9,5},{10,... | collective-permute-start | bytes 196616 | tf_op jit(solution)/shard_map/ppermute | solution.py:424
  65.8 1.3 %collective-permute-start.27 = (f32[2,64,128]{2,1,0:T(8,128)S(1)}, f32[2,64,128]{2,1,0:T(8,128)S(1)}, u32[]{:S(2)}, u32[]{:S(2)}) collective-permute-start(f32[2,64,128]{2,1,0:T(8,128)S(1)} %fusion.1.mine), channel_id=1, source_target_pairs={{0,1},{1,0},{2,3},{3,2},{4,5},{5,4},{6,7},{7,6},{8,9},{9,8},{10,11... | collective-permute-start | bytes 196616 | tf_op jit(solution)/shard_map/ppermute | solution.py:400

commit v7 on v6

--- a/solution.py
+++ b/solution.py
@@ -442,10 +442,6 @@
     rows, cols = lax.axis_size("row"), lax.axis_size("col")
     pairs = [(r * cols + c, (r ^ 1) * cols + (c ^ 2)) for r in range(rows) for c in range(cols)]
     return lax.ppermute(value, AXES, pairs)
-
-
-def chain_steps():
-    return lax.axis_size("row").bit_length() - 2
 
 
 def add_plane(part, weight):
@@ -579,7 +575,7 @@
             )
             got_1, got_2 = swap(sent_1, "row", 1), swap_rows(sent_2)
             part = add_plane(part, weight)
-            for other_step in chip_steps()[-chain_steps() : -1]:
+            for other_step in chip_steps()[2:-1]:
                 part = add_step(part, other_step)
             part = add_step(part, chip_steps()[-1])
         else:
@@ -591,7 +587,7 @@
             )
             got_1, got_2 = swap(sent_1, "row", 1), swap_rows(sent_2)
             part = add_plane(part, weight)
-            for other_step in chip_steps()[-chain_steps() : -1]:
+            for other_step in chip_steps()[2:-1]:
                 part = add_step(part, other_step)
             tall, near, far = call(
                 update_kernel,

time: 68.1 us -> 68.1 us (level)
  no operation moved by 1% of the time
where the time goes in v7:
time: 68.1 us; the launch traced here: 67.9 us
  waiting for transfers between devices  29.3 us (43%)
  starting transfers between devices  24.3 us (36%)
  Pallas kernels  10.8 us (16%)
  local copies, waits for them, and re-layouts  2.19 us (3%)
  between operations  1.04 us (2%)
    ppermute x17, waiting for transfers between devices, swap(): lax.ppermute(value, axis, [(i, i ^ bit) for i in range(lax.axis_size(axis...  22.4 us
    ppermute x17, starting transfers between devices, swap(): lax.ppermute(value, axis, [(i, i ^ bit) for i in range(lax.axis_size(axis...  16.8 us
    pallas_call x13, Pallas kernels, call(): pl.pallas_call(kernel, out_shape=tuple((jax.ShapeDtypeStruct(shape, jnp.f...  10.8 us
    ppermute x6, starting transfers between devices, swap_far(): return lax.ppermute(value, AXES, pairs)  6.23 us
    ppermute x6, waiting for transfers between devices, swap_far(): return lax.ppermute(value, AXES, pairs)  4.96 us
    ppermute x2, waiting for transfers between devices, swap_both(): return lax.ppermute(value, AXES, pairs)  1.96 us
  transfers between devices with their start and end apart: 28, of which 18 were waited for; matrix products, arithmetic and copies ran while one was open for 3% of the time, Pallas kernels for 6%

profile of v7, /device:TPU:0, one launch (start us, length us, event | category | flops | bytes accessed | tf_op | source)
XLA Modules:
  0.0 67.9 jit_solution(1483591632999775802)
XLA Ops:
  0.6 1.5 %shard_map.77 = (f32[136,128]{1,0:T(8,128)}, f32[136,128]{1,0:T(8,128)}, f32[8,128]{1,0:T(8,128)}) custom-call(f32[2,128,128]{2,1,0:T(8,128)} %tile.5, s32[2,2,4]{2,1,0:T(2,128)} %bitcast.32, s32[1,2]{1,0:T(1,128)} %bitcast.33), custom_call_target="tpu_custom_call" | custom-call | flops 1000000 | bytes 1048576 | tf_op jit(solution)/shard_map/pallas_call | solution.py:388
  2.2 3.0 %collective-permute-start = (f32[136,128]{1,0:T(8,128)}, f32[136,128]{1,0:T(8,128)S(1)}, u32[]{:S(2)}, u32[]{:S(2)}) collective-permute-start(f32[136,128]{1,0:T(8,128)} %get-tuple-element.31), channel_id=1, source_target_pairs={{0,4},{4,0},{8,12},{12,8},{16,20},{20,16},{24,28},{28,24},{1,5},{5... | collective-permute-start | bytes 208904 | tf_op jit(solution)/shard_map/ppermute | solution.py:400
  5.2 0.0 collective-permute-start.1
  5.2 1.1 %slice_bitcast_fusion = (f32[4,128,128]{2,1,0:T(8,128)S(1)}, f32[4,128,128]{2,1,0:T(8,128)S(1)}) fusion(f32[1,1,2,4,128,128]{5,4,3,2,1,0:T(8,128)} %param.10), kind=kLoop, calls=%fused_computation | loop fusion | bytes 1048576 | tf_op jit(solution)/shard_map/squeeze | solution.py:548
  6.4 2.4 %collective-permute-done.first = f32[136,128]{1,0:T(8,128)S(1)} collective-permute-done((f32[136,128]{1,0:T(8,128)}, f32[136,128]{1,0:T(8,128)S(1)}, u32[]{:S(2)}, u32[]{:S(2)}) %collective-permute-start) | collective-permute-done | bytes 69664 | tf_op jit(solution)/shard_map/ppermute | solution.py:400
  8.8 0.1 shard_map.79
  8.9 2.4 %collective-permute-start.3 = (f32[208,128]{1,0:T(8,128)S(1)}, f32[208,128]{1,0:T(8,128)S(1)}, u32[]{:S(2)}, u32[]{:S(2)}) collective-permute-start(f32[208,128]{1,0:T(8,128)S(1)} %shard_map.79), channel_id=1, source_target_pairs={{0,4},{1,2},{2,1},{3,7},{4,0},{5,6},{6,5},{7,3},{8,12},{9,10},{10,... | collective-permute-start | bytes 319496 | tf_op jit(solution)/shard_map/ppermute | solution.py:412
  11.3 0.0 collective-permute-done.1.second
  11.3 0.1 shard_map.78
  11.4 0.1 collective-permute-start.4
  11.6 0.1 copy.14
  11.7 3.8 %collective-permute-done.4 = f32[72,128]{1,0:T(8,128)S(1)} collective-permute-done((f32[72,128]{1,0:T(8,128)S(1)}, f32[72,128]{1,0:T(8,128)S(1)}, u32[]{:S(2)}, u32[]{:S(2)}) %collective-permute-start.4) | collective-permute-done | bytes 36896 | tf_op jit(solution)/shard_map/ppermute | solution.py:412
  15.6 0.1 copy.17
  15.7 0.5 shard_map.80
  16.2 0.4 copy-done.1
  16.6 0.1 copy-done.3
  16.7 2.0 %shard_map.81 = (f32[448,128]{1,0:T(8,128)S(1)}, f32[256,128]{1,0:T(8,128)S(1)}, f32[192,128]{1,0:T(8,128)S(1)}, f32[2,256,128]{2,1,0:T(8,128)S(1)}) custom-call(s32[6,4]{1,0:T(8,128)S(1)} %slice_convert_fusion.scan, f32[4,2,128,128]{3,2,1,0:T(8,128)S(1)} %get-tuple-element.36.wins, f32[128,128]{1,0:T(8,128)S(1)} %get-tuple-element.37.win_weight, ...), custom_call_target="tpu_custom_call" | custom-call | flops 805306368 | bytes 4194304 | tf_op jit(solution)/shard_map/pallas_call | solution.py:388
  18.7 0.1 collective-permute-start.5
  18.8 0.1 copy.16
  18.9 0.9 %collective-permute-start.6 = (f32[256,128]{1,0:T(8,128)S(1)}, f32[256,128]{1,0:T(8,128)S(1)}, u32[]{:S(2)}, u32[]{:S(2)}) collective-permute-start(f32[256,128]{1,0:T(8,128)S(1)} %get-tuple-element.40), channel_id=1, source_target_pairs={{0,4},{1,2},{2,1},{3,7},{4,0},{5,6},{6,5},{7,3},{8,12},{9,10},{10,... | collective-permute-start | bytes 393224 | tf_op jit(solution)/shard_map/ppermute | solution.py:412
  19.8 0.4 collective-permute-done.5.near
  20.3 1.2 %collective-permute-start.11 = (f32[192,128]{1,0:T(8,128)S(1)}, f32[192,128]{1,0:T(8,128)S(1)}, u32[]{:S(2)}, u32[]{:S(2)}) collective-permute-start(f32[192,128]{1,0:T(8,128)S(1)} %slice_add_fusion.1), channel_id=1, source_target_pairs={{0,6},{1,7},{2,4},{3,5},{4,2},{5,3},{6,0},{7,1},{8,14},{9,15},{10,... | collective-permute-start | bytes 294920 | tf_op jit(solution)/shard_map/ppermute | solution.py:444
  21.5 1.2 %collective-permute-start.10 = (f32[192,128]{1,0:T(8,128)S(1)}, f32[192,128]{1,0:T(8,128)S(1)}, u32[]{:S(2)}, u32[]{:S(2)}) collective-permute-start(f32[192,128]{1,0:T(8,128)S(1)} %slice_add_fusion.1), channel_id=1, source_target_pairs={{0,2},{1,3},{2,0},{3,1},{4,6},{5,7},{6,4},{7,5},{8,10},{9,11},{10,... | collective-permute-start | bytes 294920 | tf_op jit(solution)/shard_map/ppermute | solution.py:400
  22.7 1.1 %collective-permute-start.9 = (f32[192,128]{1,0:T(8,128)S(1)}, f32[192,128]{1,0:T(8,128)S(1)}, u32[]{:S(2)}, u32[]{:S(2)}) collective-permute-start(f32[192,128]{1,0:T(8,128)S(1)} %slice_add_fusion.1), channel_id=1, source_target_pairs={{0,4},{4,0},{8,12},{12,8},{16,20},{20,16},{24,28},{28,24},{1,5},{5... | collective-permute-start | bytes 294920 | tf_op jit(solution)/shard_map/ppermute | solution.py:400
  23.9 0.1 copy.15
  24.0 0.1 convert_element_type.10.metas
  24.1 1.4 %shard_map.83.weight = f32[256,128]{1,0:T(8,128)S(1)} custom-call(s32[9,24]{1,0:T(8,128)S(1)} %convert_element_type.10.metas, f32[2,128,128]{2,1,0:T(8,128)S(1)} %copy-done.1), custom_call_target="tpu_custom_call" | custom-call | flops 1000000 | bytes 1048576 | tf_op jit(solution)/shard_map/pallas_call | solution.py:388
  25.5 0.1 shard_map.82
  25.6 1.0 %collective-permute-start.7 = (f32[2,128,128]{2,1,0:T(8,128)S(1)}, f32[2,128,128]{2,1,0:T(8,128)S(1)}, u32[]{:S(2)}, u32[]{:S(2)}) collective-permute-start(f32[2,128,128]{2,1,0:T(8,128)S(1)} %get-tuple-element.41.sent_1), channel_id=1, source_target_pairs={{0,4},{4,0},{8,12},{12,8},{16,20},{20,16},{24,28},{28,24},{1,5},{5... | collective-permute-start | bytes 393224 | tf_op jit(solution)/shard_map/ppermute | solution.py:400
  26.6 0.3 collective-permute-done.11
  26.9 1.3 %collective-permute-done.10 = f32[192,128]{1,0:T(8,128)S(1)} collective-permute-done((f32[192,128]{1,0:T(8,128)S(1)}, f32[192,128]{1,0:T(8,128)S(1)}, u32[]{:S(2)}, u32[]{:S(2)}) %collective-permute-start.10) | collective-permute-done | bytes 98336 | tf_op jit(solution)/shard_map/ppermute | solution.py:400
  28.2 0.5 collective-permute-done.9
  28.7 1.0 %collective-permute-start.12 = (f32[192,128]{1,0:T(8,128)S(1)}, f32[192,128]{1,0:T(8,128)S(1)}, u32[]{:S(2)}, u32[]{:S(2)}) collective-permute-start(f32[192,128]{1,0:T(8,128)S(1)} %add_add_fusion.1), channel_id=1, source_target_pairs={{0,8},{4,12},{8,0},{12,4},{16,24},{20,28},{24,16},{28,20},{1,9},{5... | collective-permute-start | bytes 294920 | tf_op jit(solution)/shard_map/ppermute | solution.py:400
  29.7 4.5 %collective-permute-done.12 = f32[192,128]{1,0:T(8,128)S(1)} collective-permute-done((f32[192,128]{1,0:T(8,128)S(1)}, f32[192,128]{1,0:T(8,128)S(1)}, u32[]{:S(2)}, u32[]{:S(2)}) %collective-permute-start.12) | collective-permute-done | bytes 98336 | tf_op jit(solution)/shard_map/ppermute | solution.py:400
  34.2 2.0 %collective-permute-start.16 = (f32[192,128]{1,0:T(8,128)S(1)}, f32[192,128]{1,0:T(8,128)S(1)}, u32[]{:S(2)}, u32[]{:S(2)}) collective-permute-start(f32[192,128]{1,0:T(8,128)S(1)} %add.69), channel_id=1, source_target_pairs={{0,16},{4,20},{8,24},{12,28},{16,0},{20,4},{24,8},{28,12},{1,17},{... | collective-permute-start | bytes 294920 | tf_op jit(solution)/shard_map/ppermute | solution.py:400
  36.3 0.2 shard_map.84
  36.5 0.4 collective-permute-start.14
  36.9 1.7 %collective-permute-start.15 = (f32[128,128]{1,0:T(8,128)S(1)}, f32[128,128]{1,0:T(8,128)S(1)}, u32[]{:S(2)}, u32[]{:S(2)}) collective-permute-start(f32[128,128]{1,0:T(8,128)S(1)} %get-tuple-element.69), channel_id=1, source_target_pairs={{0,4},{1,2},{2,1},{3,7},{4,0},{5,6},{6,5},{7,3},{8,12},{9,10},{10,... | collective-permute-start | bytes 196616 | tf_op jit(solution)/shard_map/ppermute | solution.py:412
  38.6 2.0 %collective-permute-done.16 = f32[192,128]{1,0:T(8,128)S(1)} collective-permute-done((f32[192,128]{1,0:T(8,128)S(1)}, f32[192,128]{1,0:T(8,128)S(1)}, u32[]{:S(2)}, u32[]{:S(2)}) %collective-permute-start.16) | collective-permute-done | bytes 98336 | tf_op jit(solution)/shard_map/ppermute | solution.py:400
  40.6 0.1 collective-permute-start.17
  40.7 0.1 collective-permute-done.14
  40.8 0.7 %collective-permute-done.15 = f32[128,128]{1,0:T(8,128)S(1)} collective-permute-done((f32[128,128]{1,0:T(8,128)S(1)}, f32[128,128]{1,0:T(8,128)S(1)}, u32[]{:S(2)}, u32[]{:S(2)}) %collective-permute-start.15) | collective-permute-done | bytes 65568 | tf_op jit(solution)/shard_map/ppermute | solution.py:412
  41.5 0.5 shard_map.85
  42.0 2.1 %shard_map.86 = (f32[448,128]{1,0:T(8,128)S(1)}, f32[256,128]{1,0:T(8,128)S(1)}, f32[192,128]{1,0:T(8,128)S(1)}, f32[2,256,128]{2,1,0:T(8,128)S(1)}) custom-call(s32[6,4]{1,0:T(8,128)S(1)} %slice_convert_fusion.scan, f32[4,2,128,128]{3,2,1,0:T(8,128)S(1)} %get-tuple-element.48.wins, f32[128,128]{1,0:T(8,128)S(1)} %get-tuple-element.49.win_weight, ...), custom_call_target="tpu_custom_call" | custom-call | flops 805306368 | bytes 4194304 | tf_op jit(solution)/shard_map/pallas_call | solution.py:388
  44.1 0.2 collective-permute-start.18
  44.3 1.4 %collective-permute-done.18.near = f32[448,128]{1,0:T(8,128)S(1)} collective-permute-done((f32[448,128]{1,0:T(8,128)S(1)}, f32[448,128]{1,0:T(8,128)S(1)}, u32[]{:S(2)}, u32[]{:S(2)}) %collective-permute-start.18) | collective-permute-done | bytes 229408 | tf_op jit(solution)/shard_map/ppermute | solution.py:400
  45.7 0.1 collective-permute-start.24
  45.8 2.8 %collective-permute-start.23 = (f32[192,128]{1,0:T(8,128)S(1)}, f32[192,128]{1,0:T(8,128)S(1)}, u32[]{:S(2)}, u32[]{:S(2)}) collective-permute-start(f32[192,128]{1,0:T(8,128)S(1)} %slice_add_fusion), channel_id=1, source_target_pairs={{0,2},{1,3},{2,0},{3,1},{4,6},{5,7},{6,4},{7,5},{8,10},{9,11},{10,... | collective-permute-start | bytes 294920 | tf_op jit(solution)/shard_map/ppermute | solution.py:400
  48.5 0.7 %collective-permute-start.22 = (f32[192,128]{1,0:T(8,128)S(1)}, f32[192,128]{1,0:T(8,128)S(1)}, u32[]{:S(2)}, u32[]{:S(2)}) collective-permute-start(f32[192,128]{1,0:T(8,128)S(1)} %slice_add_fusion), channel_id=1, source_target_pairs={{0,4},{4,0},{8,12},{12,8},{16,20},{20,16},{24,28},{28,24},{1,5},{5... | collective-permute-start | bytes 294920 | tf_op jit(solution)/shard_map/ppermute | solution.py:400
  49.2 1.4 %shard_map.88.weight = f32[256,128]{1,0:T(8,128)S(1)} custom-call(s32[9,24]{1,0:T(8,128)S(1)} %convert_element_type.10.metas, f32[2,128,128]{2,1,0:T(8,128)S(1)} %pad_maximum_fusion.probe), custom_call_target="tpu_custom_call" | custom-call | flops 1000000 | bytes 1048576 | tf_op jit(solution)/shard_map/pallas_call | solution.py:388
  50.6 1.7 %collective-permute-done.24 = f32[192,128]{1,0:T(8,128)S(1)} collective-permute-done((f32[192,128]{1,0:T(8,128)S(1)}, f32[192,128]{1,0:T(8,128)S(1)}, u32[]{:S(2)}, u32[]{:S(2)}) %collective-permute-start.24) | collective-permute-done | bytes 98336 | tf_op jit(solution)/shard_map/ppermute | solution.py:444
  52.3 1.2 %collective-permute-done.23 = f32[192,128]{1,0:T(8,128)S(1)} collective-permute-done((f32[192,128]{1,0:T(8,128)S(1)}, f32[192,128]{1,0:T(8,128)S(1)}, u32[]{:S(2)}, u32[]{:S(2)}) %collective-permute-start.23) | collective-permute-done | bytes 98336 | tf_op jit(solution)/shard_map/ppermute | solution.py:400
  53.4 0.1 collective-permute-done.22
  53.6 1.4 %collective-permute-start.25 = (f32[192,128]{1,0:T(8,128)S(1)}, f32[192,128]{1,0:T(8,128)S(1)}, u32[]{:S(2)}, u32[]{:S(2)}) collective-permute-start(f32[192,128]{1,0:T(8,128)S(1)} %add_add_fusion), channel_id=1, source_target_pairs={{0,8},{4,12},{8,0},{12,4},{16,24},{20,28},{24,16},{28,20},{1,9},{5... | collective-permute-start | bytes 294920 | tf_op jit(solution)/shard_map/ppermute | solution.py:400
  55.0 0.7 %collective-permute-start.19 = (f32[256,128]{1,0:T(8,128)S(1)}, f32[256,128]{1,0:T(8,128)S(1)}, u32[]{:S(2)}, u32[]{:S(2)}) collective-permute-start(f32[256,128]{1,0:T(8,128)S(1)} %get-tuple-element.52), channel_id=1, source_target_pairs={{0,4},{1,2},{2,1},{3,7},{4,0},{5,6},{6,5},{7,3},{8,12},{9,10},{10,... | collective-permute-start | bytes 393224 | tf_op jit(solution)/shard_map/ppermute | solution.py:412
  55.7 2.6 %collective-permute-done.25 = f32[192,128]{1,0:T(8,128)S(1)} collective-permute-done((f32[192,128]{1,0:T(8,128)S(1)}, f32[192,128]{1,0:T(8,128)S(1)}, u32[]{:S(2)}, u32[]{:S(2)}) %collective-permute-start.25) | collective-permute-done | bytes 98336 | tf_op jit(solution)/shard_map/ppermute | solution.py:400
  58.3 1.3 %collective-permute-start.26 = (f32[192,128]{1,0:T(8,128)S(1)}, f32[192,128]{1,0:T(8,128)S(1)}, u32[]{:S(2)}, u32[]{:S(2)}) collective-permute-start(f32[192,128]{1,0:T(8,128)S(1)} %add.78), channel_id=1, source_target_pairs={{0,16},{4,20},{8,24},{12,28},{16,0},{20,4},{24,8},{28,12},{1,17},{... | collective-permute-start | bytes 294920 | tf_op jit(solution)/shard_map/ppermute | solution.py:400
  59.7 0.3 collective-permute-done.19.far
  60.0 0.1 shard_map.87
  60.1 0.8 %collective-permute-start.20 = (f32[2,64,128]{2,1,0:T(8,128)S(1)}, f32[2,64,128]{2,1,0:T(8,128)S(1)}, u32[]{:S(2)}, u32[]{:S(2)}) collective-permute-start(f32[2,64,128]{2,1,0:T(8,128)S(1)} %get-tuple-element.54), channel_id=1, source_target_pairs={{0,4},{4,0},{8,12},{12,8},{16,20},{20,16},{24,28},{28,24},{1,5},{5... | collective-permute-start | bytes 196616 | tf_op jit(solution)/shard_map/ppermute | solution.py:400
  60.9 4.8 %collective-permute-done.26 = f32[192,128]{1,0:T(8,128)S(1)} collective-permute-done((f32[192,128]{1,0:T(8,128)S(1)}, f32[192,128]{1,0:T(8,128)S(1)}, u32[]{:S(2)}, u32[]{:S(2)}) %collective-permute-start.26) | collective-permute-done | bytes 98336 | tf_op jit(solution)/shard_map/ppermute | solution.py:400
  65.8 0.1 collective-permute-start.27
  65.9 1.2 %collective-permute-done.27.other = f32[2,64,128]{2,1,0:T(8,128)S(1)} collective-permute-done((f32[2,64,128]{2,1,0:T(8,128)S(1)}, f32[2,64,128]{2,1,0:T(8,128)S(1)}, u32[]{:S(2)}, u32[]{:S(2)}) %collective-permute-start.27) | collective-permute-done | bytes 65568 | tf_op jit(solution)/shard_map/ppermute | solution.py:400
  67.2 0.7 %shard_map.89 = (f32[2,128,128]{2,1,0:T(8,128)}, f32[2,128,128]{2,1,0:T(8,128)}) custom-call(f32[2,256,128]{2,1,0:T(8,128)S(1)} %get-tuple-element.45.tall, f32[2,128,128]{2,1,0:T(8,128)S(1)} %get-tuple-element.53.middle, f32[2,64,128]{2,1,0:T(8,128)S(1)} %collective-permute-done.20.got_1, f32[2,64,128]{2,1,0:T(8,128)S(1)} %collective-permute-done.21.got_2, ...), custom_call_target="tpu_custom_call" | custom-call | flops 1000000 | bytes 4194304 | tf_op jit(solution)/shard_map/pallas_call | solution.py:388
  (51 shorter events, 0.4 us)
Async XLA Ops:
  2.2 6.6 %collective-permute-start = (f32[136,128]{1,0:T(8,128)}, f32[136,128]{1,0:T(8,128)S(1)}, u32[]{:S(2)}, u32[]{:S(2)}) collective-permute-start(f32[136,128]{1,0:T(8,128)} %get-tuple-element.31), channel_id=1, source_target_pairs={{0,4},{4,0},{8,12},{12,8},{16,20},{20,16},{24,28},{28,24},{1,5},{5... | collective-permute-start | bytes 208904 | tf_op jit(solution)/shard_map/ppermute | solution.py:400
  5.2 6.1 %collective-permute-start.1 = (f32[136,128]{1,0:T(8,128)}, f32[136,128]{1,0:T(8,128)S(1)}, u32[]{:S(2)}, u32[]{:S(2)}) collective-permute-start(f32[136,128]{1,0:T(8,128)} %get-tuple-element.32), channel_id=1, source_target_pairs={{0,1},{1,0},{2,3},{3,2},{4,8},{5,9},{6,10},{7,11},{8,4},{9,5},{10,... | collective-permute-start | bytes 208904 | tf_op jit(solution)/shard_map/ppermute | solution.py:424
  5.2 1.1 %copy-start.2 = (f32[8,128]{1,0:T(8,128)S(1)}, f32[8,128]{1,0:T(8,128)}, u32[]{:S(2)}) copy-start(f32[8,128]{1,0:T(8,128)} %get-tuple-element.30.meta) | copy-start | bytes 12292
  5.2 3.5 %copy-start = (f32[2,128,128]{2,1,0:T(8,128)S(1)}, f32[2,128,128]{2,1,0:T(8,128)}, u32[]{:S(2)}) copy-start(f32[2,128,128]{2,1,0:T(8,128)} %tile.5) | copy-start | bytes 393220
  8.9 6.6 %collective-permute-start.3 = (f32[208,128]{1,0:T(8,128)S(1)}, f32[208,128]{1,0:T(8,128)S(1)}, u32[]{:S(2)}, u32[]{:S(2)}) collective-permute-start(f32[208,128]{1,0:T(8,128)S(1)} %shard_map.79), channel_id=1, source_target_pairs={{0,4},{1,2},{2,1},{3,7},{4,0},{5,6},{6,5},{7,3},{8,12},{9,10},{10,... | collective-permute-start | bytes 319496 | tf_op jit(solution)/shard_map/ppermute | solution.py:412
  11.4 4.0 %collective-permute-start.4 = (f32[72,128]{1,0:T(8,128)S(1)}, f32[72,128]{1,0:T(8,128)S(1)}, u32[]{:S(2)}, u32[]{:S(2)}) collective-permute-start(f32[72,128]{1,0:T(8,128)S(1)} %get-tuple-element.35), channel_id=1, source_target_pairs={{0,4},{1,2},{2,1},{3,7},{4,0},{5,6},{6,5},{7,3},{8,12},{9,10},{10,... | collective-permute-start | bytes 110600 | tf_op jit(solution)/shard_map/ppermute | solution.py:412
  11.7 4.0 %collective-permute-start.2 = (f32[280,128]{1,0:T(8,128)S(1)}, f32[280,128]{1,0:T(8,128)S(1)}, u32[]{:S(2)}, u32[]{:S(2)}) collective-permute-start(f32[280,128]{1,0:T(8,128)S(1)} %get-tuple-element.34), channel_id=1, source_target_pairs={{0,1},{1,0},{2,3},{3,2},{4,5},{5,4},{6,7},{7,6},{8,9},{9,8},{10,11... | collective-permute-start | bytes 430088 | tf_op jit(solution)/shard_map/ppermute | solution.py:400
  15.7 0.9 %copy-start.1 = (f32[2,128,128]{2,1,0:T(8,128)S(1)}, f32[2,128,128]{2,1,0:T(8,128)}, u32[]{:S(2)}) copy-start(f32[2,128,128]{2,1,0:T(8,128)} %probe.3) | copy-start | bytes 393220
  15.7 1.0 %copy-start.3 = (bf16[6,128,128]{2,1,0:T(8,128)(2,1)S(1)}, bf16[6,128,128]{2,1,0:T(8,128)(2,1)}, u32[]{:S(2)}) copy-start(bf16[6,128,128]{2,1,0:T(8,128)(2,1)} %constant.41.clone.tables) | copy-start | bytes 589828
  18.7 1.6 %collective-permute-start.5 = (f32[448,128]{1,0:T(8,128)S(1)}, f32[448,128]{1,0:T(8,128)S(1)}, u32[]{:S(2)}, u32[]{:S(2)}) collective-permute-start(f32[448,128]{1,0:T(8,128)S(1)} %get-tuple-element.39), channel_id=1, source_target_pairs={{0,1},{1,0},{2,3},{3,2},{4,5},{5,4},{6,7},{7,6},{8,9},{9,8},{10,11... | collective-permute-start | bytes 688136 | tf_op jit(solution)/shard_map/ppermute | solution.py:400
  18.9 6.5 %collective-permute-start.6 = (f32[256,128]{1,0:T(8,128)S(1)}, f32[256,128]{1,0:T(8,128)S(1)}, u32[]{:S(2)}, u32[]{:S(2)}) collective-permute-start(f32[256,128]{1,0:T(8,128)S(1)} %get-tuple-element.40), channel_id=1, source_target_pairs={{0,4},{1,2},{2,1},{3,7},{4,0},{5,6},{6,5},{7,3},{8,12},{9,10},{10,... | collective-permute-start | bytes 393224 | tf_op jit(solution)/shard_map/ppermute | solution.py:412
  20.3 6.6 %collective-permute-start.11 = (f32[192,128]{1,0:T(8,128)S(1)}, f32[192,128]{1,0:T(8,128)S(1)}, u32[]{:S(2)}, u32[]{:S(2)}) collective-permute-start(f32[192,128]{1,0:T(8,128)S(1)} %slice_add_fusion.1), channel_id=1, source_target_pairs={{0,6},{1,7},{2,4},{3,5},{4,2},{5,3},{6,0},{7,1},{8,14},{9,15},{10,... | collective-permute-start | bytes 294920 | tf_op jit(solution)/shard_map/ppermute | solution.py:444
  21.5 6.7 %collective-permute-start.10 = (f32[192,128]{1,0:T(8,128)S(1)}, f32[192,128]{1,0:T(8,128)S(1)}, u32[]{:S(2)}, u32[]{:S(2)}) collective-permute-start(f32[192,128]{1,0:T(8,128)S(1)} %slice_add_fusion.1), channel_id=1, source_target_pairs={{0,2},{1,3},{2,0},{3,1},{4,6},{5,7},{6,4},{7,5},{8,10},{9,11},{10,... | collective-permute-start | bytes 294920 | tf_op jit(solution)/shard_map/ppermute | solution.py:400
  22.7 6.0 %collective-permute-start.9 = (f32[192,128]{1,0:T(8,128)S(1)}, f32[192,128]{1,0:T(8,128)S(1)}, u32[]{:S(2)}, u32[]{:S(2)}) collective-permute-start(f32[192,128]{1,0:T(8,128)S(1)} %slice_add_fusion.1), channel_id=1, source_target_pairs={{0,4},{4,0},{8,12},{12,8},{16,20},{20,16},{24,28},{28,24},{1,5},{5... | collective-permute-start | bytes 294920 | tf_op jit(solution)/shard_map/ppermute | solution.py:400
  25.6 10.7 %collective-permute-start.7 = (f32[2,128,128]{2,1,0:T(8,128)S(1)}, f32[2,128,128]{2,1,0:T(8,128)S(1)}, u32[]{:S(2)}, u32[]{:S(2)}) collective-permute-start(f32[2,128,128]{2,1,0:T(8,128)S(1)} %get-tuple-element.41.sent_1), channel_id=1, source_target_pairs={{0,4},{4,0},{8,12},{12,8},{16,20},{20,16},{24,28},{28,24},{1,5},{5... | collective-permute-start | bytes 393224 | tf_op jit(solution)/shard_map/ppermute | solution.py:400
  26.6 9.7 %collective-permute-start.8 = (f32[2,128,128]{2,1,0:T(8,128)S(1)}, f32[2,128,128]{2,1,0:T(8,128)S(1)}, u32[]{:S(2)}, u32[]{:S(2)}) collective-permute-start(f32[2,128,128]{2,1,0:T(8,128)S(1)} %get-tuple-element.42.sent_2), channel_id=1, source_target_pairs={{0,1},{1,0},{2,3},{3,2},{4,8},{5,9},{6,10},{7,11},{8,4},{9,5},{10,... | collective-permute-start | bytes 393224 | tf_op jit(solution)/shard_map/ppermute | solution.py:424
  28.7 5.5 %collective-permute-start.12 = (f32[192,128]{1,0:T(8,128)S(1)}, f32[192,128]{1,0:T(8,128)S(1)}, u32[]{:S(2)}, u32[]{:S(2)}) collective-permute-start(f32[192,128]{1,0:T(8,128)S(1)} %add_add_fusion.1), channel_id=1, source_target_pairs={{0,8},{4,12},{8,0},{12,4},{16,24},{20,28},{24,16},{28,20},{1,9},{5... | collective-permute-start | bytes 294920 | tf_op jit(solution)/shard_map/ppermute | solution.py:400
  34.2 6.3 %collective-permute-start.16 = (f32[192,128]{1,0:T(8,128)S(1)}, f32[192,128]{1,0:T(8,128)S(1)}, u32[]{:S(2)}, u32[]{:S(2)}) collective-permute-start(f32[192,128]{1,0:T(8,128)S(1)} %add.69), channel_id=1, source_target_pairs={{0,16},{4,20},{8,24},{12,28},{16,0},{20,4},{24,8},{28,12},{1,17},{... | collective-permute-start | bytes 294920 | tf_op jit(solution)/shard_map/ppermute | solution.py:400
  36.5 4.3 %collective-permute-start.14 = (f32[128,128]{1,0:T(8,128)S(1)}, f32[128,128]{1,0:T(8,128)S(1)}, u32[]{:S(2)}, u32[]{:S(2)}) collective-permute-start(f32[128,128]{1,0:T(8,128)S(1)} %get-tuple-element.68), channel_id=1, source_target_pairs={{0,4},{1,2},{2,1},{3,7},{4,0},{5,6},{6,5},{7,3},{8,12},{9,10},{10,... | collective-permute-start | bytes 196616 | tf_op jit(solution)/shard_map/ppermute | solution.py:412
  36.9 4.6 %collective-permute-start.15 = (f32[128,128]{1,0:T(8,128)S(1)}, f32[128,128]{1,0:T(8,128)S(1)}, u32[]{:S(2)}, u32[]{:S(2)}) collective-permute-start(f32[128,128]{1,0:T(8,128)S(1)} %get-tuple-element.69), channel_id=1, source_target_pairs={{0,4},{1,2},{2,1},{3,7},{4,0},{5,6},{6,5},{7,3},{8,12},{9,10},{10,... | collective-permute-start | bytes 196616 | tf_op jit(solution)/shard_map/ppermute | solution.py:412
  38.5 3.0 %collective-permute-start.13 = (f32[256,128]{1,0:T(8,128)S(1)}, f32[256,128]{1,0:T(8,128)S(1)}, u32[]{:S(2)}, u32[]{:S(2)}) collective-permute-start(f32[256,128]{1,0:T(8,128)S(1)} %get-tuple-element.46), channel_id=1, source_target_pairs={{0,1},{1,0},{2,3},{3,2},{4,5},{5,4},{6,7},{7,6},{8,9},{9,8},{10,11... | collective-permute-start | bytes 393224 | tf_op jit(solution)/shard_map/ppermute | solution.py:400
  40.6 1.4 %collective-permute-start.17 = (f32[2,64,128]{2,1,0:T(8,128)S(1)}, f32[2,64,128]{2,1,0:T(8,128)S(1)}, u32[]{:S(2)}, u32[]{:S(2)}) collective-permute-start(f32[2,64,128]{2,1,0:T(8,128)S(1)} %divide_add_fusion), channel_id=1, source_target_pairs={{0,1},{1,0},{2,3},{3,2},{4,5},{5,4},{6,7},{7,6},{8,9},{9,8},{10,11... | collective-permute-start | bytes 196616 | tf_op jit(solution)/shard_map/ppermute | solution.py:400
  44.1 1.6 %collective-permute-start.18 = (f32[448,128]{1,0:T(8,128)S(1)}, f32[448,128]{1,0:T(8,128)S(1)}, u32[]{:S(2)}, u32[]{:S(2)}) collective-permute-start(f32[448,128]{1,0:T(8,128)S(1)} %get-tuple-element.51), channel_id=1, source_target_pairs={{0,1},{1,0},{2,3},{3,2},{4,5},{5,4},{6,7},{7,6},{8,9},{9,8},{10,11... | collective-permute-start | bytes 688136 | tf_op jit(solution)/shard_map/ppermute | solution.py:400
  45.7 6.6 %collective-permute-start.24 = (f32[192,128]{1,0:T(8,128)S(1)}, f32[192,128]{1,0:T(8,128)S(1)}, u32[]{:S(2)}, u32[]{:S(2)}) collective-permute-start(f32[192,128]{1,0:T(8,128)S(1)} %slice_add_fusion), channel_id=1, source_target_pairs={{0,6},{1,7},{2,4},{3,5},{4,2},{5,3},{6,0},{7,1},{8,14},{9,15},{10,... | collective-permute-start | bytes 294920 | tf_op jit(solution)/shard_map/ppermute | solution.py:444
  45.8 7.7 %collective-permute-start.23 = (f32[192,128]{1,0:T(8,128)S(1)}, f32[192,128]{1,0:T(8,128)S(1)}, u32[]{:S(2)}, u32[]{:S(2)}) collective-permute-start(f32[192,128]{1,0:T(8,128)S(1)} %slice_add_fusion), channel_id=1, source_target_pairs={{0,2},{1,3},{2,0},{3,1},{4,6},{5,7},{6,4},{7,5},{8,10},{9,11},{10,... | collective-permute-start | bytes 294920 | tf_op jit(solution)/shard_map/ppermute | solution.py:400
  48.5 5.1 %collective-permute-start.22 = (f32[192,128]{1,0:T(8,128)S(1)}, f32[192,128]{1,0:T(8,128)S(1)}, u32[]{:S(2)}, u32[]{:S(2)}) collective-permute-start(f32[192,128]{1,0:T(8,128)S(1)} %slice_add_fusion), channel_id=1, source_target_pairs={{0,4},{4,0},{8,12},{12,8},{16,20},{20,16},{24,28},{28,24},{1,5},{5... | collective-permute-start | bytes 294920 | tf_op jit(solution)/shard_map/ppermute | solution.py:400
  53.6 4.7 %collective-permute-start.25 = (f32[192,128]{1,0:T(8,128)S(1)}, f32[192,128]{1,0:T(8,128)S(1)}, u32[]{:S(2)}, u32[]{:S(2)}) collective-permute-start(f32[192,128]{1,0:T(8,128)S(1)} %add_add_fusion), channel_id=1, source_target_pairs={{0,8},{4,12},{8,0},{12,4},{16,24},{20,28},{24,16},{28,20},{1,9},{5... | collective-permute-start | bytes 294920 | tf_op jit(solution)/shard_map/ppermute | solution.py:400
  55.0 5.0 %collective-permute-start.19 = (f32[256,128]{1,0:T(8,128)S(1)}, f32[256,128]{1,0:T(8,128)S(1)}, u32[]{:S(2)}, u32[]{:S(2)}) collective-permute-start(f32[256,128]{1,0:T(8,128)S(1)} %get-tuple-element.52), channel_id=1, source_target_pairs={{0,4},{1,2},{2,1},{3,7},{4,0},{5,6},{6,5},{7,3},{8,12},{9,10},{10,... | collective-permute-start | bytes 393224 | tf_op jit(solution)/shard_map/ppermute | solution.py:412
  58.3 7.4 %collective-permute-start.26 = (f32[192,128]{1,0:T(8,128)S(1)}, f32[192,128]{1,0:T(8,128)S(1)}, u32[]{:S(2)}, u32[]{:S(2)}) collective-permute-start(f32[192,128]{1,0:T(8,128)S(1)} %add.78), channel_id=1, source_target_pairs={{0,16},{4,20},{8,24},{12,28},{16,0},{20,4},{24,8},{28,12},{1,17},{... | collective-permute-start | bytes 294920 | tf_op jit(solution)/shard_map/ppermute | solution.py:400
  60.1 5.8 %collective-permute-start.20 = (f32[2,64,128]{2,1,0:T(8,128)S(1)}, f32[2,64,128]{2,1,0:T(8,128)S(1)}, u32[]{:S(2)}, u32[]{:S(2)}) collective-permute-start(f32[2,64,128]{2,1,0:T(8,128)S(1)} %get-tuple-element.54), channel_id=1, source_target_pairs={{0,4},{4,0},{8,12},{12,8},{16,20},{20,16},{24,28},{28,24},{1,5},{5... | collective-permute-start | bytes 196616 | tf_op jit(solution)/shard_map/ppermute | solution.py:400
  60.9 5.0 %collective-permute-start.21 = (f32[2,64,128]{2,1,0:T(8,128)S(1)}, f32[2,64,128]{2,1,0:T(8,128)S(1)}, u32[]{:S(2)}, u32[]{:S(2)}) collective-permute-start(f32[2,64,128]{2,1,0:T(8,128)S(1)} %get-tuple-element.55), channel_id=1, source_target_pairs={{0,1},{1,0},{2,3},{3,2},{4,8},{5,9},{6,10},{7,11},{8,4},{9,5},{10,... | collective-permute-start | bytes 196616 | tf_op jit(solution)/shard_map/ppermute | solution.py:424
  65.8 1.3 %collective-permute-start.27 = (f32[2,64,128]{2,1,0:T(8,128)S(1)}, f32[2,64,128]{2,1,0:T(8,128)S(1)}, u32[]{:S(2)}, u32[]{:S(2)}) collective-permute-start(f32[2,64,128]{2,1,0:T(8,128)S(1)} %fusion.1.mine), channel_id=1, source_target_pairs={{0,1},{1,0},{2,3},{3,2},{4,5},{5,4},{6,7},{7,6},{8,9},{9,8},{10,11... | collective-permute-start | bytes 196616 | tf_op jit(solution)/shard_map/ppermute | solution.py:400

commit v8 on v7

--- a/solution.py
+++ b/solution.py
@@ -563,6 +563,7 @@
             "s",
             (metas, current),
             scratch=((tall_rows + 2 * width + TILE, width),),
+            moved=8 * MIB,
         )
         part = kept + core[: 3 * half]
         if last:
@@ -594,6 +595,7 @@
                 ((2, tall_rows, side), (tall_rows, width), (tall_rows, width)),
                 "",
                 (tall, sent_1, sent_2, got_1, got_2, weight, part[:TILE]),
+                moved=8 * MIB,
             )
             near = swap(near, "col", 1)
             far_1, far_2 = swap_far(far[: tall_rows // 2]), swap_far(far[tall_rows // 2 :])

time: 68.1 us -> 68.1 us (level)
  no operation moved by 1% of the time
where the time goes in v8:
time: 68.1 us; the launch traced here: 67.9 us
  waiting for transfers between devices  29.3 us (43%)
  starting transfers between devices  24.4 us (36%)
  Pallas kernels  10.8 us (16%)
  local copies, waits for them, and re-layouts  2.19 us (3%)
  between operations  1.04 us (2%)
    ppermute x17, waiting for transfers between devices, swap(): lax.ppermute(value, axis, [(i, i ^ bit) for i in range(lax.axis_size(axis...  22.3 us
    ppermute x17, starting transfers between devices, swap(): lax.ppermute(value, axis, [(i, i ^ bit) for i in range(lax.axis_size(axis...  16.8 us
    pallas_call x13, Pallas kernels, call(): pl.pallas_call(kernel, out_shape=tuple((jax.ShapeDtypeStruct(shape, jnp.f...  10.8 us
    ppermute x6, starting transfers between devices, swap_far(): return lax.ppermute(value, AXES, pairs)  6.23 us
    ppermute x6, waiting for transfers between devices, swap_far(): return lax.ppermute(value, AXES, pairs)  4.97 us
    ppermute x2, waiting for transfers between devices, swap_both(): return lax.ppermute(value, AXES, pairs)  1.96 us
  transfers between devices with their start and end apart: 28, of which 18 were waited for; matrix products, arithmetic and copies ran while one was open for 3% of the time, Pallas kernels for 6%

profile of v8, /device:TPU:0, one launch (start us, length us, event | category | flops | bytes accessed | tf_op | source)
XLA Modules:
  0.0 67.9 jit_solution(1483591632999775802)
XLA Ops:
  0.6 1.5 %shard_map.77 = (f32[136,128]{1,0:T(8,128)}, f32[136,128]{1,0:T(8,128)}, f32[8,128]{1,0:T(8,128)}) custom-call(f32[2,128,128]{2,1,0:T(8,128)} %tile.5, s32[2,2,4]{2,1,0:T(2,128)} %bitcast.32, s32[1,2]{1,0:T(1,128)} %bitcast.33), custom_call_target="tpu_custom_call" | custom-call | flops 1000000 | bytes 1048576 | tf_op jit(solution)/shard_map/pallas_call | solution.py:388
  2.2 3.0 %collective-permute-start = (f32[136,128]{1,0:T(8,128)}, f32[136,128]{1,0:T(8,128)S(1)}, u32[]{:S(2)}, u32[]{:S(2)}) collective-permute-start(f32[136,128]{1,0:T(8,128)} %get-tuple-element.31), channel_id=1, source_target_pairs={{0,4},{4,0},{8,12},{12,8},{16,20},{20,16},{24,28},{28,24},{1,5},{5... | collective-permute-start | bytes 208904 | tf_op jit(solution)/shard_map/ppermute | solution.py:400
  5.2 1.1 %slice_bitcast_fusion = (f32[4,128,128]{2,1,0:T(8,128)S(1)}, f32[4,128,128]{2,1,0:T(8,128)S(1)}) fusion(f32[1,1,2,4,128,128]{5,4,3,2,1,0:T(8,128)} %param.10), kind=kLoop, calls=%fused_computation | loop fusion | bytes 1048576 | tf_op jit(solution)/shard_map/squeeze | solution.py:548
  6.4 2.4 %collective-permute-done.first = f32[136,128]{1,0:T(8,128)S(1)} collective-permute-done((f32[136,128]{1,0:T(8,128)}, f32[136,128]{1,0:T(8,128)S(1)}, u32[]{:S(2)}, u32[]{:S(2)}) %collective-permute-start) | collective-permute-done | bytes 69664 | tf_op jit(solution)/shard_map/ppermute | solution.py:400
  8.8 0.1 shard_map.79
  8.9 2.4 %collective-permute-start.3 = (f32[208,128]{1,0:T(8,128)S(1)}, f32[208,128]{1,0:T(8,128)S(1)}, u32[]{:S(2)}, u32[]{:S(2)}) collective-permute-start(f32[208,128]{1,0:T(8,128)S(1)} %shard_map.79), channel_id=1, source_target_pairs={{0,4},{1,2},{2,1},{3,7},{4,0},{5,6},{6,5},{7,3},{8,12},{9,10},{10,... | collective-permute-start | bytes 319496 | tf_op jit(solution)/shard_map/ppermute | solution.py:412
  11.3 0.0 collective-permute-done.1.second
  11.3 0.1 shard_map.78
  11.4 0.1 collective-permute-start.4
  11.6 0.1 copy.14
  11.7 0.0 collective-permute-start.2
  11.7 3.8 %collective-permute-done.4 = f32[72,128]{1,0:T(8,128)S(1)} collective-permute-done((f32[72,128]{1,0:T(8,128)S(1)}, f32[72,128]{1,0:T(8,128)S(1)}, u32[]{:S(2)}, u32[]{:S(2)}) %collective-permute-start.4) | collective-permute-done | bytes 36896 | tf_op jit(solution)/shard_map/ppermute | solution.py:412
  15.6 0.1 copy.17
  15.7 0.5 shard_map.80
  16.2 0.4 copy-done.1
  16.6 0.1 copy-done.3
  16.7 2.0 %shard_map.81 = (f32[448,128]{1,0:T(8,128)S(1)}, f32[256,128]{1,0:T(8,128)S(1)}, f32[192,128]{1,0:T(8,128)S(1)}, f32[2,256,128]{2,1,0:T(8,128)S(1)}) custom-call(s32[6,4]{1,0:T(8,128)S(1)} %slice_convert_fusion.scan, f32[4,2,128,128]{3,2,1,0:T(8,128)S(1)} %get-tuple-element.36.wins, f32[128,128]{1,0:T(8,128)S(1)} %get-tuple-element.37.win_weight, ...), custom_call_target="tpu_custom_call" | custom-call | flops 805306368 | bytes 4194304 | tf_op jit(solution)/shard_map/pallas_call | solution.py:388
  18.7 0.1 collective-permute-start.5
  18.8 0.1 copy.16
  18.9 0.9 %collective-permute-start.6 = (f32[256,128]{1,0:T(8,128)S(1)}, f32[256,128]{1,0:T(8,128)S(1)}, u32[]{:S(2)}, u32[]{:S(2)}) collective-permute-start(f32[256,128]{1,0:T(8,128)S(1)} %get-tuple-element.40), channel_id=1, source_target_pairs={{0,4},{1,2},{2,1},{3,7},{4,0},{5,6},{6,5},{7,3},{8,12},{9,10},{10,... | collective-permute-start | bytes 393224 | tf_op jit(solution)/shard_map/ppermute | solution.py:412
  19.8 0.4 collective-permute-done.5.near
  20.3 1.2 %collective-permute-start.11 = (f32[192,128]{1,0:T(8,128)S(1)}, f32[192,128]{1,0:T(8,128)S(1)}, u32[]{:S(2)}, u32[]{:S(2)}) collective-permute-start(f32[192,128]{1,0:T(8,128)S(1)} %slice_add_fusion.1), channel_id=1, source_target_pairs={{0,6},{1,7},{2,4},{3,5},{4,2},{5,3},{6,0},{7,1},{8,14},{9,15},{10,... | collective-permute-start | bytes 294920 | tf_op jit(solution)/shard_map/ppermute | solution.py:444
  21.5 1.2 %collective-permute-start.10 = (f32[192,128]{1,0:T(8,128)S(1)}, f32[192,128]{1,0:T(8,128)S(1)}, u32[]{:S(2)}, u32[]{:S(2)}) collective-permute-start(f32[192,128]{1,0:T(8,128)S(1)} %slice_add_fusion.1), channel_id=1, source_target_pairs={{0,2},{1,3},{2,0},{3,1},{4,6},{5,7},{6,4},{7,5},{8,10},{9,11},{10,... | collective-permute-start | bytes 294920 | tf_op jit(solution)/shard_map/ppermute | solution.py:400
  22.7 1.1 %collective-permute-start.9 = (f32[192,128]{1,0:T(8,128)S(1)}, f32[192,128]{1,0:T(8,128)S(1)}, u32[]{:S(2)}, u32[]{:S(2)}) collective-permute-start(f32[192,128]{1,0:T(8,128)S(1)} %slice_add_fusion.1), channel_id=1, source_target_pairs={{0,4},{4,0},{8,12},{12,8},{16,20},{20,16},{24,28},{28,24},{1,5},{5... | collective-permute-start | bytes 294920 | tf_op jit(solution)/shard_map/ppermute | solution.py:400
  23.9 0.1 copy.15
  24.0 0.1 convert_element_type.10.metas
  24.1 1.4 %shard_map.83.weight = f32[256,128]{1,0:T(8,128)S(1)} custom-call(s32[9,24]{1,0:T(8,128)S(1)} %convert_element_type.10.metas, f32[2,128,128]{2,1,0:T(8,128)S(1)} %copy-done.1), custom_call_target="tpu_custom_call" | custom-call | flops 1000000 | bytes 8388608 | tf_op jit(solution)/shard_map/pallas_call | solution.py:388
  25.5 0.1 shard_map.82
  25.6 1.0 %collective-permute-start.7 = (f32[2,128,128]{2,1,0:T(8,128)S(1)}, f32[2,128,128]{2,1,0:T(8,128)S(1)}, u32[]{:S(2)}, u32[]{:S(2)}) collective-permute-start(f32[2,128,128]{2,1,0:T(8,128)S(1)} %get-tuple-element.41.sent_1), channel_id=1, source_target_pairs={{0,4},{4,0},{8,12},{12,8},{16,20},{20,16},{24,28},{28,24},{1,5},{5... | collective-permute-start | bytes 393224 | tf_op jit(solution)/shard_map/ppermute | solution.py:400
  26.6 0.3 collective-permute-done.11
  26.9 1.3 %collective-permute-done.10 = f32[192,128]{1,0:T(8,128)S(1)} collective-permute-done((f32[192,128]{1,0:T(8,128)S(1)}, f32[192,128]{1,0:T(8,128)S(1)}, u32[]{:S(2)}, u32[]{:S(2)}) %collective-permute-start.10) | collective-permute-done | bytes 98336 | tf_op jit(solution)/shard_map/ppermute | solution.py:400
  28.2 0.5 collective-permute-done.9
  28.7 1.0 %collective-permute-start.12 = (f32[192,128]{1,0:T(8,128)S(1)}, f32[192,128]{1,0:T(8,128)S(1)}, u32[]{:S(2)}, u32[]{:S(2)}) collective-permute-start(f32[192,128]{1,0:T(8,128)S(1)} %add_add_fusion.1), channel_id=1, source_target_pairs={{0,8},{4,12},{8,0},{12,4},{16,24},{20,28},{24,16},{28,20},{1,9},{5... | collective-permute-start | bytes 294920 | tf_op jit(solution)/shard_map/ppermute | solution.py:400
  29.7 4.5 %collective-permute-done.12 = f32[192,128]{1,0:T(8,128)S(1)} collective-permute-done((f32[192,128]{1,0:T(8,128)S(1)}, f32[192,128]{1,0:T(8,128)S(1)}, u32[]{:S(2)}, u32[]{:S(2)}) %collective-permute-start.12) | collective-permute-done | bytes 98336 | tf_op jit(solution)/shard_map/ppermute | solution.py:400
  34.2 2.0 %collective-permute-start.16 = (f32[192,128]{1,0:T(8,128)S(1)}, f32[192,128]{1,0:T(8,128)S(1)}, u32[]{:S(2)}, u32[]{:S(2)}) collective-permute-start(f32[192,128]{1,0:T(8,128)S(1)} %add.69), channel_id=1, source_target_pairs={{0,16},{4,20},{8,24},{12,28},{16,0},{20,4},{24,8},{28,12},{1,17},{... | collective-permute-start | bytes 294920 | tf_op jit(solution)/shard_map/ppermute | solution.py:400
  36.3 0.2 shard_map.84
  36.5 0.4 collective-permute-start.14
  36.9 1.7 %collective-permute-start.15 = (f32[128,128]{1,0:T(8,128)S(1)}, f32[128,128]{1,0:T(8,128)S(1)}, u32[]{:S(2)}, u32[]{:S(2)}) collective-permute-start(f32[128,128]{1,0:T(8,128)S(1)} %get-tuple-element.69), channel_id=1, source_target_pairs={{0,4},{1,2},{2,1},{3,7},{4,0},{5,6},{6,5},{7,3},{8,12},{9,10},{10,... | collective-permute-start | bytes 196616 | tf_op jit(solution)/shard_map/ppermute | solution.py:412
  38.6 2.0 %collective-permute-done.16 = f32[192,128]{1,0:T(8,128)S(1)} collective-permute-done((f32[192,128]{1,0:T(8,128)S(1)}, f32[192,128]{1,0:T(8,128)S(1)}, u32[]{:S(2)}, u32[]{:S(2)}) %collective-permute-start.16) | collective-permute-done | bytes 98336 | tf_op jit(solution)/shard_map/ppermute | solution.py:400
  40.6 0.1 collective-permute-start.17
  40.7 0.1 collective-permute-done.14
  40.8 0.7 %collective-permute-done.15 = f32[128,128]{1,0:T(8,128)S(1)} collective-permute-done((f32[128,128]{1,0:T(8,128)S(1)}, f32[128,128]{1,0:T(8,128)S(1)}, u32[]{:S(2)}, u32[]{:S(2)}) %collective-permute-start.15) | collective-permute-done | bytes 65568 | tf_op jit(solution)/shard_map/ppermute | solution.py:412
  41.5 0.5 shard_map.85
  42.0 2.1 %shard_map.86 = (f32[448,128]{1,0:T(8,128)S(1)}, f32[256,128]{1,0:T(8,128)S(1)}, f32[192,128]{1,0:T(8,128)S(1)}, f32[2,256,128]{2,1,0:T(8,128)S(1)}) custom-call(s32[6,4]{1,0:T(8,128)S(1)} %slice_convert_fusion.scan, f32[4,2,128,128]{3,2,1,0:T(8,128)S(1)} %get-tuple-element.48.wins, f32[128,128]{1,0:T(8,128)S(1)} %get-tuple-element.49.win_weight, ...), custom_call_target="tpu_custom_call" | custom-call | flops 805306368 | bytes 4194304 | tf_op jit(solution)/shard_map/pallas_call | solution.py:388
  44.1 0.2 collective-permute-start.18
  44.3 1.4 %collective-permute-done.18.near = f32[448,128]{1,0:T(8,128)S(1)} collective-permute-done((f32[448,128]{1,0:T(8,128)S(1)}, f32[448,128]{1,0:T(8,128)S(1)}, u32[]{:S(2)}, u32[]{:S(2)}) %collective-permute-start.18) | collective-permute-done | bytes 229408 | tf_op jit(solution)/shard_map/ppermute | solution.py:400
  45.7 0.1 collective-permute-start.24
  45.8 2.8 %collective-permute-start.23 = (f32[192,128]{1,0:T(8,128)S(1)}, f32[192,128]{1,0:T(8,128)S(1)}, u32[]{:S(2)}, u32[]{:S(2)}) collective-permute-start(f32[192,128]{1,0:T(8,128)S(1)} %slice_add_fusion), channel_id=1, source_target_pairs={{0,2},{1,3},{2,0},{3,1},{4,6},{5,7},{6,4},{7,5},{8,10},{9,11},{10,... | collective-permute-start | bytes 294920 | tf_op jit(solution)/shard_map/ppermute | solution.py:400
  48.5 0.7 %collective-permute-start.22 = (f32[192,128]{1,0:T(8,128)S(1)}, f32[192,128]{1,0:T(8,128)S(1)}, u32[]{:S(2)}, u32[]{:S(2)}) collective-permute-start(f32[192,128]{1,0:T(8,128)S(1)} %slice_add_fusion), channel_id=1, source_target_pairs={{0,4},{4,0},{8,12},{12,8},{16,20},{20,16},{24,28},{28,24},{1,5},{5... | collective-permute-start | bytes 294920 | tf_op jit(solution)/shard_map/ppermute | solution.py:400
  49.2 1.4 %shard_map.88.weight = f32[256,128]{1,0:T(8,128)S(1)} custom-call(s32[9,24]{1,0:T(8,128)S(1)} %convert_element_type.10.metas, f32[2,128,128]{2,1,0:T(8,128)S(1)} %pad_maximum_fusion.probe), custom_call_target="tpu_custom_call" | custom-call | flops 1000000 | bytes 8388608 | tf_op jit(solution)/shard_map/pallas_call | solution.py:388
  50.6 1.7 %collective-permute-done.24 = f32[192,128]{1,0:T(8,128)S(1)} collective-permute-done((f32[192,128]{1,0:T(8,128)S(1)}, f32[192,128]{1,0:T(8,128)S(1)}, u32[]{:S(2)}, u32[]{:S(2)}) %collective-permute-start.24) | collective-permute-done | bytes 98336 | tf_op jit(solution)/shard_map/ppermute | solution.py:444
  52.3 1.2 %collective-permute-done.23 = f32[192,128]{1,0:T(8,128)S(1)} collective-permute-done((f32[192,128]{1,0:T(8,128)S(1)}, f32[192,128]{1,0:T(8,128)S(1)}, u32[]{:S(2)}, u32[]{:S(2)}) %collective-permute-start.23) | collective-permute-done | bytes 98336 | tf_op jit(solution)/shard_map/ppermute | solution.py:400
  53.4 0.1 collective-permute-done.22
  53.6 1.4 %collective-permute-start.25 = (f32[192,128]{1,0:T(8,128)S(1)}, f32[192,128]{1,0:T(8,128)S(1)}, u32[]{:S(2)}, u32[]{:S(2)}) collective-permute-start(f32[192,128]{1,0:T(8,128)S(1)} %add_add_fusion), channel_id=1, source_target_pairs={{0,8},{4,12},{8,0},{12,4},{16,24},{20,28},{24,16},{28,20},{1,9},{5... | collective-permute-start | bytes 294920 | tf_op jit(solution)/shard_map/ppermute | solution.py:400
  55.0 0.7 %collective-permute-start.19 = (f32[256,128]{1,0:T(8,128)S(1)}, f32[256,128]{1,0:T(8,128)S(1)}, u32[]{:S(2)}, u32[]{:S(2)}) collective-permute-start(f32[256,128]{1,0:T(8,128)S(1)} %get-tuple-element.52), channel_id=1, source_target_pairs={{0,4},{1,2},{2,1},{3,7},{4,0},{5,6},{6,5},{7,3},{8,12},{9,10},{10,... | collective-permute-start | bytes 393224 | tf_op jit(solution)/shard_map/ppermute | solution.py:412
  55.8 2.5 %collective-permute-done.25 = f32[192,128]{1,0:T(8,128)S(1)} collective-permute-done((f32[192,128]{1,0:T(8,128)S(1)}, f32[192,128]{1,0:T(8,128)S(1)}, u32[]{:S(2)}, u32[]{:S(2)}) %collective-permute-start.25) | collective-permute-done | bytes 98336 | tf_op jit(solution)/shard_map/ppermute | solution.py:400
  58.3 1.3 %collective-permute-start.26 = (f32[192,128]{1,0:T(8,128)S(1)}, f32[192,128]{1,0:T(8,128)S(1)}, u32[]{:S(2)}, u32[]{:S(2)}) collective-permute-start(f32[192,128]{1,0:T(8,128)S(1)} %add.78), channel_id=1, source_target_pairs={{0,16},{4,20},{8,24},{12,28},{16,0},{20,4},{24,8},{28,12},{1,17},{... | collective-permute-start | bytes 294920 | tf_op jit(solution)/shard_map/ppermute | solution.py:400
  59.7 0.4 collective-permute-done.19.far
  60.0 0.1 shard_map.87
  60.2 0.8 %collective-permute-start.20 = (f32[2,64,128]{2,1,0:T(8,128)S(1)}, f32[2,64,128]{2,1,0:T(8,128)S(1)}, u32[]{:S(2)}, u32[]{:S(2)}) collective-permute-start(f32[2,64,128]{2,1,0:T(8,128)S(1)} %get-tuple-element.54), channel_id=1, source_target_pairs={{0,4},{4,0},{8,12},{12,8},{16,20},{20,16},{24,28},{28,24},{1,5},{5... | collective-permute-start | bytes 196616 | tf_op jit(solution)/shard_map/ppermute | solution.py:400
  60.9 4.8 %collective-permute-done.26 = f32[192,128]{1,0:T(8,128)S(1)} collective-permute-done((f32[192,128]{1,0:T(8,128)S(1)}, f32[192,128]{1,0:T(8,128)S(1)}, u32[]{:S(2)}, u32[]{:S(2)}) %collective-permute-start.26) | collective-permute-done | bytes 98336 | tf_op jit(solution)/shard_map/ppermute | solution.py:400
  65.8 0.1 collective-permute-start.27
  65.9 1.2 %collective-permute-done.27.other = f32[2,64,128]{2,1,0:T(8,128)S(1)} collective-permute-done((f32[2,64,128]{2,1,0:T(8,128)S(1)}, f32[2,64,128]{2,1,0:T(8,128)S(1)}, u32[]{:S(2)}, u32[]{:S(2)}) %collective-permute-start.27) | collective-permute-done | bytes 65568 | tf_op jit(solution)/shard_map/ppermute | solution.py:400
  67.2 0.7 %shard_map.89 = (f32[2,128,128]{2,1,0:T(8,128)}, f32[2,128,128]{2,1,0:T(8,128)}) custom-call(f32[2,256,128]{2,1,0:T(8,128)S(1)} %get-tuple-element.45.tall, f32[2,128,128]{2,1,0:T(8,128)S(1)} %get-tuple-element.53.middle, f32[2,64,128]{2,1,0:T(8,128)S(1)} %collective-permute-done.20.got_1, f32[2,64,128]{2,1,0:T(8,128)S(1)} %collective-permute-done.21.got_2, ...), custom_call_target="tpu_custom_call" | custom-call | flops 1000000 | bytes 4194304 | tf_op jit(solution)/shard_map/pallas_call | solution.py:388
  (51 shorter events, 0.4 us)
Async XLA Ops:
  2.2 6.6 %collective-permute-start = (f32[136,128]{1,0:T(8,128)}, f32[136,128]{1,0:T(8,128)S(1)}, u32[]{:S(2)}, u32[]{:S(2)}) collective-permute-start(f32[136,128]{1,0:T(8,128)} %get-tuple-element.31), channel_id=1, source_target_pairs={{0,4},{4,0},{8,12},{12,8},{16,20},{20,16},{24,28},{28,24},{1,5},{5... | collective-permute-start | bytes 208904 | tf_op jit(solution)/shard_map/ppermute | solution.py:400
  5.2 6.1 %collective-permute-start.1 = (f32[136,128]{1,0:T(8,128)}, f32[136,128]{1,0:T(8,128)S(1)}, u32[]{:S(2)}, u32[]{:S(2)}) collective-permute-start(f32[136,128]{1,0:T(8,128)} %get-tuple-element.32), channel_id=1, source_target_pairs={{0,1},{1,0},{2,3},{3,2},{4,8},{5,9},{6,10},{7,11},{8,4},{9,5},{10,... | collective-permute-start | bytes 208904 | tf_op jit(solution)/shard_map/ppermute | solution.py:424
  5.2 1.1 %copy-start.2 = (f32[8,128]{1,0:T(8,128)S(1)}, f32[8,128]{1,0:T(8,128)}, u32[]{:S(2)}) copy-start(f32[8,128]{1,0:T(8,128)} %get-tuple-element.30.meta) | copy-start | bytes 12292
  5.2 3.5 %copy-start = (f32[2,128,128]{2,1,0:T(8,128)S(1)}, f32[2,128,128]{2,1,0:T(8,128)}, u32[]{:S(2)}) copy-start(f32[2,128,128]{2,1,0:T(8,128)} %tile.5) | copy-start | bytes 393220
  8.9 6.6 %collective-permute-start.3 = (f32[208,128]{1,0:T(8,128)S(1)}, f32[208,128]{1,0:T(8,128)S(1)}, u32[]{:S(2)}, u32[]{:S(2)}) collective-permute-start(f32[208,128]{1,0:T(8,128)S(1)} %shard_map.79), channel_id=1, source_target_pairs={{0,4},{1,2},{2,1},{3,7},{4,0},{5,6},{6,5},{7,3},{8,12},{9,10},{10,... | collective-permute-start | bytes 319496 | tf_op jit(solution)/shard_map/ppermute | solution.py:412
  11.4 4.0 %collective-permute-start.4 = (f32[72,128]{1,0:T(8,128)S(1)}, f32[72,128]{1,0:T(8,128)S(1)}, u32[]{:S(2)}, u32[]{:S(2)}) collective-permute-start(f32[72,128]{1,0:T(8,128)S(1)} %get-tuple-element.35), channel_id=1, source_target_pairs={{0,4},{1,2},{2,1},{3,7},{4,0},{5,6},{6,5},{7,3},{8,12},{9,10},{10,... | collective-permute-start | bytes 110600 | tf_op jit(solution)/shard_map/ppermute | solution.py:412
  11.7 4.0 %collective-permute-start.2 = (f32[280,128]{1,0:T(8,128)S(1)}, f32[280,128]{1,0:T(8,128)S(1)}, u32[]{:S(2)}, u32[]{:S(2)}) collective-permute-start(f32[280,128]{1,0:T(8,128)S(1)} %get-tuple-element.34), channel_id=1, source_target_pairs={{0,1},{1,0},{2,3},{3,2},{4,5},{5,4},{6,7},{7,6},{8,9},{9,8},{10,11... | collective-permute-start | bytes 430088 | tf_op jit(solution)/shard_map/ppermute | solution.py:400
  15.7 0.9 %copy-start.1 = (f32[2,128,128]{2,1,0:T(8,128)S(1)}, f32[2,128,128]{2,1,0:T(8,128)}, u32[]{:S(2)}) copy-start(f32[2,128,128]{2,1,0:T(8,128)} %probe.3) | copy-start | bytes 393220
  15.7 1.0 %copy-start.3 = (bf16[6,128,128]{2,1,0:T(8,128)(2,1)S(1)}, bf16[6,128,128]{2,1,0:T(8,128)(2,1)}, u32[]{:S(2)}) copy-start(bf16[6,128,128]{2,1,0:T(8,128)(2,1)} %constant.41.clone.tables) | copy-start | bytes 589828
  18.7 1.6 %collective-permute-start.5 = (f32[448,128]{1,0:T(8,128)S(1)}, f32[448,128]{1,0:T(8,128)S(1)}, u32[]{:S(2)}, u32[]{:S(2)}) collective-permute-start(f32[448,128]{1,0:T(8,128)S(1)} %get-tuple-element.39), channel_id=1, source_target_pairs={{0,1},{1,0},{2,3},{3,2},{4,5},{5,4},{6,7},{7,6},{8,9},{9,8},{10,11... | collective-permute-start | bytes 688136 | tf_op jit(solution)/shard_map/ppermute | solution.py:400
  18.9 6.5 %collective-permute-start.6 = (f32[256,128]{1,0:T(8,128)S(1)}, f32[256,128]{1,0:T(8,128)S(1)}, u32[]{:S(2)}, u32[]{:S(2)}) collective-permute-start(f32[256,128]{1,0:T(8,128)S(1)} %get-tuple-element.40), channel_id=1, source_target_pairs={{0,4},{1,2},{2,1},{3,7},{4,0},{5,6},{6,5},{7,3},{8,12},{9,10},{10,... | collective-permute-start | bytes 393224 | tf_op jit(solution)/shard_map/ppermute | solution.py:412
  20.3 6.6 %collective-permute-start.11 = (f32[192,128]{1,0:T(8,128)S(1)}, f32[192,128]{1,0:T(8,128)S(1)}, u32[]{:S(2)}, u32[]{:S(2)}) collective-permute-start(f32[192,128]{1,0:T(8,128)S(1)} %slice_add_fusion.1), channel_id=1, source_target_pairs={{0,6},{1,7},{2,4},{3,5},{4,2},{5,3},{6,0},{7,1},{8,14},{9,15},{10,... | collective-permute-start | bytes 294920 | tf_op jit(solution)/shard_map/ppermute | solution.py:444
  21.5 6.7 %collective-permute-start.10 = (f32[192,128]{1,0:T(8,128)S(1)}, f32[192,128]{1,0:T(8,128)S(1)}, u32[]{:S(2)}, u32[]{:S(2)}) collective-permute-start(f32[192,128]{1,0:T(8,128)S(1)} %slice_add_fusion.1), channel_id=1, source_target_pairs={{0,2},{1,3},{2,0},{3,1},{4,6},{5,7},{6,4},{7,5},{8,10},{9,11},{10,... | collective-permute-start | bytes 294920 | tf_op jit(solution)/shard_map/ppermute | solution.py:400
  22.7 6.0 %collective-permute-start.9 = (f32[192,128]{1,0:T(8,128)S(1)}, f32[192,128]{1,0:T(8,128)S(1)}, u32[]{:S(2)}, u32[]{:S(2)}) collective-permute-start(f32[192,128]{1,0:T(8,128)S(1)} %slice_add_fusion.1), channel_id=1, source_target_pairs={{0,4},{4,0},{8,12},{12,8},{16,20},{20,16},{24,28},{28,24},{1,5},{5... | collective-permute-start | bytes 294920 | tf_op jit(solution)/shard_map/ppermute | solution.py:400
  25.6 10.7 %collective-permute-start.7 = (f32[2,128,128]{2,1,0:T(8,128)S(1)}, f32[2,128,128]{2,1,0:T(8,128)S(1)}, u32[]{:S(2)}, u32[]{:S(2)}) collective-permute-start(f32[2,128,128]{2,1,0:T(8,128)S(1)} %get-tuple-element.41.sent_1), channel_id=1, source_target_pairs={{0,4},{4,0},{8,12},{12,8},{16,20},{20,16},{24,28},{28,24},{1,5},{5... | collective-permute-start | bytes 393224 | tf_op jit(solution)/shard_map/ppermute | solution.py:400
  26.6 9.7 %collective-permute-start.8 = (f32[2,128,128]{2,1,0:T(8,128)S(1)}, f32[2,128,128]{2,1,0:T(8,128)S(1)}, u32[]{:S(2)}, u32[]{:S(2)}) collective-permute-start(f32[2,128,128]{2,1,0:T(8,128)S(1)} %get-tuple-element.42.sent_2), channel_id=1, source_target_pairs={{0,1},{1,0},{2,3},{3,2},{4,8},{5,9},{6,10},{7,11},{8,4},{9,5},{10,... | collective-permute-start | bytes 393224 | tf_op jit(solution)/shard_map/ppermute | solution.py:424
  28.7 5.5 %collective-permute-start.12 = (f32[192,128]{1,0:T(8,128)S(1)}, f32[192,128]{1,0:T(8,128)S(1)}, u32[]{:S(2)}, u32[]{:S(2)}) collective-permute-start(f32[192,128]{1,0:T(8,128)S(1)} %add_add_fusion.1), channel_id=1, source_target_pairs={{0,8},{4,12},{8,0},{12,4},{16,24},{20,28},{24,16},{28,20},{1,9},{5... | collective-permute-start | bytes 294920 | tf_op jit(solution)/shard_map/ppermute | solution.py:400
  34.2 6.3 %collective-permute-start.16 = (f32[192,128]{1,0:T(8,128)S(1)}, f32[192,128]{1,0:T(8,128)S(1)}, u32[]{:S(2)}, u32[]{:S(2)}) collective-permute-start(f32[192,128]{1,0:T(8,128)S(1)} %add.69), channel_id=1, source_target_pairs={{0,16},{4,20},{8,24},{12,28},{16,0},{20,4},{24,8},{28,12},{1,17},{... | collective-permute-start | bytes 294920 | tf_op jit(solution)/shard_map/ppermute | solution.py:400
  36.5 4.3 %collective-permute-start.14 = (f32[128,128]{1,0:T(8,128)S(1)}, f32[128,128]{1,0:T(8,128)S(1)}, u32[]{:S(2)}, u32[]{:S(2)}) collective-permute-start(f32[128,128]{1,0:T(8,128)S(1)} %get-tuple-element.68), channel_id=1, source_target_pairs={{0,4},{1,2},{2,1},{3,7},{4,0},{5,6},{6,5},{7,3},{8,12},{9,10},{10,... | collective-permute-start | bytes 196616 | tf_op jit(solution)/shard_map/ppermute | solution.py:412
  36.9 4.6 %collective-permute-start.15 = (f32[128,128]{1,0:T(8,128)S(1)}, f32[128,128]{1,0:T(8,128)S(1)}, u32[]{:S(2)}, u32[]{:S(2)}) collective-permute-start(f32[128,128]{1,0:T(8,128)S(1)} %get-tuple-element.69), channel_id=1, source_target_pairs={{0,4},{1,2},{2,1},{3,7},{4,0},{5,6},{6,5},{7,3},{8,12},{9,10},{10,... | collective-permute-start | bytes 196616 | tf_op jit(solution)/shard_map/ppermute | solution.py:412
  38.5 3.0 %collective-permute-start.13 = (f32[256,128]{1,0:T(8,128)S(1)}, f32[256,128]{1,0:T(8,128)S(1)}, u32[]{:S(2)}, u32[]{:S(2)}) collective-permute-start(f32[256,128]{1,0:T(8,128)S(1)} %get-tuple-element.46), channel_id=1, source_target_pairs={{0,1},{1,0},{2,3},{3,2},{4,5},{5,4},{6,7},{7,6},{8,9},{9,8},{10,11... | collective-permute-start | bytes 393224 | tf_op jit(solution)/shard_map/ppermute | solution.py:400
  40.6 1.4 %collective-permute-start.17 = (f32[2,64,128]{2,1,0:T(8,128)S(1)}, f32[2,64,128]{2,1,0:T(8,128)S(1)}, u32[]{:S(2)}, u32[]{:S(2)}) collective-permute-start(f32[2,64,128]{2,1,0:T(8,128)S(1)} %divide_add_fusion), channel_id=1, source_target_pairs={{0,1},{1,0},{2,3},{3,2},{4,5},{5,4},{6,7},{7,6},{8,9},{9,8},{10,11... | collective-permute-start | bytes 196616 | tf_op jit(solution)/shard_map/ppermute | solution.py:400
  44.1 1.6 %collective-permute-start.18 = (f32[448,128]{1,0:T(8,128)S(1)}, f32[448,128]{1,0:T(8,128)S(1)}, u32[]{:S(2)}, u32[]{:S(2)}) collective-permute-start(f32[448,128]{1,0:T(8,128)S(1)} %get-tuple-element.51), channel_id=1, source_target_pairs={{0,1},{1,0},{2,3},{3,2},{4,5},{5,4},{6,7},{7,6},{8,9},{9,8},{10,11... | collective-permute-start | bytes 688136 | tf_op jit(solution)/shard_map/ppermute | solution.py:400
  45.7 6.6 %collective-permute-start.24 = (f32[192,128]{1,0:T(8,128)S(1)}, f32[192,128]{1,0:T(8,128)S(1)}, u32[]{:S(2)}, u32[]{:S(2)}) collective-permute-start(f32[192,128]{1,0:T(8,128)S(1)} %slice_add_fusion), channel_id=1, source_target_pairs={{0,6},{1,7},{2,4},{3,5},{4,2},{5,3},{6,0},{7,1},{8,14},{9,15},{10,... | collective-permute-start | bytes 294920 | tf_op jit(solution)/shard_map/ppermute | solution.py:444
  45.8 7.7 %collective-permute-start.23 = (f32[192,128]{1,0:T(8,128)S(1)}, f32[192,128]{1,0:T(8,128)S(1)}, u32[]{:S(2)}, u32[]{:S(2)}) collective-permute-start(f32[192,128]{1,0:T(8,128)S(1)} %slice_add_fusion), channel_id=1, source_target_pairs={{0,2},{1,3},{2,0},{3,1},{4,6},{5,7},{6,4},{7,5},{8,10},{9,11},{10,... | collective-permute-start | bytes 294920 | tf_op jit(solution)/shard_map/ppermute | solution.py:400
  48.5 5.1 %collective-permute-start.22 = (f32[192,128]{1,0:T(8,128)S(1)}, f32[192,128]{1,0:T(8,128)S(1)}, u32[]{:S(2)}, u32[]{:S(2)}) collective-permute-start(f32[192,128]{1,0:T(8,128)S(1)} %slice_add_fusion), channel_id=1, source_target_pairs={{0,4},{4,0},{8,12},{12,8},{16,20},{20,16},{24,28},{28,24},{1,5},{5... | collective-permute-start | bytes 294920 | tf_op jit(solution)/shard_map/ppermute | solution.py:400
  53.6 4.7 %collective-permute-start.25 = (f32[192,128]{1,0:T(8,128)S(1)}, f32[192,128]{1,0:T(8,128)S(1)}, u32[]{:S(2)}, u32[]{:S(2)}) collective-permute-start(f32[192,128]{1,0:T(8,128)S(1)} %add_add_fusion), channel_id=1, source_target_pairs={{0,8},{4,12},{8,0},{12,4},{16,24},{20,28},{24,16},{28,20},{1,9},{5... | collective-permute-start | bytes 294920 | tf_op jit(solution)/shard_map/ppermute | solution.py:400
  55.0 5.0 %collective-permute-start.19 = (f32[256,128]{1,0:T(8,128)S(1)}, f32[256,128]{1,0:T(8,128)S(1)}, u32[]{:S(2)}, u32[]{:S(2)}) collective-permute-start(f32[256,128]{1,0:T(8,128)S(1)} %get-tuple-element.52), channel_id=1, source_target_pairs={{0,4},{1,2},{2,1},{3,7},{4,0},{5,6},{6,5},{7,3},{8,12},{9,10},{10,... | collective-permute-start | bytes 393224 | tf_op jit(solution)/shard_map/ppermute | solution.py:412
  58.3 7.4 %collective-permute-start.26 = (f32[192,128]{1,0:T(8,128)S(1)}, f32[192,128]{1,0:T(8,128)S(1)}, u32[]{:S(2)}, u32[]{:S(2)}) collective-permute-start(f32[192,128]{1,0:T(8,128)S(1)} %add.78), channel_id=1, source_target_pairs={{0,16},{4,20},{8,24},{12,28},{16,0},{20,4},{24,8},{28,12},{1,17},{... | collective-permute-start | bytes 294920 | tf_op jit(solution)/shard_map/ppermute | solution.py:400
  60.2 5.8 %collective-permute-start.20 = (f32[2,64,128]{2,1,0:T(8,128)S(1)}, f32[2,64,128]{2,1,0:T(8,128)S(1)}, u32[]{:S(2)}, u32[]{:S(2)}) collective-permute-start(f32[2,64,128]{2,1,0:T(8,128)S(1)} %get-tuple-element.54), channel_id=1, source_target_pairs={{0,4},{4,0},{8,12},{12,8},{16,20},{20,16},{24,28},{28,24},{1,5},{5... | collective-permute-start | bytes 196616 | tf_op jit(solution)/shard_map/ppermute | solution.py:400
  60.9 5.0 %collective-permute-start.21 = (f32[2,64,128]{2,1,0:T(8,128)S(1)}, f32[2,64,128]{2,1,0:T(8,128)S(1)}, u32[]{:S(2)}, u32[]{:S(2)}) collective-permute-start(f32[2,64,128]{2,1,0:T(8,128)S(1)} %get-tuple-element.55), channel_id=1, source_target_pairs={{0,1},{1,0},{2,3},{3,2},{4,8},{5,9},{6,10},{7,11},{8,4},{9,5},{10,... | collective-permute-start | bytes 196616 | tf_op jit(solution)/shard_map/ppermute | solution.py:424
  65.8 1.3 %collective-permute-start.27 = (f32[2,64,128]{2,1,0:T(8,128)S(1)}, f32[2,64,128]{2,1,0:T(8,128)S(1)}, u32[]{:S(2)}, u32[]{:S(2)}) collective-permute-start(f32[2,64,128]{2,1,0:T(8,128)S(1)} %fusion.1.mine), channel_id=1, source_target_pairs={{0,1},{1,0},{2,3},{3,2},{4,5},{5,4},{6,7},{7,6},{8,9},{9,8},{10,11... | collective-permute-start | bytes 196616 | tf_op jit(solution)/shard_map/ppermute | solution.py:400
